TPU v7x, 128 devices: a whole 4x4x4 slice. The times are simulated.
128 devices in a mesh: segment: 4 (over x), gy: 32 (over y, z, core).
Axes of the slice: x: 4, y: 4, z: 4, core: 2. Of those that a mesh axis runs over, the one named last changes fastest.
Arguments:
- crops: bfloat16 [2, 32, 4, 128, 128], P(None, None, None, 'gy'), may hold values from -6 to 6
- cotangent: bfloat16 [2, 32, 4, 128, 128], P(None, None, None, 'gy'), may hold values from -0.59765625 to 0.59765625
- weights: bfloat16 [4, 2, 27, 32, 32], P('segment'), may hold values from -0.375 to 0.375
Outputs:
- features: bfloat16 [4, 2, 32, 4, 128, 128], P('segment', None, None, None, 'gy')
- weight_grads: float32 [4, 2, 27, 32, 32], P('segment')
- input_grads: float32 [4, 2, 32, 4, 128, 128], P('segment', None, None, None, 'gy')
All inputs are finite; a program needn't handle non-finite values.
Results may differ from a plain program's by a relative error of at most 0.025.
Values may be sent and summed in bfloat16 or wider, within the bound.
No kernel may reach another device: no remote copies, remote signals or barrier semaphores. Data moves between devices by JAX's collectives and lax.ppermute only.
A program may use at most 128 MiB of HBM per device.

v0:
```python
import jax
import jax.numpy as jnp
from jax import lax
from jax.sharding import PartitionSpec as P


def extended(block, sides, width):
    for axis, dim in sides:
        count = lax.axis_size(axis)
        forward = [(i, i + 1) for i in range(count - 1)]
        backward = [(target, source) for source, target in forward]
        low = lax.ppermute(
            lax.slice_in_dim(block, block.shape[dim] - width, None, axis=dim), axis, forward
        )
        high = lax.ppermute(lax.slice_in_dim(block, 0, width, axis=dim), axis, backward)
        block = jnp.concatenate([low, block, high], axis=dim)
    return block


def from_partner(array, axis, bit):
    return lax.ppermute(array, axis, [(i, i ^ 1 << bit) for i in range(lax.axis_size(axis))])


def passed_along(value, axis, steps):
    count = lax.axis_size(axis)
    first, last = (max(0, -steps), min(count, count - steps))
    return lax.ppermute(value, axis, [(source, source + steps) for source in range(first, last)])


def total_of_pieces(array, axis):
    return lax.all_gather(array, axis).astype(jnp.float32).sum(0)


def slices_of(padded, plane_shift, row_count):
    planes = padded.shape[1] - 2
    across = padded.shape[3] - 2
    return jnp.stack(
        [
            padded[
                :,
                plane_shift : plane_shift + planes,
                row_shift : row_shift + row_count,
                side_shift : side_shift + across,
            ]
            for row_shift in range(3)
            for side_shift in range(3)
        ]
    )


def convolve(padded, kernel, row_count):
    result = None
    for plane_shift in range(3):
        contribution = jnp.einsum(
            "tczyx,tco->ozyx",
            slices_of(padded, plane_shift, row_count),
            kernel[9 * plane_shift : 9 * plane_shift + 9],
            preferred_element_type=jnp.float32,
        )
        result = contribution if result is None else result + contribution
    return result


def kernel_grads(padded, gradient, row_count):
    pieces = []
    for plane_shift in range(3):
        pieces.append(
            jnp.einsum(
                "tczyx,ozyx->tco",
                slices_of(padded, plane_shift, row_count),
                gradient,
                preferred_element_type=jnp.float32,
            )
        )
    return jnp.concatenate(pieces, 0)


def flipped(kernel):
    return jnp.transpose(jnp.flip(kernel, 0), (0, 2, 1))


def slope(preact):
    logistic = jax.nn.sigmoid(preact)
    return logistic * (1.0 + preact * (1.0 - logistic))


def side_pad(volume):
    return jnp.pad(volume, ((0, 0), (1, 1), (0, 0), (1, 1)))


def gradient_rows(volume):
    return side_pad(extended(volume, (("gy", 2),), 1))


def mirror_forward(volume):
    for bit_number in range(2):
        volume = from_partner(volume, "segment", bit_number)
    return volume


def mirror_backward(volume):
    for bit_number in range(2):
        volume = from_partner(volume, "segment", bit_number)
    return volume


def pick(buffer, slot_index):
    return lax.dynamic_index_in_dim(buffer, slot_index, 0, keepdims=False)


def place(buffer, value, slot_index, active):
    return lax.dynamic_update_index_in_dim(
        buffer, jnp.where(active, value, pick(buffer, slot_index)), slot_index, 0
    )


def local(crops, cotangent, weights):
    micro_count, channels, planes, row_count, across = crops.shape
    segment_index = lax.axis_index("segment")
    row_offset = lax.axis_index("gy") * row_count
    all_rows = lax.axis_size("gy") * row_count
    moments = micro_count + 3
    kernel_first = weights[0, 0]
    kernel_second = weights[0, 1]
    block = (channels, planes, row_count, across)
    empty_block = jnp.zeros(block, jnp.bfloat16)
    padded_shape = (micro_count, channels, planes + 2, row_count + 2, across + 2)
    input_store = jnp.zeros(padded_shape, jnp.bfloat16)
    hidden_store = jnp.zeros(padded_shape, jnp.bfloat16)
    first_store = jnp.zeros((micro_count,) + block, jnp.float32)
    second_store = jnp.zeros((micro_count,) + block, jnp.float32)
    feature_store = jnp.zeros((micro_count,) + block, jnp.bfloat16)
    skip_store = jnp.zeros((micro_count,) + block, jnp.bfloat16)
    from_before = empty_block
    for moment in range(moments):
        position = moment - segment_index
        active = (position >= 0) & (position < micro_count)
        slot_index = jnp.clip(position, 0, micro_count - 1)
        entering = jnp.where(segment_index == 0, pick(crops, slot_index), from_before)
        skip_rows = pick(skip_store, slot_index)
        merged = jnp.where(
            segment_index >= 2,
            (entering.astype(jnp.float32) + skip_rows.astype(jnp.float32)).astype(jnp.bfloat16),
            entering,
        )
        widened = side_pad(extended(merged, (("gy", 2),), 2))
        pre_wide = convolve(widened, kernel_first, row_count + 2)
        global_rows = row_offset - 1 + jnp.arange(row_count + 2)
        inside = ((global_rows >= 0) & (global_rows < all_rows))[None, None, :, None]
        hidden_pad = side_pad(jnp.where(inside, jax.nn.silu(pre_wide), 0.0).astype(jnp.bfloat16))
        input_pad = widened[:, :, 1:-1]
        pre_first = pre_wide[:, :, 1:-1]
        pre_second = convolve(hidden_pad, kernel_second, row_count)
        leaving = jax.nn.silu(pre_second).astype(jnp.bfloat16)
        input_store = place(input_store, input_pad, slot_index, active)
        hidden_store = place(hidden_store, hidden_pad, slot_index, active)
        first_store = place(first_store, pre_first, slot_index, active)
        second_store = place(second_store, pre_second, slot_index, active)
        feature_store = place(feature_store, leaving, slot_index, active)
        if moment + 1 < moments:
            arrived_position = moment - (3 - segment_index)
            arrived = (
                (arrived_position >= 0) & (arrived_position < micro_count) & (segment_index >= 2)
            )
            skip_store = place(
                skip_store,
                mirror_forward(entering),
                jnp.clip(arrived_position, 0, micro_count - 1),
                arrived,
            )
            from_before = passed_along(leaving, "segment", 1)
    flip_first = flipped(kernel_first)
    flip_second = flipped(kernel_second)
    grad_sum = jnp.zeros((2,) + kernel_first.shape, jnp.float32)
    grad_store = jnp.zeros((micro_count,) + block, jnp.bfloat16)
    input_grads = jnp.zeros((micro_count,) + block, jnp.float32)
    from_after = empty_block
    for moment in range(moments):
        position = moment - (3 - segment_index)
        active = (position >= 0) & (position < micro_count)
        slot_index = jnp.clip(position, 0, micro_count - 1)
        incoming = jnp.where(segment_index == 3, pick(cotangent, slot_index), from_after)
        second_delta = (
            incoming.astype(jnp.float32) * slope(pick(second_store, slot_index))
        ).astype(jnp.bfloat16)
        grad_second = kernel_grads(pick(hidden_store, slot_index), second_delta, row_count)
        hidden_delta = convolve(gradient_rows(second_delta), flip_second, row_count)
        first_delta = (hidden_delta * slope(pick(first_store, slot_index))).astype(jnp.bfloat16)
        grad_first = kernel_grads(pick(input_store, slot_index), first_delta, row_count)
        grad_sum = grad_sum + jnp.where(active, jnp.stack([grad_first, grad_second]), 0.0)
        delta = convolve(gradient_rows(first_delta), flip_first, row_count).astype(jnp.bfloat16)
        extra = pick(grad_store, slot_index)
        summed = delta.astype(jnp.float32) + extra.astype(jnp.float32)
        input_grads = place(input_grads, summed, slot_index, active)
        passing = jnp.where(segment_index == 1, summed.astype(jnp.bfloat16), delta)
        if moment + 1 < moments:
            arrived_position = moment - segment_index
            arrived = (
                (arrived_position >= 0) & (arrived_position < micro_count) & (segment_index <= 1)
            )
            grad_store = place(
                grad_store,
                mirror_backward(delta),
                jnp.clip(arrived_position, 0, micro_count - 1),
                arrived,
            )
            from_after = passed_along(passing, "segment", -1)
    weight_grads = total_of_pieces(grad_sum.astype(jnp.bfloat16), "gy").astype(jnp.float32)
    return (feature_store[None], weight_grads[None], input_grads[None])


def solution(mesh):
    return jax.shard_map(
        local,
        mesh=mesh,
        in_specs=(
            P(None, None, None, "gy", None),
            P(None, None, None, "gy", None),
            P("segment", None, None, None, None),
        ),
        out_specs=(
            P("segment", None, None, None, "gy", None),
            P("segment", None, None, None, None),
            P("segment", None, None, None, "gy", None),
        ),
        check_vma=False,
    )
```

profile of v0, /device:TPU:1, one launch (start us, length us, event | category | flops | bytes accessed | tf_op | source)
XLA Modules:
  0.0 391.6 jit_solution(16455452685694898195)
XLA Ops:
  7.2 1.4 constant_dynamic-slice_fusion.38
  8.7 2.1 collective-permute-start.3
  10.9 4.4 %collective-permute-start = (bf16[32,4,2,128]{3,0,2,1:T(8,128)(2,1)S(1)}, bf16[32,4,2,128]{3,0,2,1:T(8,128)(2,1)S(1)}, u32[]{:S(2)}, u32[]{:S(2)}) collective-permute-start(bf16[32,4,2,128]{3,0,2,1:T(8,128)(2,1)S(1)} %get-tuple-element.626), channel_id=1, source_target_pairs={{0,1},{1,2},{2,3},{3,4},{4,5},{5,6},{6,7},{7,8},{8,9},{9,10},{10,1... | collective-permute-start | bytes 196616 | tf_op jit(solution)/shard_map/ppermute | solution.py:12
  15.3 1.9 collective-permute-start.1
  17.7 3.2 collective-permute-done.1
  29.8 2.5 collective-permute-start.4
  32.3 1.9 collective-permute-start.2
  35.6 1.5 collective-permute-done.2
  37.2 3.4 collective-permute-start.5
  40.6 1.9 collective-permute-start.6
  42.5 2.5 collective-permute-start.8
  54.9 4.4 %collective-permute-start.9 = (bf16[32,4,4,128]{3,0,2,1:T(8,128)(2,1)S(1)}, bf16[32,4,4,128]{3,0,2,1:T(8,128)(2,1)S(1)}, u32[]{:S(2)}, u32[]{:S(2)}) collective-permute-start(bf16[32,4,4,128]{3,0,2,1:T(8,128)(2,1)S(1)} %collective-permute-done.8), channel_id=1, source_target_pairs={{0,64},{32,96},{64,0},{96,32},{1,65},{33,97},{65,1},{97,33},{2,66}... | collective-permute-start | bytes 393224 | tf_op jit(solution)/shard_map/ppermute | solution.py:21
  60.7 1.4 collective-permute-done.9
  63.6 3.6 collective-permute-start.10
  67.2 1.9 collective-permute-start.11
  69.1 2.5 collective-permute-start.13
  81.5 4.8 %collective-permute-start.14 = (bf16[32,4,4,128]{3,0,2,1:T(8,128)(2,1)S(1)}, bf16[32,4,4,128]{3,0,2,1:T(8,128)(2,1)S(1)}, u32[]{:S(2)}, u32[]{:S(2)}) collective-permute-start(bf16[32,4,4,128]{3,0,2,1:T(8,128)(2,1)S(1)} %collective-permute-done.13), channel_id=1, source_target_pairs={{0,64},{32,96},{64,0},{96,32},{1,65},{33,97},{65,1},{97,33},{2,66}... | collective-permute-start | bytes 393224 | tf_op jit(solution)/shard_map/ppermute | solution.py:21
  87.7 1.4 collective-permute-done.14
  90.5 3.7 collective-permute-start.15
  94.2 1.9 collective-permute-start.16
  96.1 2.5 collective-permute-start.18
  108.5 4.7 %collective-permute-start.19 = (bf16[32,4,4,128]{3,0,2,1:T(8,128)(2,1)S(1)}, bf16[32,4,4,128]{3,0,2,1:T(8,128)(2,1)S(1)}, u32[]{:S(2)}, u32[]{:S(2)}) collective-permute-start(bf16[32,4,4,128]{3,0,2,1:T(8,128)(2,1)S(1)} %collective-permute-done.18), channel_id=1, source_target_pairs={{0,64},{32,96},{64,0},{96,32},{1,65},{33,97},{65,1},{97,33},{2,66}... | collective-permute-start | bytes 393224 | tf_op jit(solution)/shard_map/ppermute | solution.py:21
  117.4 4.3 %collective-permute-start.20 = (bf16[32,4,2,128]{3,0,2,1:T(8,128)(2,1)S(1)}, bf16[32,4,2,128]{3,0,2,1:T(8,128)(2,1)S(1)}, u32[]{:S(2)}, u32[]{:S(2)}) collective-permute-start(bf16[32,4,2,128]{3,0,2,1:T(8,128)(2,1)S(1)} %get-tuple-element.618), channel_id=1, source_target_pairs={{0,1},{1,2},{2,3},{3,4},{4,5},{5,6},{6,7},{7,8},{8,9},{9,10},{10,1... | collective-permute-start | bytes 196616 | tf_op jit(solution)/shard_map/ppermute | solution.py:12
  121.7 2.4 collective-permute-start.21
  124.1 3.1 collective-permute-done.21
  136.6 1.9 collective-permute-start.22
  138.5 2.6 collective-permute-start.23
  165.1 3.2 collective-permute-start.24
  168.3 1.9 collective-permute-start.25
  171.6 2.0 collective-permute-done.25
  178.1 2.9 collective-permute-start.31
  181.1 3.0 collective-permute-done.26
  184.3 2.7 collective-permute-start.27
  187.0 1.9 collective-permute-start.28
  190.3 4.6 %collective-permute-start.32 = (bf16[32,4,4,128]{3,0,2,1:T(8,128)(2,1)S(1)}, bf16[32,4,4,128]{3,0,2,1:T(8,128)(2,1)S(1)}, u32[]{:S(2)}, u32[]{:S(2)}) collective-permute-start(bf16[32,4,4,128]{3,0,2,1:T(8,128)(2,1)S(1)} %collective-permute-done.31), channel_id=1, source_target_pairs={{0,64},{32,96},{64,0},{96,32},{1,65},{33,97},{65,1},{97,33},{2,66}... | collective-permute-start | bytes 393224 | tf_op jit(solution)/shard_map/ppermute | solution.py:21
  198.3 3.9 %collective-permute-start.29 = (bf16[32,4,1,128]{3,0,2,1:T(8,128)(2,1)S(1)}, bf16[32,4,1,128]{3,0,2,1:T(8,128)(2,1)S(1)}, u32[]{:S(2)}, u32[]{:S(2)}) collective-permute-start(bf16[32,4,1,128]{3,0,2,1:T(8,128)(2,1)S(1)} %get-tuple-element.610), channel_id=1, source_target_pairs={{0,1},{1,2},{2,3},{3,4},{4,5},{5,6},{6,7},{7,8},{8,9},{9,10},{10,1... | collective-permute-start | bytes 98312 | tf_op jit(solution)/shard_map/ppermute | solution.py:12
  202.2 1.9 collective-permute-start.30
  205.5 1.9 collective-permute-done.30
  212.1 2.2 collective-permute-start.38
  214.3 3.3 collective-permute-done.33
  217.8 1.9 collective-permute-start.34
  219.8 2.4 collective-permute-start.35
  223.6 2.2 collective-permute-done.35
  229.2 3.3 collective-permute-start.36
  232.5 2.1 collective-permute-start.37
  235.9 3.3 collective-permute-done.37
  243.9 2.2 collective-permute-start.45
  246.1 2.2 collective-permute-done.40
  248.5 3.8 collective-permute-start.41
  252.3 1.9 collective-permute-start.42
  255.6 1.5 collective-permute-start.46
  257.1 3.0 collective-permute-done.42
  263.4 2.2 collective-permute-start.43
  265.5 2.2 collective-permute-start.44
  268.6 5.5 %collective-permute-done.44 = bf16[32,4,1,128]{3,0,2,1:T(8,128)(2,1)S(1)} collective-permute-done((bf16[32,4,1,128]{3,0,2,1:T(8,128)(2,1)S(1)}, bf16[32,4,1,128]{3,0,2,1:T(8,128)(2,1)S(1)}, u32[]{:S(2)}, u32[]{:S(2)}) %collective-permute-start.44) | collective-permute-done | bytes 32800 | tf_op jit(solution)/shard_map/ppermute | solution.py:15
  279.2 3.9 %collective-permute-done.47 = bf16[32,4,4,128]{3,0,2,1:T(8,128)(2,1)S(1)} collective-permute-done((bf16[32,4,4,128]{3,0,2,1:T(8,128)(2,1)S(1)}, bf16[32,4,4,128]{3,0,2,1:T(8,128)(2,1)S(1)}, u32[]{:S(2)}, u32[]{:S(2)}) %collective-permute-start.47) | collective-permute-done | bytes 131104 | tf_op jit(solution)/shard_map/ppermute | solution.py:27
  283.3 3.1 collective-permute-start.48
  286.4 2.1 collective-permute-start.49
  289.9 2.4 collective-permute-done.49
  300.7 2.9 collective-permute-start.50
  303.6 1.9 collective-permute-start.51
  306.9 4.1 %collective-permute-done.51 = bf16[32,4,1,128]{3,0,2,1:T(8,128)(2,1)S(1)} collective-permute-done((bf16[32,4,1,128]{3,0,2,1:T(8,128)(2,1)S(1)}, bf16[32,4,1,128]{3,0,2,1:T(8,128)(2,1)S(1)}, u32[]{:S(2)}, u32[]{:S(2)}) %collective-permute-start.51) | collective-permute-done | bytes 32800 | tf_op jit(solution)/shard_map/ppermute | solution.py:15
  315.5 60.3 %all-gather.2.cloned.1.call-done = bf16[32,2,27,32,32]{4,3,2,1,0:T(8,128)(2,1)} async-done(((bf16[1,2,27,32,32]{4,3,2,1,0:T(8,128)(2,1)}), bf16[32,2,27,32,32]{4,3,2,1,0:T(8,128)(2,1)}) %all-gather.2.cloned.1.call-update) | async-done | bytes 3538960 | tf_op jit(solution)/shard_map/all_gather | solution.py:31
  375.7 8.8 %convert_reduce_fusion = f32[2,27,32,32]{3,2,1,0:T(8,128)} fusion(bf16[32,2,27,32,32]{4,3,2,1,0:T(8,128)(2,1)} %all-gather.2.cloned.1.call-done), kind=kLoop, calls=%fused_computation | loop fusion | flops 3483648 | bytes 3760128 | tf_op jit(solution)/shard_map/reduce_sum | solution.py:31
  (761 shorter events, 133.6 us)
Async XLA Ops:
  7.2 10.1 %copy-start = (bf16[1,2,27,32,32]{4,3,2,1,0:T(8,128)(2,1)S(1)}, bf16[1,2,27,32,32]{4,3,2,1,0:T(8,128)(2,1)}, u32[]{:S(2)}) copy-start(bf16[1,2,27,32,32]{4,3,2,1,0:T(8,128)(2,1)} %param.5) | copy-start | bytes 331780
  7.2 368.5 %all-gather.2.cloned.1.call-start = ((), (), s32[]{:S(2)}) async-start(), calls=%async_computation | async-start | bytes 14598144 | tf_op jit(solution)/shard_map/all_gather | solution.py:31
  8.7 8.7 %copy-start.1 = (bf16[2,32,4,4,128]{4,3,2,1,0:T(4,128)(2,1)S(1)}, bf16[2,32,4,4,128]{4,3,2,1,0:T(4,128)(2,1)}, u32[]{:S(2)}) copy-start(bf16[2,32,4,4,128]{4,3,2,1,0:T(4,128)(2,1)} %param.4) | copy-start | bytes 786436
  8.7 21.1 %collective-permute-start.3 = (bf16[32,4,4,128]{3,0,2,1:T(8,128)(2,1)S(1)}, bf16[32,4,4,128]{3,0,2,1:T(8,128)(2,1)S(1)}, u32[]{:S(2)}, u32[]{:S(2)}) collective-permute-start(bf16[32,4,4,128]{3,0,2,1:T(8,128)(2,1)S(1)} %fusion.576), channel_id=1, source_target_pairs={{0,32},{32,0},{64,96},{96,64},{1,33},{33,1},{65,97},{97,65},{2,34}... | collective-permute-start | bytes 393224 | tf_op jit(solution)/shard_map/ppermute | solution.py:21
  10.9 6.8 %collective-permute-start = (bf16[32,4,2,128]{3,0,2,1:T(8,128)(2,1)S(1)}, bf16[32,4,2,128]{3,0,2,1:T(8,128)(2,1)S(1)}, u32[]{:S(2)}, u32[]{:S(2)}) collective-permute-start(bf16[32,4,2,128]{3,0,2,1:T(8,128)(2,1)S(1)} %get-tuple-element.626), channel_id=1, source_target_pairs={{0,1},{1,2},{2,3},{3,4},{4,5},{5,6},{6,7},{7,8},{8,9},{9,10},{10,1... | collective-permute-start | bytes 196616 | tf_op jit(solution)/shard_map/ppermute | solution.py:12
  15.3 5.6 %collective-permute-start.1 = (bf16[32,4,2,128]{3,0,2,1:T(8,128)(2,1)S(1)}, bf16[32,4,2,128]{3,0,2,1:T(8,128)(2,1)S(1)}, u32[]{:S(2)}, u32[]{:S(2)}) collective-permute-start(bf16[32,4,2,128]{3,0,2,1:T(8,128)(2,1)S(1)} %get-tuple-element.627), channel_id=1, source_target_pairs={{1,0},{2,1},{3,2},{4,3},{5,4},{6,5},{7,6},{8,7},{9,8},{10,9},{11,1... | collective-permute-start | bytes 196616 | tf_op jit(solution)/shard_map/ppermute | solution.py:15
  29.8 5.7 %collective-permute-start.4 = (bf16[32,4,4,128]{3,0,2,1:T(8,128)(2,1)S(1)}, bf16[32,4,4,128]{3,0,2,1:T(8,128)(2,1)S(1)}, u32[]{:S(2)}, u32[]{:S(2)}) collective-permute-start(bf16[32,4,4,128]{3,0,2,1:T(8,128)(2,1)S(1)} %collective-permute-done.3), channel_id=1, source_target_pairs={{0,64},{32,96},{64,0},{96,32},{1,65},{33,97},{65,1},{97,33},{2,66}... | collective-permute-start | bytes 393224 | tf_op jit(solution)/shard_map/ppermute | solution.py:21
  32.3 4.7 %collective-permute-start.2 = (bf16[32,4,4,128]{3,0,2,1:T(8,128)(2,1)S(1)}, bf16[32,4,4,128]{3,0,2,1:T(8,128)(2,1)S(1)}, u32[]{:S(2)}, u32[]{:S(2)}) collective-permute-start(bf16[32,4,4,128]{3,0,2,1:T(8,128)(2,1)S(1)} %get-tuple-element.38), channel_id=1, source_target_pairs={{0,32},{32,64},{64,96},{1,33},{33,65},{65,97},{2,34},{34,66},{66,9... | collective-permute-start | bytes 393224 | tf_op jit(solution)/shard_map/ppermute | solution.py:27
  37.2 7.8 %collective-permute-start.5 = (bf16[32,4,2,128]{3,0,2,1:T(8,128)(2,1)S(1)}, bf16[32,4,2,128]{3,0,2,1:T(8,128)(2,1)S(1)}, u32[]{:S(2)}, u32[]{:S(2)}) collective-permute-start(bf16[32,4,2,128]{3,0,2,1:T(8,128)(2,1)S(1)} %get-tuple-element.624), channel_id=1, source_target_pairs={{0,1},{1,2},{2,3},{3,4},{4,5},{5,6},{6,7},{7,8},{8,9},{9,10},{10,1... | collective-permute-start | bytes 196616 | tf_op jit(solution)/shard_map/ppermute | solution.py:12
  40.6 5.6 %collective-permute-start.6 = (bf16[32,4,2,128]{3,0,2,1:T(8,128)(2,1)S(1)}, bf16[32,4,2,128]{3,0,2,1:T(8,128)(2,1)S(1)}, u32[]{:S(2)}, u32[]{:S(2)}) collective-permute-start(bf16[32,4,2,128]{3,0,2,1:T(8,128)(2,1)S(1)} %get-tuple-element.625), channel_id=1, source_target_pairs={{1,0},{2,1},{3,2},{4,3},{5,4},{6,5},{7,6},{8,7},{9,8},{10,9},{11,1... | collective-permute-start | bytes 196616 | tf_op jit(solution)/shard_map/ppermute | solution.py:15
  42.5 12.4 %collective-permute-start.8 = (bf16[32,4,4,128]{3,0,2,1:T(8,128)(2,1)S(1)}, bf16[32,4,4,128]{3,0,2,1:T(8,128)(2,1)S(1)}, u32[]{:S(2)}, u32[]{:S(2)}) collective-permute-start(bf16[32,4,4,128]{3,0,2,1:T(8,128)(2,1)S(1)} %get-tuple-element.36), channel_id=1, source_target_pairs={{0,32},{32,0},{64,96},{96,64},{1,33},{33,1},{65,97},{97,65},{2,34}... | collective-permute-start | bytes 393224 | tf_op jit(solution)/shard_map/ppermute | solution.py:21
  54.9 7.2 %collective-permute-start.9 = (bf16[32,4,4,128]{3,0,2,1:T(8,128)(2,1)S(1)}, bf16[32,4,4,128]{3,0,2,1:T(8,128)(2,1)S(1)}, u32[]{:S(2)}, u32[]{:S(2)}) collective-permute-start(bf16[32,4,4,128]{3,0,2,1:T(8,128)(2,1)S(1)} %collective-permute-done.8), channel_id=1, source_target_pairs={{0,64},{32,96},{64,0},{96,32},{1,65},{33,97},{65,1},{97,33},{2,66}... | collective-permute-start | bytes 393224 | tf_op jit(solution)/shard_map/ppermute | solution.py:21
  59.3 4.1 %collective-permute-start.7 = (bf16[32,4,4,128]{3,0,2,1:T(8,128)(2,1)S(1)}, bf16[32,4,4,128]{3,0,2,1:T(8,128)(2,1)S(1)}, u32[]{:S(2)}, u32[]{:S(2)}) collective-permute-start(bf16[32,4,4,128]{3,0,2,1:T(8,128)(2,1)S(1)} %get-tuple-element.32), channel_id=1, source_target_pairs={{0,32},{32,64},{64,96},{1,33},{33,65},{65,97},{2,34},{34,66},{66,9... | collective-permute-start | bytes 393224 | tf_op jit(solution)/shard_map/ppermute | solution.py:27
  63.6 8.1 %collective-permute-start.10 = (bf16[32,4,2,128]{3,0,2,1:T(8,128)(2,1)S(1)}, bf16[32,4,2,128]{3,0,2,1:T(8,128)(2,1)S(1)}, u32[]{:S(2)}, u32[]{:S(2)}) collective-permute-start(bf16[32,4,2,128]{3,0,2,1:T(8,128)(2,1)S(1)} %get-tuple-element.622), channel_id=1, source_target_pairs={{0,1},{1,2},{2,3},{3,4},{4,5},{5,6},{6,7},{7,8},{8,9},{9,10},{10,1... | collective-permute-start | bytes 196616 | tf_op jit(solution)/shard_map/ppermute | solution.py:12
  67.2 5.6 %collective-permute-start.11 = (bf16[32,4,2,128]{3,0,2,1:T(8,128)(2,1)S(1)}, bf16[32,4,2,128]{3,0,2,1:T(8,128)(2,1)S(1)}, u32[]{:S(2)}, u32[]{:S(2)}) collective-permute-start(bf16[32,4,2,128]{3,0,2,1:T(8,128)(2,1)S(1)} %get-tuple-element.623), channel_id=1, source_target_pairs={{1,0},{2,1},{3,2},{4,3},{5,4},{6,5},{7,6},{8,7},{9,8},{10,9},{11,1... | collective-permute-start | bytes 196616 | tf_op jit(solution)/shard_map/ppermute | solution.py:15
  69.1 12.4 %collective-permute-start.13 = (bf16[32,4,4,128]{3,0,2,1:T(8,128)(2,1)S(1)}, bf16[32,4,4,128]{3,0,2,1:T(8,128)(2,1)S(1)}, u32[]{:S(2)}, u32[]{:S(2)}) collective-permute-start(bf16[32,4,4,128]{3,0,2,1:T(8,128)(2,1)S(1)} %get-tuple-element.30), channel_id=1, source_target_pairs={{0,32},{32,0},{64,96},{96,64},{1,33},{33,1},{65,97},{97,65},{2,34}... | collective-permute-start | bytes 393224 | tf_op jit(solution)/shard_map/ppermute | solution.py:21
  81.5 7.5 %collective-permute-start.14 = (bf16[32,4,4,128]{3,0,2,1:T(8,128)(2,1)S(1)}, bf16[32,4,4,128]{3,0,2,1:T(8,128)(2,1)S(1)}, u32[]{:S(2)}, u32[]{:S(2)}) collective-permute-start(bf16[32,4,4,128]{3,0,2,1:T(8,128)(2,1)S(1)} %collective-permute-done.13), channel_id=1, source_target_pairs={{0,64},{32,96},{64,0},{96,32},{1,65},{33,97},{65,1},{97,33},{2,66}... | collective-permute-start | bytes 393224 | tf_op jit(solution)/shard_map/ppermute | solution.py:21
  86.3 4.1 %collective-permute-start.12 = (bf16[32,4,4,128]{3,0,2,1:T(8,128)(2,1)S(1)}, bf16[32,4,4,128]{3,0,2,1:T(8,128)(2,1)S(1)}, u32[]{:S(2)}, u32[]{:S(2)}) collective-permute-start(bf16[32,4,4,128]{3,0,2,1:T(8,128)(2,1)S(1)} %get-tuple-element.26), channel_id=1, source_target_pairs={{0,32},{32,64},{64,96},{1,33},{33,65},{65,97},{2,34},{34,66},{66,9... | collective-permute-start | bytes 393224 | tf_op jit(solution)/shard_map/ppermute | solution.py:27
  90.5 8.2 %collective-permute-start.15 = (bf16[32,4,2,128]{3,0,2,1:T(8,128)(2,1)S(1)}, bf16[32,4,2,128]{3,0,2,1:T(8,128)(2,1)S(1)}, u32[]{:S(2)}, u32[]{:S(2)}) collective-permute-start(bf16[32,4,2,128]{3,0,2,1:T(8,128)(2,1)S(1)} %get-tuple-element.620), channel_id=1, source_target_pairs={{0,1},{1,2},{2,3},{3,4},{4,5},{5,6},{6,7},{7,8},{8,9},{9,10},{10,1... | collective-permute-start | bytes 196616 | tf_op jit(solution)/shard_map/ppermute | solution.py:12
  94.2 5.6 %collective-permute-start.16 = (bf16[32,4,2,128]{3,0,2,1:T(8,128)(2,1)S(1)}, bf16[32,4,2,128]{3,0,2,1:T(8,128)(2,1)S(1)}, u32[]{:S(2)}, u32[]{:S(2)}) collective-permute-start(bf16[32,4,2,128]{3,0,2,1:T(8,128)(2,1)S(1)} %get-tuple-element.621), channel_id=1, source_target_pairs={{1,0},{2,1},{3,2},{4,3},{5,4},{6,5},{7,6},{8,7},{9,8},{10,9},{11,1... | collective-permute-start | bytes 196616 | tf_op jit(solution)/shard_map/ppermute | solution.py:15
  96.1 12.3 %collective-permute-start.18 = (bf16[32,4,4,128]{3,0,2,1:T(8,128)(2,1)S(1)}, bf16[32,4,4,128]{3,0,2,1:T(8,128)(2,1)S(1)}, u32[]{:S(2)}, u32[]{:S(2)}) collective-permute-start(bf16[32,4,4,128]{3,0,2,1:T(8,128)(2,1)S(1)} %get-tuple-element.24), channel_id=1, source_target_pairs={{0,32},{32,0},{64,96},{96,64},{1,33},{33,1},{65,97},{97,65},{2,34}... | collective-permute-start | bytes 393224 | tf_op jit(solution)/shard_map/ppermute | solution.py:21
  108.5 7.4 %collective-permute-start.19 = (bf16[32,4,4,128]{3,0,2,1:T(8,128)(2,1)S(1)}, bf16[32,4,4,128]{3,0,2,1:T(8,128)(2,1)S(1)}, u32[]{:S(2)}, u32[]{:S(2)}) collective-permute-start(bf16[32,4,4,128]{3,0,2,1:T(8,128)(2,1)S(1)} %collective-permute-done.18), channel_id=1, source_target_pairs={{0,64},{32,96},{64,0},{96,32},{1,65},{33,97},{65,1},{97,33},{2,66}... | collective-permute-start | bytes 393224 | tf_op jit(solution)/shard_map/ppermute | solution.py:21
  113.2 4.1 %collective-permute-start.17 = (bf16[32,4,4,128]{3,0,2,1:T(8,128)(2,1)S(1)}, bf16[32,4,4,128]{3,0,2,1:T(8,128)(2,1)S(1)}, u32[]{:S(2)}, u32[]{:S(2)}) collective-permute-start(bf16[32,4,4,128]{3,0,2,1:T(8,128)(2,1)S(1)} %get-tuple-element.20), channel_id=1, source_target_pairs={{0,32},{32,64},{64,96},{1,33},{33,65},{65,97},{2,34},{34,66},{66,9... | collective-permute-start | bytes 393224 | tf_op jit(solution)/shard_map/ppermute | solution.py:27
  117.4 6.7 %collective-permute-start.20 = (bf16[32,4,2,128]{3,0,2,1:T(8,128)(2,1)S(1)}, bf16[32,4,2,128]{3,0,2,1:T(8,128)(2,1)S(1)}, u32[]{:S(2)}, u32[]{:S(2)}) collective-permute-start(bf16[32,4,2,128]{3,0,2,1:T(8,128)(2,1)S(1)} %get-tuple-element.618), channel_id=1, source_target_pairs={{0,1},{1,2},{2,3},{3,4},{4,5},{5,6},{6,7},{7,8},{8,9},{9,10},{10,1... | collective-permute-start | bytes 196616 | tf_op jit(solution)/shard_map/ppermute | solution.py:12
  121.7 5.6 %collective-permute-start.21 = (bf16[32,4,2,128]{3,0,2,1:T(8,128)(2,1)S(1)}, bf16[32,4,2,128]{3,0,2,1:T(8,128)(2,1)S(1)}, u32[]{:S(2)}, u32[]{:S(2)}) collective-permute-start(bf16[32,4,2,128]{3,0,2,1:T(8,128)(2,1)S(1)} %get-tuple-element.619), channel_id=1, source_target_pairs={{1,0},{2,1},{3,2},{4,3},{5,4},{6,5},{7,6},{8,7},{9,8},{10,9},{11,1... | collective-permute-start | bytes 196616 | tf_op jit(solution)/shard_map/ppermute | solution.py:15
  136.6 25.2 %collective-permute-start.22 = (bf16[32,4,1,128]{3,0,2,1:T(8,128)(2,1)S(1)}, bf16[32,4,1,128]{3,0,2,1:T(8,128)(2,1)S(1)}, u32[]{:S(2)}, u32[]{:S(2)}) collective-permute-start(bf16[32,4,1,128]{3,0,2,1:T(8,128)(2,1)S(1)} %get-tuple-element.616), channel_id=1, source_target_pairs={{0,1},{1,2},{2,3},{3,4},{4,5},{5,6},{6,7},{7,8},{8,9},{9,10},{10,1... | collective-permute-start | bytes 98312 | tf_op jit(solution)/shard_map/ppermute | solution.py:12
  138.5 23.2 %collective-permute-start.23 = (bf16[32,4,1,128]{3,0,2,1:T(8,128)(2,1)S(1)}, bf16[32,4,1,128]{3,0,2,1:T(8,128)(2,1)S(1)}, u32[]{:S(2)}, u32[]{:S(2)}) collective-permute-start(bf16[32,4,1,128]{3,0,2,1:T(8,128)(2,1)S(1)} %get-tuple-element.617), channel_id=1, source_target_pairs={{1,0},{2,1},{3,2},{4,3},{5,4},{6,5},{7,6},{8,7},{9,8},{10,9},{11,1... | collective-permute-start | bytes 98312 | tf_op jit(solution)/shard_map/ppermute | solution.py:15
  165.1 6.4 %collective-permute-start.24 = (bf16[32,4,1,128]{3,0,2,1:T(8,128)(2,1)S(1)}, bf16[32,4,1,128]{3,0,2,1:T(8,128)(2,1)S(1)}, u32[]{:S(2)}, u32[]{:S(2)}) collective-permute-start(bf16[32,4,1,128]{3,0,2,1:T(8,128)(2,1)S(1)} %get-tuple-element.614), channel_id=1, source_target_pairs={{0,1},{1,2},{2,3},{3,4},{4,5},{5,6},{6,7},{7,8},{8,9},{9,10},{10,1... | collective-permute-start | bytes 98312 | tf_op jit(solution)/shard_map/ppermute | solution.py:12
  168.3 5.2 %collective-permute-start.25 = (bf16[32,4,1,128]{3,0,2,1:T(8,128)(2,1)S(1)}, bf16[32,4,1,128]{3,0,2,1:T(8,128)(2,1)S(1)}, u32[]{:S(2)}, u32[]{:S(2)}) collective-permute-start(bf16[32,4,1,128]{3,0,2,1:T(8,128)(2,1)S(1)} %get-tuple-element.615), channel_id=1, source_target_pairs={{1,0},{2,1},{3,2},{4,3},{5,4},{6,5},{7,6},{8,7},{9,8},{10,9},{11,1... | collective-permute-start | bytes 98312 | tf_op jit(solution)/shard_map/ppermute | solution.py:15
  176.8 7.3 %collective-permute-start.26 = (bf16[32,4,4,128]{3,0,2,1:T(8,128)(2,1)S(1)}, bf16[32,4,4,128]{3,0,2,1:T(8,128)(2,1)S(1)}, u32[]{:S(2)}, u32[]{:S(2)}) collective-permute-start(bf16[32,4,4,128]{3,0,2,1:T(8,128)(2,1)S(1)} %get-tuple-element.16), channel_id=1, source_target_pairs={{32,0},{64,32},{96,64},{33,1},{65,33},{97,65},{34,2},{66,34},{98,6... | collective-permute-start | bytes 393224 | tf_op jit(solution)/shard_map/ppermute | solution.py:27
  178.1 12.2 %collective-permute-start.31 = (bf16[32,4,4,128]{3,0,2,1:T(8,128)(2,1)S(1)}, bf16[32,4,4,128]{3,0,2,1:T(8,128)(2,1)S(1)}, u32[]{:S(2)}, u32[]{:S(2)}) collective-permute-start(bf16[32,4,4,128]{3,0,2,1:T(8,128)(2,1)S(1)} %get-tuple-element.16), channel_id=1, source_target_pairs={{0,32},{32,0},{64,96},{96,64},{1,33},{33,1},{65,97},{97,65},{2,34}... | collective-permute-start | bytes 393224 | tf_op jit(solution)/shard_map/ppermute | solution.py:21
  184.3 10.7 %collective-permute-start.27 = (bf16[32,4,1,128]{3,0,2,1:T(8,128)(2,1)S(1)}, bf16[32,4,1,128]{3,0,2,1:T(8,128)(2,1)S(1)}, u32[]{:S(2)}, u32[]{:S(2)}) collective-permute-start(bf16[32,4,1,128]{3,0,2,1:T(8,128)(2,1)S(1)} %get-tuple-element.612), channel_id=1, source_target_pairs={{0,1},{1,2},{2,3},{3,4},{4,5},{5,6},{6,7},{7,8},{8,9},{9,10},{10,1... | collective-permute-start | bytes 98312 | tf_op jit(solution)/shard_map/ppermute | solution.py:12
  187.0 8.0 %collective-permute-start.28 = (bf16[32,4,1,128]{3,0,2,1:T(8,128)(2,1)S(1)}, bf16[32,4,1,128]{3,0,2,1:T(8,128)(2,1)S(1)}, u32[]{:S(2)}, u32[]{:S(2)}) collective-permute-start(bf16[32,4,1,128]{3,0,2,1:T(8,128)(2,1)S(1)} %get-tuple-element.613), channel_id=1, source_target_pairs={{1,0},{2,1},{3,2},{4,3},{5,4},{6,5},{7,6},{8,7},{9,8},{10,9},{11,1... | collective-permute-start | bytes 98312 | tf_op jit(solution)/shard_map/ppermute | solution.py:15
  190.3 20.2 %collective-permute-start.32 = (bf16[32,4,4,128]{3,0,2,1:T(8,128)(2,1)S(1)}, bf16[32,4,4,128]{3,0,2,1:T(8,128)(2,1)S(1)}, u32[]{:S(2)}, u32[]{:S(2)}) collective-permute-start(bf16[32,4,4,128]{3,0,2,1:T(8,128)(2,1)S(1)} %collective-permute-done.31), channel_id=1, source_target_pairs={{0,64},{32,96},{64,0},{96,32},{1,65},{33,97},{65,1},{97,33},{2,66}... | collective-permute-start | bytes 393224 | tf_op jit(solution)/shard_map/ppermute | solution.py:21
  198.3 7.2 %collective-permute-start.29 = (bf16[32,4,1,128]{3,0,2,1:T(8,128)(2,1)S(1)}, bf16[32,4,1,128]{3,0,2,1:T(8,128)(2,1)S(1)}, u32[]{:S(2)}, u32[]{:S(2)}) collective-permute-start(bf16[32,4,1,128]{3,0,2,1:T(8,128)(2,1)S(1)} %get-tuple-element.610), channel_id=1, source_target_pairs={{0,1},{1,2},{2,3},{3,4},{4,5},{5,6},{6,7},{7,8},{8,9},{9,10},{10,1... | collective-permute-start | bytes 98312 | tf_op jit(solution)/shard_map/ppermute | solution.py:12
  202.2 5.2 %collective-permute-start.30 = (bf16[32,4,1,128]{3,0,2,1:T(8,128)(2,1)S(1)}, bf16[32,4,1,128]{3,0,2,1:T(8,128)(2,1)S(1)}, u32[]{:S(2)}, u32[]{:S(2)}) collective-permute-start(bf16[32,4,1,128]{3,0,2,1:T(8,128)(2,1)S(1)} %get-tuple-element.611), channel_id=1, source_target_pairs={{1,0},{2,1},{3,2},{4,3},{5,4},{6,5},{7,6},{8,7},{9,8},{10,9},{11,1... | collective-permute-start | bytes 98312 | tf_op jit(solution)/shard_map/ppermute | solution.py:15
  210.8 6.9 %collective-permute-start.33 = (bf16[32,4,4,128]{3,0,2,1:T(8,128)(2,1)S(1)}, bf16[32,4,4,128]{3,0,2,1:T(8,128)(2,1)S(1)}, u32[]{:S(2)}, u32[]{:S(2)}) collective-permute-start(bf16[32,4,4,128]{3,0,2,1:T(8,128)(2,1)S(1)} %fusion.276), channel_id=1, source_target_pairs={{32,0},{64,32},{96,64},{33,1},{65,33},{97,65},{34,2},{66,34},{98,6... | collective-permute-start | bytes 393224 | tf_op jit(solution)/shard_map/ppermute | solution.py:27
  212.1 11.4 %collective-permute-start.38 = (bf16[32,4,4,128]{3,0,2,1:T(8,128)(2,1)S(1)}, bf16[32,4,4,128]{3,0,2,1:T(8,128)(2,1)S(1)}, u32[]{:S(2)}, u32[]{:S(2)}) collective-permute-start(bf16[32,4,4,128]{3,0,2,1:T(8,128)(2,1)S(1)} %get-tuple-element.14), channel_id=1, source_target_pairs={{0,32},{32,0},{64,96},{96,64},{1,33},{33,1},{65,97},{97,65},{2,34}... | collective-permute-start | bytes 393224 | tf_op jit(solution)/shard_map/ppermute | solution.py:21
  217.8 5.8 %collective-permute-start.34 = (bf16[32,4,1,128]{3,0,2,1:T(8,128)(2,1)S(1)}, bf16[32,4,1,128]{3,0,2,1:T(8,128)(2,1)S(1)}, u32[]{:S(2)}, u32[]{:S(2)}) collective-permute-start(bf16[32,4,1,128]{3,0,2,1:T(8,128)(2,1)S(1)} %get-tuple-element.608), channel_id=1, source_target_pairs={{0,1},{1,2},{2,3},{3,4},{4,5},{5,6},{6,7},{7,8},{8,9},{9,10},{10,1... | collective-permute-start | bytes 98312 | tf_op jit(solution)/shard_map/ppermute | solution.py:12
  219.8 6.1 %collective-permute-start.35 = (bf16[32,4,1,128]{3,0,2,1:T(8,128)(2,1)S(1)}, bf16[32,4,1,128]{3,0,2,1:T(8,128)(2,1)S(1)}, u32[]{:S(2)}, u32[]{:S(2)}) collective-permute-start(bf16[32,4,1,128]{3,0,2,1:T(8,128)(2,1)S(1)} %get-tuple-element.609), channel_id=1, source_target_pairs={{1,0},{2,1},{3,2},{4,3},{5,4},{6,5},{7,6},{8,7},{9,8},{10,9},{11,1... | collective-permute-start | bytes 98312 | tf_op jit(solution)/shard_map/ppermute | solution.py:15
  223.5 18.8 %collective-permute-start.39 = (bf16[32,4,4,128]{3,0,2,1:T(8,128)(2,1)S(1)}, bf16[32,4,4,128]{3,0,2,1:T(8,128)(2,1)S(1)}, u32[]{:S(2)}, u32[]{:S(2)}) collective-permute-start(bf16[32,4,4,128]{3,0,2,1:T(8,128)(2,1)S(1)} %collective-permute-done.38), channel_id=1, source_target_pairs={{0,64},{32,96},{64,0},{96,32},{1,65},{33,97},{65,1},{97,33},{2,66}... | collective-permute-start | bytes 393224 | tf_op jit(solution)/shard_map/ppermute | solution.py:21
  229.2 6.8 %collective-permute-start.36 = (bf16[32,4,1,128]{3,0,2,1:T(8,128)(2,1)S(1)}, bf16[32,4,1,128]{3,0,2,1:T(8,128)(2,1)S(1)}, u32[]{:S(2)}, u32[]{:S(2)}) collective-permute-start(bf16[32,4,1,128]{3,0,2,1:T(8,128)(2,1)S(1)} %get-tuple-element.606), channel_id=1, source_target_pairs={{0,1},{1,2},{2,3},{3,4},{4,5},{5,6},{6,7},{7,8},{8,9},{9,10},{10,1... | collective-permute-start | bytes 98312 | tf_op jit(solution)/shard_map/ppermute | solution.py:12
  232.5 6.8 %collective-permute-start.37 = (bf16[32,4,1,128]{3,0,2,1:T(8,128)(2,1)S(1)}, bf16[32,4,1,128]{3,0,2,1:T(8,128)(2,1)S(1)}, u32[]{:S(2)}, u32[]{:S(2)}) collective-permute-start(bf16[32,4,1,128]{3,0,2,1:T(8,128)(2,1)S(1)} %get-tuple-element.607), channel_id=1, source_target_pairs={{1,0},{2,1},{3,2},{4,3},{5,4},{6,5},{7,6},{8,7},{9,8},{10,9},{11,1... | collective-permute-start | bytes 98312 | tf_op jit(solution)/shard_map/ppermute | solution.py:15
  242.6 5.7 %collective-permute-start.40 = (bf16[32,4,4,128]{3,0,2,1:T(8,128)(2,1)S(1)}, bf16[32,4,4,128]{3,0,2,1:T(8,128)(2,1)S(1)}, u32[]{:S(2)}, u32[]{:S(2)}) collective-permute-start(bf16[32,4,4,128]{3,0,2,1:T(8,128)(2,1)S(1)} %fusion.275), channel_id=1, source_target_pairs={{32,0},{64,32},{96,64},{33,1},{65,33},{97,65},{34,2},{66,34},{98,6... | collective-permute-start | bytes 393224 | tf_op jit(solution)/shard_map/ppermute | solution.py:27
  243.9 11.7 %collective-permute-start.45 = (bf16[32,4,4,128]{3,0,2,1:T(8,128)(2,1)S(1)}, bf16[32,4,4,128]{3,0,2,1:T(8,128)(2,1)S(1)}, u32[]{:S(2)}, u32[]{:S(2)}) collective-permute-start(bf16[32,4,4,128]{3,0,2,1:T(8,128)(2,1)S(1)} %get-tuple-element.12), channel_id=1, source_target_pairs={{0,32},{32,0},{64,96},{96,64},{1,33},{33,1},{65,97},{97,65},{2,34}... | collective-permute-start | bytes 393224 | tf_op jit(solution)/shard_map/ppermute | solution.py:21
  248.5 8.7 %collective-permute-start.41 = (bf16[32,4,1,128]{3,0,2,1:T(8,128)(2,1)S(1)}, bf16[32,4,1,128]{3,0,2,1:T(8,128)(2,1)S(1)}, u32[]{:S(2)}, u32[]{:S(2)}) collective-permute-start(bf16[32,4,1,128]{3,0,2,1:T(8,128)(2,1)S(1)} %get-tuple-element.604), channel_id=1, source_target_pairs={{0,1},{1,2},{2,3},{3,4},{4,5},{5,6},{6,7},{7,8},{8,9},{9,10},{10,1... | collective-permute-start | bytes 98312 | tf_op jit(solution)/shard_map/ppermute | solution.py:12
  252.3 7.8 %collective-permute-start.42 = (bf16[32,4,1,128]{3,0,2,1:T(8,128)(2,1)S(1)}, bf16[32,4,1,128]{3,0,2,1:T(8,128)(2,1)S(1)}, u32[]{:S(2)}, u32[]{:S(2)}) collective-permute-start(bf16[32,4,1,128]{3,0,2,1:T(8,128)(2,1)S(1)} %get-tuple-element.605), channel_id=1, source_target_pairs={{1,0},{2,1},{3,2},{4,3},{5,4},{6,5},{7,6},{8,7},{9,8},{10,9},{11,1... | collective-permute-start | bytes 98312 | tf_op jit(solution)/shard_map/ppermute | solution.py:15
  255.6 21.6 %collective-permute-start.46 = (bf16[32,4,4,128]{3,0,2,1:T(8,128)(2,1)S(1)}, bf16[32,4,4,128]{3,0,2,1:T(8,128)(2,1)S(1)}, u32[]{:S(2)}, u32[]{:S(2)}) collective-permute-start(bf16[32,4,4,128]{3,0,2,1:T(8,128)(2,1)S(1)} %collective-permute-done.45), channel_id=1, source_target_pairs={{0,64},{32,96},{64,0},{96,32},{1,65},{33,97},{65,1},{97,33},{2,66}... | collective-permute-start | bytes 393224 | tf_op jit(solution)/shard_map/ppermute | solution.py:21
  263.4 5.2 %collective-permute-start.43 = (bf16[32,4,1,128]{3,0,2,1:T(8,128)(2,1)S(1)}, bf16[32,4,1,128]{3,0,2,1:T(8,128)(2,1)S(1)}, u32[]{:S(2)}, u32[]{:S(2)}) collective-permute-start(bf16[32,4,1,128]{3,0,2,1:T(8,128)(2,1)S(1)} %get-tuple-element.602), channel_id=1, source_target_pairs={{0,1},{1,2},{2,3},{3,4},{4,5},{5,6},{6,7},{7,8},{8,9},{9,10},{10,1... | collective-permute-start | bytes 98312 | tf_op jit(solution)/shard_map/ppermute | solution.py:12
  265.5 8.5 %collective-permute-start.44 = (bf16[32,4,1,128]{3,0,2,1:T(8,128)(2,1)S(1)}, bf16[32,4,1,128]{3,0,2,1:T(8,128)(2,1)S(1)}, u32[]{:S(2)}, u32[]{:S(2)}) collective-permute-start(bf16[32,4,1,128]{3,0,2,1:T(8,128)(2,1)S(1)} %get-tuple-element.603), channel_id=1, source_target_pairs={{1,0},{2,1},{3,2},{4,3},{5,4},{6,5},{7,6},{8,7},{9,8},{10,9},{11,1... | collective-permute-start | bytes 98312 | tf_op jit(solution)/shard_map/ppermute | solution.py:15
  277.5 5.7 %collective-permute-start.47 = (bf16[32,4,4,128]{3,0,2,1:T(8,128)(2,1)S(1)}, bf16[32,4,4,128]{3,0,2,1:T(8,128)(2,1)S(1)}, u32[]{:S(2)}, u32[]{:S(2)}) collective-permute-start(bf16[32,4,4,128]{3,0,2,1:T(8,128)(2,1)S(1)} %fusion.274), channel_id=1, source_target_pairs={{32,0},{64,32},{96,64},{33,1},{65,33},{97,65},{34,2},{66,34},{98,6... | collective-permute-start | bytes 393224 | tf_op jit(solution)/shard_map/ppermute | solution.py:27
  283.3 6.6 %collective-permute-start.48 = (bf16[32,4,1,128]{3,0,2,1:T(8,128)(2,1)S(1)}, bf16[32,4,1,128]{3,0,2,1:T(8,128)(2,1)S(1)}, u32[]{:S(2)}, u32[]{:S(2)}) collective-permute-start(bf16[32,4,1,128]{3,0,2,1:T(8,128)(2,1)S(1)} %get-tuple-element.600), channel_id=1, source_target_pairs={{0,1},{1,2},{2,3},{3,4},{4,5},{5,6},{6,7},{7,8},{8,9},{9,10},{10,1... | collective-permute-start | bytes 98312 | tf_op jit(solution)/shard_map/ppermute | solution.py:12
  286.4 5.9 %collective-permute-start.49 = (bf16[32,4,1,128]{3,0,2,1:T(8,128)(2,1)S(1)}, bf16[32,4,1,128]{3,0,2,1:T(8,128)(2,1)S(1)}, u32[]{:S(2)}, u32[]{:S(2)}) collective-permute-start(bf16[32,4,1,128]{3,0,2,1:T(8,128)(2,1)S(1)} %get-tuple-element.601), channel_id=1, source_target_pairs={{1,0},{2,1},{3,2},{4,3},{5,4},{6,5},{7,6},{8,7},{9,8},{10,9},{11,1... | collective-permute-start | bytes 98312 | tf_op jit(solution)/shard_map/ppermute | solution.py:15
  299.3 6.3 %collective-permute-start.52 = (bf16[32,4,4,128]{3,0,2,1:T(8,128)(2,1)S(1)}, bf16[32,4,4,128]{3,0,2,1:T(8,128)(2,1)S(1)}, u32[]{:S(2)}, u32[]{:S(2)}) collective-permute-start(bf16[32,4,4,128]{3,0,2,1:T(8,128)(2,1)S(1)} %get-tuple-element.10), channel_id=1, source_target_pairs={{0,32},{32,0},{64,96},{96,64},{1,33},{33,1},{65,97},{97,65},{2,34}... | collective-permute-start | bytes 393224 | tf_op jit(solution)/shard_map/ppermute | solution.py:21
  300.7 6.3 %collective-permute-start.50 = (bf16[32,4,1,128]{3,0,2,1:T(8,128)(2,1)S(1)}, bf16[32,4,1,128]{3,0,2,1:T(8,128)(2,1)S(1)}, u32[]{:S(2)}, u32[]{:S(2)}) collective-permute-start(bf16[32,4,1,128]{3,0,2,1:T(8,128)(2,1)S(1)} %get-tuple-element.598), channel_id=1, source_target_pairs={{0,1},{1,2},{2,3},{3,4},{4,5},{5,6},{6,7},{7,8},{8,9},{9,10},{10,1... | collective-permute-start | bytes 98312 | tf_op jit(solution)/shard_map/ppermute | solution.py:12
  303.6 7.4 %collective-permute-start.51 = (bf16[32,4,1,128]{3,0,2,1:T(8,128)(2,1)S(1)}, bf16[32,4,1,128]{3,0,2,1:T(8,128)(2,1)S(1)}, u32[]{:S(2)}, u32[]{:S(2)}) collective-permute-start(bf16[32,4,1,128]{3,0,2,1:T(8,128)(2,1)S(1)} %get-tuple-element.599), channel_id=1, source_target_pairs={{1,0},{2,1},{3,2},{4,3},{5,4},{6,5},{7,6},{8,7},{9,8},{10,9},{11,1... | collective-permute-start | bytes 98312 | tf_op jit(solution)/shard_map/ppermute | solution.py:15
  305.6 8.5 %collective-permute-start.53 = (bf16[32,4,4,128]{3,0,2,1:T(8,128)(2,1)S(1)}, bf16[32,4,4,128]{3,0,2,1:T(8,128)(2,1)S(1)}, u32[]{:S(2)}, u32[]{:S(2)}) collective-permute-start(bf16[32,4,4,128]{3,0,2,1:T(8,128)(2,1)S(1)} %collective-permute-done.52), channel_id=1, source_target_pairs={{0,64},{32,96},{64,0},{96,32},{1,65},{33,97},{65,1},{97,33},{2,66}... | collective-permute-start | bytes 393224 | tf_op jit(solution)/shard_map/ppermute | solution.py:21
Sparse Core Ops, SparseCore 0:
  298.4 77.2 all-gather.1
where the time goes:
time: 399 us; the launch traced here: 392 us
  starting transfers between devices  132 us (33%)
  waiting for transfers between devices  118 us (30%)
  local copies, waits for them, and re-layouts  63.9 us (16%)
  matrix products  36.5 us (9%)
  other arithmetic  21.3 us (5%)
  between operations  19.5 us (5%)
    all_gather x1, waiting for transfers between devices, total_of_pieces(): return lax.all_gather(array, axis).astype(jnp.float32).sum(0)  60.3 us
    ppermute x15, starting transfers between devices, extended(): lax.ppermute(lax.slice_in_dim(block, block.shape[dim] - width, None, axis...  48.3 us
    unnamed x379, local copies, waits for them, and re-layouts  48 us
    ppermute x16, starting transfers between devices, from_partner(): lax.ppermute(array, axis, [(i, i ^ 1 << bit) for i in range(lax.axis_size...  42.2 us
    ppermute x15, waiting for transfers between devices, extended(): lax.ppermute(lax.slice_in_dim(block, 0, width, axis=dim), axis, backward)  34.1 us
    ppermute x15, starting transfers between devices, extended(): lax.ppermute(lax.slice_in_dim(block, 0, width, axis=dim), axis, backward)  31 us
    dot_general x60, matrix products, convolve(): jnp.einsum('tczyx,tco->ozyx', slices_of(padded, plane_shift, row_count),...  23.5 us
    ppermute x8, waiting for transfers between devices, passed_along(): lax.ppermute(value, axis, [(source, source + steps) for source in range(f...  18 us
  transfers between devices with their start and end apart: 55, of which 26 were waited for; matrix products, arithmetic and copies ran while one was open for 23% of the time, Pallas kernels for 0%

commit v1 on v0

v1 whole, which is shorter than its diff:
```python
import functools

import jax
import jax.numpy as jnp
from jax import lax
from jax.experimental import pallas as pl
from jax.experimental.pallas import tpu as pltpu
from jax.sharding import PartitionSpec as P

ROWS = 4
WIDTH = 80
CHUNK = 4
SPAN = CHUNK * WIDTH
TOTAL = 36
LANES = 128
F32 = jnp.float32
BF16 = jnp.bfloat16


def sigmoid(v):
    return 0.5 * jnp.tanh(0.5 * v) + 0.5


def slope(v):
    s = sigmoid(v)
    return s * (1.0 + v * (1.0 - s))


def at_row(row):
    return pl.multiple_of(row * WIDTH, 16)


def main_kernel(
    own, oth, near, far, near_other, far_other, pack0, pack1, pack2, pack3,
    out0, out1, out2, out3,
    wpack, crop, cot, feats, merged, hidden, delta, sd, fd, pre1, pre2, w1, wb,
    lx, lxt, block, grads, terms, out_all,
):
    seg = lax.axis_index("segment")
    gy = lax.axis_index("gy")
    core = lax.rem(gy, 2)
    half = lax.div(seg, 2)
    column = lax.rem(lax.broadcasted_iota(jnp.int32, (SPAN, LANES), 0), WIDTH)
    first_column = column == 0
    last_column = column == WIDTH - 1
    strip = ROWS * WIDTH

    for k, pack in enumerate((pack0, pack1, pack2, pack3)):
        wpack[lax.rem(seg - k + 4, 4)] = pack[...]

    def put(dst, row, src, src_row, rows):
        dst[row * WIDTH : (row + rows) * WIDTH, :] = src[src_row * WIDTH : (src_row + rows) * WIDTH, :]

    @pl.when(core == 0)
    def _():
        put(crop, 0, far, 0, 8)
        put(crop, 8, near.at[0], 0, 8)
        put(crop, 16, own.at[0], 0, 4)
        put(crop, 20, oth.at[0], 0, 4)
        put(crop, 24, near_other.at[0], 4, 4)
        put(crop, 28, near_other.at[0], 0, 4)
        put(crop, 32, far_other, 4, 4)
        put(cot, 0, near.at[1], 0, 8)
        put(cot, 8, own.at[1], 0, 4)
        put(cot, 12, oth.at[1], 0, 4)
        put(cot, 16, near_other.at[1], 4, 4)

    @pl.when(core == 1)
    def _():
        put(crop, 0, far_other, 4, 4)
        put(crop, 4, near_other.at[0], 0, 8)
        put(crop, 12, oth.at[0], 0, 4)
        put(crop, 16, own.at[0], 0, 4)
        put(crop, 20, near.at[0], 4, 4)
        put(crop, 24, near.at[0], 0, 4)
        put(crop, 28, far, 4, 4)
        put(crop, 32, far, 0, 4)
        put(cot, 0, near_other.at[1], 4, 4)
        put(cot, 4, oth.at[1], 0, 4)
        put(cot, 8, own.at[1], 0, 4)
        put(cot, 12, near.at[1], 4, 4)
        put(cot, 16, near.at[1], 0, 4)

    er = lax.broadcasted_iota(jnp.int32, (LANES, 4 * LANES), 0)
    ec = lax.broadcasted_iota(jnp.int32, (LANES, 4 * LANES), 1)
    expand = jnp.where(er == lax.shift_right_logical(ec, 2), 1.0, 0.0).astype(BF16)
    cr = lax.broadcasted_iota(jnp.int32, (4 * LANES, LANES), 0)
    cc = lax.broadcasted_iota(jnp.int32, (4 * LANES, LANES), 1)
    collapse = jnp.where(cc == lax.shift_right_logical(cr, 2), 1.0, 0.0).astype(BF16)
    plane = lax.bitwise_and(lax.broadcasted_iota(jnp.int32, (32, LANES), 1), 3)
    on_plane = [plane == z for z in range(4)]

    def build(index, carry):
        w = wpack[lax.div(index, 2), lax.rem(index, 2)]
        lx[...] = jnp.dot(w, expand, preferred_element_type=F32)
        for q in range(7):
            lxt[q * LANES : (q + 1) * LANES, :] = lax.dot_general(
                w[q * 32 : (q + 1) * 32], expand[:32, :LANES], (((0,), (0,)), ((), ())), preferred_element_type=F32
            )
        for dy in range(3):
            for dx in range(3):
                taps = [9 * dz + 3 * dy + dx for dz in range(3)]
                fwd = [lx[t // 4 * 32 : t // 4 * 32 + 32, t % 4 * LANES : (t % 4 + 1) * LANES] for t in taps]
                bwd = [lxt[t * 32 : t * 32 + 32, :] for t in taps]
                for z in range(4):
                    vf = jnp.zeros((32, LANES), F32)
                    vb = jnp.zeros((32, LANES), F32)
                    for dz in range(3):
                        if 0 <= z + 1 - dz < 4:
                            vf = jnp.where(on_plane[z + 1 - dz], fwd[dz], vf)
                        if 0 <= z + dz - 1 < 4:
                            vb = jnp.where(on_plane[z + dz - 1], bwd[dz], vb)
                    block[0, pl.ds(z, 32, stride=4), :] = vf
                    block[1, pl.ds(z, 32, stride=4), :] = vb
                w1[index, dy * LANES : (dy + 1) * LANES, dx * LANES : (dx + 1) * LANES] = block[0].astype(BF16)
                wb[index, (2 - dy) * LANES : (3 - dy) * LANES, (2 - dx) * LANES : (3 - dx) * LANES] = block[1].astype(
                    BF16
                )
        return carry

    lax.fori_loop(0, 8, build, 0)

    def chunks(low, high, body):
        count = -(-(high - low) // CHUNK)

        def step(i, carry):
            body(at_row(jnp.minimum(low + CHUNK * i, high - CHUNK)))
            return carry

        lax.fori_loop(0, count, step, 0)

    def from_left(v):
        return jnp.where(first_column, 0.0, pltpu.roll(v, 1, 0))

    def from_right(v):
        return jnp.where(last_column, 0.0, pltpu.roll(v, SPAN - 1, 0))

    def stacked(src, base):
        return jnp.concatenate(
            [
                src[pl.ds(pl.multiple_of(base - WIDTH, 16), SPAN), :],
                src[pl.ds(base, SPAN), :],
                src[pl.ds(pl.multiple_of(base + WIDTH, 16), SPAN), :],
            ],
            axis=1,
        )

    def conv(src, matrix, low, high, then):
        def body(base):
            p = jnp.dot(stacked(src, base), matrix[...], preferred_element_type=F32)
            then(base, p[:, LANES : 2 * LANES] + from_left(p[:, :LANES]) + from_right(p[:, 2 * LANES :]))

        chunks(low, high, body)

    def clear_outside(dst, low, high):
        top = 16 - ROWS * gy
        bottom = 16 + ROWS * (lax.axis_size("gy") - gy)

        def clear(i, carry):
            dst[pl.ds(at_row(i), WIDTH), :] = jnp.zeros((WIDTH, LANES), BF16)
            return carry

        @pl.when(top > low)
        def _():
            lax.fori_loop(low, jnp.minimum(top, high), clear, 0)

        @pl.when(bottom < high)
        def _():
            lax.fori_loop(jnp.maximum(bottom, low), high, clear, 0)

    for s in range(4):
        source = crop if s == 0 else feats.at[0] if s == 1 else merged.at[s - 2]

        def first(base, v, s=s):
            pre1[s, pl.ds(base, SPAN), :] = v
            hidden[s, pl.ds(base, SPAN), :] = (v * sigmoid(v)).astype(BF16)

        conv(source, w1.at[2 * s], 2 * s + 1, 35 - 2 * s, first)
        clear_outside(hidden.at[s], 2 * s + 1, 35 - 2 * s)

        def second(base, v, s=s):
            pre2[s, pl.ds(base, SPAN), :] = v
            out = (v * sigmoid(v)).astype(BF16)
            feats[s, pl.ds(base, SPAN), :] = out
            if s == 1 or s == 2:
                skip = feats[0, pl.ds(base, SPAN), :] if s == 1 else crop[pl.ds(base, SPAN), :]
                merged[s - 1, pl.ds(base, SPAN), :] = (out.astype(F32) + skip.astype(F32)).astype(BF16)

        conv(hidden.at[s], w1.at[2 * s + 1], 2 * s + 2, 34 - 2 * s, second)
        if s == 0:
            clear_outside(feats.at[0], 2, 34)
        if s == 1 or s == 2:
            clear_outside(merged.at[s - 1], 2 * s + 2, 34 - 2 * s)

    def first_sd(base):
        incoming = cot[pl.ds(pl.multiple_of(base - 8 * WIDTH, 16), SPAN), :]
        sd[pl.ds(base, SPAN), :] = (incoming.astype(F32) * slope(pre2[3, pl.ds(base, SPAN), :])).astype(BF16)

    chunks(8, 28, first_sd)

    own_low = half * 16
    mine = (column >= own_low) & (column < own_low + 64)
    base0 = 16 * WIDTH
    slot_of = lambda s: lax.rem(s - seg + 4, 4)

    def kernel_grads(src, grad, s, which):
        d = jnp.where(mine, grad[base0 : base0 + SPAN, :].astype(F32), 0.0)
        shifted = jnp.concatenate([from_right(d).astype(BF16), d.astype(BF16), from_left(d).astype(BF16)], axis=1)
        product = lax.dot_general(
            stacked(src, base0), shifted, (((0,), (0,)), ((), ())), preferred_element_type=F32
        )
        for dx in range(3):
            grads[dx] = product[:, dx * LANES : (dx + 1) * LANES]
        terms[6 * 32 :, 3 * LANES :] = jnp.zeros((32, LANES), BF16)
        for dy in range(3):
            for dx in range(3):
                rows = [grads[dx, pl.ds(dy * LANES + z, 32, stride=4), :] for z in range(4)]
                for dz in range(3):
                    total = jnp.zeros((32, LANES), F32)
                    for z in range(4):
                        if 0 <= z + 1 - dz < 4:
                            total = jnp.where(on_plane[z + 1 - dz], rows[z], total)
                    t = 9 * dz + 3 * dy + dx
                    terms[t // 4 * 32 : t // 4 * 32 + 32, t % 4 * LANES : (t % 4 + 1) * LANES] = total.astype(BF16)
        packed = jnp.dot(terms[...], collapse, preferred_element_type=F32).astype(BF16)
        out_all[slot_of(s), 512 + 224 * which : 736 + 224 * which, :] = packed

    for s in (3, 2, 1, 0):
        source = crop if s == 0 else feats.at[0] if s == 1 else merged.at[s - 2]
        low, high = 8 + 2 * (3 - s), 28 - 2 * (3 - s)

        def to_first(base, v, s=s):
            fd[pl.ds(base, SPAN), :] = (v * slope(pre1[s, pl.ds(base, SPAN), :])).astype(BF16)

        kernel_grads(hidden.at[s], sd, s, 1)
        conv(sd, wb.at[2 * s + 1], low + 1, high - 1, to_first)
        clear_outside(fd, low + 1, high - 1)
        kernel_grads(source, fd, s, 0)

        def to_delta(base, v, s=s):
            out = v.astype(BF16)
            if s == 1 or s == 0:
                other = delta[2 if s == 1 else 3, pl.ds(base, SPAN), :]
                out = (out.astype(F32) + other.astype(F32)).astype(BF16)
            delta[s, pl.ds(base, SPAN), :] = out
            if s > 0:
                sd[pl.ds(base, SPAN), :] = (
                    out.astype(F32) * slope(pre2[s - 1, pl.ds(base, SPAN), :])
                ).astype(BF16)

        conv(fd, wb.at[2 * s], low + 2, high - 2, to_delta)
        if s > 0:
            clear_outside(sd, low + 2, high - 2)

    for s in range(4):
        for y in range(ROWS):
            place = pl.ds(pl.multiple_of(base0 + y * WIDTH + own_low, 16), 64)
            out_all[slot_of(s), 64 * y : 64 * y + 64, :] = feats[s, place, :]
            out_all[slot_of(s), 256 + 64 * y : 320 + 64 * y, :] = delta[s, place, :]
    for k, out in enumerate((out0, out1, out2, out3)):
        out[...] = out_all[k]


def main_call(*operands):
    acts = (TOTAL * WIDTH, LANES)
    vmem = pl.BlockSpec(memory_space=pltpu.VMEM)
    return pl.pallas_call(
        main_kernel,
        out_shape=[jax.ShapeDtypeStruct((960, LANES), BF16)] * 4,
        in_specs=[vmem] * 10,
        out_specs=[vmem] * 4,
        scratch_shapes=[
            pltpu.VMEM((4, 2, 224, LANES), BF16),
            pltpu.VMEM(acts, BF16),
            pltpu.VMEM((20 * WIDTH, LANES), BF16),
            pltpu.VMEM((4,) + acts, BF16),
            pltpu.VMEM((2,) + acts, BF16),
            pltpu.VMEM((4,) + acts, BF16),
            pltpu.VMEM((4,) + acts, BF16),
            pltpu.VMEM(acts, BF16),
            pltpu.VMEM(acts, BF16),
            pltpu.VMEM((4,) + acts, F32),
            pltpu.VMEM((4,) + acts, F32),
            pltpu.VMEM((8, 3 * LANES, 3 * LANES), BF16),
            pltpu.VMEM((8, 3 * LANES, 3 * LANES), BF16),
            pltpu.VMEM((224, 4 * LANES), F32),
            pltpu.VMEM((7 * LANES, LANES), F32),
            pltpu.VMEM((2, LANES, LANES), F32),
            pltpu.VMEM((3, 3 * LANES, LANES), F32),
            pltpu.VMEM((224, 4 * LANES), BF16),
            pltpu.VMEM((4, 960, LANES), BF16),
        ],
        compiler_params=pltpu.CompilerParams(vmem_limit_bytes=56 * 1024 * 1024),
        name="sections",
    )(*operands)


def rotated(value, axis, group, step, stride):
    count = lax.axis_size(axis)

    def target(i):
        place = i // stride % group
        return i + ((place + step) % group - place) * stride

    return lax.ppermute(value, axis, [(i, target(i)) for i in range(count)])


def local(crops, cotangent, weights):
    micro_count, channels, planes, rows, across = crops.shape
    seg = lax.axis_index("segment")
    micro, half = seg % 2, seg // 2
    devices = lax.axis_size("gy")
    swap = [(i, i ^ 1) for i in range(devices)]

    def tile(volume):
        field = lax.dynamic_index_in_dim(volume, micro, 0, keepdims=False)
        field = jnp.transpose(field, (2, 3, 0, 1)).reshape(rows, across, channels * planes)
        return lax.dynamic_slice_in_dim(field, half * 48, WIDTH, 1).reshape(rows * WIDTH, channels * planes)

    own = jnp.stack([tile(crops), tile(cotangent)])
    packed = jnp.pad(weights[0], ((0, 0), (0, 1), (0, 0), (0, 0))).reshape(2, 7, 4, channels, channels)
    packed = jnp.transpose(packed, (0, 1, 3, 2, 4)).reshape(2, 7 * channels, 4 * channels)

    oth = lax.ppermute(own, "gy", swap)
    block = jnp.concatenate([own, oth], axis=1)

    def outward(distance):
        return [
            (i, i + 2 * distance * (1 if i % 2 == 0 else -1))
            for i in range(devices)
            if 0 <= i + 2 * distance * (1 if i % 2 == 0 else -1) < devices
        ]

    near = lax.ppermute(block, "gy", outward(1))
    far = lax.ppermute(block[0], "gy", outward(2))
    others = [rotated(packed, "segment", 4, k, 1) for k in (1, 2, 3)]
    near_other = lax.ppermute(near, "gy", swap)
    far_other = lax.ppermute(far, "gy", swap)
    outs = main_call(own, oth, near, far, near_other, far_other, packed, *others)
    arrived = [outs[0]] + [rotated(outs[k], "segment", 4, k, 1) for k in (1, 2, 3)]
    by_step = jnp.stack(arrived)
    total = by_step[:, 512:].astype(F32).sum(0)
    total = total + lax.ppermute(total.astype(BF16), "gy", swap).astype(F32)
    for stride in (2, 8):
        mine = total.astype(BF16)
        total = mine.astype(F32)
        for k in (1, 2, 3):
            total = total + rotated(mine, "gy", 4, k, stride).astype(F32)
    grads = total.reshape(2, 7, channels, 4, channels).transpose(0, 1, 3, 2, 4)
    grads = grads.reshape(2, 28, channels, channels)[:, :27]

    fields = by_step[:, :512]
    by_source = jnp.stack([lax.dynamic_index_in_dim(fields, (seg - j) % 4, 0, keepdims=False) for j in range(4)])
    fields = by_source.reshape(2, 2, 2, rows, across // 2, channels, planes)
    fields = jnp.transpose(fields, (2, 1, 5, 6, 3, 0, 4)).reshape(2, micro_count, channels, planes, rows, across)
    return fields[0][None], grads[None], fields[1].astype(F32)[None]


def solution(mesh):
    return jax.shard_map(
        local,
        mesh=mesh,
        in_specs=(
            P(None, None, None, "gy", None),
            P(None, None, None, "gy", None),
            P("segment", None, None, None, None),
        ),
        out_specs=(
            P("segment", None, None, None, "gy", None),
            P("segment", None, None, None, None),
            P("segment", None, None, None, "gy", None),
        ),
        check_vma=False,
    )
```

time: 399 us -> 118 us (0.30); the launches traced: 392 us -> 117 us
  starting transfers between devices: 132 us -> 25.1 us
  waiting for transfers between devices: 118 us -> 37 us
  local copies, waits for them, and re-layouts: 63.9 us -> 10.9 us
  Pallas kernels: 0 us -> 41.7 us
  matrix products: 36.5 us -> 0 us
  other arithmetic: 21.3 us -> 1.65 us
  between operations: 19.5 us -> 0.97 us
    ppermute x54 -> x18, starting transfers between devices: 132 us -> 25.1 us  [the longest x12 14.5 us: rotated(): return lax.ppermute(value, axis, [(i, target(i)) for i in range(count)])]
    all_gather x1 -> x0, waiting for transfers between devices: 60.3 us -> none  [total_of_pieces(): return lax.all_gather(array, axis).astype(jnp.float32).sum(0)]
    unnamed x379 -> x30, local copies, waits for them, and re-layouts: 48 us -> 5.86 us
    pallas_call x0 -> x1, Pallas kernels: none -> 41.7 us  [main_call(): pl.pallas_call(main_kernel, out_shape=[jax.ShapeDtypeStruct((960, LANES),...]
    dot_general x90 -> x0, matrix products: 36.5 us -> none  [the longest x60 23.5 us: convolve(): jnp.einsum('tczyx,tco->ozyx', slices_of(padded, plane_shift, row_count),...]
    ppermute x54 -> x18, waiting for transfers between devices: 57.6 us -> 37 us  [the longest x12 27.7 us: rotated(): return lax.ppermute(value, axis, [(i, target(i)) for i in range(count)])]
    another operation x68 -> x1, local copies, waits for them, and re-layouts: 11.9 us -> 0.21 us  [local(): jnp.stack([lax.dynamic_index_in_dim(fields, (seg - j) % 4, 0, keepdims=Fa...]
    reduce_sum x1, other arithmetic: 8.77 us -> 1.04 us  [local(): total = by_step[:, 512:].astype(F32).sum(0)]
  transfers between devices with their start and end apart: 55 -> 18, of which waited for: 26 -> 12; matrix products, arithmetic and copies ran while one was open for 23% -> 5% of each run, Pallas kernels for 0% -> 0%
where the time goes in v1:
time: 118 us; the launch traced here: 117 us
  Pallas kernels  41.7 us (35%)
  waiting for transfers between devices  37 us (31%)
  starting transfers between devices  25.1 us (21%)
  local copies, waits for them, and re-layouts  10.9 us (9%)
  other arithmetic  1.65 us (1%)
    pallas_call x1, Pallas kernels, main_call(): pl.pallas_call(main_kernel, out_shape=[jax.ShapeDtypeStruct((960, LANES),...  41.7 us
    ppermute x12, waiting for transfers between devices, rotated(): return lax.ppermute(value, axis, [(i, target(i)) for i in range(count)])  27.7 us
    ppermute x12, starting transfers between devices, rotated(): return lax.ppermute(value, axis, [(i, target(i)) for i in range(count)])  14.5 us
    unnamed x30, local copies, waits for them, and re-layouts  5.86 us
    ppermute x1, waiting for transfers between devices, local(): near = lax.ppermute(block, 'gy', outward(1))  5.47 us
    ppermute x1, starting transfers between devices, local(): far_other = lax.ppermute(far, 'gy', swap)  2.59 us
  transfers between devices with their start and end apart: 18, of which 12 were waited for; matrix products, arithmetic and copies ran while one was open for 5% of the time, Pallas kernels for 0%

profile of v1, /device:TPU:1, one launch (start us, length us, event | category | flops | bytes accessed | tf_op | source)
XLA Modules:
  0.0 117.3 jit_solution(12899296433323603005)
XLA Ops:
  0.7 1.1 constant_dynamic-slice_fusion.5
  1.8 0.1 copy.34
  1.9 0.1 constant_dynamic-slice_fusion.4
  2.0 0.1 copy.35
  2.2 0.1 copy.31
  2.3 0.1 constant_dynamic-slice_fusion.6
  2.4 0.1 copy.32
  2.5 0.0 copy-start.4
  2.5 1.5 %collective-permute-start = (bf16[2,320,128]{2,1,0:T(8,128)(2,1)S(1)}, bf16[2,320,128]{2,1,0:T(8,128)(2,1)S(1)}, u32[]{:S(2)}, u32[]{:S(2)}) collective-permute-start(bf16[2,320,128]{2,1,0:T(8,128)(2,1)S(1)} %pad_maximum_fusion.3.own), channel_id=1, source_target_pairs={{0,1},{1,0},{2,3},{3,2},{4,5},{5,4},{6,7},{7,6},{8,9},{9,8},{10,11... | collective-permute-start | bytes 491528 | tf_op jit(solution)/shard_map/ppermute | solution.py:324
  4.0 1.0 collective-permute-done.oth
  5.1 0.6 copy-done.1
  5.7 1.3 %collective-permute-start.1 = (bf16[2,640,128]{2,1,0:T(8,128)(2,1)S(1)}, bf16[2,640,128]{2,1,0:T(8,128)(2,1)S(1)}, u32[]{:S(2)}, u32[]{:S(2)}) collective-permute-start(bf16[2,640,128]{2,1,0:T(8,128)(2,1)S(1)} %pad_maximum_fusion.2), channel_id=1, source_target_pairs={{0,2},{2,4},{3,1},{4,6},{5,3},{6,8},{7,5},{8,10},{9,7},{10,12},{11... | collective-permute-start | bytes 983048 | tf_op jit(solution)/shard_map/ppermute | solution.py:334
  7.1 1.3 %collective-permute-start.2 = (bf16[640,128]{1,0:T(8,128)(2,1)S(1)}, bf16[640,128]{1,0:T(8,128)(2,1)S(1)}, u32[]{:S(2)}, u32[]{:S(2)}) collective-permute-start(bf16[640,128]{1,0:T(8,128)(2,1)S(1)} %slice_bitcast_fusion.1), channel_id=1, source_target_pairs={{0,4},{2,6},{4,8},{5,1},{6,10},{7,3},{8,12},{9,5},{10,14},{11,7},{... | collective-permute-start | bytes 491528 | tf_op jit(solution)/shard_map/ppermute | solution.py:335
  8.4 5.5 %collective-permute-done.1.near = bf16[2,640,128]{2,1,0:T(8,128)(2,1)S(1)} collective-permute-done((bf16[2,640,128]{2,1,0:T(8,128)(2,1)S(1)}, bf16[2,640,128]{2,1,0:T(8,128)(2,1)S(1)}, u32[]{:S(2)}, u32[]{:S(2)}) %collective-permute-start.1) | collective-permute-done | bytes 327712 | tf_op jit(solution)/shard_map/ppermute | solution.py:334
  13.8 1.8 %collective-permute-start.3 = (bf16[2,640,128]{2,1,0:T(8,128)(2,1)S(1)}, bf16[2,640,128]{2,1,0:T(8,128)(2,1)S(1)}, u32[]{:S(2)}, u32[]{:S(2)}) collective-permute-start(bf16[2,640,128]{2,1,0:T(8,128)(2,1)S(1)} %collective-permute-done.1.near), channel_id=1, source_target_pairs={{0,1},{1,0},{2,3},{3,2},{4,5},{5,4},{6,7},{7,6},{8,9},{9,8},{10,11... | collective-permute-start | bytes 983048 | tf_op jit(solution)/shard_map/ppermute | solution.py:337
  15.6 1.9 %collective-permute-done.2.far = bf16[640,128]{1,0:T(8,128)(2,1)S(1)} collective-permute-done((bf16[640,128]{1,0:T(8,128)(2,1)S(1)}, bf16[640,128]{1,0:T(8,128)(2,1)S(1)}, u32[]{:S(2)}, u32[]{:S(2)}) %collective-permute-start.2) | collective-permute-done | bytes 163872 | tf_op jit(solution)/shard_map/ppermute | solution.py:335
  17.5 2.6 %collective-permute-start.4 = (bf16[640,128]{1,0:T(8,128)(2,1)S(1)}, bf16[640,128]{1,0:T(8,128)(2,1)S(1)}, u32[]{:S(2)}, u32[]{:S(2)}) collective-permute-start(bf16[640,128]{1,0:T(8,128)(2,1)S(1)} %collective-permute-done.2.far), channel_id=1, source_target_pairs={{0,1},{1,0},{2,3},{3,2},{4,5},{5,4},{6,7},{7,6},{8,9},{9,8},{10,11... | collective-permute-start | bytes 491528 | tf_op jit(solution)/shard_map/ppermute | solution.py:338
  20.1 0.1 pad.4
  20.2 0.2 copy.55
  20.5 0.2 reshape.46.pack0
  20.7 2.5 %collective-permute-start.7 = (bf16[2,224,128]{2,1,0:T(8,128)(2,1)S(1)}, bf16[2,224,128]{2,1,0:T(8,128)(2,1)S(1)}, u32[]{:S(2)}, u32[]{:S(2)}) collective-permute-start(bf16[2,224,128]{2,1,0:T(8,128)(2,1)S(1)} %reshape.46.pack0), channel_id=1, source_target_pairs={{0,96},{32,0},{64,32},{96,64},{1,97},{33,1},{65,33},{97,65},{2,98}... | collective-permute-start | bytes 344072 | tf_op jit(solution)/shard_map/ppermute | solution.py:305
  23.3 0.5 collective-permute-start.6
  23.8 0.6 collective-permute-start.5
  24.4 1.1 collective-permute-done.7.pack3
  25.5 3.0 %collective-permute-done.6.pack2 = bf16[2,224,128]{2,1,0:T(8,128)(2,1)S(1)} collective-permute-done((bf16[2,224,128]{2,1,0:T(8,128)(2,1)S(1)}, bf16[2,224,128]{2,1,0:T(8,128)(2,1)S(1)}, u32[]{:S(2)}, u32[]{:S(2)}) %collective-permute-start.6) | collective-permute-done | bytes 114720 | tf_op jit(solution)/shard_map/ppermute | solution.py:305
  28.5 3.6 %collective-permute-done.5.pack1 = bf16[2,224,128]{2,1,0:T(8,128)(2,1)S(1)} collective-permute-done((bf16[2,224,128]{2,1,0:T(8,128)(2,1)S(1)}, bf16[2,224,128]{2,1,0:T(8,128)(2,1)S(1)}, u32[]{:S(2)}, u32[]{:S(2)}) %collective-permute-start.5) | collective-permute-done | bytes 114720 | tf_op jit(solution)/shard_map/ppermute | solution.py:305
  32.1 0.6 copy-done.11
  32.7 0.1 copy-done.8
  32.8 0.7 copy-done.6
  33.5 41.7 %sections.1 = (bf16[960,128]{1,0:T(8,128)(2,1)}, bf16[960,128]{1,0:T(8,128)(2,1)}, bf16[960,128]{1,0:T(8,128)(2,1)}, bf16[960,128]{1,0:T(8,128)(2,1)}) custom-call(bf16[2,320,128]{2,1,0:T(8,128)(2,1)} %copy-done.2, bf16[2,320,128]{2,1,0:T(8,128)(2,1)} %copy-done.1, bf16[2,640,128]{2,1,0:T(8,128)(2,1)} %copy-done.5, bf16[640,128]{1,0:T(8,128)(2,1)} %copy-done.7, ...), custom_call_target="tpu_custom_call" | custom-call | tf_op jit(solution)/shard_map/sections/pallas_call | solution.py:267
  75.3 0.0 collective-permute-start.8
  75.3 0.5 collective-permute-start.9
  75.7 2.2 %collective-permute-start.10 = (bf16[960,128]{1,0:T(8,128)(2,1)}, bf16[960,128]{1,0:T(8,128)(2,1)S(1)}, u32[]{:S(2)}, u32[]{:S(2)}) collective-permute-start(bf16[960,128]{1,0:T(8,128)(2,1)} %get-tuple-element.10), channel_id=1, source_target_pairs={{0,96},{32,0},{64,32},{96,64},{1,97},{33,1},{65,33},{97,65},{2,98}... | collective-permute-start | bytes 737288 | tf_op jit(solution)/shard_map/ppermute | solution.py:305
  78.0 10.9 %collective-permute-done.8 = bf16[960,128]{1,0:T(8,128)(2,1)S(1)} collective-permute-done((bf16[960,128]{1,0:T(8,128)(2,1)}, bf16[960,128]{1,0:T(8,128)(2,1)S(1)}, u32[]{:S(2)}, u32[]{:S(2)}) %collective-permute-start.8) | collective-permute-done | bytes 245792 | tf_op jit(solution)/shard_map/ppermute | solution.py:305
  88.9 0.0 collective-permute-done.9
  88.9 0.0 collective-permute-done.10
  88.9 1.0 convert_reduce_fusion
  89.9 0.1 pad_maximum_fusion
  90.1 2.1 %collective-permute-start.11 = (bf16[448,128]{1,0:T(8,128)(2,1)S(1)}, bf16[448,128]{1,0:T(8,128)(2,1)S(1)}, u32[]{:S(2)}, u32[]{:S(2)}) collective-permute-start(bf16[448,128]{1,0:T(8,128)(2,1)S(1)} %convert_element_type.55), channel_id=1, source_target_pairs={{0,1},{1,0},{2,3},{3,2},{4,5},{5,4},{6,7},{7,6},{8,9},{9,8},{10,11... | collective-permute-start | bytes 344072 | tf_op jit(solution)/shard_map/ppermute | solution.py:343
  92.3 0.9 collective-permute-done.11
  93.3 3.3 %collective-permute-start.14 = (bf16[448,128]{1,0:T(8,128)(2,1)S(1)}, bf16[448,128]{1,0:T(8,128)(2,1)S(1)}, u32[]{:S(2)}, u32[]{:S(2)}) collective-permute-start(bf16[448,128]{1,0:T(8,128)(2,1)S(1)} %add_convert_fusion.1), channel_id=1, source_target_pairs={{0,6},{1,7},{2,0},{3,1},{4,2},{5,3},{6,4},{7,5},{8,14},{9,15},{10,... | collective-permute-start | bytes 344072 | tf_op jit(solution)/shard_map/ppermute | solution.py:305
  96.6 0.2 collective-permute-start.13
  96.8 0.8 collective-permute-start.12
  97.6 0.1 pad_maximum_fusion.1
  97.7 0.2 copy.37
  97.9 0.5 reshape.47
  98.4 0.4 copy.54
  98.8 2.3 %collective-permute-done.14 = bf16[448,128]{1,0:T(8,128)(2,1)S(1)} collective-permute-done((bf16[448,128]{1,0:T(8,128)(2,1)S(1)}, bf16[448,128]{1,0:T(8,128)(2,1)S(1)}, u32[]{:S(2)}, u32[]{:S(2)}) %collective-permute-start.14) | collective-permute-done | bytes 114720 | tf_op jit(solution)/shard_map/ppermute | solution.py:305
  101.2 1.1 collective-permute-done.13
  102.3 3.2 %collective-permute-done.12 = bf16[448,128]{1,0:T(8,128)(2,1)S(1)} collective-permute-done((bf16[448,128]{1,0:T(8,128)(2,1)S(1)}, bf16[448,128]{1,0:T(8,128)(2,1)S(1)}, u32[]{:S(2)}, u32[]{:S(2)}) %collective-permute-start.12) | collective-permute-done | bytes 114720 | tf_op jit(solution)/shard_map/ppermute | solution.py:305
  105.5 0.1 add_convert_fusion
  105.5 1.9 %collective-permute-start.17 = (bf16[448,128]{1,0:T(8,128)(2,1)S(1)}, bf16[448,128]{1,0:T(8,128)(2,1)S(1)}, u32[]{:S(2)}, u32[]{:S(2)}) collective-permute-start(bf16[448,128]{1,0:T(8,128)(2,1)S(1)} %add_convert_fusion), channel_id=1, source_target_pairs={{0,24},{1,25},{2,26},{3,27},{4,28},{5,29},{6,30},{7,31},{8,0},{9,1... | collective-permute-start | bytes 344072 | tf_op jit(solution)/shard_map/ppermute | solution.py:305
  107.4 1.3 %collective-permute-start.16 = (bf16[448,128]{1,0:T(8,128)(2,1)S(1)}, bf16[448,128]{1,0:T(8,128)(2,1)S(1)}, u32[]{:S(2)}, u32[]{:S(2)}) collective-permute-start(bf16[448,128]{1,0:T(8,128)(2,1)S(1)} %add_convert_fusion), channel_id=1, source_target_pairs={{0,16},{1,17},{2,18},{3,19},{4,20},{5,21},{6,22},{7,23},{8,24},{9,... | collective-permute-start | bytes 344072 | tf_op jit(solution)/shard_map/ppermute | solution.py:305
  108.7 0.7 collective-permute-start.15
  109.4 0.2 slice_convert_fusion
  109.6 0.8 copy.45
  110.4 1.6 %reshape.52 = f32[1,2,32,4,4,128]{5,4,3,2,1,0:T(4,128)} reshape(f32[1,2,32,4,4,2,64]{6,5,4,3,2,1,0:T(2,128)S(1)} %copy.45) | data formatting | bytes 1048576
  112.0 0.4 copy.44
  112.4 1.0 reshape.51
  113.3 2.4 %collective-permute-done.15 = bf16[448,128]{1,0:T(8,128)(2,1)S(1)} collective-permute-done((bf16[448,128]{1,0:T(8,128)(2,1)S(1)}, bf16[448,128]{1,0:T(8,128)(2,1)S(1)}, u32[]{:S(2)}, u32[]{:S(2)}) %collective-permute-start.15) | collective-permute-done | bytes 114720 | tf_op jit(solution)/shard_map/ppermute | solution.py:305
  115.8 0.1 convert_add_fusion
  115.8 0.4 reshape.48
  116.2 0.1 copy.40
  116.4 1.0 slice_bitcast_fusion
  (32 shorter events, 0.3 us)
Async XLA Ops:
  2.5 2.6 %copy-start.2 = (bf16[2,320,128]{2,1,0:T(8,128)(2,1)}, bf16[2,320,128]{2,1,0:T(8,128)(2,1)S(1)}, u32[]{:S(2)}) copy-start(bf16[2,320,128]{2,1,0:T(8,128)(2,1)S(1)} %pad_maximum_fusion.3.own) | copy-start | bytes 491524
  2.5 17.6 %copy-start.4 = (bf16[1,2,27,32,32]{4,3,2,1,0:T(8,128)(2,1)S(1)}, bf16[1,2,27,32,32]{4,3,2,1,0:T(8,128)(2,1)}, u32[]{:S(2)}) copy-start(bf16[1,2,27,32,32]{4,3,2,1,0:T(8,128)(2,1)} %param.5) | copy-start | bytes 331780
  2.5 2.5 %collective-permute-start = (bf16[2,320,128]{2,1,0:T(8,128)(2,1)S(1)}, bf16[2,320,128]{2,1,0:T(8,128)(2,1)S(1)}, u32[]{:S(2)}, u32[]{:S(2)}) collective-permute-start(bf16[2,320,128]{2,1,0:T(8,128)(2,1)S(1)} %pad_maximum_fusion.3.own), channel_id=1, source_target_pairs={{0,1},{1,0},{2,3},{3,2},{4,5},{5,4},{6,7},{7,6},{8,9},{9,8},{10,11... | collective-permute-start | bytes 491528 | tf_op jit(solution)/shard_map/ppermute | solution.py:324
  5.1 0.7 copy-start.1
  5.7 8.1 %collective-permute-start.1 = (bf16[2,640,128]{2,1,0:T(8,128)(2,1)S(1)}, bf16[2,640,128]{2,1,0:T(8,128)(2,1)S(1)}, u32[]{:S(2)}, u32[]{:S(2)}) collective-permute-start(bf16[2,640,128]{2,1,0:T(8,128)(2,1)S(1)} %pad_maximum_fusion.2), channel_id=1, source_target_pairs={{0,2},{2,4},{3,1},{4,6},{5,3},{6,8},{7,5},{8,10},{9,7},{10,12},{11... | collective-permute-start | bytes 983048 | tf_op jit(solution)/shard_map/ppermute | solution.py:334
  7.1 10.5 %collective-permute-start.2 = (bf16[640,128]{1,0:T(8,128)(2,1)S(1)}, bf16[640,128]{1,0:T(8,128)(2,1)S(1)}, u32[]{:S(2)}, u32[]{:S(2)}) collective-permute-start(bf16[640,128]{1,0:T(8,128)(2,1)S(1)} %slice_bitcast_fusion.1), channel_id=1, source_target_pairs={{0,4},{2,6},{4,8},{5,1},{6,10},{7,3},{8,12},{9,5},{10,14},{11,7},{... | collective-permute-start | bytes 491528 | tf_op jit(solution)/shard_map/ppermute | solution.py:335
  13.8 6.4 %copy-start.5 = (bf16[2,640,128]{2,1,0:T(8,128)(2,1)}, bf16[2,640,128]{2,1,0:T(8,128)(2,1)S(1)}, u32[]{:S(2)}) copy-start(bf16[2,640,128]{2,1,0:T(8,128)(2,1)S(1)} %collective-permute-done.1.near) | copy-start | bytes 983044
  13.8 18.3 %collective-permute-start.3 = (bf16[2,640,128]{2,1,0:T(8,128)(2,1)S(1)}, bf16[2,640,128]{2,1,0:T(8,128)(2,1)S(1)}, u32[]{:S(2)}, u32[]{:S(2)}) collective-permute-start(bf16[2,640,128]{2,1,0:T(8,128)(2,1)S(1)} %collective-permute-done.1.near), channel_id=1, source_target_pairs={{0,1},{1,0},{2,3},{3,2},{4,5},{5,4},{6,7},{7,6},{8,9},{9,8},{10,11... | collective-permute-start | bytes 983048 | tf_op jit(solution)/shard_map/ppermute | solution.py:337
  17.5 2.7 %copy-start.7 = (bf16[640,128]{1,0:T(8,128)(2,1)}, bf16[640,128]{1,0:T(8,128)(2,1)S(1)}, u32[]{:S(2)}) copy-start(bf16[640,128]{1,0:T(8,128)(2,1)S(1)} %collective-permute-done.2.far) | copy-start | bytes 491524
  17.5 14.6 %collective-permute-start.4 = (bf16[640,128]{1,0:T(8,128)(2,1)S(1)}, bf16[640,128]{1,0:T(8,128)(2,1)S(1)}, u32[]{:S(2)}, u32[]{:S(2)}) collective-permute-start(bf16[640,128]{1,0:T(8,128)(2,1)S(1)} %collective-permute-done.2.far), channel_id=1, source_target_pairs={{0,1},{1,0},{2,3},{3,2},{4,5},{5,4},{6,7},{7,6},{8,9},{9,8},{10,11... | collective-permute-start | bytes 491528 | tf_op jit(solution)/shard_map/ppermute | solution.py:338
  20.7 11.4 %copy-start.3 = (bf16[2,224,128]{2,1,0:T(8,128)(2,1)}, bf16[2,224,128]{2,1,0:T(8,128)(2,1)S(1)}, u32[]{:S(2)}) copy-start(bf16[2,224,128]{2,1,0:T(8,128)(2,1)S(1)} %reshape.46.pack0) | copy-start | bytes 344068
  20.7 4.8 %collective-permute-start.7 = (bf16[2,224,128]{2,1,0:T(8,128)(2,1)S(1)}, bf16[2,224,128]{2,1,0:T(8,128)(2,1)S(1)}, u32[]{:S(2)}, u32[]{:S(2)}) collective-permute-start(bf16[2,224,128]{2,1,0:T(8,128)(2,1)S(1)} %reshape.46.pack0), channel_id=1, source_target_pairs={{0,96},{32,0},{64,32},{96,64},{1,97},{33,1},{65,33},{97,65},{2,98}... | collective-permute-start | bytes 344072 | tf_op jit(solution)/shard_map/ppermute | solution.py:305
  23.3 5.3 %collective-permute-start.6 = (bf16[2,224,128]{2,1,0:T(8,128)(2,1)S(1)}, bf16[2,224,128]{2,1,0:T(8,128)(2,1)S(1)}, u32[]{:S(2)}, u32[]{:S(2)}) collective-permute-start(bf16[2,224,128]{2,1,0:T(8,128)(2,1)S(1)} %reshape.46.pack0), channel_id=1, source_target_pairs={{0,64},{32,96},{64,0},{96,32},{1,65},{33,97},{65,1},{97,33},{2,66}... | collective-permute-start | bytes 344072 | tf_op jit(solution)/shard_map/ppermute | solution.py:305
  23.8 8.3 %collective-permute-start.5 = (bf16[2,224,128]{2,1,0:T(8,128)(2,1)S(1)}, bf16[2,224,128]{2,1,0:T(8,128)(2,1)S(1)}, u32[]{:S(2)}, u32[]{:S(2)}) collective-permute-start(bf16[2,224,128]{2,1,0:T(8,128)(2,1)S(1)} %reshape.46.pack0), channel_id=1, source_target_pairs={{0,32},{32,64},{64,96},{96,0},{1,33},{33,65},{65,97},{97,1},{2,34}... | collective-permute-start | bytes 344072 | tf_op jit(solution)/shard_map/ppermute | solution.py:305
  25.5 6.6 %copy-start.9 = (bf16[2,224,128]{2,1,0:T(8,128)(2,1)}, bf16[2,224,128]{2,1,0:T(8,128)(2,1)S(1)}, u32[]{:S(2)}) copy-start(bf16[2,224,128]{2,1,0:T(8,128)(2,1)S(1)} %collective-permute-done.7.pack3) | copy-start | bytes 344068
  28.5 3.6 %copy-start.10 = (bf16[2,224,128]{2,1,0:T(8,128)(2,1)}, bf16[2,224,128]{2,1,0:T(8,128)(2,1)S(1)}, u32[]{:S(2)}) copy-start(bf16[2,224,128]{2,1,0:T(8,128)(2,1)S(1)} %collective-permute-done.6.pack2) | copy-start | bytes 344068
  32.1 0.6 copy-start.11
  32.1 0.7 copy-start.8
  32.8 0.7 copy-start.6
  75.3 13.6 %collective-permute-start.8 = (bf16[960,128]{1,0:T(8,128)(2,1)}, bf16[960,128]{1,0:T(8,128)(2,1)S(1)}, u32[]{:S(2)}, u32[]{:S(2)}) collective-permute-start(bf16[960,128]{1,0:T(8,128)(2,1)} %get-tuple-element.8), channel_id=1, source_target_pairs={{0,32},{32,64},{64,96},{96,0},{1,33},{33,65},{65,97},{97,1},{2,34}... | collective-permute-start | bytes 737288 | tf_op jit(solution)/shard_map/ppermute | solution.py:305
  75.3 13.6 %collective-permute-start.9 = (bf16[960,128]{1,0:T(8,128)(2,1)}, bf16[960,128]{1,0:T(8,128)(2,1)S(1)}, u32[]{:S(2)}, u32[]{:S(2)}) collective-permute-start(bf16[960,128]{1,0:T(8,128)(2,1)} %get-tuple-element.9), channel_id=1, source_target_pairs={{0,64},{32,96},{64,0},{96,32},{1,65},{33,97},{65,1},{97,33},{2,66}... | collective-permute-start | bytes 737288 | tf_op jit(solution)/shard_map/ppermute | solution.py:305
  75.7 13.2 %collective-permute-start.10 = (bf16[960,128]{1,0:T(8,128)(2,1)}, bf16[960,128]{1,0:T(8,128)(2,1)S(1)}, u32[]{:S(2)}, u32[]{:S(2)}) collective-permute-start(bf16[960,128]{1,0:T(8,128)(2,1)} %get-tuple-element.10), channel_id=1, source_target_pairs={{0,96},{32,0},{64,32},{96,64},{1,97},{33,1},{65,33},{97,65},{2,98}... | collective-permute-start | bytes 737288 | tf_op jit(solution)/shard_map/ppermute | solution.py:305
  88.9 1.0 copy-start
  90.1 3.1 %collective-permute-start.11 = (bf16[448,128]{1,0:T(8,128)(2,1)S(1)}, bf16[448,128]{1,0:T(8,128)(2,1)S(1)}, u32[]{:S(2)}, u32[]{:S(2)}) collective-permute-start(bf16[448,128]{1,0:T(8,128)(2,1)S(1)} %convert_element_type.55), channel_id=1, source_target_pairs={{0,1},{1,0},{2,3},{3,2},{4,5},{5,4},{6,7},{7,6},{8,9},{9,8},{10,11... | collective-permute-start | bytes 344072 | tf_op jit(solution)/shard_map/ppermute | solution.py:343
  93.3 7.9 %collective-permute-start.14 = (bf16[448,128]{1,0:T(8,128)(2,1)S(1)}, bf16[448,128]{1,0:T(8,128)(2,1)S(1)}, u32[]{:S(2)}, u32[]{:S(2)}) collective-permute-start(bf16[448,128]{1,0:T(8,128)(2,1)S(1)} %add_convert_fusion.1), channel_id=1, source_target_pairs={{0,6},{1,7},{2,0},{3,1},{4,2},{5,3},{6,4},{7,5},{8,14},{9,15},{10,... | collective-permute-start | bytes 344072 | tf_op jit(solution)/shard_map/ppermute | solution.py:305
  96.6 5.7 %collective-permute-start.13 = (bf16[448,128]{1,0:T(8,128)(2,1)S(1)}, bf16[448,128]{1,0:T(8,128)(2,1)S(1)}, u32[]{:S(2)}, u32[]{:S(2)}) collective-permute-start(bf16[448,128]{1,0:T(8,128)(2,1)S(1)} %add_convert_fusion.1), channel_id=1, source_target_pairs={{0,4},{1,5},{2,6},{3,7},{4,0},{5,1},{6,2},{7,3},{8,12},{9,13},{10,... | collective-permute-start | bytes 344072 | tf_op jit(solution)/shard_map/ppermute | solution.py:305
  96.8 8.6 %collective-permute-start.12 = (bf16[448,128]{1,0:T(8,128)(2,1)S(1)}, bf16[448,128]{1,0:T(8,128)(2,1)S(1)}, u32[]{:S(2)}, u32[]{:S(2)}) collective-permute-start(bf16[448,128]{1,0:T(8,128)(2,1)S(1)} %add_convert_fusion.1), channel_id=1, source_target_pairs={{0,2},{1,3},{2,4},{3,5},{4,6},{5,7},{6,0},{7,1},{8,10},{9,11},{10,... | collective-permute-start | bytes 344072 | tf_op jit(solution)/shard_map/ppermute | solution.py:305
  105.5 7.8 %collective-permute-start.17 = (bf16[448,128]{1,0:T(8,128)(2,1)S(1)}, bf16[448,128]{1,0:T(8,128)(2,1)S(1)}, u32[]{:S(2)}, u32[]{:S(2)}) collective-permute-start(bf16[448,128]{1,0:T(8,128)(2,1)S(1)} %add_convert_fusion), channel_id=1, source_target_pairs={{0,24},{1,25},{2,26},{3,27},{4,28},{5,29},{6,30},{7,31},{8,0},{9,1... | collective-permute-start | bytes 344072 | tf_op jit(solution)/shard_map/ppermute | solution.py:305
  107.4 5.9 %collective-permute-start.16 = (bf16[448,128]{1,0:T(8,128)(2,1)S(1)}, bf16[448,128]{1,0:T(8,128)(2,1)S(1)}, u32[]{:S(2)}, u32[]{:S(2)}) collective-permute-start(bf16[448,128]{1,0:T(8,128)(2,1)S(1)} %add_convert_fusion), channel_id=1, source_target_pairs={{0,16},{1,17},{2,18},{3,19},{4,20},{5,21},{6,22},{7,23},{8,24},{9,... | collective-permute-start | bytes 344072 | tf_op jit(solution)/shard_map/ppermute | solution.py:305
  108.7 7.1 %collective-permute-start.15 = (bf16[448,128]{1,0:T(8,128)(2,1)S(1)}, bf16[448,128]{1,0:T(8,128)(2,1)S(1)}, u32[]{:S(2)}, u32[]{:S(2)}) collective-permute-start(bf16[448,128]{1,0:T(8,128)(2,1)S(1)} %add_convert_fusion), channel_id=1, source_target_pairs={{0,8},{1,9},{2,10},{3,11},{4,12},{5,13},{6,14},{7,15},{8,16},{9,17... | collective-permute-start | bytes 344072 | tf_op jit(solution)/shard_map/ppermute | solution.py:305

commit v2 on v1

v2 whole, which is shorter than its diff:
```python
import jax
import jax.numpy as jnp
from jax import lax
from jax.experimental import pallas as pl
from jax.experimental.pallas import tpu as pltpu
from jax.sharding import PartitionSpec as P

ROWS = 4
WIDTH = 80
SINGLE = 12
TOTAL = 36
LANES = 128
F32 = jnp.float32
BF16 = jnp.bfloat16


def sigmoid(v):
    return 0.5 * jnp.tanh(0.5 * v) + 0.5


def slope(v):
    s = sigmoid(v)
    return s * (1.0 + v * (1.0 - s))


def at_row(row):
    return pl.multiple_of(row * WIDTH, 16)


def constants():
    er = lax.broadcasted_iota(jnp.int32, (LANES, 4 * LANES), 0)
    ec = lax.broadcasted_iota(jnp.int32, (LANES, 4 * LANES), 1)
    expand = jnp.where(er == lax.shift_right_logical(ec, 2), 1.0, 0.0).astype(BF16)
    cr = lax.broadcasted_iota(jnp.int32, (4 * LANES, LANES), 0)
    cc = lax.broadcasted_iota(jnp.int32, (4 * LANES, LANES), 1)
    collapse = jnp.where(cc == lax.shift_right_logical(cr, 2), 1.0, 0.0).astype(BF16)
    plane = lax.bitwise_and(lax.broadcasted_iota(jnp.int32, (32, LANES), 1), 3)
    return expand, collapse, [plane == z for z in range(4)]


def build_kernel(pack0, pack1, pack2, pack3, w1, wb, wpack, lx, lxt, block):
    seg = lax.axis_index("segment")
    for k, pack in enumerate((pack0, pack1, pack2, pack3)):
        wpack[lax.rem(seg - k + 4, 4)] = pack[...]
    expand, _, on_plane = constants()

    def build(index, carry):
        w = wpack[lax.div(index, 2), lax.rem(index, 2)]
        lx[...] = jnp.dot(w, expand, preferred_element_type=F32)
        for q in range(7):
            lxt[q * LANES : (q + 1) * LANES, :] = lax.dot_general(
                w[q * 32 : (q + 1) * 32], expand[:32, :LANES], (((0,), (0,)), ((), ())), preferred_element_type=F32
            )
        for dy in range(3):
            for dx in range(3):
                taps = [9 * dz + 3 * dy + dx for dz in range(3)]
                fwd = [lx[t // 4 * 32 : t // 4 * 32 + 32, t % 4 * LANES : (t % 4 + 1) * LANES] for t in taps]
                bwd = [lxt[t * 32 : t * 32 + 32, :] for t in taps]
                for z in range(4):
                    vf = jnp.zeros((32, LANES), F32)
                    vb = jnp.zeros((32, LANES), F32)
                    for dz in range(3):
                        if 0 <= z + 1 - dz < 4:
                            vf = jnp.where(on_plane[z + 1 - dz], fwd[dz], vf)
                        if 0 <= z + dz - 1 < 4:
                            vb = jnp.where(on_plane[z + dz - 1], bwd[dz], vb)
                    block[0, pl.ds(z, 32, stride=4), :] = vf
                    block[1, pl.ds(z, 32, stride=4), :] = vb
                w1[index, dy * LANES : (dy + 1) * LANES, dx * LANES : (dx + 1) * LANES] = block[0].astype(BF16)
                wb[index, (2 - dy) * LANES : (3 - dy) * LANES, (2 - dx) * LANES : (3 - dx) * LANES] = block[1].astype(
                    BF16
                )
        return carry

    lax.fori_loop(0, 8, build, 0)


def main_kernel(
    own, oth, near, far, near_other, far_other, w1, wb,
    out0, out1, out2, out3, keep0, keep1, keep2, keep3, send,
    crop, cot, feats, merged, hidden, delta, sd, fd, pre1, pre2, grads, terms, out_all, wg_all,
):
    seg = lax.axis_index("segment")
    gy = lax.axis_index("gy")
    core = lax.rem(gy, 2)
    half = lax.div(seg, 2)
    column = lax.broadcasted_iota(jnp.int32, (1, WIDTH, LANES), 1)

    def put(dst, row, src, src_row, rows):
        dst[row * WIDTH : (row + rows) * WIDTH, :] = src[src_row * WIDTH : (src_row + rows) * WIDTH, :]

    @pl.when(core == 0)
    def _():
        put(crop, 0, far, 0, 8)
        put(crop, 8, near.at[0], 0, 8)
        put(crop, 16, own.at[0], 0, 4)
        put(crop, 20, oth.at[0], 0, 4)
        put(crop, 24, near_other.at[0], 4, 4)
        put(crop, 28, near_other.at[0], 0, 4)
        put(crop, 32, far_other, 4, 4)
        put(cot, 0, near.at[1], 0, 8)
        put(cot, 8, own.at[1], 0, 4)
        put(cot, 12, oth.at[1], 0, 4)
        put(cot, 16, near_other.at[1], 4, 4)

    @pl.when(core == 1)
    def _():
        put(crop, 0, far_other, 4, 4)
        put(crop, 4, near_other.at[0], 0, 8)
        put(crop, 12, oth.at[0], 0, 4)
        put(crop, 16, own.at[0], 0, 4)
        put(crop, 20, near.at[0], 4, 4)
        put(crop, 24, near.at[0], 0, 4)
        put(crop, 28, far, 4, 4)
        put(crop, 32, far, 0, 4)
        put(cot, 0, near_other.at[1], 4, 4)
        put(cot, 4, oth.at[1], 0, 4)
        put(cot, 8, own.at[1], 0, 4)
        put(cot, 12, near.at[1], 4, 4)
        put(cot, 16, near.at[1], 0, 4)

    _, collapse, on_plane = constants()

    def chunks(low, high, body):
        count = 1 if high - low <= SINGLE else 2
        rows = (high - low) // count

        def step(i, carry):
            body(at_row(low + rows * i), rows * WIDTH)
            return carry

        lax.fori_loop(0, count, step, 0)

    def by_rows(v):
        return v.reshape(v.shape[0] // WIDTH, WIDTH, LANES)

    def from_left(v):
        return jnp.where(column == 0, 0.0, pltpu.roll(by_rows(v), 1, 1)).reshape(v.shape)

    def from_right(v):
        return jnp.where(column == WIDTH - 1, 0.0, pltpu.roll(by_rows(v), WIDTH - 1, 1)).reshape(v.shape)

    def stacked(src, base, span):
        return jnp.concatenate(
            [
                src[pl.ds(pl.multiple_of(base - WIDTH, 16), span), :],
                src[pl.ds(base, span), :],
                src[pl.ds(pl.multiple_of(base + WIDTH, 16), span), :],
            ],
            axis=1,
        )

    def conv(src, matrix, low, high, then):
        def body(base, span):
            p = jnp.dot(stacked(src, base, span), matrix[...], preferred_element_type=F32)
            then(base, span, p[:, LANES : 2 * LANES] + from_left(p[:, :LANES]) + from_right(p[:, 2 * LANES :]))

        chunks(low, high, body)

    def clear_outside(dst, low, high):
        top = 16 - ROWS * gy
        bottom = 16 + ROWS * (lax.axis_size("gy") - gy)

        def clear(i, carry):
            dst[pl.ds(at_row(i), WIDTH), :] = jnp.zeros((WIDTH, LANES), BF16)
            return carry

        @pl.when(top > low)
        def _():
            lax.fori_loop(low, jnp.minimum(top, high), clear, 0)

        @pl.when(bottom < high)
        def _():
            lax.fori_loop(jnp.maximum(bottom, low), high, clear, 0)

    for s in range(4):
        source = crop if s == 0 else feats.at[0] if s == 1 else merged.at[s - 2]

        def first(base, span, v, s=s):
            pre1[s, pl.ds(base, span), :] = v
            hidden[s, pl.ds(base, span), :] = (v * sigmoid(v)).astype(BF16)

        conv(source, w1.at[2 * s], 2 * s + 1, 35 - 2 * s, first)
        clear_outside(hidden.at[s], 2 * s + 1, 35 - 2 * s)

        def second(base, span, v, s=s):
            pre2[s, pl.ds(base, span), :] = v
            out = (v * sigmoid(v)).astype(BF16)
            feats[s, pl.ds(base, span), :] = out
            if s == 1 or s == 2:
                skip = feats[0, pl.ds(base, span), :] if s == 1 else crop[pl.ds(base, span), :]
                merged[s - 1, pl.ds(base, span), :] = (out.astype(F32) + skip.astype(F32)).astype(BF16)

        conv(hidden.at[s], w1.at[2 * s + 1], 2 * s + 2, 34 - 2 * s, second)
        if s == 0:
            clear_outside(feats.at[0], 2, 34)
        if s == 1 or s == 2:
            clear_outside(merged.at[s - 1], 2 * s + 2, 34 - 2 * s)

    def first_sd(base, span):
        incoming = cot[pl.ds(pl.multiple_of(base - 8 * WIDTH, 16), span), :]
        sd[pl.ds(base, span), :] = (incoming.astype(F32) * slope(pre2[3, pl.ds(base, span), :])).astype(BF16)

    chunks(8, 28, first_sd)

    own_low = half * 16
    mine = (column >= own_low) & (column < own_low + 64)
    base0 = 16 * WIDTH
    span = ROWS * WIDTH
    slot_of = lambda s: lax.rem(s - seg + 4, 4)

    def kernel_grads(src, grad, s, which):
        d = jnp.where(mine, by_rows(grad[base0 : base0 + span, :].astype(F32)), 0.0).reshape(span, LANES)
        shifted = jnp.concatenate([from_right(d).astype(BF16), d.astype(BF16), from_left(d).astype(BF16)], axis=1)
        product = lax.dot_general(
            stacked(src, base0, span), shifted, (((0,), (0,)), ((), ())), preferred_element_type=F32
        )
        for dx in range(3):
            grads[dx] = product[:, dx * LANES : (dx + 1) * LANES]
        terms[6 * 32 :, 3 * LANES :] = jnp.zeros((32, LANES), BF16)
        for dy in range(3):
            for dx in range(3):
                rows = [grads[dx, pl.ds(dy * LANES + z, 32, stride=4), :] for z in range(4)]
                for dz in range(3):
                    total = jnp.zeros((32, LANES), F32)
                    for z in range(4):
                        if 0 <= z + 1 - dz < 4:
                            total = jnp.where(on_plane[z + 1 - dz], rows[z], total)
                    t = 9 * dz + 3 * dy + dx
                    terms[t // 4 * 32 : t // 4 * 32 + 32, t % 4 * LANES : (t % 4 + 1) * LANES] = total.astype(BF16)
        packed = jnp.dot(terms[...], collapse, preferred_element_type=F32).astype(BF16)
        wg_all[which, slot_of(s)] = packed

    for s in (3, 2, 1, 0):
        source = crop if s == 0 else feats.at[0] if s == 1 else merged.at[s - 2]
        low, high = 8 + 2 * (3 - s), 28 - 2 * (3 - s)

        def to_first(base, span, v, s=s):
            fd[pl.ds(base, span), :] = (v * slope(pre1[s, pl.ds(base, span), :])).astype(BF16)

        kernel_grads(hidden.at[s], sd, s, 1)
        conv(sd, wb.at[2 * s + 1], low + 1, high - 1, to_first)
        clear_outside(fd, low + 1, high - 1)
        kernel_grads(source, fd, s, 0)

        def to_delta(base, span, v, s=s):
            out = v.astype(BF16)
            if s == 1 or s == 0:
                other = delta[2 if s == 1 else 3, pl.ds(base, span), :]
                out = (out.astype(F32) + other.astype(F32)).astype(BF16)
            delta[s, pl.ds(base, span), :] = out
            if s > 0:
                sd[pl.ds(base, span), :] = (
                    out.astype(F32) * slope(pre2[s - 1, pl.ds(base, span), :])
                ).astype(BF16)

        conv(fd, wb.at[2 * s], low + 2, high - 2, to_delta)
        if s > 0:
            clear_outside(sd, low + 2, high - 2)

    for s in range(4):
        for y in range(ROWS):
            place = pl.ds(pl.multiple_of(base0 + y * WIDTH + own_low, 16), 64)
            out_all[slot_of(s), 64 * y : 64 * y + 64, :] = feats[s, place, :]
            out_all[slot_of(s), 256 + 64 * y : 320 + 64 * y, :] = delta[s, place, :]
    for k, out in enumerate((out0, out1, out2, out3)):
        out[...] = out_all[k]
    for k, keep in enumerate((keep0, keep1, keep2, keep3)):
        keep[...] = wg_all[core, k]
    send[...] = wg_all[1 - core]


VMEM = pl.BlockSpec(memory_space=pltpu.VMEM)
MATRICES = (8, 3 * LANES, 3 * LANES)


def build_call(*packs):
    return pl.pallas_call(
        build_kernel,
        out_shape=[jax.ShapeDtypeStruct(MATRICES, BF16)] * 2,
        in_specs=[VMEM] * 4,
        out_specs=[VMEM] * 2,
        scratch_shapes=[
            pltpu.VMEM((4, 2, 224, LANES), BF16),
            pltpu.VMEM((224, 4 * LANES), F32),
            pltpu.VMEM((7 * LANES, LANES), F32),
            pltpu.VMEM((2, LANES, LANES), F32),
        ],
        compiler_params=pltpu.CompilerParams(vmem_limit_bytes=8 * 1024 * 1024),
        cost_estimate=pl.CostEstimate(flops=5_000_000_000, bytes_accessed=10_000_000, transcendentals=0),
        name="banded",
    )(*packs)


def main_call(*operands):
    acts = (TOTAL * WIDTH, LANES)
    return pl.pallas_call(
        main_kernel,
        out_shape=[jax.ShapeDtypeStruct((512, LANES), BF16)] * 4
        + [jax.ShapeDtypeStruct((224, LANES), BF16)] * 4
        + [jax.ShapeDtypeStruct((4, 224, LANES), BF16)],
        in_specs=[VMEM] * 8,
        out_specs=[VMEM] * 9,
        scratch_shapes=[
            pltpu.VMEM(acts, BF16),
            pltpu.VMEM((20 * WIDTH, LANES), BF16),
            pltpu.VMEM((4,) + acts, BF16),
            pltpu.VMEM((2,) + acts, BF16),
            pltpu.VMEM((4,) + acts, BF16),
            pltpu.VMEM((4,) + acts, BF16),
            pltpu.VMEM(acts, BF16),
            pltpu.VMEM(acts, BF16),
            pltpu.VMEM((4,) + acts, F32),
            pltpu.VMEM((4,) + acts, F32),
            pltpu.VMEM((3, 3 * LANES, LANES), F32),
            pltpu.VMEM((224, 4 * LANES), BF16),
            pltpu.VMEM((4, 512, LANES), BF16),
            pltpu.VMEM((2, 4, 224, LANES), BF16),
        ],
        compiler_params=pltpu.CompilerParams(vmem_limit_bytes=40 * 1024 * 1024),
        cost_estimate=pl.CostEstimate(flops=20_000_000_000, bytes_accessed=10_000_000, transcendentals=0),
        name="sections",
    )(*operands)


def rotated(value, axis, group, step, stride):
    count = lax.axis_size(axis)

    def target(i):
        place = i // stride % group
        return i + ((place + step) % group - place) * stride

    return lax.ppermute(value, axis, [(i, target(i)) for i in range(count)])


def local(crops, cotangent, weights):
    micro_count, channels, planes, rows, across = crops.shape
    seg = lax.axis_index("segment")
    micro, half = seg % 2, seg // 2
    devices = lax.axis_size("gy")
    swap = [(i, i ^ 1) for i in range(devices)]

    def tile(volume):
        field = lax.dynamic_index_in_dim(volume, micro, 0, keepdims=False)
        field = jnp.transpose(field, (2, 3, 0, 1)).reshape(rows, across, channels * planes)
        return lax.dynamic_slice_in_dim(field, half * 48, WIDTH, 1).reshape(rows * WIDTH, channels * planes)

    own = jnp.stack([tile(crops), tile(cotangent)])
    packed = jnp.pad(weights[0], ((0, 0), (0, 1), (0, 0), (0, 0))).reshape(2, 7, 4, channels, channels)
    packed = jnp.transpose(packed, (0, 1, 3, 2, 4)).reshape(2, 7 * channels, 4 * channels)

    oth = lax.ppermute(own, "gy", swap)
    block = jnp.concatenate([own, oth], axis=1)

    def outward(distance):
        return [
            (i, i + 2 * distance * (1 if i % 2 == 0 else -1))
            for i in range(devices)
            if 0 <= i + 2 * distance * (1 if i % 2 == 0 else -1) < devices
        ]

    near = lax.ppermute(block, "gy", outward(1))
    far = lax.ppermute(block[0], "gy", outward(2))
    others = [rotated(packed, "segment", 4, k, 1) for k in (1, 2, 3)]
    near_other = lax.ppermute(near, "gy", swap)
    far_other = lax.ppermute(far, "gy", swap)
    w1, wb = build_call(packed, *others)
    outs = main_call(own, oth, near, far, near_other, far_other, w1, wb)
    fields, keep, send = outs[:4], outs[4:8], outs[8]

    got = lax.ppermute(send, "gy", swap)
    part = [(keep[k].astype(F32) + got[k].astype(F32)).astype(BF16) for k in range(4)]
    total = part[0].astype(F32)
    for k in (1, 2, 3):
        total = total + rotated(part[k], "segment", 4, k, 1).astype(F32)
    for stride in (2, 8):
        mine = total.astype(BF16)
        total = mine.astype(F32)
        for k in (1, 2, 3):
            total = total + rotated(mine, "gy", 4, k, stride).astype(F32)
    mine = total.astype(BF16)
    other = lax.ppermute(mine, "gy", swap)
    low_core = lax.axis_index("gy") % 2 == 0
    both = jnp.stack([jnp.where(low_core, mine, other), jnp.where(low_core, other, mine)])
    grads = both.reshape(2, 7, channels, 4, channels).transpose(0, 1, 3, 2, 4)
    grads = grads.reshape(2, 28, channels, channels)[:, :27].astype(F32)

    by_step = jnp.stack([fields[0]] + [rotated(fields[k], "segment", 4, k, 1) for k in (1, 2, 3)])
    by_source = jnp.stack([lax.dynamic_index_in_dim(by_step, (seg - j) % 4, 0, keepdims=False) for j in range(4)])
    fields = by_source.reshape(2, 2, 2, rows, across // 2, channels, planes)
    fields = jnp.transpose(fields, (2, 1, 5, 6, 3, 0, 4)).reshape(2, micro_count, channels, planes, rows, across)
    return fields[0][None], grads[None], fields[1].astype(F32)[None]


def solution(mesh):
    return jax.shard_map(
        local,
        mesh=mesh,
        in_specs=(
            P(None, None, None, "gy", None),
            P(None, None, None, "gy", None),
            P("segment", None, None, None, None),
        ),
        out_specs=(
            P("segment", None, None, None, "gy", None),
            P("segment", None, None, None, None),
            P("segment", None, None, None, "gy", None),
        ),
        check_vma=False,
    )
```

time: 118 us -> 88 us (0.75)
  waiting for transfers between devices: 37 us -> 13.5 us
  Pallas kernels: 41.7 us -> 28.3 us
  starting transfers between devices: 25.1 us -> 35.4 us
  local copies, waits for them, and re-layouts: 10.9 us -> 7.69 us
    ppermute x12 -> x15, waiting for transfers between devices: 27.7 us -> 8.88 us  [rotated(): return lax.ppermute(value, axis, [(i, target(i)) for i in range(count)])]
    pallas_call x1 -> x2, Pallas kernels: 41.7 us -> 28.3 us  [the longest x1 23.3 us: main_call(): pl.pallas_call(main_kernel, out_shape=[jax.ShapeDtypeStruct((512, LANES),...]
    ppermute x1 -> x2, starting transfers between devices: 2.14 us -> 7.72 us  [the longest x1 4.12 us: local(): other = lax.ppermute(mine, 'gy', swap)]
    ppermute x1, waiting for transfers between devices: 5.47 us -> 0.01 us  [local(): near = lax.ppermute(block, 'gy', outward(1))]
    ppermute x12 -> x15, starting transfers between devices: 14.5 us -> 19.2 us  [rotated(): return lax.ppermute(value, axis, [(i, target(i)) for i in range(count)])]
    unnamed x30 -> x8, local copies, waits for them, and re-layouts: 5.86 us -> 3.8 us
    ppermute x1, starting transfers between devices: 2.59 us -> 4.37 us  [local(): far_other = lax.ppermute(far, 'gy', swap)]
    ppermute x1, starting transfers between devices: 1.82 us -> 0.08 us  [local(): near_other = lax.ppermute(near, 'gy', swap)]
  transfers between devices with their start and end apart: 18 -> 22, of which waited for: 12 -> 9; matrix products, arithmetic and copies ran while one was open for 5% -> 7% of each run, Pallas kernels for 0% -> 6%
where the time goes in v2:
time: 88 us; the launch traced here: 87.9 us
  starting transfers between devices  35.4 us (40%)
  Pallas kernels  28.3 us (32%)
  waiting for transfers between devices  13.5 us (15%)
  local copies, waits for them, and re-layouts  7.69 us (9%)
  other arithmetic  1.98 us (2%)
  between operations  0.97 us (1%)
    pallas_call x1, Pallas kernels, main_call(): pl.pallas_call(main_kernel, out_shape=[jax.ShapeDtypeStruct((512, LANES),...  23.3 us
    ppermute x15, starting transfers between devices, rotated(): return lax.ppermute(value, axis, [(i, target(i)) for i in range(count)])  19.2 us
    ppermute x15, waiting for transfers between devices, rotated(): return lax.ppermute(value, axis, [(i, target(i)) for i in range(count)])  8.88 us
    pallas_call x1, Pallas kernels, build_call(): pl.pallas_call(build_kernel, out_shape=[jax.ShapeDtypeStruct(MATRICES, BF...  4.96 us
    ppermute x1, starting transfers between devices, local(): far_other = lax.ppermute(far, 'gy', swap)  4.37 us
    ppermute x1, starting transfers between devices, local(): other = lax.ppermute(mine, 'gy', swap)  4.12 us
    unnamed x8, local copies, waits for them, and re-layouts  3.8 us
    ppermute x1, starting transfers between devices, local(): got = lax.ppermute(send, 'gy', swap)  3.6 us
  transfers between devices with their start and end apart: 22, of which 9 were waited for; matrix products, arithmetic and copies ran while one was open for 7% of the time, Pallas kernels for 6%

profile of v2, /device:TPU:1, one launch (start us, length us, event | category | flops | bytes accessed | tf_op | source)
XLA Modules:
  0.0 87.9 jit_solution(7045301055625213704)
XLA Ops:
  0.7 1.1 %constant_dynamic-slice_fusion.5 = (bf16[1,32,4,4,128]{4,3,2,1,0:T(4,128)(2,1)S(1)}, bf16[1,32,4,4,128]{4,3,2,1,0:T(4,128)(2,1)S(1)}) fusion(bf16[2,32,4,4,128]{4,3,2,1,0:T(4,128)(2,1)} %param.4, s32[]{:T(128)S(6)} %select_n.66, bf16[2,32,4,4,128]{4,3,2,1,0:T(4,128)(2,1)} %param.3), kind=kLoop, calls=%fused_computation.35 | loop fusion | bytes 524292 | tf_op jit(solution)/shard_map/jit(dynamic_index_in_dim)/dynamic_slice | solution.py:344
  1.8 0.1 copy.33
  2.0 0.1 constant_dynamic-slice_fusion.6
  2.1 0.1 copy.34
  2.2 0.1 copy.36
  2.3 0.1 constant_dynamic-slice_fusion.4
  2.4 0.1 copy.37
  2.6 1.5 %collective-permute-start = (bf16[2,320,128]{2,1,0:T(8,128)(2,1)S(1)}, bf16[2,320,128]{2,1,0:T(8,128)(2,1)S(1)}, u32[]{:S(2)}, u32[]{:S(2)}) collective-permute-start(bf16[2,320,128]{2,1,0:T(8,128)(2,1)S(1)} %pad_maximum_fusion.3.own), channel_id=1, source_target_pairs={{0,1},{1,0},{2,3},{3,2},{4,5},{5,4},{6,7},{7,6},{8,9},{9,8},{10,11... | collective-permute-start | bytes 491528 | tf_op jit(solution)/shard_map/ppermute | solution.py:352
  4.1 1.0 %collective-permute-done.oth = bf16[2,320,128]{2,1,0:T(8,128)(2,1)S(1)} collective-permute-done((bf16[2,320,128]{2,1,0:T(8,128)(2,1)S(1)}, bf16[2,320,128]{2,1,0:T(8,128)(2,1)S(1)}, u32[]{:S(2)}, u32[]{:S(2)}) %collective-permute-start) | collective-permute-done | bytes 163872 | tf_op jit(solution)/shard_map/ppermute | solution.py:352
  5.1 1.3 %collective-permute-start.1 = (bf16[2,640,128]{2,1,0:T(8,128)(2,1)S(1)}, bf16[2,640,128]{2,1,0:T(8,128)(2,1)S(1)}, u32[]{:S(2)}, u32[]{:S(2)}) collective-permute-start(bf16[2,640,128]{2,1,0:T(8,128)(2,1)S(1)} %pad_maximum_fusion.2), channel_id=1, source_target_pairs={{0,2},{2,4},{3,1},{4,6},{5,3},{6,8},{7,5},{8,10},{9,7},{10,12},{11... | collective-permute-start | bytes 983048 | tf_op jit(solution)/shard_map/ppermute | solution.py:362
  6.5 1.3 %collective-permute-start.2 = (bf16[640,128]{1,0:T(8,128)(2,1)S(1)}, bf16[640,128]{1,0:T(8,128)(2,1)S(1)}, u32[]{:S(2)}, u32[]{:S(2)}) collective-permute-start(bf16[640,128]{1,0:T(8,128)(2,1)S(1)} %slice_bitcast_fusion.1), channel_id=1, source_target_pairs={{0,4},{2,6},{4,8},{5,1},{6,10},{7,3},{8,12},{9,5},{10,14},{11,7},{... | collective-permute-start | bytes 491528 | tf_op jit(solution)/shard_map/ppermute | solution.py:363
  7.8 0.1 pad.4
  7.9 0.2 copy.57
  8.1 0.2 reshape.56.pack0
  8.4 1.4 %collective-permute-start.5 = (bf16[2,224,128]{2,1,0:T(8,128)(2,1)S(1)}, bf16[2,224,128]{2,1,0:T(8,128)(2,1)S(1)}, u32[]{:S(2)}, u32[]{:S(2)}) collective-permute-start(bf16[2,224,128]{2,1,0:T(8,128)(2,1)S(1)} %reshape.56.pack0), channel_id=1, source_target_pairs={{0,32},{32,64},{64,96},{96,0},{1,33},{33,65},{65,97},{97,1},{2,34}... | collective-permute-start | bytes 344072 | tf_op jit(solution)/shard_map/ppermute | solution.py:333
  9.7 2.5 %collective-permute-start.6 = (bf16[2,224,128]{2,1,0:T(8,128)(2,1)S(1)}, bf16[2,224,128]{2,1,0:T(8,128)(2,1)S(1)}, u32[]{:S(2)}, u32[]{:S(2)}) collective-permute-start(bf16[2,224,128]{2,1,0:T(8,128)(2,1)S(1)} %reshape.56.pack0), channel_id=1, source_target_pairs={{0,64},{32,96},{64,0},{96,32},{1,65},{33,97},{65,1},{97,33},{2,66}... | collective-permute-start | bytes 344072 | tf_op jit(solution)/shard_map/ppermute | solution.py:333
  12.2 1.2 %collective-permute-start.7 = (bf16[2,224,128]{2,1,0:T(8,128)(2,1)S(1)}, bf16[2,224,128]{2,1,0:T(8,128)(2,1)S(1)}, u32[]{:S(2)}, u32[]{:S(2)}) collective-permute-start(bf16[2,224,128]{2,1,0:T(8,128)(2,1)S(1)} %reshape.56.pack0), channel_id=1, source_target_pairs={{0,96},{32,0},{64,32},{96,64},{1,97},{33,1},{65,33},{97,65},{2,98}... | collective-permute-start | bytes 344072 | tf_op jit(solution)/shard_map/ppermute | solution.py:333
  13.3 3.6 %collective-permute-done.2.far = bf16[640,128]{1,0:T(8,128)(2,1)S(1)} collective-permute-done((bf16[640,128]{1,0:T(8,128)(2,1)S(1)}, bf16[640,128]{1,0:T(8,128)(2,1)S(1)}, u32[]{:S(2)}, u32[]{:S(2)}) %collective-permute-start.2) | collective-permute-done | bytes 163872 | tf_op jit(solution)/shard_map/ppermute | solution.py:363
  16.9 4.4 %collective-permute-start.4 = (bf16[640,128]{1,0:T(8,128)(2,1)S(1)}, bf16[640,128]{1,0:T(8,128)(2,1)S(1)}, u32[]{:S(2)}, u32[]{:S(2)}) collective-permute-start(bf16[640,128]{1,0:T(8,128)(2,1)S(1)} %collective-permute-done.2.far), channel_id=1, source_target_pairs={{0,1},{1,0},{2,3},{3,2},{4,5},{5,4},{6,7},{7,6},{8,9},{9,8},{10,11... | collective-permute-start | bytes 491528 | tf_op jit(solution)/shard_map/ppermute | solution.py:366
  21.3 0.1 collective-permute-start.3
  21.4 0.0 collective-permute-done.7.pack3
  21.4 5.0 %banded.1 = (bf16[8,384,384]{2,1,0:T(8,128)(2,1)S(1)}, bf16[8,384,384]{2,1,0:T(8,128)(2,1)S(1)}) custom-call(bf16[2,224,128]{2,1,0:T(8,128)(2,1)S(1)} %reshape.56.pack0, bf16[2,224,128]{2,1,0:T(8,128)(2,1)S(1)} %collective-permute-done.5.pack1, bf16[2,224,128]{2,1,0:T(8,128)(2,1)S(1)} %collective-permute-done.6.pack2, ...), custom_call_target="tpu_custom_call" | custom-call | flops 5000000000 | bytes 10000000 | tf_op jit(solution)/shard_map/banded/pallas_call | solution.py:278
  26.4 0.0 collective-permute-done.4.far_other
  26.4 23.3 %sections.1 = (bf16[512,128]{1,0:T(8,128)(2,1)S(1)}, bf16[512,128]{1,0:T(8,128)(2,1)S(1)}, bf16[512,128]{1,0:T(8,128)(2,1)S(1)}, bf16[512,128]{1,0:T(8,128)(2,1)...) custom-call(bf16[2,320,128]{2,1,0:T(8,128)(2,1)S(1)} %pad_maximum_fu, ...), custom_call_target="tpu_custom_call" | custom-call | flops 20000000000 | bytes 10000000 | tf_op jit(solution)/shard_map/sections/pallas_call | solution.py:297
  49.7 3.6 %collective-permute-start.11 = (bf16[4,224,128]{2,1,0:T(8,128)(2,1)S(1)}, bf16[4,224,128]{2,1,0:T(8,128)(2,1)S(1)}, u32[]{:S(2)}, u32[]{:S(2)}) collective-permute-start(bf16[4,224,128]{2,1,0:T(8,128)(2,1)S(1)} %get-tuple-element.21), channel_id=1, source_target_pairs={{0,1},{1,0},{2,3},{3,2},{4,5},{5,4},{6,7},{7,6},{8,9},{9,8},{10,11... | collective-permute-start | bytes 688136 | tf_op jit(solution)/shard_map/ppermute | solution.py:371
  53.3 0.8 collective-permute-start.8
  54.1 2.7 %collective-permute-start.9 = (bf16[512,128]{1,0:T(8,128)(2,1)S(1)}, bf16[512,128]{1,0:T(8,128)(2,1)S(1)}, u32[]{:S(2)}, u32[]{:S(2)}) collective-permute-start(bf16[512,128]{1,0:T(8,128)(2,1)S(1)} %get-tuple-element.18), channel_id=1, source_target_pairs={{0,64},{32,96},{64,0},{96,32},{1,65},{33,97},{65,1},{97,33},{2,66}... | collective-permute-start | bytes 393224 | tf_op jit(solution)/shard_map/ppermute | solution.py:333
  56.9 0.4 collective-permute-start.10
  57.2 0.0 collective-permute-done.11
  57.2 0.1 fusion.3
  57.3 1.1 %collective-permute-start.12 = (bf16[224,128]{1,0:T(8,128)(2,1)S(1)}, bf16[224,128]{1,0:T(8,128)(2,1)S(1)}, u32[]{:S(2)}, u32[]{:S(2)}) collective-permute-start(bf16[224,128]{1,0:T(8,128)(2,1)S(1)} %get-tuple-element.37), channel_id=1, source_target_pairs={{0,32},{32,64},{64,96},{96,0},{1,33},{33,65},{65,97},{97,1},{2,34}... | collective-permute-start | bytes 172040 | tf_op jit(solution)/shard_map/ppermute | solution.py:333
  58.5 0.2 collective-permute-start.13
  58.7 0.8 collective-permute-done.8
  59.5 1.5 %collective-permute-start.14 = (bf16[224,128]{1,0:T(8,128)(2,1)S(1)}, bf16[224,128]{1,0:T(8,128)(2,1)S(1)}, u32[]{:S(2)}, u32[]{:S(2)}) collective-permute-start(bf16[224,128]{1,0:T(8,128)(2,1)S(1)} %get-tuple-element.38), channel_id=1, source_target_pairs={{0,96},{32,0},{64,32},{96,64},{1,97},{33,1},{65,33},{97,65},{2,98}... | collective-permute-start | bytes 172040 | tf_op jit(solution)/shard_map/ppermute | solution.py:333
  60.9 2.2 %collective-permute-done.9 = bf16[512,128]{1,0:T(8,128)(2,1)S(1)} collective-permute-done((bf16[512,128]{1,0:T(8,128)(2,1)S(1)}, bf16[512,128]{1,0:T(8,128)(2,1)S(1)}, u32[]{:S(2)}, u32[]{:S(2)}) %collective-permute-start.9) | collective-permute-done | bytes 131104 | tf_op jit(solution)/shard_map/ppermute | solution.py:333
  63.2 0.0 collective-permute-done.10
  63.2 0.1 pad_maximum_fusion
  63.3 1.6 %collective-permute-done.12 = bf16[224,128]{1,0:T(8,128)(2,1)S(1)} collective-permute-done((bf16[224,128]{1,0:T(8,128)(2,1)S(1)}, bf16[224,128]{1,0:T(8,128)(2,1)S(1)}, u32[]{:S(2)}, u32[]{:S(2)}) %collective-permute-start.12) | collective-permute-done | bytes 57376 | tf_op jit(solution)/shard_map/ppermute | solution.py:333
  64.9 0.7 collective-permute-done.13
  65.6 0.0 collective-permute-done.14
  65.7 0.1 collective-permute-start.15
  65.8 2.3 %collective-permute-start.16 = (bf16[224,128]{1,0:T(8,128)(2,1)S(1)}, bf16[224,128]{1,0:T(8,128)(2,1)S(1)}, u32[]{:S(2)}, u32[]{:S(2)}) collective-permute-start(bf16[224,128]{1,0:T(8,128)(2,1)S(1)} %add_convert_fusion.2), channel_id=1, source_target_pairs={{0,4},{1,5},{2,6},{3,7},{4,0},{5,1},{6,2},{7,3},{8,12},{9,13},{10,... | collective-permute-start | bytes 172040 | tf_op jit(solution)/shard_map/ppermute | solution.py:333
  68.1 0.4 collective-permute-start.17
  68.5 2.1 %collective-permute-done.15 = bf16[224,128]{1,0:T(8,128)(2,1)S(1)} collective-permute-done((bf16[224,128]{1,0:T(8,128)(2,1)S(1)}, bf16[224,128]{1,0:T(8,128)(2,1)S(1)}, u32[]{:S(2)}, u32[]{:S(2)}) %collective-permute-start.15) | collective-permute-done | bytes 57376 | tf_op jit(solution)/shard_map/ppermute | solution.py:333
  70.6 0.9 collective-permute-done.17
  71.5 1.4 %collective-permute-start.18 = (bf16[224,128]{1,0:T(8,128)(2,1)S(1)}, bf16[224,128]{1,0:T(8,128)(2,1)S(1)}, u32[]{:S(2)}, u32[]{:S(2)}) collective-permute-start(bf16[224,128]{1,0:T(8,128)(2,1)S(1)} %add_convert_fusion.1), channel_id=1, source_target_pairs={{0,8},{1,9},{2,10},{3,11},{4,12},{5,13},{6,14},{7,15},{8,16},{9,17... | collective-permute-start | bytes 172040 | tf_op jit(solution)/shard_map/ppermute | solution.py:333
  72.9 2.0 %collective-permute-start.19 = (bf16[224,128]{1,0:T(8,128)(2,1)S(1)}, bf16[224,128]{1,0:T(8,128)(2,1)S(1)}, u32[]{:S(2)}, u32[]{:S(2)}) collective-permute-start(bf16[224,128]{1,0:T(8,128)(2,1)S(1)} %add_convert_fusion.1), channel_id=1, source_target_pairs={{0,16},{1,17},{2,18},{3,19},{4,20},{5,21},{6,22},{7,23},{8,24},{9,... | collective-permute-start | bytes 172040 | tf_op jit(solution)/shard_map/ppermute | solution.py:333
  74.9 1.3 %collective-permute-start.20 = (bf16[224,128]{1,0:T(8,128)(2,1)S(1)}, bf16[224,128]{1,0:T(8,128)(2,1)S(1)}, u32[]{:S(2)}, u32[]{:S(2)}) collective-permute-start(bf16[224,128]{1,0:T(8,128)(2,1)S(1)} %add_convert_fusion.1), channel_id=1, source_target_pairs={{0,24},{1,25},{2,26},{3,27},{4,28},{5,29},{6,30},{7,31},{8,0},{9,1... | collective-permute-start | bytes 172040 | tf_op jit(solution)/shard_map/ppermute | solution.py:333
  76.2 0.1 pad_maximum_fusion.1
  76.3 0.2 copy.39
  76.5 0.5 reshape.57
  77.0 0.4 copy.56
  77.5 0.5 collective-permute-done.20
  78.0 4.1 %collective-permute-start.21 = (bf16[224,128]{1,0:T(8,128)(2,1)S(1)}, bf16[224,128]{1,0:T(8,128)(2,1)S(1)}, u32[]{:S(2)}, u32[]{:S(2)}) collective-permute-start(bf16[224,128]{1,0:T(8,128)(2,1)S(1)} %add_convert_fusion), channel_id=1, source_target_pairs={{0,1},{1,0},{2,3},{3,2},{4,5},{5,4},{6,7},{7,6},{8,9},{9,8},{10,11... | collective-permute-start | bytes 172040 | tf_op jit(solution)/shard_map/ppermute | solution.py:382
  82.1 0.2 slice_convert_fusion
  82.3 0.8 copy.47
  83.1 1.6 %reshape.66 = f32[1,2,32,4,4,128]{5,4,3,2,1,0:T(4,128)} reshape(f32[1,2,32,4,4,2,64]{6,5,4,3,2,1,0:T(2,128)S(1)} %copy.47) | data formatting | bytes 1048576
  84.7 0.4 copy.46
  85.1 1.0 %reshape.65 = bf16[1,2,32,4,4,128]{5,4,3,2,1,0:T(4,128)(2,1)} reshape(bf16[1,2,32,4,4,2,64]{6,5,4,3,2,1,0:T(2,128)(2,1)S(1)} %copy.46) | data formatting | bytes 524288
  86.1 0.1 stack.41
  86.2 0.1 stack.42
  86.4 0.4 maximum_bitcast_fusion
  86.8 0.1 copy.42
  86.8 1.0 %fusion = f32[1,2,27,32,32]{4,3,2,1,0:T(8,128)} fusion(bf16[2,28,32,32]{3,2,1,0:T(8,128)(2,1)S(1)} %bitcast.62), kind=kLoop, calls=%fused_computation.7 | loop fusion | flops 55296 | bytes 331776 | tf_op jit(solution)/shard_map/broadcast_in_dim | solution.py:392
  (20 shorter events, 0.3 us)
Async XLA Ops:
  0.6 7.1 %copy-start = (bf16[1,2,27,32,32]{4,3,2,1,0:T(8,128)(2,1)S(1)}, bf16[1,2,27,32,32]{4,3,2,1,0:T(8,128)(2,1)}, u32[]{:S(2)}) copy-start(bf16[1,2,27,32,32]{4,3,2,1,0:T(8,128)(2,1)} %param.5) | copy-start | bytes 331780
  2.6 2.5 %collective-permute-start = (bf16[2,320,128]{2,1,0:T(8,128)(2,1)S(1)}, bf16[2,320,128]{2,1,0:T(8,128)(2,1)S(1)}, u32[]{:S(2)}, u32[]{:S(2)}) collective-permute-start(bf16[2,320,128]{2,1,0:T(8,128)(2,1)S(1)} %pad_maximum_fusion.3.own), channel_id=1, source_target_pairs={{0,1},{1,0},{2,3},{3,2},{4,5},{5,4},{6,7},{7,6},{8,9},{9,8},{10,11... | collective-permute-start | bytes 491528 | tf_op jit(solution)/shard_map/ppermute | solution.py:352
  5.1 16.2 %collective-permute-start.1 = (bf16[2,640,128]{2,1,0:T(8,128)(2,1)S(1)}, bf16[2,640,128]{2,1,0:T(8,128)(2,1)S(1)}, u32[]{:S(2)}, u32[]{:S(2)}) collective-permute-start(bf16[2,640,128]{2,1,0:T(8,128)(2,1)S(1)} %pad_maximum_fusion.2), channel_id=1, source_target_pairs={{0,2},{2,4},{3,1},{4,6},{5,3},{6,8},{7,5},{8,10},{9,7},{10,12},{11... | collective-permute-start | bytes 983048 | tf_op jit(solution)/shard_map/ppermute | solution.py:362
  6.5 10.5 %collective-permute-start.2 = (bf16[640,128]{1,0:T(8,128)(2,1)S(1)}, bf16[640,128]{1,0:T(8,128)(2,1)S(1)}, u32[]{:S(2)}, u32[]{:S(2)}) collective-permute-start(bf16[640,128]{1,0:T(8,128)(2,1)S(1)} %slice_bitcast_fusion.1), channel_id=1, source_target_pairs={{0,4},{2,6},{4,8},{5,1},{6,10},{7,3},{8,12},{9,5},{10,14},{11,7},{... | collective-permute-start | bytes 491528 | tf_op jit(solution)/shard_map/ppermute | solution.py:363
  8.4 13.0 %collective-permute-start.5 = (bf16[2,224,128]{2,1,0:T(8,128)(2,1)S(1)}, bf16[2,224,128]{2,1,0:T(8,128)(2,1)S(1)}, u32[]{:S(2)}, u32[]{:S(2)}) collective-permute-start(bf16[2,224,128]{2,1,0:T(8,128)(2,1)S(1)} %reshape.56.pack0), channel_id=1, source_target_pairs={{0,32},{32,64},{64,96},{96,0},{1,33},{33,65},{65,97},{97,1},{2,34}... | collective-permute-start | bytes 344072 | tf_op jit(solution)/shard_map/ppermute | solution.py:333
  9.7 11.6 %collective-permute-start.6 = (bf16[2,224,128]{2,1,0:T(8,128)(2,1)S(1)}, bf16[2,224,128]{2,1,0:T(8,128)(2,1)S(1)}, u32[]{:S(2)}, u32[]{:S(2)}) collective-permute-start(bf16[2,224,128]{2,1,0:T(8,128)(2,1)S(1)} %reshape.56.pack0), channel_id=1, source_target_pairs={{0,64},{32,96},{64,0},{96,32},{1,65},{33,97},{65,1},{97,33},{2,66}... | collective-permute-start | bytes 344072 | tf_op jit(solution)/shard_map/ppermute | solution.py:333
  12.2 9.2 %collective-permute-start.7 = (bf16[2,224,128]{2,1,0:T(8,128)(2,1)S(1)}, bf16[2,224,128]{2,1,0:T(8,128)(2,1)S(1)}, u32[]{:S(2)}, u32[]{:S(2)}) collective-permute-start(bf16[2,224,128]{2,1,0:T(8,128)(2,1)S(1)} %reshape.56.pack0), channel_id=1, source_target_pairs={{0,96},{32,0},{64,32},{96,64},{1,97},{33,1},{65,33},{97,65},{2,98}... | collective-permute-start | bytes 344072 | tf_op jit(solution)/shard_map/ppermute | solution.py:333
  16.9 9.4 %collective-permute-start.4 = (bf16[640,128]{1,0:T(8,128)(2,1)S(1)}, bf16[640,128]{1,0:T(8,128)(2,1)S(1)}, u32[]{:S(2)}, u32[]{:S(2)}) collective-permute-start(bf16[640,128]{1,0:T(8,128)(2,1)S(1)} %collective-permute-done.2.far), channel_id=1, source_target_pairs={{0,1},{1,0},{2,3},{3,2},{4,5},{5,4},{6,7},{7,6},{8,9},{9,8},{10,11... | collective-permute-start | bytes 491528 | tf_op jit(solution)/shard_map/ppermute | solution.py:366
  21.3 5.1 %collective-permute-start.3 = (bf16[2,640,128]{2,1,0:T(8,128)(2,1)S(1)}, bf16[2,640,128]{2,1,0:T(8,128)(2,1)S(1)}, u32[]{:S(2)}, u32[]{:S(2)}) collective-permute-start(bf16[2,640,128]{2,1,0:T(8,128)(2,1)S(1)} %collective-permute-done.1.near), channel_id=1, source_target_pairs={{0,1},{1,0},{2,3},{3,2},{4,5},{5,4},{6,7},{7,6},{8,9},{9,8},{10,11... | collective-permute-start | bytes 983048 | tf_op jit(solution)/shard_map/ppermute | solution.py:365
  49.7 7.5 %collective-permute-start.11 = (bf16[4,224,128]{2,1,0:T(8,128)(2,1)S(1)}, bf16[4,224,128]{2,1,0:T(8,128)(2,1)S(1)}, u32[]{:S(2)}, u32[]{:S(2)}) collective-permute-start(bf16[4,224,128]{2,1,0:T(8,128)(2,1)S(1)} %get-tuple-element.21), channel_id=1, source_target_pairs={{0,1},{1,0},{2,3},{3,2},{4,5},{5,4},{6,7},{7,6},{8,9},{9,8},{10,11... | collective-permute-start | bytes 688136 | tf_op jit(solution)/shard_map/ppermute | solution.py:371
  53.3 6.2 %collective-permute-start.8 = (bf16[512,128]{1,0:T(8,128)(2,1)S(1)}, bf16[512,128]{1,0:T(8,128)(2,1)S(1)}, u32[]{:S(2)}, u32[]{:S(2)}) collective-permute-start(bf16[512,128]{1,0:T(8,128)(2,1)S(1)} %get-tuple-element.17), channel_id=1, source_target_pairs={{0,32},{32,64},{64,96},{96,0},{1,33},{33,65},{65,97},{97,1},{2,34}... | collective-permute-start | bytes 393224 | tf_op jit(solution)/shard_map/ppermute | solution.py:333
  54.1 9.1 %collective-permute-start.9 = (bf16[512,128]{1,0:T(8,128)(2,1)S(1)}, bf16[512,128]{1,0:T(8,128)(2,1)S(1)}, u32[]{:S(2)}, u32[]{:S(2)}) collective-permute-start(bf16[512,128]{1,0:T(8,128)(2,1)S(1)} %get-tuple-element.18), channel_id=1, source_target_pairs={{0,64},{32,96},{64,0},{96,32},{1,65},{33,97},{65,1},{97,33},{2,66}... | collective-permute-start | bytes 393224 | tf_op jit(solution)/shard_map/ppermute | solution.py:333
  56.9 6.3 %collective-permute-start.10 = (bf16[512,128]{1,0:T(8,128)(2,1)S(1)}, bf16[512,128]{1,0:T(8,128)(2,1)S(1)}, u32[]{:S(2)}, u32[]{:S(2)}) collective-permute-start(bf16[512,128]{1,0:T(8,128)(2,1)S(1)} %get-tuple-element.19), channel_id=1, source_target_pairs={{0,96},{32,0},{64,32},{96,64},{1,97},{33,1},{65,33},{97,65},{2,98}... | collective-permute-start | bytes 393224 | tf_op jit(solution)/shard_map/ppermute | solution.py:333
  57.3 7.6 %collective-permute-start.12 = (bf16[224,128]{1,0:T(8,128)(2,1)S(1)}, bf16[224,128]{1,0:T(8,128)(2,1)S(1)}, u32[]{:S(2)}, u32[]{:S(2)}) collective-permute-start(bf16[224,128]{1,0:T(8,128)(2,1)S(1)} %get-tuple-element.37), channel_id=1, source_target_pairs={{0,32},{32,64},{64,96},{96,0},{1,33},{33,65},{65,97},{97,1},{2,34}... | collective-permute-start | bytes 172040 | tf_op jit(solution)/shard_map/ppermute | solution.py:333
  58.5 7.2 %collective-permute-start.13 = (bf16[224,128]{1,0:T(8,128)(2,1)S(1)}, bf16[224,128]{1,0:T(8,128)(2,1)S(1)}, u32[]{:S(2)}, u32[]{:S(2)}) collective-permute-start(bf16[224,128]{1,0:T(8,128)(2,1)S(1)} %get-tuple-element.39), channel_id=1, source_target_pairs={{0,64},{32,96},{64,0},{96,32},{1,65},{33,97},{65,1},{97,33},{2,66}... | collective-permute-start | bytes 172040 | tf_op jit(solution)/shard_map/ppermute | solution.py:333
  59.5 6.2 %collective-permute-start.14 = (bf16[224,128]{1,0:T(8,128)(2,1)S(1)}, bf16[224,128]{1,0:T(8,128)(2,1)S(1)}, u32[]{:S(2)}, u32[]{:S(2)}) collective-permute-start(bf16[224,128]{1,0:T(8,128)(2,1)S(1)} %get-tuple-element.38), channel_id=1, source_target_pairs={{0,96},{32,0},{64,32},{96,64},{1,97},{33,1},{65,33},{97,65},{2,98}... | collective-permute-start | bytes 172040 | tf_op jit(solution)/shard_map/ppermute | solution.py:333
  65.7 4.9 %collective-permute-start.15 = (bf16[224,128]{1,0:T(8,128)(2,1)S(1)}, bf16[224,128]{1,0:T(8,128)(2,1)S(1)}, u32[]{:S(2)}, u32[]{:S(2)}) collective-permute-start(bf16[224,128]{1,0:T(8,128)(2,1)S(1)} %add_convert_fusion.2), channel_id=1, source_target_pairs={{0,2},{1,3},{2,4},{3,5},{4,6},{5,7},{6,0},{7,1},{8,10},{9,11},{10,... | collective-permute-start | bytes 172040 | tf_op jit(solution)/shard_map/ppermute | solution.py:333
  65.8 4.8 %collective-permute-start.16 = (bf16[224,128]{1,0:T(8,128)(2,1)S(1)}, bf16[224,128]{1,0:T(8,128)(2,1)S(1)}, u32[]{:S(2)}, u32[]{:S(2)}) collective-permute-start(bf16[224,128]{1,0:T(8,128)(2,1)S(1)} %add_convert_fusion.2), channel_id=1, source_target_pairs={{0,4},{1,5},{2,6},{3,7},{4,0},{5,1},{6,2},{7,3},{8,12},{9,13},{10,... | collective-permute-start | bytes 172040 | tf_op jit(solution)/shard_map/ppermute | solution.py:333
  68.1 3.4 %collective-permute-start.17 = (bf16[224,128]{1,0:T(8,128)(2,1)S(1)}, bf16[224,128]{1,0:T(8,128)(2,1)S(1)}, u32[]{:S(2)}, u32[]{:S(2)}) collective-permute-start(bf16[224,128]{1,0:T(8,128)(2,1)S(1)} %add_convert_fusion.2), channel_id=1, source_target_pairs={{0,6},{1,7},{2,0},{3,1},{4,2},{5,3},{6,4},{7,5},{8,14},{9,15},{10,... | collective-permute-start | bytes 172040 | tf_op jit(solution)/shard_map/ppermute | solution.py:333
  71.5 5.9 %collective-permute-start.18 = (bf16[224,128]{1,0:T(8,128)(2,1)S(1)}, bf16[224,128]{1,0:T(8,128)(2,1)S(1)}, u32[]{:S(2)}, u32[]{:S(2)}) collective-permute-start(bf16[224,128]{1,0:T(8,128)(2,1)S(1)} %add_convert_fusion.1), channel_id=1, source_target_pairs={{0,8},{1,9},{2,10},{3,11},{4,12},{5,13},{6,14},{7,15},{8,16},{9,17... | collective-permute-start | bytes 172040 | tf_op jit(solution)/shard_map/ppermute | solution.py:333
  72.9 4.6 %collective-permute-start.19 = (bf16[224,128]{1,0:T(8,128)(2,1)S(1)}, bf16[224,128]{1,0:T(8,128)(2,1)S(1)}, u32[]{:S(2)}, u32[]{:S(2)}) collective-permute-start(bf16[224,128]{1,0:T(8,128)(2,1)S(1)} %add_convert_fusion.1), channel_id=1, source_target_pairs={{0,16},{1,17},{2,18},{3,19},{4,20},{5,21},{6,22},{7,23},{8,24},{9,... | collective-permute-start | bytes 172040 | tf_op jit(solution)/shard_map/ppermute | solution.py:333
  74.9 3.0 %collective-permute-start.20 = (bf16[224,128]{1,0:T(8,128)(2,1)S(1)}, bf16[224,128]{1,0:T(8,128)(2,1)S(1)}, u32[]{:S(2)}, u32[]{:S(2)}) collective-permute-start(bf16[224,128]{1,0:T(8,128)(2,1)S(1)} %add_convert_fusion.1), channel_id=1, source_target_pairs={{0,24},{1,25},{2,26},{3,27},{4,28},{5,29},{6,30},{7,31},{8,0},{9,1... | collective-permute-start | bytes 172040 | tf_op jit(solution)/shard_map/ppermute | solution.py:333
  78.0 8.1 %collective-permute-start.21 = (bf16[224,128]{1,0:T(8,128)(2,1)S(1)}, bf16[224,128]{1,0:T(8,128)(2,1)S(1)}, u32[]{:S(2)}, u32[]{:S(2)}) collective-permute-start(bf16[224,128]{1,0:T(8,128)(2,1)S(1)} %add_convert_fusion), channel_id=1, source_target_pairs={{0,1},{1,0},{2,3},{3,2},{4,5},{5,4},{6,7},{7,6},{8,9},{9,8},{10,11... | collective-permute-start | bytes 172040 | tf_op jit(solution)/shard_map/ppermute | solution.py:382

commit v3 on v2

--- a/solution.py
+++ b/solution.py
@@ -323,6 +323,36 @@
     )(*operands)
 
 
+def layout_kernel(in0, in1, in2, in3, features, gradients, by_source):
+    seg = lax.axis_index("segment")
+    for k, arrived in enumerate((in0, in1, in2, in3)):
+        by_source[lax.rem(seg - k + 4, 4)] = arrived[...]
+    for which, out in enumerate((features, gradients)):
+        for m in range(2):
+            planes = []
+            for y in range(ROWS):
+                start = 256 * which + 64 * y
+                row = jnp.concatenate([by_source[m, start : start + 64, :], by_source[2 + m, start : start + 64, :]])
+                planes.append(row.astype(F32).T[:, None, :])
+            out[m] = jnp.concatenate(planes, axis=1).astype(out.dtype)
+
+
+def layout_call(*arrived):
+    return pl.pallas_call(
+        layout_kernel,
+        out_shape=[
+            jax.ShapeDtypeStruct((2, LANES, ROWS, LANES), BF16),
+            jax.ShapeDtypeStruct((2, LANES, ROWS, LANES), F32),
+        ],
+        in_specs=[VMEM] * 4,
+        out_specs=[VMEM] * 2,
+        scratch_shapes=[pltpu.VMEM((4, 512, LANES), BF16)],
+        compiler_params=pltpu.CompilerParams(vmem_limit_bytes=8 * 1024 * 1024),
+        cost_estimate=pl.CostEstimate(flops=4_000_000_000, bytes_accessed=4_000_000, transcendentals=0),
+        name="layout",
+    )(*arrived)
+
+
 def rotated(value, axis, group, step, stride):
     count = lax.axis_size(axis)
 
@@ -349,6 +379,7 @@
     packed = jnp.pad(weights[0], ((0, 0), (0, 1), (0, 0), (0, 0))).reshape(2, 7, 4, channels, channels)
     packed = jnp.transpose(packed, (0, 1, 3, 2, 4)).reshape(2, 7 * channels, 4 * channels)
 
+    others = [rotated(packed, "segment", 4, k, 1) for k in (1, 2, 3)]
     oth = lax.ppermute(own, "gy", swap)
     block = jnp.concatenate([own, oth], axis=1)
 
@@ -361,10 +392,10 @@
 
     near = lax.ppermute(block, "gy", outward(1))
     far = lax.ppermute(block[0], "gy", outward(2))
-    others = [rotated(packed, "segment", 4, k, 1) for k in (1, 2, 3)]
+    w1, wb = build_call(packed, *others)
+    near, far, w1 = lax.optimization_barrier((near, far, w1))
     near_other = lax.ppermute(near, "gy", swap)
     far_other = lax.ppermute(far, "gy", swap)
-    w1, wb = build_call(packed, *others)
     outs = main_call(own, oth, near, far, near_other, far_other, w1, wb)
     fields, keep, send = outs[:4], outs[4:8], outs[8]
 
@@ -373,23 +404,24 @@
     total = part[0].astype(F32)
     for k in (1, 2, 3):
         total = total + rotated(part[k], "segment", 4, k, 1).astype(F32)
+    arrived = [rotated(fields[k], "segment", 4, k, 1) for k in (1, 2, 3)]
     for stride in (2, 8):
         mine = total.astype(BF16)
+        if stride == 2:
+            mine, *arrived = lax.optimization_barrier((mine, *arrived))
         total = mine.astype(F32)
         for k in (1, 2, 3):
             total = total + rotated(mine, "gy", 4, k, stride).astype(F32)
-    mine = total.astype(BF16)
+    features, input_grads = layout_call(fields[0], *arrived)
+    mine, features, input_grads = lax.optimization_barrier((total.astype(BF16), features, input_grads))
     other = lax.ppermute(mine, "gy", swap)
     low_core = lax.axis_index("gy") % 2 == 0
     both = jnp.stack([jnp.where(low_core, mine, other), jnp.where(low_core, other, mine)])
     grads = both.reshape(2, 7, channels, 4, channels).transpose(0, 1, 3, 2, 4)
     grads = grads.reshape(2, 28, channels, channels)[:, :27].astype(F32)
 
-    by_step = jnp.stack([fields[0]] + [rotated(fields[k], "segment", 4, k, 1) for k in (1, 2, 3)])
-    by_source = jnp.stack([lax.dynamic_index_in_dim(by_step, (seg - j) % 4, 0, keepdims=False) for j in range(4)])
-    fields = by_source.reshape(2, 2, 2, rows, across // 2, channels, planes)
-    fields = jnp.transpose(fields, (2, 1, 5, 6, 3, 0, 4)).reshape(2, micro_count, channels, planes, rows, across)
-    return fields[0][None], grads[None], fields[1].astype(F32)[None]
+    shape = (1, micro_count, channels, planes, rows, across)
+    return features.reshape(shape), grads[None], input_grads.reshape(shape)
 
 
 def solution(mesh):

time: 88 us -> 85.7 us (0.974)
  waiting for transfers between devices: 13.5 us -> 19.3 us
  local copies, waits for them, and re-layouts: 7.69 us -> 2.78 us
  starting transfers between devices: 35.4 us -> 30.8 us
  Pallas kernels: 28.3 us -> 30.1 us
    ppermute x15, waiting for transfers between devices: 8.88 us -> 15.9 us  [rotated(): return lax.ppermute(value, axis, [(i, target(i)) for i in range(count)])]
    ppermute x1, starting transfers between devices: 4.37 us -> 0.09 us  [local(): far_other = lax.ppermute(far, 'gy', swap)]
    unnamed x8 -> x4, local copies, waits for them, and re-layouts: 3.8 us -> 0.08 us
    ppermute x1, waiting for transfers between devices: 3.58 us -> 0.01 us  [local(): far = lax.ppermute(block[0], 'gy', outward(2))]
    ppermute x1, starting transfers between devices: 3.6 us -> 0.74 us  [local(): got = lax.ppermute(send, 'gy', swap)]
    ppermute x1, starting transfers between devices: 0.08 us -> 2.46 us  [local(): near_other = lax.ppermute(near, 'gy', swap)]
    pallas_call x0 -> x1, Pallas kernels: none -> 1.85 us  [layout_call(): pl.pallas_call(layout_kernel, out_shape=[jax.ShapeDtypeStruct((2, LANES,...]
    ppermute x1, waiting for transfers between devices: 0.01 us -> 1.4 us  [local(): far_other = lax.ppermute(far, 'gy', swap)]
  transfers between devices with their start and end apart: 22 -> 22, of which waited for: 9 -> 12; matrix products, arithmetic and copies ran while one was open for 7% -> 1% of each run, Pallas kernels for 6% -> 8%
where the time goes in v3:
time: 85.7 us; the launch traced here: 85.5 us
  starting transfers between devices  30.8 us (36%)
  Pallas kernels  30.1 us (35%)
  waiting for transfers between devices  19.3 us (23%)
  local copies, waits for them, and re-layouts  2.78 us (3%)
  other arithmetic  1.63 us (2%)
  between operations  0.88 us (1%)
    pallas_call x1, Pallas kernels, main_call(): pl.pallas_call(main_kernel, out_shape=[jax.ShapeDtypeStruct((512, LANES),...  23.3 us
    ppermute x15, starting transfers between devices, rotated(): return lax.ppermute(value, axis, [(i, target(i)) for i in range(count)])  18.7 us
    ppermute x15, waiting for transfers between devices, rotated(): return lax.ppermute(value, axis, [(i, target(i)) for i in range(count)])  15.9 us
    pallas_call x1, Pallas kernels, build_call(): pl.pallas_call(build_kernel, out_shape=[jax.ShapeDtypeStruct(MATRICES, BF...  4.96 us
    ppermute x1, starting transfers between devices, local(): other = lax.ppermute(mine, 'gy', swap)  4.72 us
    ppermute x1, starting transfers between devices, local(): near_other = lax.ppermute(near, 'gy', swap)  2.46 us
    pallas_call x1, Pallas kernels, layout_call(): pl.pallas_call(layout_kernel, out_shape=[jax.ShapeDtypeStruct((2, LANES,...  1.85 us
  transfers between devices with their start and end apart: 22, of which 12 were waited for; matrix products, arithmetic and copies ran while one was open for 1% of the time, Pallas kernels for 8%

profile of v3, /device:TPU:1, one launch (start us, length us, event | category | flops | bytes accessed | tf_op | source)
XLA Modules:
  0.0 85.5 jit_solution(11980908529617195284)
XLA Ops:
  0.6 0.0 copy-start
  0.7 1.1 %constant_dynamic-slice_fusion.1 = (bf16[1,32,4,4,128]{4,3,2,1,0:T(4,128)(2,1)S(1)}, bf16[1,32,4,4,128]{4,3,2,1,0:T(4,128)(2,1)S(1)}) fusion(bf16[2,32,4,4,128]{4,3,2,1,0:T(4,128)(2,1)} %param.4, s32[]{:T(128)S(6)} %select_n.37, bf16[2,32,4,4,128]{4,3,2,1,0:T(4,128)(2,1)} %param.3), kind=kLoop, calls=%fused_computation.27 | loop fusion | bytes 524292 | tf_op jit(solution)/shard_map/jit(dynamic_index_in_dim)/dynamic_slice | solution.py:374
  1.8 0.1 copy.12
  1.9 0.1 constant_dynamic-slice_fusion
  2.1 0.1 copy.13
  2.2 0.1 copy.9
  2.3 0.1 constant_dynamic-slice_fusion.2
  2.4 0.1 copy.10
  2.6 1.5 %collective-permute-start = (bf16[2,320,128]{2,1,0:T(8,128)(2,1)S(1)}, bf16[2,320,128]{2,1,0:T(8,128)(2,1)S(1)}, u32[]{:S(2)}, u32[]{:S(2)}) collective-permute-start(bf16[2,320,128]{2,1,0:T(8,128)(2,1)S(1)} %pad_maximum_fusion.1.own), channel_id=1, source_target_pairs={{0,1},{1,0},{2,3},{3,2},{4,5},{5,4},{6,7},{7,6},{8,9},{9,8},{10,11... | collective-permute-start | bytes 491528 | tf_op jit(solution)/shard_map/ppermute | solution.py:383
  4.1 0.1 pad.4
  4.2 0.2 copy.21
  4.4 0.2 reshape.43.pack0
  4.7 2.6 %collective-permute-start.5 = (bf16[2,224,128]{2,1,0:T(8,128)(2,1)S(1)}, bf16[2,224,128]{2,1,0:T(8,128)(2,1)S(1)}, u32[]{:S(2)}, u32[]{:S(2)}) collective-permute-start(bf16[2,224,128]{2,1,0:T(8,128)(2,1)S(1)} %reshape.43.pack0), channel_id=1, source_target_pairs={{0,96},{32,0},{64,32},{96,64},{1,97},{33,1},{65,33},{97,65},{2,98}... | collective-permute-start | bytes 344072 | tf_op jit(solution)/shard_map/ppermute | solution.py:363
  7.3 0.5 collective-permute-start.4
  7.8 0.6 collective-permute-start.3
  8.4 0.0 collective-permute-done.oth
  8.5 1.3 %collective-permute-start.1 = (bf16[2,640,128]{2,1,0:T(8,128)(2,1)S(1)}, bf16[2,640,128]{2,1,0:T(8,128)(2,1)S(1)}, u32[]{:S(2)}, u32[]{:S(2)}) collective-permute-start(bf16[2,640,128]{2,1,0:T(8,128)(2,1)S(1)} %pad_maximum_fusion), channel_id=1, source_target_pairs={{0,2},{2,4},{3,1},{4,6},{5,3},{6,8},{7,5},{8,10},{9,7},{10,12},{11... | collective-permute-start | bytes 983048 | tf_op jit(solution)/shard_map/ppermute | solution.py:393
  9.8 1.3 %collective-permute-start.2 = (bf16[640,128]{1,0:T(8,128)(2,1)S(1)}, bf16[640,128]{1,0:T(8,128)(2,1)S(1)}, u32[]{:S(2)}, u32[]{:S(2)}) collective-permute-start(bf16[640,128]{1,0:T(8,128)(2,1)S(1)} %slice_bitcast_fusion.1), channel_id=1, source_target_pairs={{0,4},{2,6},{4,8},{5,1},{6,10},{7,3},{8,12},{9,5},{10,14},{11,7},{... | collective-permute-start | bytes 491528 | tf_op jit(solution)/shard_map/ppermute | solution.py:394
  11.1 1.1 %collective-permute-done.5.pack3 = bf16[2,224,128]{2,1,0:T(8,128)(2,1)S(1)} collective-permute-done((bf16[2,224,128]{2,1,0:T(8,128)(2,1)S(1)}, bf16[2,224,128]{2,1,0:T(8,128)(2,1)S(1)}, u32[]{:S(2)}, u32[]{:S(2)}) %collective-permute-start.5) | collective-permute-done | bytes 114720 | tf_op jit(solution)/shard_map/ppermute | solution.py:363
  12.2 1.1 %collective-permute-done.4.pack2 = bf16[2,224,128]{2,1,0:T(8,128)(2,1)S(1)} collective-permute-done((bf16[2,224,128]{2,1,0:T(8,128)(2,1)S(1)}, bf16[2,224,128]{2,1,0:T(8,128)(2,1)S(1)}, u32[]{:S(2)}, u32[]{:S(2)}) %collective-permute-start.4) | collective-permute-done | bytes 114720 | tf_op jit(solution)/shard_map/ppermute | solution.py:363
  13.2 3.1 %collective-permute-done.3.pack1 = bf16[2,224,128]{2,1,0:T(8,128)(2,1)S(1)} collective-permute-done((bf16[2,224,128]{2,1,0:T(8,128)(2,1)S(1)}, bf16[2,224,128]{2,1,0:T(8,128)(2,1)S(1)}, u32[]{:S(2)}, u32[]{:S(2)}) %collective-permute-start.3) | collective-permute-done | bytes 114720 | tf_op jit(solution)/shard_map/ppermute | solution.py:363
  16.3 5.0 %banded.1 = (bf16[8,384,384]{2,1,0:T(8,128)(2,1)S(1)}, bf16[8,384,384]{2,1,0:T(8,128)(2,1)S(1)}) custom-call(bf16[2,224,128]{2,1,0:T(8,128)(2,1)S(1)} %reshape.43.pack0, bf16[2,224,128]{2,1,0:T(8,128)(2,1)S(1)} %collective-permute-done.3.pack1, bf16[2,224,128]{2,1,0:T(8,128)(2,1)S(1)} %collective-permute-done.4.pack2, ...), custom_call_target="tpu_custom_call" | custom-call | flops 5000000000 | bytes 10000000 | tf_op jit(solution)/shard_map/banded/pallas_call | solution.py:278
  21.3 0.0 collective-permute-done.2.far
  21.3 0.0 collective-permute-done.1.near
  21.3 2.5 %collective-permute-start.6 = (bf16[2,640,128]{2,1,0:T(8,128)(2,1)S(1)}, bf16[2,640,128]{2,1,0:T(8,128)(2,1)S(1)}, u32[]{:S(2)}, u32[]{:S(2)}) collective-permute-start(bf16[2,640,128]{2,1,0:T(8,128)(2,1)S(1)} %collective-permute-done.1.near), channel_id=1, source_target_pairs={{0,1},{1,0},{2,3},{3,2},{4,5},{5,4},{6,7},{7,6},{8,9},{9,8},{10,11... | collective-permute-start | bytes 983048 | tf_op jit(solution)/shard_map/ppermute | solution.py:397
  23.8 0.1 collective-permute-start.7
  23.9 1.4 %collective-permute-done.7.far_other = bf16[640,128]{1,0:T(8,128)(2,1)S(1)} collective-permute-done((bf16[640,128]{1,0:T(8,128)(2,1)S(1)}, bf16[640,128]{1,0:T(8,128)(2,1)S(1)}, u32[]{:S(2)}, u32[]{:S(2)}) %collective-permute-start.7) | collective-permute-done | bytes 163872 | tf_op jit(solution)/shard_map/ppermute | solution.py:398
  25.3 0.0 collective-permute-done.6.near_other
  25.3 23.3 %sections.1 = (bf16[512,128]{1,0:T(8,128)(2,1)S(1)}, bf16[512,128]{1,0:T(8,128)(2,1)S(1)}, bf16[512,128]{1,0:T(8,128)(2,1)S(1)}, bf16[512,128]{1,0:T(8,128)(2,1)...) custom-call(bf16[2,320,128]{2,1,0:T(8,128)(2,1)S(1)} %pad_maximum_fu, ...), custom_call_target="tpu_custom_call" | custom-call | flops 20000000000 | bytes 10000000 | tf_op jit(solution)/shard_map/sections/pallas_call | solution.py:297
  48.6 0.7 collective-permute-start.8
  49.3 1.1 %collective-permute-done.8 = bf16[4,224,128]{2,1,0:T(8,128)(2,1)S(1)} collective-permute-done((bf16[4,224,128]{2,1,0:T(8,128)(2,1)S(1)}, bf16[4,224,128]{2,1,0:T(8,128)(2,1)S(1)}, u32[]{:S(2)}, u32[]{:S(2)}) %collective-permute-start.8) | collective-permute-done | bytes 229408 | tf_op jit(solution)/shard_map/ppermute | solution.py:402
  50.4 0.1 fusion.3
  50.5 1.6 %collective-permute-start.9 = (bf16[224,128]{1,0:T(8,128)(2,1)S(1)}, bf16[224,128]{1,0:T(8,128)(2,1)S(1)}, u32[]{:S(2)}, u32[]{:S(2)}) collective-permute-start(bf16[224,128]{1,0:T(8,128)(2,1)S(1)} %get-tuple-element.49), channel_id=1, source_target_pairs={{0,32},{32,64},{64,96},{96,0},{1,33},{33,65},{65,97},{97,1},{2,34}... | collective-permute-start | bytes 172040 | tf_op jit(solution)/shard_map/ppermute | solution.py:363
  52.1 1.2 %collective-permute-start.11 = (bf16[224,128]{1,0:T(8,128)(2,1)S(1)}, bf16[224,128]{1,0:T(8,128)(2,1)S(1)}, u32[]{:S(2)}, u32[]{:S(2)}) collective-permute-start(bf16[224,128]{1,0:T(8,128)(2,1)S(1)} %get-tuple-element.50), channel_id=1, source_target_pairs={{0,96},{32,0},{64,32},{96,64},{1,97},{33,1},{65,33},{97,65},{2,98}... | collective-permute-start | bytes 172040 | tf_op jit(solution)/shard_map/ppermute | solution.py:363
  53.2 0.7 collective-permute-start.10
  53.9 0.7 collective-permute-start.12
  54.7 2.4 %collective-permute-start.13 = (bf16[512,128]{1,0:T(8,128)(2,1)S(1)}, bf16[512,128]{1,0:T(8,128)(2,1)S(1)}, u32[]{:S(2)}, u32[]{:S(2)}) collective-permute-start(bf16[512,128]{1,0:T(8,128)(2,1)S(1)} %get-tuple-element.37), channel_id=1, source_target_pairs={{0,64},{32,96},{64,0},{96,32},{1,65},{33,97},{65,1},{97,33},{2,66}... | collective-permute-start | bytes 393224 | tf_op jit(solution)/shard_map/ppermute | solution.py:363
  57.1 0.0 collective-permute-done.9
  57.1 1.2 %collective-permute-start.14 = (bf16[512,128]{1,0:T(8,128)(2,1)S(1)}, bf16[512,128]{1,0:T(8,128)(2,1)S(1)}, u32[]{:S(2)}, u32[]{:S(2)}) collective-permute-start(bf16[512,128]{1,0:T(8,128)(2,1)S(1)} %get-tuple-element.38), channel_id=1, source_target_pairs={{0,96},{32,0},{64,32},{96,64},{1,97},{33,1},{65,33},{97,65},{2,98}... | collective-permute-start | bytes 393224 | tf_op jit(solution)/shard_map/ppermute | solution.py:363
  58.3 0.0 collective-permute-done.11
  58.3 0.0 collective-permute-done.10
  58.3 2.1 %collective-permute-done.12.in1 = bf16[512,128]{1,0:T(8,128)(2,1)S(1)} collective-permute-done((bf16[512,128]{1,0:T(8,128)(2,1)S(1)}, bf16[512,128]{1,0:T(8,128)(2,1)S(1)}, u32[]{:S(2)}, u32[]{:S(2)}) %collective-permute-start.12) | collective-permute-done | bytes 131104 | tf_op jit(solution)/shard_map/ppermute | solution.py:363
  60.5 3.0 %collective-permute-done.13.in2 = bf16[512,128]{1,0:T(8,128)(2,1)S(1)} collective-permute-done((bf16[512,128]{1,0:T(8,128)(2,1)S(1)}, bf16[512,128]{1,0:T(8,128)(2,1)S(1)}, u32[]{:S(2)}, u32[]{:S(2)}) %collective-permute-start.13) | collective-permute-done | bytes 131104 | tf_op jit(solution)/shard_map/ppermute | solution.py:363
  63.5 0.0 collective-permute-done.14.in3
  63.5 2.0 %collective-permute-start.17 = (bf16[224,128]{1,0:T(8,128)(2,1)S(1)}, bf16[224,128]{1,0:T(8,128)(2,1)S(1)}, u32[]{:S(2)}, u32[]{:S(2)}) collective-permute-start(bf16[224,128]{1,0:T(8,128)(2,1)S(1)} %add_convert_fusion.2), channel_id=1, source_target_pairs={{0,6},{1,7},{2,0},{3,1},{4,2},{5,3},{6,4},{7,5},{8,14},{9,15},{10,... | collective-permute-start | bytes 172040 | tf_op jit(solution)/shard_map/ppermute | solution.py:363
  65.5 0.5 collective-permute-start.16
  65.9 0.9 %collective-permute-start.15 = (bf16[224,128]{1,0:T(8,128)(2,1)S(1)}, bf16[224,128]{1,0:T(8,128)(2,1)S(1)}, u32[]{:S(2)}, u32[]{:S(2)}) collective-permute-start(bf16[224,128]{1,0:T(8,128)(2,1)S(1)} %add_convert_fusion.2), channel_id=1, source_target_pairs={{0,2},{1,3},{2,4},{3,5},{4,6},{5,7},{6,0},{7,1},{8,10},{9,11},{10,... | collective-permute-start | bytes 172040 | tf_op jit(solution)/shard_map/ppermute | solution.py:363
  66.8 0.0 collective-permute-done.17
  66.8 3.3 %collective-permute-done.16 = bf16[224,128]{1,0:T(8,128)(2,1)S(1)} collective-permute-done((bf16[224,128]{1,0:T(8,128)(2,1)S(1)}, bf16[224,128]{1,0:T(8,128)(2,1)S(1)}, u32[]{:S(2)}, u32[]{:S(2)}) %collective-permute-start.16) | collective-permute-done | bytes 57376 | tf_op jit(solution)/shard_map/ppermute | solution.py:363
  70.0 0.6 collective-permute-done.15
  70.6 2.3 %collective-permute-start.20 = (bf16[224,128]{1,0:T(8,128)(2,1)S(1)}, bf16[224,128]{1,0:T(8,128)(2,1)S(1)}, u32[]{:S(2)}, u32[]{:S(2)}) collective-permute-start(bf16[224,128]{1,0:T(8,128)(2,1)S(1)} %add_convert_fusion.1), channel_id=1, source_target_pairs={{0,24},{1,25},{2,26},{3,27},{4,28},{5,29},{6,30},{7,31},{8,0},{9,1... | collective-permute-start | bytes 172040 | tf_op jit(solution)/shard_map/ppermute | solution.py:363
  72.9 0.9 %collective-permute-start.19 = (bf16[224,128]{1,0:T(8,128)(2,1)S(1)}, bf16[224,128]{1,0:T(8,128)(2,1)S(1)}, u32[]{:S(2)}, u32[]{:S(2)}) collective-permute-start(bf16[224,128]{1,0:T(8,128)(2,1)S(1)} %add_convert_fusion.1), channel_id=1, source_target_pairs={{0,16},{1,17},{2,18},{3,19},{4,20},{5,21},{6,22},{7,23},{8,24},{9,... | collective-permute-start | bytes 172040 | tf_op jit(solution)/shard_map/ppermute | solution.py:363
  73.8 0.7 collective-permute-start.18
  74.5 1.8 %layout.1 = (bf16[2,128,4,128]{3,2,1,0:T(4,128)(2,1)}, f32[2,128,4,128]{3,2,1,0:T(4,128)}) custom-call(bf16[512,128]{1,0:T(8,128)(2,1)S(1)} %get-tuple-element.40.in0, bf16[512,128]{1,0:T(8,128)(2,1)S(1)} %collective-permute-done.12.in1, bf16[512,128]{1,0:T(8,128)(2,1)S(1)} %collective-permute-done.13.in2, bf16[512,128]{1,0:T(8,128)(2,1)S(1)} %collective-permute-done.14.in3), custom_call_target="tpu_custom_call" | custom-call | flops 4000000000 | bytes 4000000 | tf_op jit(solution)/shard_map/layout/pallas_call | solution.py:341
  76.3 0.0 collective-permute-done.20
  76.3 1.1 %collective-permute-done.19 = bf16[224,128]{1,0:T(8,128)(2,1)S(1)} collective-permute-done((bf16[224,128]{1,0:T(8,128)(2,1)S(1)}, bf16[224,128]{1,0:T(8,128)(2,1)S(1)}, u32[]{:S(2)}, u32[]{:S(2)}) %collective-permute-start.19) | collective-permute-done | bytes 57376 | tf_op jit(solution)/shard_map/ppermute | solution.py:363
  77.5 0.6 collective-permute-done.18
  78.1 4.7 %collective-permute-start.21 = (bf16[224,128]{1,0:T(8,128)(2,1)S(1)}, bf16[224,128]{1,0:T(8,128)(2,1)S(1)}, u32[]{:S(2)}, u32[]{:S(2)}) collective-permute-start(bf16[224,128]{1,0:T(8,128)(2,1)S(1)} %add_convert_fusion), channel_id=1, source_target_pairs={{0,1},{1,0},{2,3},{3,2},{4,5},{5,4},{6,7},{7,6},{8,9},{9,8},{10,11... | collective-permute-start | bytes 172040 | tf_op jit(solution)/shard_map/ppermute | solution.py:417
  82.8 0.9 %collective-permute-done.21 = bf16[224,128]{1,0:T(8,128)(2,1)S(1)} collective-permute-done((bf16[224,128]{1,0:T(8,128)(2,1)S(1)}, bf16[224,128]{1,0:T(8,128)(2,1)S(1)}, u32[]{:S(2)}, u32[]{:S(2)}) %collective-permute-start.21) | collective-permute-done | bytes 57376 | tf_op jit(solution)/shard_map/ppermute | solution.py:417
  83.7 0.1 stack.13
  83.9 0.1 stack.14
  84.0 0.4 maximum_bitcast_fusion
  84.4 0.1 copy.15
  84.5 1.0 %fusion = f32[1,2,27,32,32]{4,3,2,1,0:T(8,128)} fusion(bf16[2,28,32,32]{3,2,1,0:T(8,128)(2,1)S(1)} %bitcast.53), kind=kLoop, calls=%fused_computation.3 | loop fusion | flops 55296 | bytes 331776 | tf_op jit(solution)/shard_map/broadcast_in_dim | solution.py:424
  (10 shorter events, 0.3 us)
Async XLA Ops:
  0.6 3.4 %copy-start = (bf16[1,2,27,32,32]{4,3,2,1,0:T(8,128)(2,1)S(1)}, bf16[1,2,27,32,32]{4,3,2,1,0:T(8,128)(2,1)}, u32[]{:S(2)}) copy-start(bf16[1,2,27,32,32]{4,3,2,1,0:T(8,128)(2,1)} %param.5) | copy-start | bytes 331780
  2.6 5.9 %collective-permute-start = (bf16[2,320,128]{2,1,0:T(8,128)(2,1)S(1)}, bf16[2,320,128]{2,1,0:T(8,128)(2,1)S(1)}, u32[]{:S(2)}, u32[]{:S(2)}) collective-permute-start(bf16[2,320,128]{2,1,0:T(8,128)(2,1)S(1)} %pad_maximum_fusion.1.own), channel_id=1, source_target_pairs={{0,1},{1,0},{2,3},{3,2},{4,5},{5,4},{6,7},{7,6},{8,9},{9,8},{10,11... | collective-permute-start | bytes 491528 | tf_op jit(solution)/shard_map/ppermute | solution.py:383
  4.7 7.5 %collective-permute-start.5 = (bf16[2,224,128]{2,1,0:T(8,128)(2,1)S(1)}, bf16[2,224,128]{2,1,0:T(8,128)(2,1)S(1)}, u32[]{:S(2)}, u32[]{:S(2)}) collective-permute-start(bf16[2,224,128]{2,1,0:T(8,128)(2,1)S(1)} %reshape.43.pack0), channel_id=1, source_target_pairs={{0,96},{32,0},{64,32},{96,64},{1,97},{33,1},{65,33},{97,65},{2,98}... | collective-permute-start | bytes 344072 | tf_op jit(solution)/shard_map/ppermute | solution.py:363
  7.3 5.9 %collective-permute-start.4 = (bf16[2,224,128]{2,1,0:T(8,128)(2,1)S(1)}, bf16[2,224,128]{2,1,0:T(8,128)(2,1)S(1)}, u32[]{:S(2)}, u32[]{:S(2)}) collective-permute-start(bf16[2,224,128]{2,1,0:T(8,128)(2,1)S(1)} %reshape.43.pack0), channel_id=1, source_target_pairs={{0,64},{32,96},{64,0},{96,32},{1,65},{33,97},{65,1},{97,33},{2,66}... | collective-permute-start | bytes 344072 | tf_op jit(solution)/shard_map/ppermute | solution.py:363
  7.8 8.5 %collective-permute-start.3 = (bf16[2,224,128]{2,1,0:T(8,128)(2,1)S(1)}, bf16[2,224,128]{2,1,0:T(8,128)(2,1)S(1)}, u32[]{:S(2)}, u32[]{:S(2)}) collective-permute-start(bf16[2,224,128]{2,1,0:T(8,128)(2,1)S(1)} %reshape.43.pack0), channel_id=1, source_target_pairs={{0,32},{32,64},{64,96},{96,0},{1,33},{33,65},{65,97},{97,1},{2,34}... | collective-permute-start | bytes 344072 | tf_op jit(solution)/shard_map/ppermute | solution.py:363
  8.5 12.8 %collective-permute-start.1 = (bf16[2,640,128]{2,1,0:T(8,128)(2,1)S(1)}, bf16[2,640,128]{2,1,0:T(8,128)(2,1)S(1)}, u32[]{:S(2)}, u32[]{:S(2)}) collective-permute-start(bf16[2,640,128]{2,1,0:T(8,128)(2,1)S(1)} %pad_maximum_fusion), channel_id=1, source_target_pairs={{0,2},{2,4},{3,1},{4,6},{5,3},{6,8},{7,5},{8,10},{9,7},{10,12},{11... | collective-permute-start | bytes 983048 | tf_op jit(solution)/shard_map/ppermute | solution.py:393
  9.8 11.5 %collective-permute-start.2 = (bf16[640,128]{1,0:T(8,128)(2,1)S(1)}, bf16[640,128]{1,0:T(8,128)(2,1)S(1)}, u32[]{:S(2)}, u32[]{:S(2)}) collective-permute-start(bf16[640,128]{1,0:T(8,128)(2,1)S(1)} %slice_bitcast_fusion.1), channel_id=1, source_target_pairs={{0,4},{2,6},{4,8},{5,1},{6,10},{7,3},{8,12},{9,5},{10,14},{11,7},{... | collective-permute-start | bytes 491528 | tf_op jit(solution)/shard_map/ppermute | solution.py:394
  21.3 4.0 %collective-permute-start.6 = (bf16[2,640,128]{2,1,0:T(8,128)(2,1)S(1)}, bf16[2,640,128]{2,1,0:T(8,128)(2,1)S(1)}, u32[]{:S(2)}, u32[]{:S(2)}) collective-permute-start(bf16[2,640,128]{2,1,0:T(8,128)(2,1)S(1)} %collective-permute-done.1.near), channel_id=1, source_target_pairs={{0,1},{1,0},{2,3},{3,2},{4,5},{5,4},{6,7},{7,6},{8,9},{9,8},{10,11... | collective-permute-start | bytes 983048 | tf_op jit(solution)/shard_map/ppermute | solution.py:397
  23.8 1.5 %collective-permute-start.7 = (bf16[640,128]{1,0:T(8,128)(2,1)S(1)}, bf16[640,128]{1,0:T(8,128)(2,1)S(1)}, u32[]{:S(2)}, u32[]{:S(2)}) collective-permute-start(bf16[640,128]{1,0:T(8,128)(2,1)S(1)} %collective-permute-done.2.far), channel_id=1, source_target_pairs={{0,1},{1,0},{2,3},{3,2},{4,5},{5,4},{6,7},{7,6},{8,9},{9,8},{10,11... | collective-permute-start | bytes 491528 | tf_op jit(solution)/shard_map/ppermute | solution.py:398
  48.6 1.9 %collective-permute-start.8 = (bf16[4,224,128]{2,1,0:T(8,128)(2,1)S(1)}, bf16[4,224,128]{2,1,0:T(8,128)(2,1)S(1)}, u32[]{:S(2)}, u32[]{:S(2)}) collective-permute-start(bf16[4,224,128]{2,1,0:T(8,128)(2,1)S(1)} %get-tuple-element.32), channel_id=1, source_target_pairs={{0,1},{1,0},{2,3},{3,2},{4,5},{5,4},{6,7},{7,6},{8,9},{9,8},{10,11... | collective-permute-start | bytes 688136 | tf_op jit(solution)/shard_map/ppermute | solution.py:402
  50.5 6.6 %collective-permute-start.9 = (bf16[224,128]{1,0:T(8,128)(2,1)S(1)}, bf16[224,128]{1,0:T(8,128)(2,1)S(1)}, u32[]{:S(2)}, u32[]{:S(2)}) collective-permute-start(bf16[224,128]{1,0:T(8,128)(2,1)S(1)} %get-tuple-element.49), channel_id=1, source_target_pairs={{0,32},{32,64},{64,96},{96,0},{1,33},{33,65},{65,97},{97,1},{2,34}... | collective-permute-start | bytes 172040 | tf_op jit(solution)/shard_map/ppermute | solution.py:363
  52.1 6.2 %collective-permute-start.11 = (bf16[224,128]{1,0:T(8,128)(2,1)S(1)}, bf16[224,128]{1,0:T(8,128)(2,1)S(1)}, u32[]{:S(2)}, u32[]{:S(2)}) collective-permute-start(bf16[224,128]{1,0:T(8,128)(2,1)S(1)} %get-tuple-element.50), channel_id=1, source_target_pairs={{0,96},{32,0},{64,32},{96,64},{1,97},{33,1},{65,33},{97,65},{2,98}... | collective-permute-start | bytes 172040 | tf_op jit(solution)/shard_map/ppermute | solution.py:363
  53.2 5.1 %collective-permute-start.10 = (bf16[224,128]{1,0:T(8,128)(2,1)S(1)}, bf16[224,128]{1,0:T(8,128)(2,1)S(1)}, u32[]{:S(2)}, u32[]{:S(2)}) collective-permute-start(bf16[224,128]{1,0:T(8,128)(2,1)S(1)} %get-tuple-element.51), channel_id=1, source_target_pairs={{0,64},{32,96},{64,0},{96,32},{1,65},{33,97},{65,1},{97,33},{2,66}... | collective-permute-start | bytes 172040 | tf_op jit(solution)/shard_map/ppermute | solution.py:363
  53.9 6.5 %collective-permute-start.12 = (bf16[512,128]{1,0:T(8,128)(2,1)S(1)}, bf16[512,128]{1,0:T(8,128)(2,1)S(1)}, u32[]{:S(2)}, u32[]{:S(2)}) collective-permute-start(bf16[512,128]{1,0:T(8,128)(2,1)S(1)} %get-tuple-element.36), channel_id=1, source_target_pairs={{0,32},{32,64},{64,96},{96,0},{1,33},{33,65},{65,97},{97,1},{2,34}... | collective-permute-start | bytes 393224 | tf_op jit(solution)/shard_map/ppermute | solution.py:363
  54.7 8.8 %collective-permute-start.13 = (bf16[512,128]{1,0:T(8,128)(2,1)S(1)}, bf16[512,128]{1,0:T(8,128)(2,1)S(1)}, u32[]{:S(2)}, u32[]{:S(2)}) collective-permute-start(bf16[512,128]{1,0:T(8,128)(2,1)S(1)} %get-tuple-element.37), channel_id=1, source_target_pairs={{0,64},{32,96},{64,0},{96,32},{1,65},{33,97},{65,1},{97,33},{2,66}... | collective-permute-start | bytes 393224 | tf_op jit(solution)/shard_map/ppermute | solution.py:363
  57.1 6.3 %collective-permute-start.14 = (bf16[512,128]{1,0:T(8,128)(2,1)S(1)}, bf16[512,128]{1,0:T(8,128)(2,1)S(1)}, u32[]{:S(2)}, u32[]{:S(2)}) collective-permute-start(bf16[512,128]{1,0:T(8,128)(2,1)S(1)} %get-tuple-element.38), channel_id=1, source_target_pairs={{0,96},{32,0},{64,32},{96,64},{1,97},{33,1},{65,33},{97,65},{2,98}... | collective-permute-start | bytes 393224 | tf_op jit(solution)/shard_map/ppermute | solution.py:363
  63.5 3.3 %collective-permute-start.17 = (bf16[224,128]{1,0:T(8,128)(2,1)S(1)}, bf16[224,128]{1,0:T(8,128)(2,1)S(1)}, u32[]{:S(2)}, u32[]{:S(2)}) collective-permute-start(bf16[224,128]{1,0:T(8,128)(2,1)S(1)} %add_convert_fusion.2), channel_id=1, source_target_pairs={{0,6},{1,7},{2,0},{3,1},{4,2},{5,3},{6,4},{7,5},{8,14},{9,15},{10,... | collective-permute-start | bytes 172040 | tf_op jit(solution)/shard_map/ppermute | solution.py:363
  65.5 4.6 %collective-permute-start.16 = (bf16[224,128]{1,0:T(8,128)(2,1)S(1)}, bf16[224,128]{1,0:T(8,128)(2,1)S(1)}, u32[]{:S(2)}, u32[]{:S(2)}) collective-permute-start(bf16[224,128]{1,0:T(8,128)(2,1)S(1)} %add_convert_fusion.2), channel_id=1, source_target_pairs={{0,4},{1,5},{2,6},{3,7},{4,0},{5,1},{6,2},{7,3},{8,12},{9,13},{10,... | collective-permute-start | bytes 172040 | tf_op jit(solution)/shard_map/ppermute | solution.py:363
  65.9 4.7 %collective-permute-start.15 = (bf16[224,128]{1,0:T(8,128)(2,1)S(1)}, bf16[224,128]{1,0:T(8,128)(2,1)S(1)}, u32[]{:S(2)}, u32[]{:S(2)}) collective-permute-start(bf16[224,128]{1,0:T(8,128)(2,1)S(1)} %add_convert_fusion.2), channel_id=1, source_target_pairs={{0,2},{1,3},{2,4},{3,5},{4,6},{5,7},{6,0},{7,1},{8,10},{9,11},{10,... | collective-permute-start | bytes 172040 | tf_op jit(solution)/shard_map/ppermute | solution.py:363
  70.6 5.7 %collective-permute-start.20 = (bf16[224,128]{1,0:T(8,128)(2,1)S(1)}, bf16[224,128]{1,0:T(8,128)(2,1)S(1)}, u32[]{:S(2)}, u32[]{:S(2)}) collective-permute-start(bf16[224,128]{1,0:T(8,128)(2,1)S(1)} %add_convert_fusion.1), channel_id=1, source_target_pairs={{0,24},{1,25},{2,26},{3,27},{4,28},{5,29},{6,30},{7,31},{8,0},{9,1... | collective-permute-start | bytes 172040 | tf_op jit(solution)/shard_map/ppermute | solution.py:363
  72.9 4.5 %collective-permute-start.19 = (bf16[224,128]{1,0:T(8,128)(2,1)S(1)}, bf16[224,128]{1,0:T(8,128)(2,1)S(1)}, u32[]{:S(2)}, u32[]{:S(2)}) collective-permute-start(bf16[224,128]{1,0:T(8,128)(2,1)S(1)} %add_convert_fusion.1), channel_id=1, source_target_pairs={{0,16},{1,17},{2,18},{3,19},{4,20},{5,21},{6,22},{7,23},{8,24},{9,... | collective-permute-start | bytes 172040 | tf_op jit(solution)/shard_map/ppermute | solution.py:363
  73.8 4.3 %collective-permute-start.18 = (bf16[224,128]{1,0:T(8,128)(2,1)S(1)}, bf16[224,128]{1,0:T(8,128)(2,1)S(1)}, u32[]{:S(2)}, u32[]{:S(2)}) collective-permute-start(bf16[224,128]{1,0:T(8,128)(2,1)S(1)} %add_convert_fusion.1), channel_id=1, source_target_pairs={{0,8},{1,9},{2,10},{3,11},{4,12},{5,13},{6,14},{7,15},{8,16},{9,17... | collective-permute-start | bytes 172040 | tf_op jit(solution)/shard_map/ppermute | solution.py:363
  78.1 5.6 %collective-permute-start.21 = (bf16[224,128]{1,0:T(8,128)(2,1)S(1)}, bf16[224,128]{1,0:T(8,128)(2,1)S(1)}, u32[]{:S(2)}, u32[]{:S(2)}) collective-permute-start(bf16[224,128]{1,0:T(8,128)(2,1)S(1)} %add_convert_fusion), channel_id=1, source_target_pairs={{0,1},{1,0},{2,3},{3,2},{4,5},{5,4},{6,7},{7,6},{8,9},{9,8},{10,11... | collective-permute-start | bytes 172040 | tf_op jit(solution)/shard_map/ppermute | solution.py:417

commit v4 on v3

--- a/solution.py
+++ b/solution.py
@@ -7,9 +7,9 @@
 
 ROWS = 4
 WIDTH = 80
-SINGLE = 12
 TOTAL = 36
 LANES = 128
+PAIRS = 4
 F32 = jnp.float32
 BF16 = jnp.bfloat16
 
@@ -43,8 +43,16 @@
     for k, pack in enumerate((pack0, pack1, pack2, pack3)):
         wpack[lax.rem(seg - k + 4, 4)] = pack[...]
     expand, _, on_plane = constants()
+    nothing = jnp.zeros((LANES, LANES), BF16)
+
+    def place(dst, index, row, col, value):
+        dst[index, row * LANES : (row + 1) * LANES, col * LANES : (col + 1) * LANES] = value
 
     def build(index, carry):
+        for dx in range(3):
+            for dst in (w1, wb):
+                place(dst, index, 3, dx, nothing)
+                place(dst, index, 0, 3 + dx, nothing)
         w = wpack[lax.div(index, 2), lax.rem(index, 2)]
         lx[...] = jnp.dot(w, expand, preferred_element_type=F32)
         for q in range(7):
@@ -64,12 +72,15 @@
                             vf = jnp.where(on_plane[z + 1 - dz], fwd[dz], vf)
                         if 0 <= z + dz - 1 < 4:
                             vb = jnp.where(on_plane[z + dz - 1], bwd[dz], vb)
-                    block[0, pl.ds(z, 32, stride=4), :] = vf
-                    block[1, pl.ds(z, 32, stride=4), :] = vb
-                w1[index, dy * LANES : (dy + 1) * LANES, dx * LANES : (dx + 1) * LANES] = block[0].astype(BF16)
-                wb[index, (2 - dy) * LANES : (3 - dy) * LANES, (2 - dx) * LANES : (3 - dx) * LANES] = block[1].astype(
-                    BF16
-                )
+                    block[6 * dy + 2 * dx, pl.ds(z, 32, stride=4), :] = vf
+                    block[6 * dy + 2 * dx + 1, pl.ds(z, 32, stride=4), :] = vb
+        for dy in range(3):
+            for dx in range(3):
+                ahead = block[6 * dy + 2 * dx].astype(BF16)
+                back = block[6 * dy + 2 * dx + 1].astype(BF16)
+                for r in range(2):
+                    place(w1, index, dy + r, 3 * r + dx, ahead)
+                    place(wb, index, 2 - dy + r, 3 * r + 2 - dx, back)
         return carry
 
     lax.fori_loop(0, 8, build, 0)
@@ -78,7 +89,7 @@
 def main_kernel(
     own, oth, near, far, near_other, far_other, w1, wb,
     out0, out1, out2, out3, keep0, keep1, keep2, keep3, send,
-    crop, cot, feats, merged, hidden, delta, sd, fd, pre1, pre2, grads, terms, out_all, wg_all,
+    crop, cot, feats, merged, hidden, delta, sd, fd, pre1, pre2, product, grads, terms, out_all, wg_all,
 ):
     seg = lax.axis_index("segment")
     gy = lax.axis_index("gy")
@@ -121,16 +132,6 @@
 
     _, collapse, on_plane = constants()
 
-    def chunks(low, high, body):
-        count = 1 if high - low <= SINGLE else 2
-        rows = (high - low) // count
-
-        def step(i, carry):
-            body(at_row(low + rows * i), rows * WIDTH)
-            return carry
-
-        lax.fori_loop(0, count, step, 0)
-
     def by_rows(v):
         return v.reshape(v.shape[0] // WIDTH, WIDTH, LANES)
 
@@ -140,26 +141,36 @@
     def from_right(v):
         return jnp.where(column == WIDTH - 1, 0.0, pltpu.roll(by_rows(v), WIDTH - 1, 1)).reshape(v.shape)
 
-    def stacked(src, base, span):
+    def stacked(src, first_rows, count):
         return jnp.concatenate(
             [
-                src[pl.ds(pl.multiple_of(base - WIDTH, 16), span), :],
-                src[pl.ds(base, span), :],
-                src[pl.ds(pl.multiple_of(base + WIDTH, 16), span), :],
+                jnp.concatenate([src[(row + j) * WIDTH : (row + j + 1) * WIDTH, :] for row in first_rows], axis=0)
+                for j in range(count)
             ],
             axis=1,
         )
 
     def conv(src, matrix, low, high, then):
-        def body(base, span):
-            p = jnp.dot(stacked(src, base, span), matrix[...], preferred_element_type=F32)
-            then(base, span, p[:, LANES : 2 * LANES] + from_left(p[:, :LANES]) + from_right(p[:, 2 * LANES :]))
-
-        chunks(low, high, body)
-
-    def clear_outside(dst, low, high):
-        top = 16 - ROWS * gy
-        bottom = 16 + ROWS * (lax.axis_size("gy") - gy)
+        rows = range(low, high, 2)
+        for at in range(0, len(rows), PAIRS):
+            some = rows[at : at + PAIRS]
+            product[at * WIDTH : (at + len(some)) * WIDTH, :] = jnp.dot(
+                stacked(src, [row - 1 for row in some], 4), matrix[...], preferred_element_type=F32
+            )
+
+            def finish(i, row):
+                for r in range(2):
+                    block = product.at[i * WIDTH : (i + 1) * WIDTH]
+                    q = [block[:, (3 * r + b) * LANES : (3 * r + b + 1) * LANES] for b in range(3)]
+                    here = slice((row + r) * WIDTH, (row + r + 1) * WIDTH)
+                    then(here, q[1] + from_left(q[0]) + from_right(q[2]))
+
+            for i, row in enumerate(some):
+                finish(at + i, row)
+
+    def clear_outside(dst, low, high, first=16):
+        top = first - ROWS * gy
+        bottom = first + ROWS * (lax.axis_size("gy") - gy)
 
         def clear(i, carry):
             dst[pl.ds(at_row(i), WIDTH), :] = jnp.zeros((WIDTH, LANES), BF16)
@@ -173,23 +184,26 @@
         def _():
             lax.fori_loop(jnp.maximum(bottom, low), high, clear, 0)
 
+    clear_outside(crop, 0, 36)
+    clear_outside(cot, 0, 20, 8)
+
     for s in range(4):
         source = crop if s == 0 else feats.at[0] if s == 1 else merged.at[s - 2]
 
-        def first(base, span, v, s=s):
-            pre1[s, pl.ds(base, span), :] = v
-            hidden[s, pl.ds(base, span), :] = (v * sigmoid(v)).astype(BF16)
+        def first(here, v, s=s):
+            pre1[s, here, :] = v
+            hidden[s, here, :] = (v * sigmoid(v)).astype(BF16)
 
         conv(source, w1.at[2 * s], 2 * s + 1, 35 - 2 * s, first)
         clear_outside(hidden.at[s], 2 * s + 1, 35 - 2 * s)
 
-        def second(base, span, v, s=s):
-            pre2[s, pl.ds(base, span), :] = v
+        def second(here, v, s=s):
+            pre2[s, here, :] = v
             out = (v * sigmoid(v)).astype(BF16)
-            feats[s, pl.ds(base, span), :] = out
+            feats[s, here, :] = out
             if s == 1 or s == 2:
-                skip = feats[0, pl.ds(base, span), :] if s == 1 else crop[pl.ds(base, span), :]
-                merged[s - 1, pl.ds(base, span), :] = (out.astype(F32) + skip.astype(F32)).astype(BF16)
+                skip = feats[0, here, :] if s == 1 else crop[here, :]
+                merged[s - 1, here, :] = (out.astype(F32) + skip.astype(F32)).astype(BF16)
 
         conv(hidden.at[s], w1.at[2 * s + 1], 2 * s + 2, 34 - 2 * s, second)
         if s == 0:
@@ -197,11 +211,8 @@
         if s == 1 or s == 2:
             clear_outside(merged.at[s - 1], 2 * s + 2, 34 - 2 * s)
 
-    def first_sd(base, span):
-        incoming = cot[pl.ds(pl.multiple_of(base - 8 * WIDTH, 16), span), :]
-        sd[pl.ds(base, span), :] = (incoming.astype(F32) * slope(pre2[3, pl.ds(base, span), :])).astype(BF16)
-
-    chunks(8, 28, first_sd)
+    here = slice(8 * WIDTH, 28 * WIDTH)
+    sd[here, :] = (cot[...].astype(F32) * slope(pre2[3, here, :])).astype(BF16)
 
     own_low = half * 16
     mine = (column >= own_low) & (column < own_low + 64)
@@ -213,7 +224,7 @@
         d = jnp.where(mine, by_rows(grad[base0 : base0 + span, :].astype(F32)), 0.0).reshape(span, LANES)
         shifted = jnp.concatenate([from_right(d).astype(BF16), d.astype(BF16), from_left(d).astype(BF16)], axis=1)
         product = lax.dot_general(
-            stacked(src, base0, span), shifted, (((0,), (0,)), ((), ())), preferred_element_type=F32
+            stacked(src, range(15, 19), 3), shifted, (((0,), (0,)), ((), ())), preferred_element_type=F32
         )
         for dx in range(3):
             grads[dx] = product[:, dx * LANES : (dx + 1) * LANES]
@@ -235,23 +246,23 @@
         source = crop if s == 0 else feats.at[0] if s == 1 else merged.at[s - 2]
         low, high = 8 + 2 * (3 - s), 28 - 2 * (3 - s)
 
-        def to_first(base, span, v, s=s):
-            fd[pl.ds(base, span), :] = (v * slope(pre1[s, pl.ds(base, span), :])).astype(BF16)
+        def to_first(here, v, s=s):
+            fd[here, :] = (v * slope(pre1[s, here, :])).astype(BF16)
 
         kernel_grads(hidden.at[s], sd, s, 1)
         conv(sd, wb.at[2 * s + 1], low + 1, high - 1, to_first)
         clear_outside(fd, low + 1, high - 1)
         kernel_grads(source, fd, s, 0)
 
-        def to_delta(base, span, v, s=s):
+        def to_delta(here, v, s=s):
             out = v.astype(BF16)
             if s == 1 or s == 0:
-                other = delta[2 if s == 1 else 3, pl.ds(base, span), :]
+                other = delta[2 if s == 1 else 3, here, :]
                 out = (out.astype(F32) + other.astype(F32)).astype(BF16)
-            delta[s, pl.ds(base, span), :] = out
+            delta[s, here, :] = out
             if s > 0:
-                sd[pl.ds(base, span), :] = (
-                    out.astype(F32) * slope(pre2[s - 1, pl.ds(base, span), :])
+                sd[here, :] = (
+                    out.astype(F32) * slope(pre2[s - 1, here, :])
                 ).astype(BF16)
 
         conv(fd, wb.at[2 * s], low + 2, high - 2, to_delta)
@@ -271,7 +282,7 @@
 
 
 VMEM = pl.BlockSpec(memory_space=pltpu.VMEM)
-MATRICES = (8, 3 * LANES, 3 * LANES)
+MATRICES = (8, 4 * LANES, 6 * LANES)
 
 
 def build_call(*packs):
@@ -284,7 +295,7 @@
             pltpu.VMEM((4, 2, 224, LANES), BF16),
             pltpu.VMEM((224, 4 * LANES), F32),
             pltpu.VMEM((7 * LANES, LANES), F32),
-            pltpu.VMEM((2, LANES, LANES), F32),
+            pltpu.VMEM((18, LANES, LANES), F32),
         ],
         compiler_params=pltpu.CompilerParams(vmem_limit_bytes=8 * 1024 * 1024),
         cost_estimate=pl.CostEstimate(flops=5_000_000_000, bytes_accessed=10_000_000, transcendentals=0),
@@ -312,12 +323,13 @@
             pltpu.VMEM(acts, BF16),
             pltpu.VMEM((4,) + acts, F32),
             pltpu.VMEM((4,) + acts, F32),
+            pltpu.VMEM((17 * WIDTH, 6 * LANES), F32),
             pltpu.VMEM((3, 3 * LANES, LANES), F32),
             pltpu.VMEM((224, 4 * LANES), BF16),
             pltpu.VMEM((4, 512, LANES), BF16),
             pltpu.VMEM((2, 4, 224, LANES), BF16),
         ],
-        compiler_params=pltpu.CompilerParams(vmem_limit_bytes=40 * 1024 * 1024),
+        compiler_params=pltpu.CompilerParams(vmem_limit_bytes=36 * 1024 * 1024),
         cost_estimate=pl.CostEstimate(flops=20_000_000_000, bytes_accessed=10_000_000, transcendentals=0),
         name="sections",
     )(*operands)
@@ -384,11 +396,7 @@
     block = jnp.concatenate([own, oth], axis=1)
 
     def outward(distance):
-        return [
-            (i, i + 2 * distance * (1 if i % 2 == 0 else -1))
-            for i in range(devices)
-            if 0 <= i + 2 * distance * (1 if i % 2 == 0 else -1) < devices
-        ]
+        return [(i, (i + 2 * distance * (1 if i % 2 == 0 else -1)) % devices) for i in range(devices)]
 
     near = lax.ppermute(block, "gy", outward(1))
     far = lax.ppermute(block[0], "gy", outward(2))

time: 85.7 us -> 81.9 us (0.956)
  Pallas kernels: 30.1 us -> 25.9 us
  local copies, waits for them, and re-layouts: 2.78 us -> 3.74 us
    pallas_call x1, Pallas kernels: 23.3 us -> 18.3 us  [main_call(): pl.pallas_call(main_kernel, out_shape=[jax.ShapeDtypeStruct((512, LANES),...]
    ppermute x1, starting transfers between devices: 1.29 us -> 6.28 us  [local(): near = lax.ppermute(block, 'gy', outward(1))]
    ppermute x1, starting transfers between devices: 2.46 us -> 0.01 us  [local(): near_other = lax.ppermute(near, 'gy', swap)]
    ppermute x15, waiting for transfers between devices: 15.9 us -> 13.5 us  [rotated(): return lax.ppermute(value, axis, [(i, target(i)) for i in range(count)])]
    ppermute x1, waiting for transfers between devices: 0.01 us -> 1.68 us  [local(): far = lax.ppermute(block[0], 'gy', outward(2))]
    ppermute x1, starting transfers between devices: 1.29 us -> 0.01 us  [local(): far = lax.ppermute(block[0], 'gy', outward(2))]
    pad x1, local copies, waits for them, and re-layouts: 0.09 us -> 1.1 us  [local(): jnp.pad(weights[0], ((0, 0), (0, 1), (0, 0), (0, 0)))]
    ppermute x15, starting transfers between devices: 18.7 us -> 17.7 us  [rotated(): return lax.ppermute(value, axis, [(i, target(i)) for i in range(count)])]
  transfers between devices with their start and end apart: 22 -> 22, of which waited for: 12 -> 12; matrix products, arithmetic and copies ran while one was open for 1% -> 2% of each run, Pallas kernels for 8% -> 9%
where the time goes in v4:
time: 81.9 us; the launch traced here: 81.7 us
  starting transfers between devices  31.1 us (38%)
  Pallas kernels  25.9 us (32%)
  waiting for transfers between devices  18.5 us (23%)
  local copies, waits for them, and re-layouts  3.74 us (5%)
  other arithmetic  1.63 us (2%)
  between operations  0.84 us (1%)
    pallas_call x1, Pallas kernels, main_call(): pl.pallas_call(main_kernel, out_shape=[jax.ShapeDtypeStruct((512, LANES),...  18.3 us
    ppermute x15, starting transfers between devices, rotated(): return lax.ppermute(value, axis, [(i, target(i)) for i in range(count)])  17.7 us
    ppermute x15, waiting for transfers between devices, rotated(): return lax.ppermute(value, axis, [(i, target(i)) for i in range(count)])  13.5 us
    ppermute x1, starting transfers between devices, local(): near = lax.ppermute(block, 'gy', outward(1))  6.28 us
    pallas_call x1, Pallas kernels, build_call(): pl.pallas_call(build_kernel, out_shape=[jax.ShapeDtypeStruct(MATRICES, BF...  5.75 us
    ppermute x1, starting transfers between devices, local(): other = lax.ppermute(mine, 'gy', swap)  4.55 us
    pallas_call x1, Pallas kernels, layout_call(): pl.pallas_call(layout_kernel, out_shape=[jax.ShapeDtypeStruct((2, LANES,...  1.85 us
    ppermute x1, waiting for transfers between devices, local(): far = lax.ppermute(block[0], 'gy', outward(2))  1.68 us
  transfers between devices with their start and end apart: 22, of which 12 were waited for; matrix products, arithmetic and copies ran while one was open for 2% of the time, Pallas kernels for 9%

profile of v4, /device:TPU:1, one launch (start us, length us, event | category | flops | bytes accessed | tf_op | source)
XLA Modules:
  0.0 81.7 jit_solution(8387263152373933233)
XLA Ops:
  0.7 1.1 %constant_dynamic-slice_fusion.1 = (bf16[1,32,4,4,128]{4,3,2,1,0:T(4,128)(2,1)S(1)}, bf16[1,32,4,4,128]{4,3,2,1,0:T(4,128)(2,1)S(1)}) fusion(bf16[2,32,4,4,128]{4,3,2,1,0:T(4,128)(2,1)} %param.4, s32[]{:T(128)S(6)} %select_n.37, bf16[2,32,4,4,128]{4,3,2,1,0:T(4,128)(2,1)} %param.3), kind=kLoop, calls=%fused_computation.27 | loop fusion | bytes 524292 | tf_op jit(solution)/shard_map/jit(dynamic_index_in_dim)/dynamic_slice | solution.py:386
  1.8 0.1 copy.12
  1.9 0.1 constant_dynamic-slice_fusion
  2.0 0.1 copy.13
  2.2 0.1 copy.9
  2.3 0.1 constant_dynamic-slice_fusion.2
  2.4 0.1 copy.10
  2.5 1.5 %collective-permute-start = (bf16[2,320,128]{2,1,0:T(8,128)(2,1)S(1)}, bf16[2,320,128]{2,1,0:T(8,128)(2,1)S(1)}, u32[]{:S(2)}, u32[]{:S(2)}) collective-permute-start(bf16[2,320,128]{2,1,0:T(8,128)(2,1)S(1)} %pad_maximum_fusion.1.own), channel_id=1, source_target_pairs={{0,1},{1,0},{2,3},{3,2},{4,5},{5,4},{6,7},{7,6},{8,9},{9,8},{10,11... | collective-permute-start | bytes 491528 | tf_op jit(solution)/shard_map/ppermute | solution.py:395
  4.0 1.1 %pad.4 = bf16[2,28,32,32]{3,2,1,0:T(8,128)(2,1)S(1)} pad(bf16[2,27,32,32]{3,2,1,0:T(8,128)(2,1)} %bitcast.62, bf16[]{:T(256)} %constant.48.clone.1), padding=0_0x0_1x0_0x0_0 | pad | bytes 225282 | tf_op jit(solution)/shard_map/jit(_pad)/pad | solution.py:391
  5.1 0.2 copy.21
  5.4 0.2 reshape.43.pack0
  5.6 2.6 %collective-permute-start.5 = (bf16[2,224,128]{2,1,0:T(8,128)(2,1)S(1)}, bf16[2,224,128]{2,1,0:T(8,128)(2,1)S(1)}, u32[]{:S(2)}, u32[]{:S(2)}) collective-permute-start(bf16[2,224,128]{2,1,0:T(8,128)(2,1)S(1)} %reshape.43.pack0), channel_id=1, source_target_pairs={{0,96},{32,0},{64,32},{96,64},{1,97},{33,1},{65,33},{97,65},{2,98}... | collective-permute-start | bytes 344072 | tf_op jit(solution)/shard_map/ppermute | solution.py:375
  8.3 0.5 collective-permute-start.4
  8.8 0.6 collective-permute-start.3
  9.4 0.0 collective-permute-done.oth
  9.4 6.3 %collective-permute-start.1 = (bf16[2,640,128]{2,1,0:T(8,128)(2,1)S(1)}, bf16[2,640,128]{2,1,0:T(8,128)(2,1)S(1)}, u32[]{:S(2)}, u32[]{:S(2)}) collective-permute-start(bf16[2,640,128]{2,1,0:T(8,128)(2,1)S(1)} %pad_maximum_fusion), channel_id=1, source_target_pairs={{0,2},{1,31},{2,4},{3,1},{4,6},{5,3},{6,8},{7,5},{8,10},{9,7},{10,... | collective-permute-start | bytes 983048 | tf_op jit(solution)/shard_map/ppermute | solution.py:401
  15.7 0.0 collective-permute-start.2
  15.7 0.0 collective-permute-done.5.pack3
  15.7 0.0 collective-permute-done.4.pack2
  15.7 1.6 %collective-permute-done.3.pack1 = bf16[2,224,128]{2,1,0:T(8,128)(2,1)S(1)} collective-permute-done((bf16[2,224,128]{2,1,0:T(8,128)(2,1)S(1)}, bf16[2,224,128]{2,1,0:T(8,128)(2,1)S(1)}, u32[]{:S(2)}, u32[]{:S(2)}) %collective-permute-start.3) | collective-permute-done | bytes 114720 | tf_op jit(solution)/shard_map/ppermute | solution.py:375
  17.3 5.8 %banded.1 = (bf16[8,512,768]{2,1,0:T(8,128)(2,1)S(1)}, bf16[8,512,768]{2,1,0:T(8,128)(2,1)S(1)}) custom-call(bf16[2,224,128]{2,1,0:T(8,128)(2,1)S(1)} %reshape.43.pack0, bf16[2,224,128]{2,1,0:T(8,128)(2,1)S(1)} %collective-permute-done.3.pack1, bf16[2,224,128]{2,1,0:T(8,128)(2,1)S(1)} %collective-permute-done.4.pack2, ...), custom_call_target="tpu_custom_call" | custom-call | flops 5000000000 | bytes 10000000 | tf_op jit(solution)/shard_map/banded/pallas_call | solution.py:289
  23.0 1.7 %collective-permute-done.2.far = bf16[640,128]{1,0:T(8,128)(2,1)S(1)} collective-permute-done((bf16[640,128]{1,0:T(8,128)(2,1)S(1)}, bf16[640,128]{1,0:T(8,128)(2,1)S(1)}, u32[]{:S(2)}, u32[]{:S(2)}) %collective-permute-start.2) | collective-permute-done | bytes 163872 | tf_op jit(solution)/shard_map/ppermute | solution.py:402
  24.7 0.0 collective-permute-done.1.near
  24.7 0.0 collective-permute-start.6
  24.7 0.5 collective-permute-start.7
  25.2 1.4 %collective-permute-done.7.far_other = bf16[640,128]{1,0:T(8,128)(2,1)S(1)} collective-permute-done((bf16[640,128]{1,0:T(8,128)(2,1)S(1)}, bf16[640,128]{1,0:T(8,128)(2,1)S(1)}, u32[]{:S(2)}, u32[]{:S(2)}) %collective-permute-start.7) | collective-permute-done | bytes 163872 | tf_op jit(solution)/shard_map/ppermute | solution.py:406
  26.6 0.0 collective-permute-done.6.near_other
  26.6 18.3 %sections.1 = (bf16[512,128]{1,0:T(8,128)(2,1)S(1)}, bf16[512,128]{1,0:T(8,128)(2,1)S(1)}, bf16[512,128]{1,0:T(8,128)(2,1)S(1)}, bf16[512,128]{1,0:T(8,128)(2,1)...) custom-call(bf16[2,320,128]{2,1,0:T(8,128)(2,1)S(1)} %pad_maximum_fu, ...), custom_call_target="tpu_custom_call" | custom-call | flops 20000000000 | bytes 10000000 | tf_op jit(solution)/shard_map/sections/pallas_call | solution.py:308
  44.9 0.5 collective-permute-start.8
  45.4 1.1 %collective-permute-done.8 = bf16[4,224,128]{2,1,0:T(8,128)(2,1)S(1)} collective-permute-done((bf16[4,224,128]{2,1,0:T(8,128)(2,1)S(1)}, bf16[4,224,128]{2,1,0:T(8,128)(2,1)S(1)}, u32[]{:S(2)}, u32[]{:S(2)}) %collective-permute-start.8) | collective-permute-done | bytes 229408 | tf_op jit(solution)/shard_map/ppermute | solution.py:410
  46.5 0.1 fusion.3
  46.6 1.6 %collective-permute-start.9 = (bf16[224,128]{1,0:T(8,128)(2,1)S(1)}, bf16[224,128]{1,0:T(8,128)(2,1)S(1)}, u32[]{:S(2)}, u32[]{:S(2)}) collective-permute-start(bf16[224,128]{1,0:T(8,128)(2,1)S(1)} %get-tuple-element.49), channel_id=1, source_target_pairs={{0,32},{32,64},{64,96},{96,0},{1,33},{33,65},{65,97},{97,1},{2,34}... | collective-permute-start | bytes 172040 | tf_op jit(solution)/shard_map/ppermute | solution.py:375
  48.2 1.2 %collective-permute-start.11 = (bf16[224,128]{1,0:T(8,128)(2,1)S(1)}, bf16[224,128]{1,0:T(8,128)(2,1)S(1)}, u32[]{:S(2)}, u32[]{:S(2)}) collective-permute-start(bf16[224,128]{1,0:T(8,128)(2,1)S(1)} %get-tuple-element.50), channel_id=1, source_target_pairs={{0,96},{32,0},{64,32},{96,64},{1,97},{33,1},{65,33},{97,65},{2,98}... | collective-permute-start | bytes 172040 | tf_op jit(solution)/shard_map/ppermute | solution.py:375
  49.3 0.7 collective-permute-start.10
  50.1 0.7 collective-permute-start.12
  50.8 2.5 %collective-permute-start.13 = (bf16[512,128]{1,0:T(8,128)(2,1)S(1)}, bf16[512,128]{1,0:T(8,128)(2,1)S(1)}, u32[]{:S(2)}, u32[]{:S(2)}) collective-permute-start(bf16[512,128]{1,0:T(8,128)(2,1)S(1)} %get-tuple-element.37), channel_id=1, source_target_pairs={{0,64},{32,96},{64,0},{96,32},{1,65},{33,97},{65,1},{97,33},{2,66}... | collective-permute-start | bytes 393224 | tf_op jit(solution)/shard_map/ppermute | solution.py:375
  53.2 0.0 collective-permute-done.9
  53.2 1.2 %collective-permute-start.14 = (bf16[512,128]{1,0:T(8,128)(2,1)S(1)}, bf16[512,128]{1,0:T(8,128)(2,1)S(1)}, u32[]{:S(2)}, u32[]{:S(2)}) collective-permute-start(bf16[512,128]{1,0:T(8,128)(2,1)S(1)} %get-tuple-element.38), channel_id=1, source_target_pairs={{0,96},{32,0},{64,32},{96,64},{1,97},{33,1},{65,33},{97,65},{2,98}... | collective-permute-start | bytes 393224 | tf_op jit(solution)/shard_map/ppermute | solution.py:375
  54.4 0.0 collective-permute-done.11
  54.4 0.0 collective-permute-done.10
  54.4 2.1 %collective-permute-done.12.in1 = bf16[512,128]{1,0:T(8,128)(2,1)S(1)} collective-permute-done((bf16[512,128]{1,0:T(8,128)(2,1)S(1)}, bf16[512,128]{1,0:T(8,128)(2,1)S(1)}, u32[]{:S(2)}, u32[]{:S(2)}) %collective-permute-start.12) | collective-permute-done | bytes 131104 | tf_op jit(solution)/shard_map/ppermute | solution.py:375
  56.6 3.0 %collective-permute-done.13.in2 = bf16[512,128]{1,0:T(8,128)(2,1)S(1)} collective-permute-done((bf16[512,128]{1,0:T(8,128)(2,1)S(1)}, bf16[512,128]{1,0:T(8,128)(2,1)S(1)}, u32[]{:S(2)}, u32[]{:S(2)}) %collective-permute-start.13) | collective-permute-done | bytes 131104 | tf_op jit(solution)/shard_map/ppermute | solution.py:375
  59.6 0.0 collective-permute-done.14.in3
  59.6 0.9 %collective-permute-start.17 = (bf16[224,128]{1,0:T(8,128)(2,1)S(1)}, bf16[224,128]{1,0:T(8,128)(2,1)S(1)}, u32[]{:S(2)}, u32[]{:S(2)}) collective-permute-start(bf16[224,128]{1,0:T(8,128)(2,1)S(1)} %add_convert_fusion.2), channel_id=1, source_target_pairs={{0,6},{1,7},{2,0},{3,1},{4,2},{5,3},{6,4},{7,5},{8,14},{9,15},{10,... | collective-permute-start | bytes 172040 | tf_op jit(solution)/shard_map/ppermute | solution.py:375
  60.5 0.0 collective-permute-start.16
  60.5 0.7 collective-permute-start.15
  61.1 1.5 %collective-permute-done.17 = bf16[224,128]{1,0:T(8,128)(2,1)S(1)} collective-permute-done((bf16[224,128]{1,0:T(8,128)(2,1)S(1)}, bf16[224,128]{1,0:T(8,128)(2,1)S(1)}, u32[]{:S(2)}, u32[]{:S(2)}) %collective-permute-start.17) | collective-permute-done | bytes 57376 | tf_op jit(solution)/shard_map/ppermute | solution.py:375
  62.6 2.5 %collective-permute-done.16 = bf16[224,128]{1,0:T(8,128)(2,1)S(1)} collective-permute-done((bf16[224,128]{1,0:T(8,128)(2,1)S(1)}, bf16[224,128]{1,0:T(8,128)(2,1)S(1)}, u32[]{:S(2)}, u32[]{:S(2)}) %collective-permute-start.16) | collective-permute-done | bytes 57376 | tf_op jit(solution)/shard_map/ppermute | solution.py:375
  65.1 0.5 collective-permute-done.15
  65.6 3.9 %collective-permute-start.20 = (bf16[224,128]{1,0:T(8,128)(2,1)S(1)}, bf16[224,128]{1,0:T(8,128)(2,1)S(1)}, u32[]{:S(2)}, u32[]{:S(2)}) collective-permute-start(bf16[224,128]{1,0:T(8,128)(2,1)S(1)} %add_convert_fusion.1), channel_id=1, source_target_pairs={{0,24},{1,25},{2,26},{3,27},{4,28},{5,29},{6,30},{7,31},{8,0},{9,1... | collective-permute-start | bytes 172040 | tf_op jit(solution)/shard_map/ppermute | solution.py:375
  69.6 0.0 collective-permute-start.19
  69.6 0.7 collective-permute-start.18
  70.3 1.8 %layout.1 = (bf16[2,128,4,128]{3,2,1,0:T(4,128)(2,1)}, f32[2,128,4,128]{3,2,1,0:T(4,128)}) custom-call(bf16[512,128]{1,0:T(8,128)(2,1)S(1)} %get-tuple-element.40.in0, bf16[512,128]{1,0:T(8,128)(2,1)S(1)} %collective-permute-done.12.in1, bf16[512,128]{1,0:T(8,128)(2,1)S(1)} %collective-permute-done.13.in2, bf16[512,128]{1,0:T(8,128)(2,1)S(1)} %collective-permute-done.14.in3), custom_call_target="tpu_custom_call" | custom-call | flops 4000000000 | bytes 4000000 | tf_op jit(solution)/shard_map/layout/pallas_call | solution.py:353
  72.1 0.0 collective-permute-done.20
  72.1 2.1 %collective-permute-done.19 = bf16[224,128]{1,0:T(8,128)(2,1)S(1)} collective-permute-done((bf16[224,128]{1,0:T(8,128)(2,1)S(1)}, bf16[224,128]{1,0:T(8,128)(2,1)S(1)}, u32[]{:S(2)}, u32[]{:S(2)}) %collective-permute-start.19) | collective-permute-done | bytes 57376 | tf_op jit(solution)/shard_map/ppermute | solution.py:375
  74.2 0.2 collective-permute-done.18
  74.5 4.5 %collective-permute-start.21 = (bf16[224,128]{1,0:T(8,128)(2,1)S(1)}, bf16[224,128]{1,0:T(8,128)(2,1)S(1)}, u32[]{:S(2)}, u32[]{:S(2)}) collective-permute-start(bf16[224,128]{1,0:T(8,128)(2,1)S(1)} %add_convert_fusion), channel_id=1, source_target_pairs={{0,1},{1,0},{2,3},{3,2},{4,5},{5,4},{6,7},{7,6},{8,9},{9,8},{10,11... | collective-permute-start | bytes 172040 | tf_op jit(solution)/shard_map/ppermute | solution.py:425
  79.0 0.9 %collective-permute-done.21 = bf16[224,128]{1,0:T(8,128)(2,1)S(1)} collective-permute-done((bf16[224,128]{1,0:T(8,128)(2,1)S(1)}, bf16[224,128]{1,0:T(8,128)(2,1)S(1)}, u32[]{:S(2)}, u32[]{:S(2)}) %collective-permute-start.21) | collective-permute-done | bytes 57376 | tf_op jit(solution)/shard_map/ppermute | solution.py:425
  79.9 0.1 stack.13
  80.1 0.1 stack.14
  80.2 0.4 maximum_bitcast_fusion
  80.6 0.1 copy.15
  80.7 1.0 %fusion = f32[1,2,27,32,32]{4,3,2,1,0:T(8,128)} fusion(bf16[2,28,32,32]{3,2,1,0:T(8,128)(2,1)S(1)} %bitcast.53), kind=kLoop, calls=%fused_computation.3 | loop fusion | flops 55296 | bytes 331776 | tf_op jit(solution)/shard_map/broadcast_in_dim | solution.py:432
  (9 shorter events, 0.3 us)
Async XLA Ops:
  2.5 6.9 %collective-permute-start = (bf16[2,320,128]{2,1,0:T(8,128)(2,1)S(1)}, bf16[2,320,128]{2,1,0:T(8,128)(2,1)S(1)}, u32[]{:S(2)}, u32[]{:S(2)}) collective-permute-start(bf16[2,320,128]{2,1,0:T(8,128)(2,1)S(1)} %pad_maximum_fusion.1.own), channel_id=1, source_target_pairs={{0,1},{1,0},{2,3},{3,2},{4,5},{5,4},{6,7},{7,6},{8,9},{9,8},{10,11... | collective-permute-start | bytes 491528 | tf_op jit(solution)/shard_map/ppermute | solution.py:395
  5.6 10.1 %collective-permute-start.5 = (bf16[2,224,128]{2,1,0:T(8,128)(2,1)S(1)}, bf16[2,224,128]{2,1,0:T(8,128)(2,1)S(1)}, u32[]{:S(2)}, u32[]{:S(2)}) collective-permute-start(bf16[2,224,128]{2,1,0:T(8,128)(2,1)S(1)} %reshape.43.pack0), channel_id=1, source_target_pairs={{0,96},{32,0},{64,32},{96,64},{1,97},{33,1},{65,33},{97,65},{2,98}... | collective-permute-start | bytes 344072 | tf_op jit(solution)/shard_map/ppermute | solution.py:375
  8.3 7.5 %collective-permute-start.4 = (bf16[2,224,128]{2,1,0:T(8,128)(2,1)S(1)}, bf16[2,224,128]{2,1,0:T(8,128)(2,1)S(1)}, u32[]{:S(2)}, u32[]{:S(2)}) collective-permute-start(bf16[2,224,128]{2,1,0:T(8,128)(2,1)S(1)} %reshape.43.pack0), channel_id=1, source_target_pairs={{0,64},{32,96},{64,0},{96,32},{1,65},{33,97},{65,1},{97,33},{2,66}... | collective-permute-start | bytes 344072 | tf_op jit(solution)/shard_map/ppermute | solution.py:375
  8.8 8.5 %collective-permute-start.3 = (bf16[2,224,128]{2,1,0:T(8,128)(2,1)S(1)}, bf16[2,224,128]{2,1,0:T(8,128)(2,1)S(1)}, u32[]{:S(2)}, u32[]{:S(2)}) collective-permute-start(bf16[2,224,128]{2,1,0:T(8,128)(2,1)S(1)} %reshape.43.pack0), channel_id=1, source_target_pairs={{0,32},{32,64},{64,96},{96,0},{1,33},{33,65},{65,97},{97,1},{2,34}... | collective-permute-start | bytes 344072 | tf_op jit(solution)/shard_map/ppermute | solution.py:375
  9.4 15.3 %collective-permute-start.1 = (bf16[2,640,128]{2,1,0:T(8,128)(2,1)S(1)}, bf16[2,640,128]{2,1,0:T(8,128)(2,1)S(1)}, u32[]{:S(2)}, u32[]{:S(2)}) collective-permute-start(bf16[2,640,128]{2,1,0:T(8,128)(2,1)S(1)} %pad_maximum_fusion), channel_id=1, source_target_pairs={{0,2},{1,31},{2,4},{3,1},{4,6},{5,3},{6,8},{7,5},{8,10},{9,7},{10,... | collective-permute-start | bytes 983048 | tf_op jit(solution)/shard_map/ppermute | solution.py:401
  15.7 9.0 %collective-permute-start.2 = (bf16[640,128]{1,0:T(8,128)(2,1)S(1)}, bf16[640,128]{1,0:T(8,128)(2,1)S(1)}, u32[]{:S(2)}, u32[]{:S(2)}) collective-permute-start(bf16[640,128]{1,0:T(8,128)(2,1)S(1)} %slice_bitcast_fusion.1), channel_id=1, source_target_pairs={{0,4},{1,29},{2,6},{3,31},{4,8},{5,1},{6,10},{7,3},{8,12},{9,5},{1... | collective-permute-start | bytes 491528 | tf_op jit(solution)/shard_map/ppermute | solution.py:402
  24.7 1.9 %collective-permute-start.6 = (bf16[2,640,128]{2,1,0:T(8,128)(2,1)S(1)}, bf16[2,640,128]{2,1,0:T(8,128)(2,1)S(1)}, u32[]{:S(2)}, u32[]{:S(2)}) collective-permute-start(bf16[2,640,128]{2,1,0:T(8,128)(2,1)S(1)} %collective-permute-done.1.near), channel_id=1, source_target_pairs={{0,1},{1,0},{2,3},{3,2},{4,5},{5,4},{6,7},{7,6},{8,9},{9,8},{10,11... | collective-permute-start | bytes 983048 | tf_op jit(solution)/shard_map/ppermute | solution.py:405
  24.7 1.9 %collective-permute-start.7 = (bf16[640,128]{1,0:T(8,128)(2,1)S(1)}, bf16[640,128]{1,0:T(8,128)(2,1)S(1)}, u32[]{:S(2)}, u32[]{:S(2)}) collective-permute-start(bf16[640,128]{1,0:T(8,128)(2,1)S(1)} %collective-permute-done.2.far), channel_id=1, source_target_pairs={{0,1},{1,0},{2,3},{3,2},{4,5},{5,4},{6,7},{7,6},{8,9},{9,8},{10,11... | collective-permute-start | bytes 491528 | tf_op jit(solution)/shard_map/ppermute | solution.py:406
  44.9 1.7 %collective-permute-start.8 = (bf16[4,224,128]{2,1,0:T(8,128)(2,1)S(1)}, bf16[4,224,128]{2,1,0:T(8,128)(2,1)S(1)}, u32[]{:S(2)}, u32[]{:S(2)}) collective-permute-start(bf16[4,224,128]{2,1,0:T(8,128)(2,1)S(1)} %get-tuple-element.32), channel_id=1, source_target_pairs={{0,1},{1,0},{2,3},{3,2},{4,5},{5,4},{6,7},{7,6},{8,9},{9,8},{10,11... | collective-permute-start | bytes 688136 | tf_op jit(solution)/shard_map/ppermute | solution.py:410
  46.6 6.6 %collective-permute-start.9 = (bf16[224,128]{1,0:T(8,128)(2,1)S(1)}, bf16[224,128]{1,0:T(8,128)(2,1)S(1)}, u32[]{:S(2)}, u32[]{:S(2)}) collective-permute-start(bf16[224,128]{1,0:T(8,128)(2,1)S(1)} %get-tuple-element.49), channel_id=1, source_target_pairs={{0,32},{32,64},{64,96},{96,0},{1,33},{33,65},{65,97},{97,1},{2,34}... | collective-permute-start | bytes 172040 | tf_op jit(solution)/shard_map/ppermute | solution.py:375
  48.2 6.2 %collective-permute-start.11 = (bf16[224,128]{1,0:T(8,128)(2,1)S(1)}, bf16[224,128]{1,0:T(8,128)(2,1)S(1)}, u32[]{:S(2)}, u32[]{:S(2)}) collective-permute-start(bf16[224,128]{1,0:T(8,128)(2,1)S(1)} %get-tuple-element.50), channel_id=1, source_target_pairs={{0,96},{32,0},{64,32},{96,64},{1,97},{33,1},{65,33},{97,65},{2,98}... | collective-permute-start | bytes 172040 | tf_op jit(solution)/shard_map/ppermute | solution.py:375
  49.3 5.1 %collective-permute-start.10 = (bf16[224,128]{1,0:T(8,128)(2,1)S(1)}, bf16[224,128]{1,0:T(8,128)(2,1)S(1)}, u32[]{:S(2)}, u32[]{:S(2)}) collective-permute-start(bf16[224,128]{1,0:T(8,128)(2,1)S(1)} %get-tuple-element.51), channel_id=1, source_target_pairs={{0,64},{32,96},{64,0},{96,32},{1,65},{33,97},{65,1},{97,33},{2,66}... | collective-permute-start | bytes 172040 | tf_op jit(solution)/shard_map/ppermute | solution.py:375
  50.1 6.5 %collective-permute-start.12 = (bf16[512,128]{1,0:T(8,128)(2,1)S(1)}, bf16[512,128]{1,0:T(8,128)(2,1)S(1)}, u32[]{:S(2)}, u32[]{:S(2)}) collective-permute-start(bf16[512,128]{1,0:T(8,128)(2,1)S(1)} %get-tuple-element.36), channel_id=1, source_target_pairs={{0,32},{32,64},{64,96},{96,0},{1,33},{33,65},{65,97},{97,1},{2,34}... | collective-permute-start | bytes 393224 | tf_op jit(solution)/shard_map/ppermute | solution.py:375
  50.8 8.8 %collective-permute-start.13 = (bf16[512,128]{1,0:T(8,128)(2,1)S(1)}, bf16[512,128]{1,0:T(8,128)(2,1)S(1)}, u32[]{:S(2)}, u32[]{:S(2)}) collective-permute-start(bf16[512,128]{1,0:T(8,128)(2,1)S(1)} %get-tuple-element.37), channel_id=1, source_target_pairs={{0,64},{32,96},{64,0},{96,32},{1,65},{33,97},{65,1},{97,33},{2,66}... | collective-permute-start | bytes 393224 | tf_op jit(solution)/shard_map/ppermute | solution.py:375
  53.2 6.3 %collective-permute-start.14 = (bf16[512,128]{1,0:T(8,128)(2,1)S(1)}, bf16[512,128]{1,0:T(8,128)(2,1)S(1)}, u32[]{:S(2)}, u32[]{:S(2)}) collective-permute-start(bf16[512,128]{1,0:T(8,128)(2,1)S(1)} %get-tuple-element.38), channel_id=1, source_target_pairs={{0,96},{32,0},{64,32},{96,64},{1,97},{33,1},{65,33},{97,65},{2,98}... | collective-permute-start | bytes 393224 | tf_op jit(solution)/shard_map/ppermute | solution.py:375
  59.6 3.0 %collective-permute-start.17 = (bf16[224,128]{1,0:T(8,128)(2,1)S(1)}, bf16[224,128]{1,0:T(8,128)(2,1)S(1)}, u32[]{:S(2)}, u32[]{:S(2)}) collective-permute-start(bf16[224,128]{1,0:T(8,128)(2,1)S(1)} %add_convert_fusion.2), channel_id=1, source_target_pairs={{0,6},{1,7},{2,0},{3,1},{4,2},{5,3},{6,4},{7,5},{8,14},{9,15},{10,... | collective-permute-start | bytes 172040 | tf_op jit(solution)/shard_map/ppermute | solution.py:375
  60.5 4.6 %collective-permute-start.16 = (bf16[224,128]{1,0:T(8,128)(2,1)S(1)}, bf16[224,128]{1,0:T(8,128)(2,1)S(1)}, u32[]{:S(2)}, u32[]{:S(2)}) collective-permute-start(bf16[224,128]{1,0:T(8,128)(2,1)S(1)} %add_convert_fusion.2), channel_id=1, source_target_pairs={{0,4},{1,5},{2,6},{3,7},{4,0},{5,1},{6,2},{7,3},{8,12},{9,13},{10,... | collective-permute-start | bytes 172040 | tf_op jit(solution)/shard_map/ppermute | solution.py:375
  60.5 5.1 %collective-permute-start.15 = (bf16[224,128]{1,0:T(8,128)(2,1)S(1)}, bf16[224,128]{1,0:T(8,128)(2,1)S(1)}, u32[]{:S(2)}, u32[]{:S(2)}) collective-permute-start(bf16[224,128]{1,0:T(8,128)(2,1)S(1)} %add_convert_fusion.2), channel_id=1, source_target_pairs={{0,2},{1,3},{2,4},{3,5},{4,6},{5,7},{6,0},{7,1},{8,10},{9,11},{10,... | collective-permute-start | bytes 172040 | tf_op jit(solution)/shard_map/ppermute | solution.py:375
  65.6 6.5 %collective-permute-start.20 = (bf16[224,128]{1,0:T(8,128)(2,1)S(1)}, bf16[224,128]{1,0:T(8,128)(2,1)S(1)}, u32[]{:S(2)}, u32[]{:S(2)}) collective-permute-start(bf16[224,128]{1,0:T(8,128)(2,1)S(1)} %add_convert_fusion.1), channel_id=1, source_target_pairs={{0,24},{1,25},{2,26},{3,27},{4,28},{5,29},{6,30},{7,31},{8,0},{9,1... | collective-permute-start | bytes 172040 | tf_op jit(solution)/shard_map/ppermute | solution.py:375
  69.6 4.6 %collective-permute-start.19 = (bf16[224,128]{1,0:T(8,128)(2,1)S(1)}, bf16[224,128]{1,0:T(8,128)(2,1)S(1)}, u32[]{:S(2)}, u32[]{:S(2)}) collective-permute-start(bf16[224,128]{1,0:T(8,128)(2,1)S(1)} %add_convert_fusion.1), channel_id=1, source_target_pairs={{0,16},{1,17},{2,18},{3,19},{4,20},{5,21},{6,22},{7,23},{8,24},{9,... | collective-permute-start | bytes 172040 | tf_op jit(solution)/shard_map/ppermute | solution.py:375
  69.6 4.9 %collective-permute-start.18 = (bf16[224,128]{1,0:T(8,128)(2,1)S(1)}, bf16[224,128]{1,0:T(8,128)(2,1)S(1)}, u32[]{:S(2)}, u32[]{:S(2)}) collective-permute-start(bf16[224,128]{1,0:T(8,128)(2,1)S(1)} %add_convert_fusion.1), channel_id=1, source_target_pairs={{0,8},{1,9},{2,10},{3,11},{4,12},{5,13},{6,14},{7,15},{8,16},{9,17... | collective-permute-start | bytes 172040 | tf_op jit(solution)/shard_map/ppermute | solution.py:375
  74.5 5.4 %collective-permute-start.21 = (bf16[224,128]{1,0:T(8,128)(2,1)S(1)}, bf16[224,128]{1,0:T(8,128)(2,1)S(1)}, u32[]{:S(2)}, u32[]{:S(2)}) collective-permute-start(bf16[224,128]{1,0:T(8,128)(2,1)S(1)} %add_convert_fusion), channel_id=1, source_target_pairs={{0,1},{1,0},{2,3},{3,2},{4,5},{5,4},{6,7},{7,6},{8,9},{9,8},{10,11... | collective-permute-start | bytes 172040 | tf_op jit(solution)/shard_map/ppermute | solution.py:425

commit v5 on v4

--- a/solution.py
+++ b/solution.py
@@ -27,32 +27,37 @@
     return pl.multiple_of(row * WIDTH, 16)
 
 
+def grouped(i):
+    return lax.shift_right_logical(i, 7) * 32 + lax.bitwise_and(i, 31)
+
+
 def constants():
     er = lax.broadcasted_iota(jnp.int32, (LANES, 4 * LANES), 0)
     ec = lax.broadcasted_iota(jnp.int32, (LANES, 4 * LANES), 1)
-    expand = jnp.where(er == lax.shift_right_logical(ec, 2), 1.0, 0.0).astype(BF16)
+    expand = jnp.where(er == grouped(ec), 1.0, 0.0).astype(BF16)
     cr = lax.broadcasted_iota(jnp.int32, (4 * LANES, LANES), 0)
     cc = lax.broadcasted_iota(jnp.int32, (4 * LANES, LANES), 1)
-    collapse = jnp.where(cc == lax.shift_right_logical(cr, 2), 1.0, 0.0).astype(BF16)
-    plane = lax.bitwise_and(lax.broadcasted_iota(jnp.int32, (32, LANES), 1), 3)
+    collapse = jnp.where(cc == grouped(cr), 1.0, 0.0).astype(BF16)
+    plane = lax.shift_right_logical(lax.broadcasted_iota(jnp.int32, (32, LANES), 1), 5)
     return expand, collapse, [plane == z for z in range(4)]
 
 
-def build_kernel(pack0, pack1, pack2, pack3, w1, wb, wpack, lx, lxt, block):
+def build_kernel(pack0, pack1, pack2, pack3, w1, wb, wpack, lx, lxt):
     seg = lax.axis_index("segment")
     for k, pack in enumerate((pack0, pack1, pack2, pack3)):
         wpack[lax.rem(seg - k + 4, 4)] = pack[...]
     expand, _, on_plane = constants()
-    nothing = jnp.zeros((LANES, LANES), BF16)
+    nothing = jnp.zeros((32, LANES), BF16)
 
     def place(dst, index, row, col, value):
-        dst[index, row * LANES : (row + 1) * LANES, col * LANES : (col + 1) * LANES] = value
+        dst[index, row * 32 : (row + 1) * 32, col * LANES : (col + 1) * LANES] = value
 
     def build(index, carry):
         for dx in range(3):
             for dst in (w1, wb):
-                place(dst, index, 3, dx, nothing)
-                place(dst, index, 0, 3 + dx, nothing)
+                for z in range(4):
+                    place(dst, index, 12 + z, dx, nothing)
+                    place(dst, index, z, 3 + dx, nothing)
         w = wpack[lax.div(index, 2), lax.rem(index, 2)]
         lx[...] = jnp.dot(w, expand, preferred_element_type=F32)
         for q in range(7):
@@ -72,24 +77,42 @@
                             vf = jnp.where(on_plane[z + 1 - dz], fwd[dz], vf)
                         if 0 <= z + dz - 1 < 4:
                             vb = jnp.where(on_plane[z + dz - 1], bwd[dz], vb)
-                    block[6 * dy + 2 * dx, pl.ds(z, 32, stride=4), :] = vf
-                    block[6 * dy + 2 * dx + 1, pl.ds(z, 32, stride=4), :] = vb
-        for dy in range(3):
-            for dx in range(3):
-                ahead = block[6 * dy + 2 * dx].astype(BF16)
-                back = block[6 * dy + 2 * dx + 1].astype(BF16)
-                for r in range(2):
-                    place(w1, index, dy + r, 3 * r + dx, ahead)
-                    place(wb, index, 2 - dy + r, 3 * r + 2 - dx, back)
+                    for r in range(2):
+                        place(w1, index, 4 * (dy + r) + z, 3 * r + dx, vf.astype(BF16))
+                        place(wb, index, 4 * (2 - dy + r) + z, 3 * r + 2 - dx, vb.astype(BF16))
         return carry
 
     lax.fori_loop(0, 8, build, 0)
+
+
+def by_rows(v):
+    return v.reshape(v.shape[0] // WIDTH, WIDTH, LANES)
+
+
+def from_left(v):
+    column = lax.broadcasted_iota(jnp.int32, (1, WIDTH, LANES), 1)
+    return jnp.where(column == 0, 0.0, pltpu.roll(by_rows(v), 1, 1)).reshape(v.shape)
+
+
+def from_right(v):
+    column = lax.broadcasted_iota(jnp.int32, (1, WIDTH, LANES), 1)
+    return jnp.where(column == WIDTH - 1, 0.0, pltpu.roll(by_rows(v), WIDTH - 1, 1)).reshape(v.shape)
+
+
+def stacked(src, first_rows, count):
+    return jnp.concatenate(
+        [
+            jnp.concatenate([src[(row + j) * WIDTH : (row + j + 1) * WIDTH, :] for row in first_rows], axis=0)
+            for j in range(count)
+        ],
+        axis=1,
+    )
 
 
 def main_kernel(
     own, oth, near, far, near_other, far_other, w1, wb,
-    out0, out1, out2, out3, keep0, keep1, keep2, keep3, send,
-    crop, cot, feats, merged, hidden, delta, sd, fd, pre1, pre2, product, grads, terms, out_all, wg_all,
+    out0, out1, out2, out3, windows, deltas,
+    crop, cot, feats, merged, hidden, delta, sd, fd, pre1, pre2, product, out_all,
 ):
     seg = lax.axis_index("segment")
     gy = lax.axis_index("gy")
@@ -130,26 +153,6 @@
         put(cot, 12, near.at[1], 4, 4)
         put(cot, 16, near.at[1], 0, 4)
 
-    _, collapse, on_plane = constants()
-
-    def by_rows(v):
-        return v.reshape(v.shape[0] // WIDTH, WIDTH, LANES)
-
-    def from_left(v):
-        return jnp.where(column == 0, 0.0, pltpu.roll(by_rows(v), 1, 1)).reshape(v.shape)
-
-    def from_right(v):
-        return jnp.where(column == WIDTH - 1, 0.0, pltpu.roll(by_rows(v), WIDTH - 1, 1)).reshape(v.shape)
-
-    def stacked(src, first_rows, count):
-        return jnp.concatenate(
-            [
-                jnp.concatenate([src[(row + j) * WIDTH : (row + j + 1) * WIDTH, :] for row in first_rows], axis=0)
-                for j in range(count)
-            ],
-            axis=1,
-        )
-
     def conv(src, matrix, low, high, then):
         rows = range(low, high, 2)
         for at in range(0, len(rows), PAIRS):
@@ -215,32 +218,12 @@
     sd[here, :] = (cot[...].astype(F32) * slope(pre2[3, here, :])).astype(BF16)
 
     own_low = half * 16
-    mine = (column >= own_low) & (column < own_low + 64)
     base0 = 16 * WIDTH
-    span = ROWS * WIDTH
     slot_of = lambda s: lax.rem(s - seg + 4, 4)
 
-    def kernel_grads(src, grad, s, which):
-        d = jnp.where(mine, by_rows(grad[base0 : base0 + span, :].astype(F32)), 0.0).reshape(span, LANES)
-        shifted = jnp.concatenate([from_right(d).astype(BF16), d.astype(BF16), from_left(d).astype(BF16)], axis=1)
-        product = lax.dot_general(
-            stacked(src, range(15, 19), 3), shifted, (((0,), (0,)), ((), ())), preferred_element_type=F32
-        )
-        for dx in range(3):
-            grads[dx] = product[:, dx * LANES : (dx + 1) * LANES]
-        terms[6 * 32 :, 3 * LANES :] = jnp.zeros((32, LANES), BF16)
-        for dy in range(3):
-            for dx in range(3):
-                rows = [grads[dx, pl.ds(dy * LANES + z, 32, stride=4), :] for z in range(4)]
-                for dz in range(3):
-                    total = jnp.zeros((32, LANES), F32)
-                    for z in range(4):
-                        if 0 <= z + 1 - dz < 4:
-                            total = jnp.where(on_plane[z + 1 - dz], rows[z], total)
-                    t = 9 * dz + 3 * dy + dx
-                    terms[t // 4 * 32 : t // 4 * 32 + 32, t % 4 * LANES : (t % 4 + 1) * LANES] = total.astype(BF16)
-        packed = jnp.dot(terms[...], collapse, preferred_element_type=F32).astype(BF16)
-        wg_all[which, slot_of(s)] = packed
+    def keep(index, src, grad):
+        windows[index] = src[15 * WIDTH : 21 * WIDTH, :]
+        deltas[index] = grad[16 * WIDTH : 20 * WIDTH, :]
 
     for s in (3, 2, 1, 0):
         source = crop if s == 0 else feats.at[0] if s == 1 else merged.at[s - 2]
@@ -249,10 +232,10 @@
         def to_first(here, v, s=s):
             fd[here, :] = (v * slope(pre1[s, here, :])).astype(BF16)
 
-        kernel_grads(hidden.at[s], sd, s, 1)
+        keep(2 * s + 1, hidden.at[s], sd)
         conv(sd, wb.at[2 * s + 1], low + 1, high - 1, to_first)
         clear_outside(fd, low + 1, high - 1)
-        kernel_grads(source, fd, s, 0)
+        keep(2 * s, source, fd)
 
         def to_delta(here, v, s=s):
             out = v.astype(BF16)
@@ -276,6 +259,42 @@
             out_all[slot_of(s), 256 + 64 * y : 320 + 64 * y, :] = delta[s, place, :]
     for k, out in enumerate((out0, out1, out2, out3)):
         out[...] = out_all[k]
+
+
+def grads_kernel(windows, deltas, keep0, keep1, keep2, keep3, send, grads, terms, wg_all):
+    seg = lax.axis_index("segment")
+    core = lax.rem(lax.axis_index("gy"), 2)
+    own_low = lax.div(seg, 2) * 16
+    column = lax.broadcasted_iota(jnp.int32, (1, WIDTH, LANES), 1)
+    mine = (column >= own_low) & (column < own_low + 64)
+    _, collapse, on_plane = constants()
+    for index in range(8):
+        d = jnp.where(mine, by_rows(deltas[index].astype(F32)), 0.0).reshape(ROWS * WIDTH, LANES)
+        shifted = jnp.concatenate([from_right(d).astype(BF16), d.astype(BF16), from_left(d).astype(BF16)], axis=1)
+        product = lax.dot_general(
+            stacked(windows.at[index], range(ROWS), 3), shifted, (((0,), (0,)), ((), ())), preferred_element_type=F32
+        )
+        for dx in range(3):
+            grads[index, dx] = product[:, dx * LANES : (dx + 1) * LANES]
+        top = 224 * index
+        terms[top + 6 * 32 : top + 7 * 32, 3 * LANES :] = jnp.zeros((32, LANES), BF16)
+        for dy in range(3):
+            for dx in range(3):
+                first = [dy * LANES + z * 32 for z in range(4)]
+                rows = [grads[index, dx, at : at + 32, :] for at in first]
+                for dz in range(3):
+                    total = jnp.zeros((32, LANES), F32)
+                    for z in range(4):
+                        if 0 <= z + 1 - dz < 4:
+                            total = jnp.where(on_plane[z + 1 - dz], rows[z], total)
+                    t = 9 * dz + 3 * dy + dx
+                    at = top + t // 4 * 32
+                    terms[at : at + 32, t % 4 * LANES : (t % 4 + 1) * LANES] = total.astype(BF16)
+    packed = jnp.dot(terms[...], collapse, preferred_element_type=F32).astype(BF16)
+    for s in range(4):
+        for which in range(2):
+            top = 224 * (2 * s + which)
+            wg_all[which, lax.rem(s - seg + 4, 4)] = packed[top : top + 224]
     for k, keep in enumerate((keep0, keep1, keep2, keep3)):
         keep[...] = wg_all[core, k]
     send[...] = wg_all[1 - core]
@@ -295,7 +314,6 @@
             pltpu.VMEM((4, 2, 224, LANES), BF16),
             pltpu.VMEM((224, 4 * LANES), F32),
             pltpu.VMEM((7 * LANES, LANES), F32),
-            pltpu.VMEM((18, LANES, LANES), F32),
         ],
         compiler_params=pltpu.CompilerParams(vmem_limit_bytes=8 * 1024 * 1024),
         cost_estimate=pl.CostEstimate(flops=5_000_000_000, bytes_accessed=10_000_000, transcendentals=0),
@@ -308,10 +326,12 @@
     return pl.pallas_call(
         main_kernel,
         out_shape=[jax.ShapeDtypeStruct((512, LANES), BF16)] * 4
-        + [jax.ShapeDtypeStruct((224, LANES), BF16)] * 4
-        + [jax.ShapeDtypeStruct((4, 224, LANES), BF16)],
+        + [
+            jax.ShapeDtypeStruct((8, 6 * WIDTH, LANES), BF16),
+            jax.ShapeDtypeStruct((8, 4 * WIDTH, LANES), BF16),
+        ],
         in_specs=[VMEM] * 8,
-        out_specs=[VMEM] * 9,
+        out_specs=[VMEM] * 6,
         scratch_shapes=[
             pltpu.VMEM(acts, BF16),
             pltpu.VMEM((20 * WIDTH, LANES), BF16),
@@ -324,15 +344,29 @@
             pltpu.VMEM((4,) + acts, F32),
             pltpu.VMEM((4,) + acts, F32),
             pltpu.VMEM((17 * WIDTH, 6 * LANES), F32),
-            pltpu.VMEM((3, 3 * LANES, LANES), F32),
-            pltpu.VMEM((224, 4 * LANES), BF16),
             pltpu.VMEM((4, 512, LANES), BF16),
-            pltpu.VMEM((2, 4, 224, LANES), BF16),
         ],
         compiler_params=pltpu.CompilerParams(vmem_limit_bytes=36 * 1024 * 1024),
         cost_estimate=pl.CostEstimate(flops=20_000_000_000, bytes_accessed=10_000_000, transcendentals=0),
         name="sections",
     )(*operands)
+
+
+def grads_call(windows, deltas):
+    return pl.pallas_call(
+        grads_kernel,
+        out_shape=[jax.ShapeDtypeStruct((224, LANES), BF16)] * 4 + [jax.ShapeDtypeStruct((4, 224, LANES), BF16)],
+        in_specs=[VMEM] * 2,
+        out_specs=[VMEM] * 5,
+        scratch_shapes=[
+            pltpu.VMEM((8, 3, 3 * LANES, LANES), F32),
+            pltpu.VMEM((8 * 224, 4 * LANES), BF16),
+            pltpu.VMEM((2, 4, 224, LANES), BF16),
+        ],
+        compiler_params=pltpu.CompilerParams(vmem_limit_bytes=16 * 1024 * 1024),
+        cost_estimate=pl.CostEstimate(flops=6_000_000_000, bytes_accessed=4_000_000, transcendentals=0),
+        name="kernel_grads",
+    )(windows, deltas)
 
 
 def layout_kernel(in0, in1, in2, in3, features, gradients, by_source):
@@ -346,15 +380,17 @@
                 start = 256 * which + 64 * y
                 row = jnp.concatenate([by_source[m, start : start + 64, :], by_source[2 + m, start : start + 64, :]])
                 planes.append(row.astype(F32).T[:, None, :])
-            out[m] = jnp.concatenate(planes, axis=1).astype(out.dtype)
+            for z in range(4):
+                part = [plane[32 * z : 32 * z + 32] for plane in planes]
+                out[m, :, z] = jnp.concatenate(part, axis=1).astype(out.dtype)
 
 
 def layout_call(*arrived):
     return pl.pallas_call(
         layout_kernel,
         out_shape=[
-            jax.ShapeDtypeStruct((2, LANES, ROWS, LANES), BF16),
-            jax.ShapeDtypeStruct((2, LANES, ROWS, LANES), F32),
+            jax.ShapeDtypeStruct((2, 32, 4, ROWS, LANES), BF16),
+            jax.ShapeDtypeStruct((2, 32, 4, ROWS, LANES), F32),
         ],
         in_specs=[VMEM] * 4,
         out_specs=[VMEM] * 2,
@@ -384,7 +420,7 @@
 
     def tile(volume):
         field = lax.dynamic_index_in_dim(volume, micro, 0, keepdims=False)
-        field = jnp.transpose(field, (2, 3, 0, 1)).reshape(rows, across, channels * planes)
+        field = jnp.transpose(field, (2, 3, 1, 0)).reshape(rows, across, channels * planes)
         return lax.dynamic_slice_in_dim(field, half * 48, WIDTH, 1).reshape(rows * WIDTH, channels * planes)
 
     own = jnp.stack([tile(crops), tile(cotangent)])
@@ -401,22 +437,21 @@
     near = lax.ppermute(block, "gy", outward(1))
     far = lax.ppermute(block[0], "gy", outward(2))
     w1, wb = build_call(packed, *others)
-    near, far, w1 = lax.optimization_barrier((near, far, w1))
     near_other = lax.ppermute(near, "gy", swap)
+    far, w1 = lax.optimization_barrier((far, w1))
     far_other = lax.ppermute(far, "gy", swap)
     outs = main_call(own, oth, near, far, near_other, far_other, w1, wb)
-    fields, keep, send = outs[:4], outs[4:8], outs[8]
+    fields = outs[:4]
+    arrived = [rotated(fields[k], "segment", 4, k, 1) for k in (1, 2, 3)]
+    *keep, send = grads_call(outs[4], outs[5])
 
     got = lax.ppermute(send, "gy", swap)
     part = [(keep[k].astype(F32) + got[k].astype(F32)).astype(BF16) for k in range(4)]
     total = part[0].astype(F32)
     for k in (1, 2, 3):
         total = total + rotated(part[k], "segment", 4, k, 1).astype(F32)
-    arrived = [rotated(fields[k], "segment", 4, k, 1) for k in (1, 2, 3)]
     for stride in (2, 8):
         mine = total.astype(BF16)
-        if stride == 2:
-            mine, *arrived = lax.optimization_barrier((mine, *arrived))
         total = mine.astype(F32)
         for k in (1, 2, 3):
             total = total + rotated(mine, "gy", 4, k, stride).astype(F32)

time: 81.9 us -> 75.1 us (0.917)
  starting transfers between devices: 31.1 us -> 27.7 us
  Pallas kernels: 25.9 us -> 23.5 us
    pallas_call x1, Pallas kernels: 18.3 us -> 14.2 us  [main_call(): pl.pallas_call(main_kernel, out_shape=[jax.ShapeDtypeStruct((512, LANES),...]
    ppermute x15, starting transfers between devices: 17.7 us -> 13.7 us  [rotated(): return lax.ppermute(value, axis, [(i, target(i)) for i in range(count)])]
    pallas_call x1 -> x2, Pallas kernels: 1.85 us -> 4.5 us  [the longest x1 2.65 us: grads_call(): pl.pallas_call(grads_kernel, out_shape=[jax.ShapeDtypeStruct((224, LANES)...]
    ppermute x1, waiting for transfers between devices: 1.68 us -> 0.01 us  [local(): far = lax.ppermute(block[0], 'gy', outward(2))]
    ppermute x1, waiting for transfers between devices: 0.01 us -> 1.03 us  [local(): oth = lax.ppermute(own, 'gy', swap)]
    pallas_call x1, Pallas kernels: 5.75 us -> 4.8 us  [build_call(): pl.pallas_call(build_kernel, out_shape=[jax.ShapeDtypeStruct(MATRICES, BF...]
  transfers between devices with their start and end apart: 22 -> 22, of which waited for: 12 -> 16; matrix products, arithmetic and copies ran while one was open for 2% -> 2% of each run, Pallas kernels for 9% -> 9%
where the time goes in v5:
time: 75.1 us; the launch traced here: 75 us
  starting transfers between devices  27.7 us (37%)
  Pallas kernels  23.5 us (31%)
  waiting for transfers between devices  17.8 us (24%)
  local copies, waits for them, and re-layouts  3.53 us (5%)
  other arithmetic  1.62 us (2%)
  between operations  0.87 us (1%)
    pallas_call x1, Pallas kernels, main_call(): pl.pallas_call(main_kernel, out_shape=[jax.ShapeDtypeStruct((512, LANES),...  14.2 us
    ppermute x15, starting transfers between devices, rotated(): return lax.ppermute(value, axis, [(i, target(i)) for i in range(count)])  13.7 us
    ppermute x15, waiting for transfers between devices, rotated(): return lax.ppermute(value, axis, [(i, target(i)) for i in range(count)])  13.4 us
    ppermute x1, starting transfers between devices, local(): near = lax.ppermute(block, 'gy', outward(1))  6.36 us
    ppermute x1, starting transfers between devices, local(): other = lax.ppermute(mine, 'gy', swap)  4.94 us
    pallas_call x1, Pallas kernels, build_call(): pl.pallas_call(build_kernel, out_shape=[jax.ShapeDtypeStruct(MATRICES, BF...  4.8 us
    pallas_call x1, Pallas kernels, grads_call(): pl.pallas_call(grads_kernel, out_shape=[jax.ShapeDtypeStruct((224, LANES)...  2.65 us
    pallas_call x1, Pallas kernels, layout_call(): pl.pallas_call(layout_kernel, out_shape=[jax.ShapeDtypeStruct((2, 32, 4,...  1.85 us
  transfers between devices with their start and end apart: 22, of which 16 were waited for; matrix products, arithmetic and copies ran while one was open for 2% of the time, Pallas kernels for 9%

profile of v5, /device:TPU:1, one launch (start us, length us, event | category | flops | bytes accessed | tf_op | source)
XLA Modules:
  0.0 75.0 jit_solution(2641344792379091553)
XLA Ops:
  0.7 1.1 %constant_dynamic-slice_fusion.1 = (bf16[1,32,4,4,128]{4,3,2,1,0:T(4,128)(2,1)S(1)}, bf16[1,32,4,4,128]{4,3,2,1,0:T(4,128)(2,1)S(1)}) fusion(bf16[2,32,4,4,128]{4,3,2,1,0:T(4,128)(2,1)} %param.4, s32[]{:T(128)S(6)} %select_n.37, bf16[2,32,4,4,128]{4,3,2,1,0:T(4,128)(2,1)} %param.3), kind=kLoop, calls=%fused_computation.25 | loop fusion | bytes 524292 | tf_op jit(solution)/shard_map/jit(dynamic_index_in_dim)/dynamic_slice | solution.py:422
  1.8 0.1 constant_dynamic-slice_fusion
  1.9 0.1 copy.13
  2.0 0.1 constant_dynamic-slice_fusion.2
  2.2 0.1 copy.10
  2.3 1.5 %collective-permute-start = (bf16[2,320,128]{2,1,0:T(8,128)(2,1)S(1)}, bf16[2,320,128]{2,1,0:T(8,128)(2,1)S(1)}, u32[]{:S(2)}, u32[]{:S(2)}) collective-permute-start(bf16[2,320,128]{2,1,0:T(8,128)(2,1)S(1)} %pad_maximum_fusion.1.own), channel_id=1, source_target_pairs={{0,1},{1,0},{2,3},{3,2},{4,5},{5,4},{6,7},{7,6},{8,9},{9,8},{10,11... | collective-permute-start | bytes 491528 | tf_op jit(solution)/shard_map/ppermute | solution.py:431
  3.8 1.0 %collective-permute-done.oth = bf16[2,320,128]{2,1,0:T(8,128)(2,1)S(1)} collective-permute-done((bf16[2,320,128]{2,1,0:T(8,128)(2,1)S(1)}, bf16[2,320,128]{2,1,0:T(8,128)(2,1)S(1)}, u32[]{:S(2)}, u32[]{:S(2)}) %collective-permute-start) | collective-permute-done | bytes 163872 | tf_op jit(solution)/shard_map/ppermute | solution.py:431
  4.8 6.4 %collective-permute-start.1 = (bf16[2,640,128]{2,1,0:T(8,128)(2,1)S(1)}, bf16[2,640,128]{2,1,0:T(8,128)(2,1)S(1)}, u32[]{:S(2)}, u32[]{:S(2)}) collective-permute-start(bf16[2,640,128]{2,1,0:T(8,128)(2,1)S(1)} %pad_maximum_fusion), channel_id=1, source_target_pairs={{0,2},{1,31},{2,4},{3,1},{4,6},{5,3},{6,8},{7,5},{8,10},{9,7},{10,... | collective-permute-start | bytes 983048 | tf_op jit(solution)/shard_map/ppermute | solution.py:437
  11.2 1.1 %pad.4 = bf16[2,28,32,32]{3,2,1,0:T(8,128)(2,1)S(1)} pad(bf16[2,27,32,32]{3,2,1,0:T(8,128)(2,1)} %bitcast.60, bf16[]{:T(256)} %constant.48.clone.1), padding=0_0x0_1x0_0x0_0 | pad | bytes 225282 | tf_op jit(solution)/shard_map/jit(_pad)/pad | solution.py:427
  12.3 0.2 copy.21
  12.6 0.2 reshape.43.pack0
  12.8 2.5 %collective-permute-start.5 = (bf16[2,224,128]{2,1,0:T(8,128)(2,1)S(1)}, bf16[2,224,128]{2,1,0:T(8,128)(2,1)S(1)}, u32[]{:S(2)}, u32[]{:S(2)}) collective-permute-start(bf16[2,224,128]{2,1,0:T(8,128)(2,1)S(1)} %reshape.43.pack0), channel_id=1, source_target_pairs={{0,96},{32,0},{64,32},{96,64},{1,97},{33,1},{65,33},{97,65},{2,98}... | collective-permute-start | bytes 344072 | tf_op jit(solution)/shard_map/ppermute | solution.py:411
  15.4 0.5 collective-permute-start.4
  15.9 0.6 collective-permute-start.3
  16.5 0.1 collective-permute-start.2
  16.6 0.0 collective-permute-done.1.near
  16.6 0.5 collective-permute-start.6
  17.1 1.3 %collective-permute-done.5.pack3 = bf16[2,224,128]{2,1,0:T(8,128)(2,1)S(1)} collective-permute-done((bf16[2,224,128]{2,1,0:T(8,128)(2,1)S(1)}, bf16[2,224,128]{2,1,0:T(8,128)(2,1)S(1)}, u32[]{:S(2)}, u32[]{:S(2)}) %collective-permute-start.5) | collective-permute-done | bytes 114720 | tf_op jit(solution)/shard_map/ppermute | solution.py:411
  18.3 2.5 %collective-permute-done.4.pack2 = bf16[2,224,128]{2,1,0:T(8,128)(2,1)S(1)} collective-permute-done((bf16[2,224,128]{2,1,0:T(8,128)(2,1)S(1)}, bf16[2,224,128]{2,1,0:T(8,128)(2,1)S(1)}, u32[]{:S(2)}, u32[]{:S(2)}) %collective-permute-start.4) | collective-permute-done | bytes 114720 | tf_op jit(solution)/shard_map/ppermute | solution.py:411
  20.8 1.2 %collective-permute-done.3.pack1 = bf16[2,224,128]{2,1,0:T(8,128)(2,1)S(1)} collective-permute-done((bf16[2,224,128]{2,1,0:T(8,128)(2,1)S(1)}, bf16[2,224,128]{2,1,0:T(8,128)(2,1)S(1)}, u32[]{:S(2)}, u32[]{:S(2)}) %collective-permute-start.3) | collective-permute-done | bytes 114720 | tf_op jit(solution)/shard_map/ppermute | solution.py:411
  22.0 4.8 %banded.1 = (bf16[8,512,768]{2,1,0:T(8,128)(2,1)S(1)}, bf16[8,512,768]{2,1,0:T(8,128)(2,1)S(1)}) custom-call(bf16[2,224,128]{2,1,0:T(8,128)(2,1)S(1)} %reshape.43.pack0, bf16[2,224,128]{2,1,0:T(8,128)(2,1)S(1)} %collective-permute-done.3.pack1, bf16[2,224,128]{2,1,0:T(8,128)(2,1)S(1)} %collective-permute-done.4.pack2, ...), custom_call_target="tpu_custom_call" | custom-call | flops 5000000000 | bytes 10000000 | tf_op jit(solution)/shard_map/banded/pallas_call | solution.py:308
  26.8 0.0 collective-permute-done.2.far
  26.9 0.1 collective-permute-start.7
  26.9 1.4 %collective-permute-done.7.far_other = bf16[640,128]{1,0:T(8,128)(2,1)S(1)} collective-permute-done((bf16[640,128]{1,0:T(8,128)(2,1)S(1)}, bf16[640,128]{1,0:T(8,128)(2,1)S(1)}, u32[]{:S(2)}, u32[]{:S(2)}) %collective-permute-start.7) | collective-permute-done | bytes 163872 | tf_op jit(solution)/shard_map/ppermute | solution.py:442
  28.3 0.0 collective-permute-done.6.near_other
  28.3 14.2 %sections.1 = (bf16[512,128]{1,0:T(8,128)(2,1)S(1)}, bf16[512,128]{1,0:T(8,128)(2,1)S(1)}, bf16[512,128]{1,0:T(8,128)(2,1)S(1)}, bf16[512,128]{1,0:T(8,128)(2,1)...) custom-call(bf16[2,320,128]{2,1,0:T(8,128)(2,1)S(1)} %pad_maximum_fusion.1.own, ...), custom_call_target="tpu_custom_call" | custom-call | flops 20000000000 | bytes 10000000 | tf_op jit(solution)/shard_map/sections/pallas_call | solution.py:326
  42.5 2.6 %kernel_grads.1 = (bf16[224,128]{1,0:T(8,128)(2,1)S(1)}, bf16[224,128]{1,0:T(8,128)(2,1)S(1)}, bf16[224,128]{1,0:T(8,128)(2,1)S(1)}, bf16[224,128]{1,0:T(8,128)(2,1)S(1)}, bf16[4,224,128]{2,1,0:T(8,128)(2,1)S(1)}) custom-call(bf16[8,480,128]{2,1,0:T(8,128)(2,1)S(1)} %get-tuple-element.27.windows, bf16[8,320,128]{2,1,0:T(8,128)(2,1)S(1)} %get-tuple-element.28.deltas), custom_call_target="tpu_custom_call" | custom-call | flops 6000000000 | bytes 4000000 | tf_op jit(solution)/shard_map/kernel_grads/pallas_call | solution.py:356
  45.1 0.5 collective-permute-start.8
  45.7 1.1 %collective-permute-done.8 = bf16[4,224,128]{2,1,0:T(8,128)(2,1)S(1)} collective-permute-done((bf16[4,224,128]{2,1,0:T(8,128)(2,1)S(1)}, bf16[4,224,128]{2,1,0:T(8,128)(2,1)S(1)}, u32[]{:S(2)}, u32[]{:S(2)}) %collective-permute-start.8) | collective-permute-done | bytes 229408 | tf_op jit(solution)/shard_map/ppermute | solution.py:448
  46.8 0.1 fusion.3
  46.8 0.1 collective-permute-start.9
  46.9 2.7 %collective-permute-start.11 = (bf16[224,128]{1,0:T(8,128)(2,1)S(1)}, bf16[224,128]{1,0:T(8,128)(2,1)S(1)}, u32[]{:S(2)}, u32[]{:S(2)}) collective-permute-start(bf16[224,128]{1,0:T(8,128)(2,1)S(1)} %get-tuple-element.44), channel_id=1, source_target_pairs={{0,96},{32,0},{64,32},{96,64},{1,97},{33,1},{65,33},{97,65},{2,98}... | collective-permute-start | bytes 172040 | tf_op jit(solution)/shard_map/ppermute | solution.py:411
  49.6 0.0 collective-permute-start.10
  49.6 1.6 %collective-permute-done.9 = bf16[224,128]{1,0:T(8,128)(2,1)S(1)} collective-permute-done((bf16[224,128]{1,0:T(8,128)(2,1)S(1)}, bf16[224,128]{1,0:T(8,128)(2,1)S(1)}, u32[]{:S(2)}, u32[]{:S(2)}) %collective-permute-start.9) | collective-permute-done | bytes 57376 | tf_op jit(solution)/shard_map/ppermute | solution.py:411
  51.1 0.2 collective-permute-done.11
  51.3 2.8 %collective-permute-done.10 = bf16[224,128]{1,0:T(8,128)(2,1)S(1)} collective-permute-done((bf16[224,128]{1,0:T(8,128)(2,1)S(1)}, bf16[224,128]{1,0:T(8,128)(2,1)S(1)}, u32[]{:S(2)}, u32[]{:S(2)}) %collective-permute-start.10) | collective-permute-done | bytes 57376 | tf_op jit(solution)/shard_map/ppermute | solution.py:411
  54.2 0.1 collective-permute-start.14
  54.2 0.1 collective-permute-start.13
  54.3 1.4 %collective-permute-start.12 = (bf16[224,128]{1,0:T(8,128)(2,1)S(1)}, bf16[224,128]{1,0:T(8,128)(2,1)S(1)}, u32[]{:S(2)}, u32[]{:S(2)}) collective-permute-start(bf16[224,128]{1,0:T(8,128)(2,1)S(1)} %add_convert_fusion.2), channel_id=1, source_target_pairs={{0,2},{1,3},{2,4},{3,5},{4,6},{5,7},{6,0},{7,1},{8,10},{9,11},{10,... | collective-permute-start | bytes 172040 | tf_op jit(solution)/shard_map/ppermute | solution.py:411
  55.7 0.0 collective-permute-start.18
  55.7 1.9 %collective-permute-start.19 = (bf16[512,128]{1,0:T(8,128)(2,1)S(1)}, bf16[512,128]{1,0:T(8,128)(2,1)S(1)}, u32[]{:S(2)}, u32[]{:S(2)}) collective-permute-start(bf16[512,128]{1,0:T(8,128)(2,1)S(1)} %get-tuple-element.36), channel_id=1, source_target_pairs={{0,64},{32,96},{64,0},{96,32},{1,65},{33,97},{65,1},{97,33},{2,66}... | collective-permute-start | bytes 393224 | tf_op jit(solution)/shard_map/ppermute | solution.py:411
  57.6 0.0 collective-permute-done.14
  57.6 0.8 %collective-permute-start.20 = (bf16[512,128]{1,0:T(8,128)(2,1)S(1)}, bf16[512,128]{1,0:T(8,128)(2,1)S(1)}, u32[]{:S(2)}, u32[]{:S(2)}) collective-permute-start(bf16[512,128]{1,0:T(8,128)(2,1)S(1)} %get-tuple-element.37), channel_id=1, source_target_pairs={{0,96},{32,0},{64,32},{96,64},{1,97},{33,1},{65,33},{97,65},{2,98}... | collective-permute-start | bytes 393224 | tf_op jit(solution)/shard_map/ppermute | solution.py:411
  58.4 0.5 collective-permute-done.13
  58.9 0.8 %collective-permute-done.12 = bf16[224,128]{1,0:T(8,128)(2,1)S(1)} collective-permute-done((bf16[224,128]{1,0:T(8,128)(2,1)S(1)}, bf16[224,128]{1,0:T(8,128)(2,1)S(1)}, u32[]{:S(2)}, u32[]{:S(2)}) %collective-permute-start.12) | collective-permute-done | bytes 57376 | tf_op jit(solution)/shard_map/ppermute | solution.py:411
  59.7 2.6 %collective-permute-start.17 = (bf16[224,128]{1,0:T(8,128)(2,1)S(1)}, bf16[224,128]{1,0:T(8,128)(2,1)S(1)}, u32[]{:S(2)}, u32[]{:S(2)}) collective-permute-start(bf16[224,128]{1,0:T(8,128)(2,1)S(1)} %add_convert_fusion.1), channel_id=1, source_target_pairs={{0,24},{1,25},{2,26},{3,27},{4,28},{5,29},{6,30},{7,31},{8,0},{9,1... | collective-permute-start | bytes 172040 | tf_op jit(solution)/shard_map/ppermute | solution.py:411
  62.3 0.0 collective-permute-start.16
  62.3 0.1 collective-permute-done.18.in1
  62.4 0.5 collective-permute-start.15
  63.0 0.0 collective-permute-done.19.in2
  63.0 0.1 collective-permute-done.20.in3
  63.1 1.8 %layout.1 = (bf16[2,32,4,4,128]{4,3,2,1,0:T(4,128)(2,1)}, f32[2,32,4,4,128]{4,3,2,1,0:T(4,128)}) custom-call(bf16[512,128]{1,0:T(8,128)(2,1)S(1)} %get-tuple-element.34.in0, bf16[512,128]{1,0:T(8,128)(2,1)S(1)} %collective-permute-done.18.in1, bf16[512,128]{1,0:T(8,128)(2,1)S(1)} %collective-permute-done.19.in2, bf16[512,128]{1,0:T(8,128)(2,1)S(1)} %collective-permute-done.20.in3), custom_call_target="tpu_custom_call" | custom-call | flops 4000000000 | bytes 4000000 | tf_op jit(solution)/shard_map/layout/pallas_call | solution.py:389
  64.9 0.0 collective-permute-done.17
  64.9 2.0 %collective-permute-done.16 = bf16[224,128]{1,0:T(8,128)(2,1)S(1)} collective-permute-done((bf16[224,128]{1,0:T(8,128)(2,1)S(1)}, bf16[224,128]{1,0:T(8,128)(2,1)S(1)}, u32[]{:S(2)}, u32[]{:S(2)}) %collective-permute-start.16) | collective-permute-done | bytes 57376 | tf_op jit(solution)/shard_map/ppermute | solution.py:411
  66.9 0.4 collective-permute-done.15
  67.3 4.9 %collective-permute-start.21 = (bf16[224,128]{1,0:T(8,128)(2,1)S(1)}, bf16[224,128]{1,0:T(8,128)(2,1)S(1)}, u32[]{:S(2)}, u32[]{:S(2)}) collective-permute-start(bf16[224,128]{1,0:T(8,128)(2,1)S(1)} %add_convert_fusion), channel_id=1, source_target_pairs={{0,1},{1,0},{2,3},{3,2},{4,5},{5,4},{6,7},{7,6},{8,9},{9,8},{10,11... | collective-permute-start | bytes 172040 | tf_op jit(solution)/shard_map/ppermute | solution.py:460
  72.3 0.9 %collective-permute-done.21 = bf16[224,128]{1,0:T(8,128)(2,1)S(1)} collective-permute-done((bf16[224,128]{1,0:T(8,128)(2,1)S(1)}, bf16[224,128]{1,0:T(8,128)(2,1)S(1)}, u32[]{:S(2)}, u32[]{:S(2)}) %collective-permute-start.21) | collective-permute-done | bytes 57376 | tf_op jit(solution)/shard_map/ppermute | solution.py:460
  73.2 0.1 stack.13
  73.3 0.1 stack.14
  73.5 0.4 maximum_bitcast_fusion
  73.9 0.1 copy.15
  73.9 1.0 %fusion = f32[1,2,27,32,32]{4,3,2,1,0:T(8,128)} fusion(bf16[2,28,32,32]{3,2,1,0:T(8,128)(2,1)S(1)} %bitcast.53), kind=kLoop, calls=%fused_computation.3 | loop fusion | flops 55296 | bytes 331776 | tf_op jit(solution)/shard_map/broadcast_in_dim | solution.py:467
  (9 shorter events, 0.2 us)
Async XLA Ops:
  2.3 2.5 %collective-permute-start = (bf16[2,320,128]{2,1,0:T(8,128)(2,1)S(1)}, bf16[2,320,128]{2,1,0:T(8,128)(2,1)S(1)}, u32[]{:S(2)}, u32[]{:S(2)}) collective-permute-start(bf16[2,320,128]{2,1,0:T(8,128)(2,1)S(1)} %pad_maximum_fusion.1.own), channel_id=1, source_target_pairs={{0,1},{1,0},{2,3},{3,2},{4,5},{5,4},{6,7},{7,6},{8,9},{9,8},{10,11... | collective-permute-start | bytes 491528 | tf_op jit(solution)/shard_map/ppermute | solution.py:431
  4.8 11.7 %collective-permute-start.1 = (bf16[2,640,128]{2,1,0:T(8,128)(2,1)S(1)}, bf16[2,640,128]{2,1,0:T(8,128)(2,1)S(1)}, u32[]{:S(2)}, u32[]{:S(2)}) collective-permute-start(bf16[2,640,128]{2,1,0:T(8,128)(2,1)S(1)} %pad_maximum_fusion), channel_id=1, source_target_pairs={{0,2},{1,31},{2,4},{3,1},{4,6},{5,3},{6,8},{7,5},{8,10},{9,7},{10,... | collective-permute-start | bytes 983048 | tf_op jit(solution)/shard_map/ppermute | solution.py:437
  12.8 5.5 %collective-permute-start.5 = (bf16[2,224,128]{2,1,0:T(8,128)(2,1)S(1)}, bf16[2,224,128]{2,1,0:T(8,128)(2,1)S(1)}, u32[]{:S(2)}, u32[]{:S(2)}) collective-permute-start(bf16[2,224,128]{2,1,0:T(8,128)(2,1)S(1)} %reshape.43.pack0), channel_id=1, source_target_pairs={{0,96},{32,0},{64,32},{96,64},{1,97},{33,1},{65,33},{97,65},{2,98}... | collective-permute-start | bytes 344072 | tf_op jit(solution)/shard_map/ppermute | solution.py:411
  15.4 5.4 %collective-permute-start.4 = (bf16[2,224,128]{2,1,0:T(8,128)(2,1)S(1)}, bf16[2,224,128]{2,1,0:T(8,128)(2,1)S(1)}, u32[]{:S(2)}, u32[]{:S(2)}) collective-permute-start(bf16[2,224,128]{2,1,0:T(8,128)(2,1)S(1)} %reshape.43.pack0), channel_id=1, source_target_pairs={{0,64},{32,96},{64,0},{96,32},{1,65},{33,97},{65,1},{97,33},{2,66}... | collective-permute-start | bytes 344072 | tf_op jit(solution)/shard_map/ppermute | solution.py:411
  15.9 6.2 %collective-permute-start.3 = (bf16[2,224,128]{2,1,0:T(8,128)(2,1)S(1)}, bf16[2,224,128]{2,1,0:T(8,128)(2,1)S(1)}, u32[]{:S(2)}, u32[]{:S(2)}) collective-permute-start(bf16[2,224,128]{2,1,0:T(8,128)(2,1)S(1)} %reshape.43.pack0), channel_id=1, source_target_pairs={{0,32},{32,64},{64,96},{96,0},{1,33},{33,65},{65,97},{97,1},{2,34}... | collective-permute-start | bytes 344072 | tf_op jit(solution)/shard_map/ppermute | solution.py:411
  16.5 10.3 %collective-permute-start.2 = (bf16[640,128]{1,0:T(8,128)(2,1)S(1)}, bf16[640,128]{1,0:T(8,128)(2,1)S(1)}, u32[]{:S(2)}, u32[]{:S(2)}) collective-permute-start(bf16[640,128]{1,0:T(8,128)(2,1)S(1)} %slice_bitcast_fusion.1), channel_id=1, source_target_pairs={{0,4},{1,29},{2,6},{3,31},{4,8},{5,1},{6,10},{7,3},{8,12},{9,5},{1... | collective-permute-start | bytes 491528 | tf_op jit(solution)/shard_map/ppermute | solution.py:438
  16.6 11.7 %collective-permute-start.6 = (bf16[2,640,128]{2,1,0:T(8,128)(2,1)S(1)}, bf16[2,640,128]{2,1,0:T(8,128)(2,1)S(1)}, u32[]{:S(2)}, u32[]{:S(2)}) collective-permute-start(bf16[2,640,128]{2,1,0:T(8,128)(2,1)S(1)} %collective-permute-done.1.near), channel_id=1, source_target_pairs={{0,1},{1,0},{2,3},{3,2},{4,5},{5,4},{6,7},{7,6},{8,9},{9,8},{10,11... | collective-permute-start | bytes 983048 | tf_op jit(solution)/shard_map/ppermute | solution.py:440
  26.9 1.5 %collective-permute-start.7 = (bf16[640,128]{1,0:T(8,128)(2,1)S(1)}, bf16[640,128]{1,0:T(8,128)(2,1)S(1)}, u32[]{:S(2)}, u32[]{:S(2)}) collective-permute-start(bf16[640,128]{1,0:T(8,128)(2,1)S(1)} %collective-permute-done.2.far), channel_id=1, source_target_pairs={{0,1},{1,0},{2,3},{3,2},{4,5},{5,4},{6,7},{7,6},{8,9},{9,8},{10,11... | collective-permute-start | bytes 491528 | tf_op jit(solution)/shard_map/ppermute | solution.py:442
  45.1 1.6 %collective-permute-start.8 = (bf16[4,224,128]{2,1,0:T(8,128)(2,1)S(1)}, bf16[4,224,128]{2,1,0:T(8,128)(2,1)S(1)}, u32[]{:S(2)}, u32[]{:S(2)}) collective-permute-start(bf16[4,224,128]{2,1,0:T(8,128)(2,1)S(1)} %get-tuple-element.30), channel_id=1, source_target_pairs={{0,1},{1,0},{2,3},{3,2},{4,5},{5,4},{6,7},{7,6},{8,9},{9,8},{10,11... | collective-permute-start | bytes 688136 | tf_op jit(solution)/shard_map/ppermute | solution.py:448
  46.8 4.3 %collective-permute-start.9 = (bf16[224,128]{1,0:T(8,128)(2,1)S(1)}, bf16[224,128]{1,0:T(8,128)(2,1)S(1)}, u32[]{:S(2)}, u32[]{:S(2)}) collective-permute-start(bf16[224,128]{1,0:T(8,128)(2,1)S(1)} %get-tuple-element.43), channel_id=1, source_target_pairs={{0,32},{32,64},{64,96},{96,0},{1,33},{33,65},{65,97},{97,1},{2,34}... | collective-permute-start | bytes 172040 | tf_op jit(solution)/shard_map/ppermute | solution.py:411
  46.9 4.4 %collective-permute-start.11 = (bf16[224,128]{1,0:T(8,128)(2,1)S(1)}, bf16[224,128]{1,0:T(8,128)(2,1)S(1)}, u32[]{:S(2)}, u32[]{:S(2)}) collective-permute-start(bf16[224,128]{1,0:T(8,128)(2,1)S(1)} %get-tuple-element.44), channel_id=1, source_target_pairs={{0,96},{32,0},{64,32},{96,64},{1,97},{33,1},{65,33},{97,65},{2,98}... | collective-permute-start | bytes 172040 | tf_op jit(solution)/shard_map/ppermute | solution.py:411
  49.6 4.5 %collective-permute-start.10 = (bf16[224,128]{1,0:T(8,128)(2,1)S(1)}, bf16[224,128]{1,0:T(8,128)(2,1)S(1)}, u32[]{:S(2)}, u32[]{:S(2)}) collective-permute-start(bf16[224,128]{1,0:T(8,128)(2,1)S(1)} %get-tuple-element.45), channel_id=1, source_target_pairs={{0,64},{32,96},{64,0},{96,32},{1,65},{33,97},{65,1},{97,33},{2,66}... | collective-permute-start | bytes 172040 | tf_op jit(solution)/shard_map/ppermute | solution.py:411
  54.2 3.4 %collective-permute-start.14 = (bf16[224,128]{1,0:T(8,128)(2,1)S(1)}, bf16[224,128]{1,0:T(8,128)(2,1)S(1)}, u32[]{:S(2)}, u32[]{:S(2)}) collective-permute-start(bf16[224,128]{1,0:T(8,128)(2,1)S(1)} %add_convert_fusion.2), channel_id=1, source_target_pairs={{0,6},{1,7},{2,0},{3,1},{4,2},{5,3},{6,4},{7,5},{8,14},{9,15},{10,... | collective-permute-start | bytes 172040 | tf_op jit(solution)/shard_map/ppermute | solution.py:411
  54.2 4.6 %collective-permute-start.13 = (bf16[224,128]{1,0:T(8,128)(2,1)S(1)}, bf16[224,128]{1,0:T(8,128)(2,1)S(1)}, u32[]{:S(2)}, u32[]{:S(2)}) collective-permute-start(bf16[224,128]{1,0:T(8,128)(2,1)S(1)} %add_convert_fusion.2), channel_id=1, source_target_pairs={{0,4},{1,5},{2,6},{3,7},{4,0},{5,1},{6,2},{7,3},{8,12},{9,13},{10,... | collective-permute-start | bytes 172040 | tf_op jit(solution)/shard_map/ppermute | solution.py:411
  54.3 5.3 %collective-permute-start.12 = (bf16[224,128]{1,0:T(8,128)(2,1)S(1)}, bf16[224,128]{1,0:T(8,128)(2,1)S(1)}, u32[]{:S(2)}, u32[]{:S(2)}) collective-permute-start(bf16[224,128]{1,0:T(8,128)(2,1)S(1)} %add_convert_fusion.2), channel_id=1, source_target_pairs={{0,2},{1,3},{2,4},{3,5},{4,6},{5,7},{6,0},{7,1},{8,10},{9,11},{10,... | collective-permute-start | bytes 172040 | tf_op jit(solution)/shard_map/ppermute | solution.py:411
  55.7 6.7 %collective-permute-start.18 = (bf16[512,128]{1,0:T(8,128)(2,1)S(1)}, bf16[512,128]{1,0:T(8,128)(2,1)S(1)}, u32[]{:S(2)}, u32[]{:S(2)}) collective-permute-start(bf16[512,128]{1,0:T(8,128)(2,1)S(1)} %get-tuple-element.35), channel_id=1, source_target_pairs={{0,32},{32,64},{64,96},{96,0},{1,33},{33,65},{65,97},{97,1},{2,34}... | collective-permute-start | bytes 393224 | tf_op jit(solution)/shard_map/ppermute | solution.py:411
  55.7 7.3 %collective-permute-start.19 = (bf16[512,128]{1,0:T(8,128)(2,1)S(1)}, bf16[512,128]{1,0:T(8,128)(2,1)S(1)}, u32[]{:S(2)}, u32[]{:S(2)}) collective-permute-start(bf16[512,128]{1,0:T(8,128)(2,1)S(1)} %get-tuple-element.36), channel_id=1, source_target_pairs={{0,64},{32,96},{64,0},{96,32},{1,65},{33,97},{65,1},{97,33},{2,66}... | collective-permute-start | bytes 393224 | tf_op jit(solution)/shard_map/ppermute | solution.py:411
  57.6 5.4 %collective-permute-start.20 = (bf16[512,128]{1,0:T(8,128)(2,1)S(1)}, bf16[512,128]{1,0:T(8,128)(2,1)S(1)}, u32[]{:S(2)}, u32[]{:S(2)}) collective-permute-start(bf16[512,128]{1,0:T(8,128)(2,1)S(1)} %get-tuple-element.37), channel_id=1, source_target_pairs={{0,96},{32,0},{64,32},{96,64},{1,97},{33,1},{65,33},{97,65},{2,98}... | collective-permute-start | bytes 393224 | tf_op jit(solution)/shard_map/ppermute | solution.py:411
  59.7 5.2 %collective-permute-start.17 = (bf16[224,128]{1,0:T(8,128)(2,1)S(1)}, bf16[224,128]{1,0:T(8,128)(2,1)S(1)}, u32[]{:S(2)}, u32[]{:S(2)}) collective-permute-start(bf16[224,128]{1,0:T(8,128)(2,1)S(1)} %add_convert_fusion.1), channel_id=1, source_target_pairs={{0,24},{1,25},{2,26},{3,27},{4,28},{5,29},{6,30},{7,31},{8,0},{9,1... | collective-permute-start | bytes 172040 | tf_op jit(solution)/shard_map/ppermute | solution.py:411
  62.3 4.6 %collective-permute-start.16 = (bf16[224,128]{1,0:T(8,128)(2,1)S(1)}, bf16[224,128]{1,0:T(8,128)(2,1)S(1)}, u32[]{:S(2)}, u32[]{:S(2)}) collective-permute-start(bf16[224,128]{1,0:T(8,128)(2,1)S(1)} %add_convert_fusion.1), channel_id=1, source_target_pairs={{0,16},{1,17},{2,18},{3,19},{4,20},{5,21},{6,22},{7,23},{8,24},{9,... | collective-permute-start | bytes 172040 | tf_op jit(solution)/shard_map/ppermute | solution.py:411
  62.4 4.9 %collective-permute-start.15 = (bf16[224,128]{1,0:T(8,128)(2,1)S(1)}, bf16[224,128]{1,0:T(8,128)(2,1)S(1)}, u32[]{:S(2)}, u32[]{:S(2)}) collective-permute-start(bf16[224,128]{1,0:T(8,128)(2,1)S(1)} %add_convert_fusion.1), channel_id=1, source_target_pairs={{0,8},{1,9},{2,10},{3,11},{4,12},{5,13},{6,14},{7,15},{8,16},{9,17... | collective-permute-start | bytes 172040 | tf_op jit(solution)/shard_map/ppermute | solution.py:411
  67.3 5.8 %collective-permute-start.21 = (bf16[224,128]{1,0:T(8,128)(2,1)S(1)}, bf16[224,128]{1,0:T(8,128)(2,1)S(1)}, u32[]{:S(2)}, u32[]{:S(2)}) collective-permute-start(bf16[224,128]{1,0:T(8,128)(2,1)S(1)} %add_convert_fusion), channel_id=1, source_target_pairs={{0,1},{1,0},{2,3},{3,2},{4,5},{5,4},{6,7},{7,6},{8,9},{9,8},{10,11... | collective-permute-start | bytes 172040 | tf_op jit(solution)/shard_map/ppermute | solution.py:460

commit v6 on v5

--- a/solution.py
+++ b/solution.py
@@ -429,6 +429,7 @@
 
     others = [rotated(packed, "segment", 4, k, 1) for k in (1, 2, 3)]
     oth = lax.ppermute(own, "gy", swap)
+    oth, packed = lax.optimization_barrier((oth, packed))
     block = jnp.concatenate([own, oth], axis=1)
 
     def outward(distance):

time: 75.1 us -> 74 us (0.985)
  waiting for transfers between devices: 17.8 us -> 15.9 us
    ppermute x15, waiting for transfers between devices: 13.4 us -> 12.2 us  [rotated(): return lax.ppermute(value, axis, [(i, target(i)) for i in range(count)])]
    ppermute x1, waiting for transfers between devices: 1.03 us -> 0.01 us  [local(): oth = lax.ppermute(own, 'gy', swap)]
    ppermute x1, starting transfers between devices: 0.48 us -> 1.33 us  [local(): near_other = lax.ppermute(near, 'gy', swap)]
where the time goes in v6:
time: 74 us; the launch traced here: 73.8 us
  starting transfers between devices  28.4 us (38%)
  Pallas kernels  23.5 us (32%)
  waiting for transfers between devices  15.9 us (21%)
  local copies, waits for them, and re-layouts  3.53 us (5%)
  other arithmetic  1.63 us (2%)
  between operations  0.88 us (1%)
    pallas_call x1, Pallas kernels, main_call(): pl.pallas_call(main_kernel, out_shape=[jax.ShapeDtypeStruct((512, LANES),...  14.2 us
    ppermute x15, starting transfers between devices, rotated(): return lax.ppermute(value, axis, [(i, target(i)) for i in range(count)])  13.7 us
    ppermute x15, waiting for transfers between devices, rotated(): return lax.ppermute(value, axis, [(i, target(i)) for i in range(count)])  12.2 us
    ppermute x1, starting transfers between devices, local(): near = lax.ppermute(block, 'gy', outward(1))  6.36 us
    ppermute x1, starting transfers between devices, local(): other = lax.ppermute(mine, 'gy', swap)  4.84 us
    pallas_call x1, Pallas kernels, build_call(): pl.pallas_call(build_kernel, out_shape=[jax.ShapeDtypeStruct(MATRICES, BF...  4.8 us
    pallas_call x1, Pallas kernels, grads_call(): pl.pallas_call(grads_kernel, out_shape=[jax.ShapeDtypeStruct((224, LANES)...  2.65 us
    pallas_call x1, Pallas kernels, layout_call(): pl.pallas_call(layout_kernel, out_shape=[jax.ShapeDtypeStruct((2, 32, 4,...  1.85 us
  transfers between devices with their start and end apart: 22, of which 16 were waited for; matrix products, arithmetic and copies ran while one was open for 2% of the time, Pallas kernels for 9%

profile of v6, /device:TPU:1, one launch (start us, length us, event | category | flops | bytes accessed | tf_op | source)
XLA Modules:
  0.0 73.8 jit_solution(6890929506921387328)
XLA Ops:
  0.7 1.1 %constant_dynamic-slice_fusion.1 = (bf16[1,32,4,4,128]{4,3,2,1,0:T(4,128)(2,1)S(1)}, bf16[1,32,4,4,128]{4,3,2,1,0:T(4,128)(2,1)S(1)}) fusion(bf16[2,32,4,4,128]{4,3,2,1,0:T(4,128)(2,1)} %param.4, s32[]{:T(128)S(6)} %select_n.37, bf16[2,32,4,4,128]{4,3,2,1,0:T(4,128)(2,1)} %param.3), kind=kLoop, calls=%fused_computation.25 | loop fusion | bytes 524292 | tf_op jit(solution)/shard_map/jit(dynamic_index_in_dim)/dynamic_slice | solution.py:422
  1.8 0.1 constant_dynamic-slice_fusion
  1.9 0.1 copy.13
  2.0 0.1 constant_dynamic-slice_fusion.2
  2.2 0.1 copy.10
  2.3 1.5 %collective-permute-start = (bf16[2,320,128]{2,1,0:T(8,128)(2,1)S(1)}, bf16[2,320,128]{2,1,0:T(8,128)(2,1)S(1)}, u32[]{:S(2)}, u32[]{:S(2)}) collective-permute-start(bf16[2,320,128]{2,1,0:T(8,128)(2,1)S(1)} %pad_maximum_fusion.1.own), channel_id=1, source_target_pairs={{0,1},{1,0},{2,3},{3,2},{4,5},{5,4},{6,7},{7,6},{8,9},{9,8},{10,11... | collective-permute-start | bytes 491528 | tf_op jit(solution)/shard_map/ppermute | solution.py:431
  3.8 1.1 %pad.4 = bf16[2,28,32,32]{3,2,1,0:T(8,128)(2,1)S(1)} pad(bf16[2,27,32,32]{3,2,1,0:T(8,128)(2,1)} %bitcast.60, bf16[]{:T(256)} %constant.48.clone.1), padding=0_0x0_1x0_0x0_0 | pad | bytes 225282 | tf_op jit(solution)/shard_map/jit(_pad)/pad | solution.py:427
  4.9 0.2 copy.21
  5.1 0.2 reshape.43.pack0
  5.4 0.0 collective-permute-done.oth
  5.4 6.4 %collective-permute-start.1 = (bf16[2,640,128]{2,1,0:T(8,128)(2,1)S(1)}, bf16[2,640,128]{2,1,0:T(8,128)(2,1)S(1)}, u32[]{:S(2)}, u32[]{:S(2)}) collective-permute-start(bf16[2,640,128]{2,1,0:T(8,128)(2,1)S(1)} %pad_maximum_fusion), channel_id=1, source_target_pairs={{0,2},{1,31},{2,4},{3,1},{4,6},{5,3},{6,8},{7,5},{8,10},{9,7},{10,... | collective-permute-start | bytes 983048 | tf_op jit(solution)/shard_map/ppermute | solution.py:438
  11.8 2.5 %collective-permute-start.5 = (bf16[2,224,128]{2,1,0:T(8,128)(2,1)S(1)}, bf16[2,224,128]{2,1,0:T(8,128)(2,1)S(1)}, u32[]{:S(2)}, u32[]{:S(2)}) collective-permute-start(bf16[2,224,128]{2,1,0:T(8,128)(2,1)S(1)} %reshape.43.pack0), channel_id=1, source_target_pairs={{0,96},{32,0},{64,32},{96,64},{1,97},{33,1},{65,33},{97,65},{2,98}... | collective-permute-start | bytes 344072 | tf_op jit(solution)/shard_map/ppermute | solution.py:411
  14.3 0.5 collective-permute-start.4
  14.8 0.6 collective-permute-start.3
  15.4 0.1 collective-permute-start.2
  15.5 0.3 collective-permute-done.1.near
  15.8 1.3 %collective-permute-start.6 = (bf16[2,640,128]{2,1,0:T(8,128)(2,1)S(1)}, bf16[2,640,128]{2,1,0:T(8,128)(2,1)S(1)}, u32[]{:S(2)}, u32[]{:S(2)}) collective-permute-start(bf16[2,640,128]{2,1,0:T(8,128)(2,1)S(1)} %collective-permute-done.1.near), channel_id=1, source_target_pairs={{0,1},{1,0},{2,3},{3,2},{4,5},{5,4},{6,7},{7,6},{8,9},{9,8},{10,11... | collective-permute-start | bytes 983048 | tf_op jit(solution)/shard_map/ppermute | solution.py:441
  17.2 0.1 collective-permute-done.5.pack3
  17.3 2.5 %collective-permute-done.4.pack2 = bf16[2,224,128]{2,1,0:T(8,128)(2,1)S(1)} collective-permute-done((bf16[2,224,128]{2,1,0:T(8,128)(2,1)S(1)}, bf16[2,224,128]{2,1,0:T(8,128)(2,1)S(1)}, u32[]{:S(2)}, u32[]{:S(2)}) %collective-permute-start.4) | collective-permute-done | bytes 114720 | tf_op jit(solution)/shard_map/ppermute | solution.py:411
  19.7 1.2 %collective-permute-done.3.pack1 = bf16[2,224,128]{2,1,0:T(8,128)(2,1)S(1)} collective-permute-done((bf16[2,224,128]{2,1,0:T(8,128)(2,1)S(1)}, bf16[2,224,128]{2,1,0:T(8,128)(2,1)S(1)}, u32[]{:S(2)}, u32[]{:S(2)}) %collective-permute-start.3) | collective-permute-done | bytes 114720 | tf_op jit(solution)/shard_map/ppermute | solution.py:411
  21.0 4.8 %banded.1 = (bf16[8,512,768]{2,1,0:T(8,128)(2,1)S(1)}, bf16[8,512,768]{2,1,0:T(8,128)(2,1)S(1)}) custom-call(bf16[2,224,128]{2,1,0:T(8,128)(2,1)S(1)} %reshape.43.pack0, bf16[2,224,128]{2,1,0:T(8,128)(2,1)S(1)} %collective-permute-done.3.pack1, bf16[2,224,128]{2,1,0:T(8,128)(2,1)S(1)} %collective-permute-done.4.pack2, ...), custom_call_target="tpu_custom_call" | custom-call | flops 5000000000 | bytes 10000000 | tf_op jit(solution)/shard_map/banded/pallas_call | solution.py:308
  25.8 0.0 collective-permute-done.2.far
  25.8 0.1 collective-permute-start.7
  25.9 1.4 %collective-permute-done.7.far_other = bf16[640,128]{1,0:T(8,128)(2,1)S(1)} collective-permute-done((bf16[640,128]{1,0:T(8,128)(2,1)S(1)}, bf16[640,128]{1,0:T(8,128)(2,1)S(1)}, u32[]{:S(2)}, u32[]{:S(2)}) %collective-permute-start.7) | collective-permute-done | bytes 163872 | tf_op jit(solution)/shard_map/ppermute | solution.py:443
  27.3 0.0 collective-permute-done.6.near_other
  27.3 14.2 %sections.1 = (bf16[512,128]{1,0:T(8,128)(2,1)S(1)}, bf16[512,128]{1,0:T(8,128)(2,1)S(1)}, bf16[512,128]{1,0:T(8,128)(2,1)S(1)}, bf16[512,128]{1,0:T(8,128)(2,1)...) custom-call(bf16[2,320,128]{2,1,0:T(8,128)(2,1)S(1)} %pad_maximum_fusion.1.own, ...), custom_call_target="tpu_custom_call" | custom-call | flops 20000000000 | bytes 10000000 | tf_op jit(solution)/shard_map/sections/pallas_call | solution.py:326
  41.4 2.6 %kernel_grads.1 = (bf16[224,128]{1,0:T(8,128)(2,1)S(1)}, bf16[224,128]{1,0:T(8,128)(2,1)S(1)}, bf16[224,128]{1,0:T(8,128)(2,1)S(1)}, bf16[224,128]{1,0:T(8,128)(2,1)S(1)}, bf16[4,224,128]{2,1,0:T(8,128)(2,1)S(1)}) custom-call(bf16[8,480,128]{2,1,0:T(8,128)(2,1)S(1)} %get-tuple-element.31.windows, bf16[8,320,128]{2,1,0:T(8,128)(2,1)S(1)} %get-tuple-element.32.deltas), custom_call_target="tpu_custom_call" | custom-call | flops 6000000000 | bytes 4000000 | tf_op jit(solution)/shard_map/kernel_grads/pallas_call | solution.py:356
  44.1 0.5 collective-permute-start.8
  44.6 1.1 %collective-permute-done.8 = bf16[4,224,128]{2,1,0:T(8,128)(2,1)S(1)} collective-permute-done((bf16[4,224,128]{2,1,0:T(8,128)(2,1)S(1)}, bf16[4,224,128]{2,1,0:T(8,128)(2,1)S(1)}, u32[]{:S(2)}, u32[]{:S(2)}) %collective-permute-start.8) | collective-permute-done | bytes 229408 | tf_op jit(solution)/shard_map/ppermute | solution.py:449
  45.7 0.1 fusion.3
  45.8 0.1 collective-permute-start.9
  45.8 2.7 %collective-permute-start.11 = (bf16[224,128]{1,0:T(8,128)(2,1)S(1)}, bf16[224,128]{1,0:T(8,128)(2,1)S(1)}, u32[]{:S(2)}, u32[]{:S(2)}) collective-permute-start(bf16[224,128]{1,0:T(8,128)(2,1)S(1)} %get-tuple-element.48), channel_id=1, source_target_pairs={{0,96},{32,0},{64,32},{96,64},{1,97},{33,1},{65,33},{97,65},{2,98}... | collective-permute-start | bytes 172040 | tf_op jit(solution)/shard_map/ppermute | solution.py:411
  48.5 0.0 collective-permute-start.10
  48.5 1.6 %collective-permute-done.9 = bf16[224,128]{1,0:T(8,128)(2,1)S(1)} collective-permute-done((bf16[224,128]{1,0:T(8,128)(2,1)S(1)}, bf16[224,128]{1,0:T(8,128)(2,1)S(1)}, u32[]{:S(2)}, u32[]{:S(2)}) %collective-permute-start.9) | collective-permute-done | bytes 57376 | tf_op jit(solution)/shard_map/ppermute | solution.py:411
  50.1 0.2 collective-permute-done.11
  50.2 2.8 %collective-permute-done.10 = bf16[224,128]{1,0:T(8,128)(2,1)S(1)} collective-permute-done((bf16[224,128]{1,0:T(8,128)(2,1)S(1)}, bf16[224,128]{1,0:T(8,128)(2,1)S(1)}, u32[]{:S(2)}, u32[]{:S(2)}) %collective-permute-start.10) | collective-permute-done | bytes 57376 | tf_op jit(solution)/shard_map/ppermute | solution.py:411
  53.1 0.1 collective-permute-start.14
  53.2 0.1 collective-permute-start.13
  53.3 1.4 %collective-permute-start.12 = (bf16[224,128]{1,0:T(8,128)(2,1)S(1)}, bf16[224,128]{1,0:T(8,128)(2,1)S(1)}, u32[]{:S(2)}, u32[]{:S(2)}) collective-permute-start(bf16[224,128]{1,0:T(8,128)(2,1)S(1)} %add_convert_fusion.2), channel_id=1, source_target_pairs={{0,2},{1,3},{2,4},{3,5},{4,6},{5,7},{6,0},{7,1},{8,10},{9,11},{10,... | collective-permute-start | bytes 172040 | tf_op jit(solution)/shard_map/ppermute | solution.py:411
  54.6 0.0 collective-permute-start.18
  54.6 1.9 %collective-permute-start.19 = (bf16[512,128]{1,0:T(8,128)(2,1)S(1)}, bf16[512,128]{1,0:T(8,128)(2,1)S(1)}, u32[]{:S(2)}, u32[]{:S(2)}) collective-permute-start(bf16[512,128]{1,0:T(8,128)(2,1)S(1)} %get-tuple-element.40), channel_id=1, source_target_pairs={{0,64},{32,96},{64,0},{96,32},{1,65},{33,97},{65,1},{97,33},{2,66}... | collective-permute-start | bytes 393224 | tf_op jit(solution)/shard_map/ppermute | solution.py:411
  56.5 0.0 collective-permute-done.14
  56.5 0.8 %collective-permute-start.20 = (bf16[512,128]{1,0:T(8,128)(2,1)S(1)}, bf16[512,128]{1,0:T(8,128)(2,1)S(1)}, u32[]{:S(2)}, u32[]{:S(2)}) collective-permute-start(bf16[512,128]{1,0:T(8,128)(2,1)S(1)} %get-tuple-element.41), channel_id=1, source_target_pairs={{0,96},{32,0},{64,32},{96,64},{1,97},{33,1},{65,33},{97,65},{2,98}... | collective-permute-start | bytes 393224 | tf_op jit(solution)/shard_map/ppermute | solution.py:411
  57.3 0.5 collective-permute-done.13
  57.8 0.8 %collective-permute-done.12 = bf16[224,128]{1,0:T(8,128)(2,1)S(1)} collective-permute-done((bf16[224,128]{1,0:T(8,128)(2,1)S(1)}, bf16[224,128]{1,0:T(8,128)(2,1)S(1)}, u32[]{:S(2)}, u32[]{:S(2)}) %collective-permute-start.12) | collective-permute-done | bytes 57376 | tf_op jit(solution)/shard_map/ppermute | solution.py:411
  58.6 2.6 %collective-permute-start.17 = (bf16[224,128]{1,0:T(8,128)(2,1)S(1)}, bf16[224,128]{1,0:T(8,128)(2,1)S(1)}, u32[]{:S(2)}, u32[]{:S(2)}) collective-permute-start(bf16[224,128]{1,0:T(8,128)(2,1)S(1)} %add_convert_fusion.1), channel_id=1, source_target_pairs={{0,24},{1,25},{2,26},{3,27},{4,28},{5,29},{6,30},{7,31},{8,0},{9,1... | collective-permute-start | bytes 172040 | tf_op jit(solution)/shard_map/ppermute | solution.py:411
  61.2 0.0 collective-permute-start.16
  61.2 0.1 collective-permute-done.18.in1
  61.4 0.5 collective-permute-start.15
  61.9 0.0 collective-permute-done.19.in2
  61.9 0.1 collective-permute-done.20.in3
  62.0 1.8 %layout.1 = (bf16[2,32,4,4,128]{4,3,2,1,0:T(4,128)(2,1)}, f32[2,32,4,4,128]{4,3,2,1,0:T(4,128)}) custom-call(bf16[512,128]{1,0:T(8,128)(2,1)S(1)} %get-tuple-element.38.in0, bf16[512,128]{1,0:T(8,128)(2,1)S(1)} %collective-permute-done.18.in1, bf16[512,128]{1,0:T(8,128)(2,1)S(1)} %collective-permute-done.19.in2, bf16[512,128]{1,0:T(8,128)(2,1)S(1)} %collective-permute-done.20.in3), custom_call_target="tpu_custom_call" | custom-call | flops 4000000000 | bytes 4000000 | tf_op jit(solution)/shard_map/layout/pallas_call | solution.py:389
  63.8 0.0 collective-permute-done.17
  63.8 2.0 %collective-permute-done.16 = bf16[224,128]{1,0:T(8,128)(2,1)S(1)} collective-permute-done((bf16[224,128]{1,0:T(8,128)(2,1)S(1)}, bf16[224,128]{1,0:T(8,128)(2,1)S(1)}, u32[]{:S(2)}, u32[]{:S(2)}) %collective-permute-start.16) | collective-permute-done | bytes 57376 | tf_op jit(solution)/shard_map/ppermute | solution.py:411
  65.8 0.4 collective-permute-done.15
  66.2 4.8 %collective-permute-start.21 = (bf16[224,128]{1,0:T(8,128)(2,1)S(1)}, bf16[224,128]{1,0:T(8,128)(2,1)S(1)}, u32[]{:S(2)}, u32[]{:S(2)}) collective-permute-start(bf16[224,128]{1,0:T(8,128)(2,1)S(1)} %add_convert_fusion), channel_id=1, source_target_pairs={{0,1},{1,0},{2,3},{3,2},{4,5},{5,4},{6,7},{7,6},{8,9},{9,8},{10,11... | collective-permute-start | bytes 172040 | tf_op jit(solution)/shard_map/ppermute | solution.py:461
  71.1 0.9 %collective-permute-done.21 = bf16[224,128]{1,0:T(8,128)(2,1)S(1)} collective-permute-done((bf16[224,128]{1,0:T(8,128)(2,1)S(1)}, bf16[224,128]{1,0:T(8,128)(2,1)S(1)}, u32[]{:S(2)}, u32[]{:S(2)}) %collective-permute-start.21) | collective-permute-done | bytes 57376 | tf_op jit(solution)/shard_map/ppermute | solution.py:461
  72.0 0.1 stack.13
  72.2 0.1 stack.14
  72.3 0.4 maximum_bitcast_fusion
  72.7 0.1 copy.15
  72.8 1.0 %fusion = f32[1,2,27,32,32]{4,3,2,1,0:T(8,128)} fusion(bf16[2,28,32,32]{3,2,1,0:T(8,128)(2,1)S(1)} %bitcast.53), kind=kLoop, calls=%fused_computation.3 | loop fusion | flops 55296 | bytes 331776 | tf_op jit(solution)/shard_map/broadcast_in_dim | solution.py:468
  (9 shorter events, 0.3 us)
Async XLA Ops:
  2.3 3.1 %collective-permute-start = (bf16[2,320,128]{2,1,0:T(8,128)(2,1)S(1)}, bf16[2,320,128]{2,1,0:T(8,128)(2,1)S(1)}, u32[]{:S(2)}, u32[]{:S(2)}) collective-permute-start(bf16[2,320,128]{2,1,0:T(8,128)(2,1)S(1)} %pad_maximum_fusion.1.own), channel_id=1, source_target_pairs={{0,1},{1,0},{2,3},{3,2},{4,5},{5,4},{6,7},{7,6},{8,9},{9,8},{10,11... | collective-permute-start | bytes 491528 | tf_op jit(solution)/shard_map/ppermute | solution.py:431
  5.4 10.4 %collective-permute-start.1 = (bf16[2,640,128]{2,1,0:T(8,128)(2,1)S(1)}, bf16[2,640,128]{2,1,0:T(8,128)(2,1)S(1)}, u32[]{:S(2)}, u32[]{:S(2)}) collective-permute-start(bf16[2,640,128]{2,1,0:T(8,128)(2,1)S(1)} %pad_maximum_fusion), channel_id=1, source_target_pairs={{0,2},{1,31},{2,4},{3,1},{4,6},{5,3},{6,8},{7,5},{8,10},{9,7},{10,... | collective-permute-start | bytes 983048 | tf_op jit(solution)/shard_map/ppermute | solution.py:438
  11.8 5.4 %collective-permute-start.5 = (bf16[2,224,128]{2,1,0:T(8,128)(2,1)S(1)}, bf16[2,224,128]{2,1,0:T(8,128)(2,1)S(1)}, u32[]{:S(2)}, u32[]{:S(2)}) collective-permute-start(bf16[2,224,128]{2,1,0:T(8,128)(2,1)S(1)} %reshape.43.pack0), channel_id=1, source_target_pairs={{0,96},{32,0},{64,32},{96,64},{1,97},{33,1},{65,33},{97,65},{2,98}... | collective-permute-start | bytes 344072 | tf_op jit(solution)/shard_map/ppermute | solution.py:411
  14.3 5.4 %collective-permute-start.4 = (bf16[2,224,128]{2,1,0:T(8,128)(2,1)S(1)}, bf16[2,224,128]{2,1,0:T(8,128)(2,1)S(1)}, u32[]{:S(2)}, u32[]{:S(2)}) collective-permute-start(bf16[2,224,128]{2,1,0:T(8,128)(2,1)S(1)} %reshape.43.pack0), channel_id=1, source_target_pairs={{0,64},{32,96},{64,0},{96,32},{1,65},{33,97},{65,1},{97,33},{2,66}... | collective-permute-start | bytes 344072 | tf_op jit(solution)/shard_map/ppermute | solution.py:411
  14.8 6.2 %collective-permute-start.3 = (bf16[2,224,128]{2,1,0:T(8,128)(2,1)S(1)}, bf16[2,224,128]{2,1,0:T(8,128)(2,1)S(1)}, u32[]{:S(2)}, u32[]{:S(2)}) collective-permute-start(bf16[2,224,128]{2,1,0:T(8,128)(2,1)S(1)} %reshape.43.pack0), channel_id=1, source_target_pairs={{0,32},{32,64},{64,96},{96,0},{1,33},{33,65},{65,97},{97,1},{2,34}... | collective-permute-start | bytes 344072 | tf_op jit(solution)/shard_map/ppermute | solution.py:411
  15.4 10.3 %collective-permute-start.2 = (bf16[640,128]{1,0:T(8,128)(2,1)S(1)}, bf16[640,128]{1,0:T(8,128)(2,1)S(1)}, u32[]{:S(2)}, u32[]{:S(2)}) collective-permute-start(bf16[640,128]{1,0:T(8,128)(2,1)S(1)} %slice_bitcast_fusion.1), channel_id=1, source_target_pairs={{0,4},{1,29},{2,6},{3,31},{4,8},{5,1},{6,10},{7,3},{8,12},{9,5},{1... | collective-permute-start | bytes 491528 | tf_op jit(solution)/shard_map/ppermute | solution.py:439
  15.8 11.4 %collective-permute-start.6 = (bf16[2,640,128]{2,1,0:T(8,128)(2,1)S(1)}, bf16[2,640,128]{2,1,0:T(8,128)(2,1)S(1)}, u32[]{:S(2)}, u32[]{:S(2)}) collective-permute-start(bf16[2,640,128]{2,1,0:T(8,128)(2,1)S(1)} %collective-permute-done.1.near), channel_id=1, source_target_pairs={{0,1},{1,0},{2,3},{3,2},{4,5},{5,4},{6,7},{7,6},{8,9},{9,8},{10,11... | collective-permute-start | bytes 983048 | tf_op jit(solution)/shard_map/ppermute | solution.py:441
  25.8 1.5 %collective-permute-start.7 = (bf16[640,128]{1,0:T(8,128)(2,1)S(1)}, bf16[640,128]{1,0:T(8,128)(2,1)S(1)}, u32[]{:S(2)}, u32[]{:S(2)}) collective-permute-start(bf16[640,128]{1,0:T(8,128)(2,1)S(1)} %collective-permute-done.2.far), channel_id=1, source_target_pairs={{0,1},{1,0},{2,3},{3,2},{4,5},{5,4},{6,7},{7,6},{8,9},{9,8},{10,11... | collective-permute-start | bytes 491528 | tf_op jit(solution)/shard_map/ppermute | solution.py:443
  44.1 1.6 %collective-permute-start.8 = (bf16[4,224,128]{2,1,0:T(8,128)(2,1)S(1)}, bf16[4,224,128]{2,1,0:T(8,128)(2,1)S(1)}, u32[]{:S(2)}, u32[]{:S(2)}) collective-permute-start(bf16[4,224,128]{2,1,0:T(8,128)(2,1)S(1)} %get-tuple-element.34), channel_id=1, source_target_pairs={{0,1},{1,0},{2,3},{3,2},{4,5},{5,4},{6,7},{7,6},{8,9},{9,8},{10,11... | collective-permute-start | bytes 688136 | tf_op jit(solution)/shard_map/ppermute | solution.py:449
  45.8 4.3 %collective-permute-start.9 = (bf16[224,128]{1,0:T(8,128)(2,1)S(1)}, bf16[224,128]{1,0:T(8,128)(2,1)S(1)}, u32[]{:S(2)}, u32[]{:S(2)}) collective-permute-start(bf16[224,128]{1,0:T(8,128)(2,1)S(1)} %get-tuple-element.47), channel_id=1, source_target_pairs={{0,32},{32,64},{64,96},{96,0},{1,33},{33,65},{65,97},{97,1},{2,34}... | collective-permute-start | bytes 172040 | tf_op jit(solution)/shard_map/ppermute | solution.py:411
  45.8 4.4 %collective-permute-start.11 = (bf16[224,128]{1,0:T(8,128)(2,1)S(1)}, bf16[224,128]{1,0:T(8,128)(2,1)S(1)}, u32[]{:S(2)}, u32[]{:S(2)}) collective-permute-start(bf16[224,128]{1,0:T(8,128)(2,1)S(1)} %get-tuple-element.48), channel_id=1, source_target_pairs={{0,96},{32,0},{64,32},{96,64},{1,97},{33,1},{65,33},{97,65},{2,98}... | collective-permute-start | bytes 172040 | tf_op jit(solution)/shard_map/ppermute | solution.py:411
  48.5 4.5 %collective-permute-start.10 = (bf16[224,128]{1,0:T(8,128)(2,1)S(1)}, bf16[224,128]{1,0:T(8,128)(2,1)S(1)}, u32[]{:S(2)}, u32[]{:S(2)}) collective-permute-start(bf16[224,128]{1,0:T(8,128)(2,1)S(1)} %get-tuple-element.49), channel_id=1, source_target_pairs={{0,64},{32,96},{64,0},{96,32},{1,65},{33,97},{65,1},{97,33},{2,66}... | collective-permute-start | bytes 172040 | tf_op jit(solution)/shard_map/ppermute | solution.py:411
  53.1 3.4 %collective-permute-start.14 = (bf16[224,128]{1,0:T(8,128)(2,1)S(1)}, bf16[224,128]{1,0:T(8,128)(2,1)S(1)}, u32[]{:S(2)}, u32[]{:S(2)}) collective-permute-start(bf16[224,128]{1,0:T(8,128)(2,1)S(1)} %add_convert_fusion.2), channel_id=1, source_target_pairs={{0,6},{1,7},{2,0},{3,1},{4,2},{5,3},{6,4},{7,5},{8,14},{9,15},{10,... | collective-permute-start | bytes 172040 | tf_op jit(solution)/shard_map/ppermute | solution.py:411
  53.2 4.6 %collective-permute-start.13 = (bf16[224,128]{1,0:T(8,128)(2,1)S(1)}, bf16[224,128]{1,0:T(8,128)(2,1)S(1)}, u32[]{:S(2)}, u32[]{:S(2)}) collective-permute-start(bf16[224,128]{1,0:T(8,128)(2,1)S(1)} %add_convert_fusion.2), channel_id=1, source_target_pairs={{0,4},{1,5},{2,6},{3,7},{4,0},{5,1},{6,2},{7,3},{8,12},{9,13},{10,... | collective-permute-start | bytes 172040 | tf_op jit(solution)/shard_map/ppermute | solution.py:411
  53.3 5.3 %collective-permute-start.12 = (bf16[224,128]{1,0:T(8,128)(2,1)S(1)}, bf16[224,128]{1,0:T(8,128)(2,1)S(1)}, u32[]{:S(2)}, u32[]{:S(2)}) collective-permute-start(bf16[224,128]{1,0:T(8,128)(2,1)S(1)} %add_convert_fusion.2), channel_id=1, source_target_pairs={{0,2},{1,3},{2,4},{3,5},{4,6},{5,7},{6,0},{7,1},{8,10},{9,11},{10,... | collective-permute-start | bytes 172040 | tf_op jit(solution)/shard_map/ppermute | solution.py:411
  54.6 6.7 %collective-permute-start.18 = (bf16[512,128]{1,0:T(8,128)(2,1)S(1)}, bf16[512,128]{1,0:T(8,128)(2,1)S(1)}, u32[]{:S(2)}, u32[]{:S(2)}) collective-permute-start(bf16[512,128]{1,0:T(8,128)(2,1)S(1)} %get-tuple-element.39), channel_id=1, source_target_pairs={{0,32},{32,64},{64,96},{96,0},{1,33},{33,65},{65,97},{97,1},{2,34}... | collective-permute-start | bytes 393224 | tf_op jit(solution)/shard_map/ppermute | solution.py:411
  54.6 7.3 %collective-permute-start.19 = (bf16[512,128]{1,0:T(8,128)(2,1)S(1)}, bf16[512,128]{1,0:T(8,128)(2,1)S(1)}, u32[]{:S(2)}, u32[]{:S(2)}) collective-permute-start(bf16[512,128]{1,0:T(8,128)(2,1)S(1)} %get-tuple-element.40), channel_id=1, source_target_pairs={{0,64},{32,96},{64,0},{96,32},{1,65},{33,97},{65,1},{97,33},{2,66}... | collective-permute-start | bytes 393224 | tf_op jit(solution)/shard_map/ppermute | solution.py:411
  56.5 5.4 %collective-permute-start.20 = (bf16[512,128]{1,0:T(8,128)(2,1)S(1)}, bf16[512,128]{1,0:T(8,128)(2,1)S(1)}, u32[]{:S(2)}, u32[]{:S(2)}) collective-permute-start(bf16[512,128]{1,0:T(8,128)(2,1)S(1)} %get-tuple-element.41), channel_id=1, source_target_pairs={{0,96},{32,0},{64,32},{96,64},{1,97},{33,1},{65,33},{97,65},{2,98}... | collective-permute-start | bytes 393224 | tf_op jit(solution)/shard_map/ppermute | solution.py:411
  58.6 5.2 %collective-permute-start.17 = (bf16[224,128]{1,0:T(8,128)(2,1)S(1)}, bf16[224,128]{1,0:T(8,128)(2,1)S(1)}, u32[]{:S(2)}, u32[]{:S(2)}) collective-permute-start(bf16[224,128]{1,0:T(8,128)(2,1)S(1)} %add_convert_fusion.1), channel_id=1, source_target_pairs={{0,24},{1,25},{2,26},{3,27},{4,28},{5,29},{6,30},{7,31},{8,0},{9,1... | collective-permute-start | bytes 172040 | tf_op jit(solution)/shard_map/ppermute | solution.py:411
  61.2 4.6 %collective-permute-start.16 = (bf16[224,128]{1,0:T(8,128)(2,1)S(1)}, bf16[224,128]{1,0:T(8,128)(2,1)S(1)}, u32[]{:S(2)}, u32[]{:S(2)}) collective-permute-start(bf16[224,128]{1,0:T(8,128)(2,1)S(1)} %add_convert_fusion.1), channel_id=1, source_target_pairs={{0,16},{1,17},{2,18},{3,19},{4,20},{5,21},{6,22},{7,23},{8,24},{9,... | collective-permute-start | bytes 172040 | tf_op jit(solution)/shard_map/ppermute | solution.py:411
  61.4 4.9 %collective-permute-start.15 = (bf16[224,128]{1,0:T(8,128)(2,1)S(1)}, bf16[224,128]{1,0:T(8,128)(2,1)S(1)}, u32[]{:S(2)}, u32[]{:S(2)}) collective-permute-start(bf16[224,128]{1,0:T(8,128)(2,1)S(1)} %add_convert_fusion.1), channel_id=1, source_target_pairs={{0,8},{1,9},{2,10},{3,11},{4,12},{5,13},{6,14},{7,15},{8,16},{9,17... | collective-permute-start | bytes 172040 | tf_op jit(solution)/shard_map/ppermute | solution.py:411
  66.2 5.7 %collective-permute-start.21 = (bf16[224,128]{1,0:T(8,128)(2,1)S(1)}, bf16[224,128]{1,0:T(8,128)(2,1)S(1)}, u32[]{:S(2)}, u32[]{:S(2)}) collective-permute-start(bf16[224,128]{1,0:T(8,128)(2,1)S(1)} %add_convert_fusion), channel_id=1, source_target_pairs={{0,1},{1,0},{2,3},{3,2},{4,5},{5,4},{6,7},{7,6},{8,9},{9,8},{10,11... | collective-permute-start | bytes 172040 | tf_op jit(solution)/shard_map/ppermute | solution.py:461

commit v7 on v6

--- a/solution.py
+++ b/solution.py
@@ -42,10 +42,13 @@
     return expand, collapse, [plane == z for z in range(4)]
 
 
-def build_kernel(pack0, pack1, pack2, pack3, w1, wb, wpack, lx, lxt):
+def build_kernel(pack0, half1, half2, half3, rest1, rest2, rest3, w1, wb, wpack, lx, lxt):
     seg = lax.axis_index("segment")
-    for k, pack in enumerate((pack0, pack1, pack2, pack3)):
-        wpack[lax.rem(seg - k + 4, 4)] = pack[...]
+    core = lax.rem(lax.axis_index("gy"), 2)
+    wpack[seg] = pack0[...]
+    for k, half, rest in ((1, half1, rest1), (2, half2, rest2), (3, half3, rest3)):
+        wpack[lax.rem(seg - k + 4, 4), core] = half[...]
+        wpack[lax.rem(seg - k + 4, 4), 1 - core] = rest[...]
     expand, _, on_plane = constants()
     nothing = jnp.zeros((32, LANES), BF16)
 
@@ -308,7 +311,7 @@
     return pl.pallas_call(
         build_kernel,
         out_shape=[jax.ShapeDtypeStruct(MATRICES, BF16)] * 2,
-        in_specs=[VMEM] * 4,
+        in_specs=[VMEM] * 7,
         out_specs=[VMEM] * 2,
         scratch_shapes=[
             pltpu.VMEM((4, 2, 224, LANES), BF16),
@@ -427,7 +430,9 @@
     packed = jnp.pad(weights[0], ((0, 0), (0, 1), (0, 0), (0, 0))).reshape(2, 7, 4, channels, channels)
     packed = jnp.transpose(packed, (0, 1, 3, 2, 4)).reshape(2, 7 * channels, 4 * channels)
 
-    others = [rotated(packed, "segment", 4, k, 1) for k in (1, 2, 3)]
+    share = lax.dynamic_index_in_dim(packed, lax.axis_index("gy") % 2, 0, keepdims=False)
+    others = [rotated(share, "segment", 4, k, 1) for k in (1, 2, 3)]
+    others += [lax.ppermute(other, "gy", swap) for other in others]
     oth = lax.ppermute(own, "gy", swap)
     oth, packed = lax.optimization_barrier((oth, packed))
     block = jnp.concatenate([own, oth], axis=1)
@@ -439,7 +444,6 @@
     far = lax.ppermute(block[0], "gy", outward(2))
     w1, wb = build_call(packed, *others)
     near_other = lax.ppermute(near, "gy", swap)
-    far, w1 = lax.optimization_barrier((far, w1))
     far_other = lax.ppermute(far, "gy", swap)
     outs = main_call(own, oth, near, far, near_other, far_other, w1, wb)
     fields = outs[:4]

time: 74 us -> 73.7 us (level)
    ppermute x1, waiting for transfers between devices: 1.38 us -> 0.01 us  [local(): far_other = lax.ppermute(far, 'gy', swap)]
    ppermute x0 -> x3, starting transfers between devices: none -> 0.99 us  [local(): others += [lax.ppermute(other, 'gy', swap) for other in others]]
    ppermute x1, starting transfers between devices: 1.33 us -> 0.42 us  [local(): near_other = lax.ppermute(near, 'gy', swap)]
    ppermute x15, waiting for transfers between devices: 12.2 us -> 13.1 us  [rotated(): return lax.ppermute(value, axis, [(i, target(i)) for i in range(count)])]
  transfers between devices with their start and end apart: 22 -> 25, of which waited for: 16 -> 15; matrix products, arithmetic and copies ran while one was open for 2% -> 2% of each run, Pallas kernels for 9% -> 9%
where the time goes in v7:
time: 73.7 us; the launch traced here: 73.5 us
  starting transfers between devices  28.4 us (39%)
  Pallas kernels  23.5 us (32%)
  waiting for transfers between devices  15.5 us (21%)
  local copies, waits for them, and re-layouts  3.54 us (5%)
  other arithmetic  1.63 us (2%)
  between operations  0.89 us (1%)
    pallas_call x1, Pallas kernels, main_call(): pl.pallas_call(main_kernel, out_shape=[jax.ShapeDtypeStruct((512, LANES),...  14.2 us
    ppermute x15, starting transfers between devices, rotated(): return lax.ppermute(value, axis, [(i, target(i)) for i in range(count)])  13.4 us
    ppermute x15, waiting for transfers between devices, rotated(): return lax.ppermute(value, axis, [(i, target(i)) for i in range(count)])  13.1 us
    ppermute x1, starting transfers between devices, local(): near = lax.ppermute(block, 'gy', outward(1))  6.36 us
    ppermute x1, starting transfers between devices, local(): other = lax.ppermute(mine, 'gy', swap)  4.89 us
    pallas_call x1, Pallas kernels, build_call(): pl.pallas_call(build_kernel, out_shape=[jax.ShapeDtypeStruct(MATRICES, BF...  4.83 us
    pallas_call x1, Pallas kernels, grads_call(): pl.pallas_call(grads_kernel, out_shape=[jax.ShapeDtypeStruct((224, LANES)...  2.64 us
    pallas_call x1, Pallas kernels, layout_call(): pl.pallas_call(layout_kernel, out_shape=[jax.ShapeDtypeStruct((2, 32, 4,...  1.85 us
  transfers between devices with their start and end apart: 25, of which 15 were waited for; matrix products, arithmetic and copies ran while one was open for 2% of the time, Pallas kernels for 9%

profile of v7, /device:TPU:1, one launch (start us, length us, event | category | flops | bytes accessed | tf_op | source)
XLA Modules:
  0.0 73.5 jit_solution(4324868479340823992)
XLA Ops:
  0.7 1.1 %constant_dynamic-slice_fusion.1 = (bf16[1,32,4,4,128]{4,3,2,1,0:T(4,128)(2,1)S(1)}, bf16[1,32,4,4,128]{4,3,2,1,0:T(4,128)(2,1)S(1)}) fusion(bf16[2,32,4,4,128]{4,3,2,1,0:T(4,128)(2,1)} %param.4, s32[]{:T(128)S(6)} %select_n.43, bf16[2,32,4,4,128]{4,3,2,1,0:T(4,128)(2,1)} %param.3), kind=kLoop, calls=%fused_computation.26 | loop fusion | bytes 524292 | tf_op jit(solution)/shard_map/jit(dynamic_index_in_dim)/dynamic_slice | solution.py:425
  1.8 0.1 constant_dynamic-slice_fusion
  1.9 0.1 copy.13
  2.0 0.1 constant_dynamic-slice_fusion.2
  2.2 0.1 copy.10
  2.3 1.5 %collective-permute-start = (bf16[2,320,128]{2,1,0:T(8,128)(2,1)S(1)}, bf16[2,320,128]{2,1,0:T(8,128)(2,1)S(1)}, u32[]{:S(2)}, u32[]{:S(2)}) collective-permute-start(bf16[2,320,128]{2,1,0:T(8,128)(2,1)S(1)} %pad_maximum_fusion.1.own), channel_id=1, source_target_pairs={{0,1},{1,0},{2,3},{3,2},{4,5},{5,4},{6,7},{7,6},{8,9},{9,8},{10,11... | collective-permute-start | bytes 491528 | tf_op jit(solution)/shard_map/ppermute | solution.py:436
  3.8 1.1 %pad.4 = bf16[2,28,32,32]{3,2,1,0:T(8,128)(2,1)S(1)} pad(bf16[2,27,32,32]{3,2,1,0:T(8,128)(2,1)} %bitcast.62, bf16[]{:T(256)} %constant.54.clone.1), padding=0_0x0_1x0_0x0_0 | pad | bytes 225282 | tf_op jit(solution)/shard_map/jit(_pad)/pad | solution.py:430
  4.9 0.2 copy.21
  5.1 0.2 reshape.43.pack0
  5.4 0.0 collective-permute-done.oth
  5.5 6.4 %collective-permute-start.1 = (bf16[2,640,128]{2,1,0:T(8,128)(2,1)S(1)}, bf16[2,640,128]{2,1,0:T(8,128)(2,1)S(1)}, u32[]{:S(2)}, u32[]{:S(2)}) collective-permute-start(bf16[2,640,128]{2,1,0:T(8,128)(2,1)S(1)} %pad_maximum_fusion), channel_id=1, source_target_pairs={{0,2},{1,31},{2,4},{3,1},{4,6},{5,3},{6,8},{7,5},{8,10},{9,7},{10,... | collective-permute-start | bytes 983048 | tf_op jit(solution)/shard_map/ppermute | solution.py:443
  11.8 0.1 collective-permute-start.2
  11.9 2.5 %collective-permute-start.7 = (bf16[224,128]{1,0:T(8,128)(2,1)S(1)}, bf16[224,128]{1,0:T(8,128)(2,1)S(1)}, u32[]{:S(2)}, u32[]{:S(2)}) collective-permute-start(bf16[224,128]{1,0:T(8,128)(2,1)S(1)} %dynamic-slice_bitcast_fusion), channel_id=1, source_target_pairs={{0,96},{32,0},{64,32},{96,64},{1,97},{33,1},{65,33},{97,65},{2,98}... | collective-permute-start | bytes 172040 | tf_op jit(solution)/shard_map/ppermute | solution.py:414
  14.5 0.5 collective-permute-start.6
  15.0 0.6 collective-permute-start.5
  15.6 0.3 collective-permute-done.7.half3
  15.9 0.1 collective-permute-start.10
  16.0 3.9 %collective-permute-done.6.half2 = bf16[224,128]{1,0:T(8,128)(2,1)S(1)} collective-permute-done((bf16[224,128]{1,0:T(8,128)(2,1)S(1)}, bf16[224,128]{1,0:T(8,128)(2,1)S(1)}, u32[]{:S(2)}, u32[]{:S(2)}) %collective-permute-start.6) | collective-permute-done | bytes 57376 | tf_op jit(solution)/shard_map/ppermute | solution.py:414
  19.9 0.5 collective-permute-start.9
  20.3 0.8 %collective-permute-done.5.half1 = bf16[224,128]{1,0:T(8,128)(2,1)S(1)} collective-permute-done((bf16[224,128]{1,0:T(8,128)(2,1)S(1)}, bf16[224,128]{1,0:T(8,128)(2,1)S(1)}, u32[]{:S(2)}, u32[]{:S(2)}) %collective-permute-start.5) | collective-permute-done | bytes 57376 | tf_op jit(solution)/shard_map/ppermute | solution.py:414
  21.1 0.4 collective-permute-start.8
  21.5 0.0 collective-permute-done.2.far
  21.5 0.1 collective-permute-start.4
  21.6 0.0 collective-permute-done.1.near
  21.6 0.4 collective-permute-start.3
  22.0 0.0 collective-permute-done.10.rest3
  22.0 0.0 collective-permute-done.9.rest2
  22.0 0.4 collective-permute-done.8.rest1
  22.4 4.8 %banded.1 = (bf16[8,512,768]{2,1,0:T(8,128)(2,1)S(1)}, bf16[8,512,768]{2,1,0:T(8,128)(2,1)S(1)}) custom-call(bf16[2,224,128]{2,1,0:T(8,128)(2,1)S(1)} %reshape.43.pack0, bf16[224,128]{1,0:T(8,128)(2,1)S(1)} %collective-permute-done.5.half1, bf16[224,128]{1,0:T(8,128)(2,1)S(1)} %collective-permute-done.6.half2, ...), custom_call_target="tpu_custom_call" | custom-call | flops 5000000000 | bytes 10000000 | tf_op jit(solution)/shard_map/banded/pallas_call | solution.py:311
  27.3 0.0 collective-permute-done.3.near_other
  27.3 14.2 %sections.1 = (bf16[512,128]{1,0:T(8,128)(2,1)S(1)}, bf16[512,128]{1,0:T(8,128)(2,1)S(1)}, bf16[512,128]{1,0:T(8,128)(2,1)S(1)}, bf16[512,128]{1,0:T(8,128)(2,1)...) custom-call(bf16[2,320,128]{2,1,0:T(8,128)(2,1)S(1)} %pad_maximum_fusion.1.own, ...), custom_call_target="tpu_custom_call" | custom-call | flops 20000000000 | bytes 10000000 | tf_op jit(solution)/shard_map/sections/pallas_call | solution.py:329
  41.5 2.6 %kernel_grads.1 = (bf16[224,128]{1,0:T(8,128)(2,1)S(1)}, bf16[224,128]{1,0:T(8,128)(2,1)S(1)}, bf16[224,128]{1,0:T(8,128)(2,1)S(1)}, bf16[224,128]{1,0:T(8,128)(2,1)S(1)}, bf16[4,224,128]{2,1,0:T(8,128)(2,1)S(1)}) custom-call(bf16[8,480,128]{2,1,0:T(8,128)(2,1)S(1)} %get-tuple-element.27.windows, bf16[8,320,128]{2,1,0:T(8,128)(2,1)S(1)} %get-tuple-element.28.deltas), custom_call_target="tpu_custom_call" | custom-call | flops 6000000000 | bytes 4000000 | tf_op jit(solution)/shard_map/kernel_grads/pallas_call | solution.py:359
  44.1 0.7 collective-permute-start.11
  44.8 1.1 %collective-permute-done.11 = bf16[4,224,128]{2,1,0:T(8,128)(2,1)S(1)} collective-permute-done((bf16[4,224,128]{2,1,0:T(8,128)(2,1)S(1)}, bf16[4,224,128]{2,1,0:T(8,128)(2,1)S(1)}, u32[]{:S(2)}, u32[]{:S(2)}) %collective-permute-start.11) | collective-permute-done | bytes 229408 | tf_op jit(solution)/shard_map/ppermute | solution.py:453
  45.9 0.1 fusion.3
  46.0 0.1 collective-permute-start.12
  46.1 2.7 %collective-permute-start.14 = (bf16[224,128]{1,0:T(8,128)(2,1)S(1)}, bf16[224,128]{1,0:T(8,128)(2,1)S(1)}, u32[]{:S(2)}, u32[]{:S(2)}) collective-permute-start(bf16[224,128]{1,0:T(8,128)(2,1)S(1)} %get-tuple-element.44), channel_id=1, source_target_pairs={{0,96},{32,0},{64,32},{96,64},{1,97},{33,1},{65,33},{97,65},{2,98}... | collective-permute-start | bytes 172040 | tf_op jit(solution)/shard_map/ppermute | solution.py:414
  48.8 0.0 collective-permute-start.13
  48.8 1.6 %collective-permute-done.12 = bf16[224,128]{1,0:T(8,128)(2,1)S(1)} collective-permute-done((bf16[224,128]{1,0:T(8,128)(2,1)S(1)}, bf16[224,128]{1,0:T(8,128)(2,1)S(1)}, u32[]{:S(2)}, u32[]{:S(2)}) %collective-permute-start.12) | collective-permute-done | bytes 57376 | tf_op jit(solution)/shard_map/ppermute | solution.py:414
  50.3 0.2 collective-permute-done.14
  50.5 2.8 %collective-permute-done.13 = bf16[224,128]{1,0:T(8,128)(2,1)S(1)} collective-permute-done((bf16[224,128]{1,0:T(8,128)(2,1)S(1)}, bf16[224,128]{1,0:T(8,128)(2,1)S(1)}, u32[]{:S(2)}, u32[]{:S(2)}) %collective-permute-start.13) | collective-permute-done | bytes 57376 | tf_op jit(solution)/shard_map/ppermute | solution.py:414
  53.3 0.1 collective-permute-start.17
  53.4 0.7 collective-permute-start.16
  54.1 0.8 %collective-permute-start.15 = (bf16[224,128]{1,0:T(8,128)(2,1)S(1)}, bf16[224,128]{1,0:T(8,128)(2,1)S(1)}, u32[]{:S(2)}, u32[]{:S(2)}) collective-permute-start(bf16[224,128]{1,0:T(8,128)(2,1)S(1)} %add_convert_fusion.2), channel_id=1, source_target_pairs={{0,2},{1,3},{2,4},{3,5},{4,6},{5,7},{6,0},{7,1},{8,10},{9,11},{10,... | collective-permute-start | bytes 172040 | tf_op jit(solution)/shard_map/ppermute | solution.py:414
  54.9 2.0 %collective-permute-start.22 = (bf16[512,128]{1,0:T(8,128)(2,1)S(1)}, bf16[512,128]{1,0:T(8,128)(2,1)S(1)}, u32[]{:S(2)}, u32[]{:S(2)}) collective-permute-start(bf16[512,128]{1,0:T(8,128)(2,1)S(1)} %get-tuple-element.36), channel_id=1, source_target_pairs={{0,64},{32,96},{64,0},{96,32},{1,65},{33,97},{65,1},{97,33},{2,66}... | collective-permute-start | bytes 393224 | tf_op jit(solution)/shard_map/ppermute | solution.py:414
  56.9 0.6 collective-permute-start.23
  57.6 0.4 collective-permute-done.16
  58.0 0.8 %collective-permute-done.15 = bf16[224,128]{1,0:T(8,128)(2,1)S(1)} collective-permute-done((bf16[224,128]{1,0:T(8,128)(2,1)S(1)}, bf16[224,128]{1,0:T(8,128)(2,1)S(1)}, u32[]{:S(2)}, u32[]{:S(2)}) %collective-permute-start.15) | collective-permute-done | bytes 57376 | tf_op jit(solution)/shard_map/ppermute | solution.py:414
  58.9 1.7 %collective-permute-start.20 = (bf16[224,128]{1,0:T(8,128)(2,1)S(1)}, bf16[224,128]{1,0:T(8,128)(2,1)S(1)}, u32[]{:S(2)}, u32[]{:S(2)}) collective-permute-start(bf16[224,128]{1,0:T(8,128)(2,1)S(1)} %add_convert_fusion.1), channel_id=1, source_target_pairs={{0,24},{1,25},{2,26},{3,27},{4,28},{5,29},{6,30},{7,31},{8,0},{9,1... | collective-permute-start | bytes 172040 | tf_op jit(solution)/shard_map/ppermute | solution.py:414
  60.5 0.8 %collective-permute-start.19 = (bf16[224,128]{1,0:T(8,128)(2,1)S(1)}, bf16[224,128]{1,0:T(8,128)(2,1)S(1)}, u32[]{:S(2)}, u32[]{:S(2)}) collective-permute-start(bf16[224,128]{1,0:T(8,128)(2,1)S(1)} %add_convert_fusion.1), channel_id=1, source_target_pairs={{0,16},{1,17},{2,18},{3,19},{4,20},{5,21},{6,22},{7,23},{8,24},{9,... | collective-permute-start | bytes 172040 | tf_op jit(solution)/shard_map/ppermute | solution.py:414
  61.3 0.3 collective-permute-done.21.in1
  61.6 0.3 collective-permute-start.18
  61.9 0.0 collective-permute-done.22.in2
  61.9 0.3 collective-permute-done.23.in3
  62.3 1.8 %layout.1 = (bf16[2,32,4,4,128]{4,3,2,1,0:T(4,128)(2,1)}, f32[2,32,4,4,128]{4,3,2,1,0:T(4,128)}) custom-call(bf16[512,128]{1,0:T(8,128)(2,1)S(1)} %get-tuple-element.34.in0, bf16[512,128]{1,0:T(8,128)(2,1)S(1)} %collective-permute-done.21.in1, bf16[512,128]{1,0:T(8,128)(2,1)S(1)} %collective-permute-done.22.in2, bf16[512,128]{1,0:T(8,128)(2,1)S(1)} %collective-permute-done.23.in3), custom_call_target="tpu_custom_call" | custom-call | flops 4000000000 | bytes 4000000 | tf_op jit(solution)/shard_map/layout/pallas_call | solution.py:392
  64.1 0.9 %collective-permute-done.19 = bf16[224,128]{1,0:T(8,128)(2,1)S(1)} collective-permute-done((bf16[224,128]{1,0:T(8,128)(2,1)S(1)}, bf16[224,128]{1,0:T(8,128)(2,1)S(1)}, u32[]{:S(2)}, u32[]{:S(2)}) %collective-permute-start.19) | collective-permute-done | bytes 57376 | tf_op jit(solution)/shard_map/ppermute | solution.py:414
  65.1 0.8 %collective-permute-done.18 = bf16[224,128]{1,0:T(8,128)(2,1)S(1)} collective-permute-done((bf16[224,128]{1,0:T(8,128)(2,1)S(1)}, bf16[224,128]{1,0:T(8,128)(2,1)S(1)}, u32[]{:S(2)}, u32[]{:S(2)}) %collective-permute-start.18) | collective-permute-done | bytes 57376 | tf_op jit(solution)/shard_map/ppermute | solution.py:414
  65.9 4.9 %collective-permute-start.24 = (bf16[224,128]{1,0:T(8,128)(2,1)S(1)}, bf16[224,128]{1,0:T(8,128)(2,1)S(1)}, u32[]{:S(2)}, u32[]{:S(2)}) collective-permute-start(bf16[224,128]{1,0:T(8,128)(2,1)S(1)} %add_convert_fusion), channel_id=1, source_target_pairs={{0,1},{1,0},{2,3},{3,2},{4,5},{5,4},{6,7},{7,6},{8,9},{9,8},{10,11... | collective-permute-start | bytes 172040 | tf_op jit(solution)/shard_map/ppermute | solution.py:465
  70.8 0.9 %collective-permute-done.24 = bf16[224,128]{1,0:T(8,128)(2,1)S(1)} collective-permute-done((bf16[224,128]{1,0:T(8,128)(2,1)S(1)}, bf16[224,128]{1,0:T(8,128)(2,1)S(1)}, u32[]{:S(2)}, u32[]{:S(2)}) %collective-permute-start.24) | collective-permute-done | bytes 57376 | tf_op jit(solution)/shard_map/ppermute | solution.py:465
  71.7 0.1 stack.13
  71.9 0.1 stack.14
  72.0 0.4 maximum_bitcast_fusion
  72.4 0.1 copy.15
  72.5 1.0 %fusion = f32[1,2,27,32,32]{4,3,2,1,0:T(8,128)} fusion(bf16[2,28,32,32]{3,2,1,0:T(8,128)(2,1)S(1)} %bitcast.55), kind=kLoop, calls=%fused_computation.3 | loop fusion | flops 55296 | bytes 331776 | tf_op jit(solution)/shard_map/broadcast_in_dim | solution.py:472
  (14 shorter events, 0.3 us)
Async XLA Ops:
  2.3 3.1 %collective-permute-start = (bf16[2,320,128]{2,1,0:T(8,128)(2,1)S(1)}, bf16[2,320,128]{2,1,0:T(8,128)(2,1)S(1)}, u32[]{:S(2)}, u32[]{:S(2)}) collective-permute-start(bf16[2,320,128]{2,1,0:T(8,128)(2,1)S(1)} %pad_maximum_fusion.1.own), channel_id=1, source_target_pairs={{0,1},{1,0},{2,3},{3,2},{4,5},{5,4},{6,7},{7,6},{8,9},{9,8},{10,11... | collective-permute-start | bytes 491528 | tf_op jit(solution)/shard_map/ppermute | solution.py:436
  5.5 16.2 %collective-permute-start.1 = (bf16[2,640,128]{2,1,0:T(8,128)(2,1)S(1)}, bf16[2,640,128]{2,1,0:T(8,128)(2,1)S(1)}, u32[]{:S(2)}, u32[]{:S(2)}) collective-permute-start(bf16[2,640,128]{2,1,0:T(8,128)(2,1)S(1)} %pad_maximum_fusion), channel_id=1, source_target_pairs={{0,2},{1,31},{2,4},{3,1},{4,6},{5,3},{6,8},{7,5},{8,10},{9,7},{10,... | collective-permute-start | bytes 983048 | tf_op jit(solution)/shard_map/ppermute | solution.py:443
  11.8 9.7 %collective-permute-start.2 = (bf16[640,128]{1,0:T(8,128)(2,1)S(1)}, bf16[640,128]{1,0:T(8,128)(2,1)S(1)}, u32[]{:S(2)}, u32[]{:S(2)}) collective-permute-start(bf16[640,128]{1,0:T(8,128)(2,1)S(1)} %slice_bitcast_fusion.1), channel_id=1, source_target_pairs={{0,4},{1,29},{2,6},{3,31},{4,8},{5,1},{6,10},{7,3},{8,12},{9,5},{1... | collective-permute-start | bytes 491528 | tf_op jit(solution)/shard_map/ppermute | solution.py:444
  11.9 4.0 %collective-permute-start.7 = (bf16[224,128]{1,0:T(8,128)(2,1)S(1)}, bf16[224,128]{1,0:T(8,128)(2,1)S(1)}, u32[]{:S(2)}, u32[]{:S(2)}) collective-permute-start(bf16[224,128]{1,0:T(8,128)(2,1)S(1)} %dynamic-slice_bitcast_fusion), channel_id=1, source_target_pairs={{0,96},{32,0},{64,32},{96,64},{1,97},{33,1},{65,33},{97,65},{2,98}... | collective-permute-start | bytes 172040 | tf_op jit(solution)/shard_map/ppermute | solution.py:414
  14.5 5.4 %collective-permute-start.6 = (bf16[224,128]{1,0:T(8,128)(2,1)S(1)}, bf16[224,128]{1,0:T(8,128)(2,1)S(1)}, u32[]{:S(2)}, u32[]{:S(2)}) collective-permute-start(bf16[224,128]{1,0:T(8,128)(2,1)S(1)} %dynamic-slice_bitcast_fusion), channel_id=1, source_target_pairs={{0,64},{32,96},{64,0},{96,32},{1,65},{33,97},{65,1},{97,33},{2,66}... | collective-permute-start | bytes 172040 | tf_op jit(solution)/shard_map/ppermute | solution.py:414
  15.0 6.1 %collective-permute-start.5 = (bf16[224,128]{1,0:T(8,128)(2,1)S(1)}, bf16[224,128]{1,0:T(8,128)(2,1)S(1)}, u32[]{:S(2)}, u32[]{:S(2)}) collective-permute-start(bf16[224,128]{1,0:T(8,128)(2,1)S(1)} %dynamic-slice_bitcast_fusion), channel_id=1, source_target_pairs={{0,32},{32,64},{64,96},{96,0},{1,33},{33,65},{65,97},{97,1},{2,34}... | collective-permute-start | bytes 172040 | tf_op jit(solution)/shard_map/ppermute | solution.py:414
  15.9 6.1 %collective-permute-start.10 = (bf16[224,128]{1,0:T(8,128)(2,1)S(1)}, bf16[224,128]{1,0:T(8,128)(2,1)S(1)}, u32[]{:S(2)}, u32[]{:S(2)}) collective-permute-start(bf16[224,128]{1,0:T(8,128)(2,1)S(1)} %collective-permute-done.7.half3), channel_id=1, source_target_pairs={{0,1},{1,0},{2,3},{3,2},{4,5},{5,4},{6,7},{7,6},{8,9},{9,8},{10,11... | collective-permute-start | bytes 172040 | tf_op jit(solution)/shard_map/ppermute | solution.py:435
  19.9 2.2 %collective-permute-start.9 = (bf16[224,128]{1,0:T(8,128)(2,1)S(1)}, bf16[224,128]{1,0:T(8,128)(2,1)S(1)}, u32[]{:S(2)}, u32[]{:S(2)}) collective-permute-start(bf16[224,128]{1,0:T(8,128)(2,1)S(1)} %collective-permute-done.6.half2), channel_id=1, source_target_pairs={{0,1},{1,0},{2,3},{3,2},{4,5},{5,4},{6,7},{7,6},{8,9},{9,8},{10,11... | collective-permute-start | bytes 172040 | tf_op jit(solution)/shard_map/ppermute | solution.py:435
  21.1 1.3 %collective-permute-start.8 = (bf16[224,128]{1,0:T(8,128)(2,1)S(1)}, bf16[224,128]{1,0:T(8,128)(2,1)S(1)}, u32[]{:S(2)}, u32[]{:S(2)}) collective-permute-start(bf16[224,128]{1,0:T(8,128)(2,1)S(1)} %collective-permute-done.5.half1), channel_id=1, source_target_pairs={{0,1},{1,0},{2,3},{3,2},{4,5},{5,4},{6,7},{7,6},{8,9},{9,8},{10,11... | collective-permute-start | bytes 172040 | tf_op jit(solution)/shard_map/ppermute | solution.py:435
  21.5 5.7 %collective-permute-start.4 = (bf16[640,128]{1,0:T(8,128)(2,1)S(1)}, bf16[640,128]{1,0:T(8,128)(2,1)S(1)}, u32[]{:S(2)}, u32[]{:S(2)}) collective-permute-start(bf16[640,128]{1,0:T(8,128)(2,1)S(1)} %collective-permute-done.2.far), channel_id=1, source_target_pairs={{0,1},{1,0},{2,3},{3,2},{4,5},{5,4},{6,7},{7,6},{8,9},{9,8},{10,11... | collective-permute-start | bytes 491528 | tf_op jit(solution)/shard_map/ppermute | solution.py:447
  21.6 5.6 %collective-permute-start.3 = (bf16[2,640,128]{2,1,0:T(8,128)(2,1)S(1)}, bf16[2,640,128]{2,1,0:T(8,128)(2,1)S(1)}, u32[]{:S(2)}, u32[]{:S(2)}) collective-permute-start(bf16[2,640,128]{2,1,0:T(8,128)(2,1)S(1)} %collective-permute-done.1.near), channel_id=1, source_target_pairs={{0,1},{1,0},{2,3},{3,2},{4,5},{5,4},{6,7},{7,6},{8,9},{9,8},{10,11... | collective-permute-start | bytes 983048 | tf_op jit(solution)/shard_map/ppermute | solution.py:446
  44.1 1.9 %collective-permute-start.11 = (bf16[4,224,128]{2,1,0:T(8,128)(2,1)S(1)}, bf16[4,224,128]{2,1,0:T(8,128)(2,1)S(1)}, u32[]{:S(2)}, u32[]{:S(2)}) collective-permute-start(bf16[4,224,128]{2,1,0:T(8,128)(2,1)S(1)} %get-tuple-element.30), channel_id=1, source_target_pairs={{0,1},{1,0},{2,3},{3,2},{4,5},{5,4},{6,7},{7,6},{8,9},{9,8},{10,11... | collective-permute-start | bytes 688136 | tf_op jit(solution)/shard_map/ppermute | solution.py:453
  46.0 4.3 %collective-permute-start.12 = (bf16[224,128]{1,0:T(8,128)(2,1)S(1)}, bf16[224,128]{1,0:T(8,128)(2,1)S(1)}, u32[]{:S(2)}, u32[]{:S(2)}) collective-permute-start(bf16[224,128]{1,0:T(8,128)(2,1)S(1)} %get-tuple-element.43), channel_id=1, source_target_pairs={{0,32},{32,64},{64,96},{96,0},{1,33},{33,65},{65,97},{97,1},{2,34}... | collective-permute-start | bytes 172040 | tf_op jit(solution)/shard_map/ppermute | solution.py:414
  46.1 4.4 %collective-permute-start.14 = (bf16[224,128]{1,0:T(8,128)(2,1)S(1)}, bf16[224,128]{1,0:T(8,128)(2,1)S(1)}, u32[]{:S(2)}, u32[]{:S(2)}) collective-permute-start(bf16[224,128]{1,0:T(8,128)(2,1)S(1)} %get-tuple-element.44), channel_id=1, source_target_pairs={{0,96},{32,0},{64,32},{96,64},{1,97},{33,1},{65,33},{97,65},{2,98}... | collective-permute-start | bytes 172040 | tf_op jit(solution)/shard_map/ppermute | solution.py:414
  48.8 4.5 %collective-permute-start.13 = (bf16[224,128]{1,0:T(8,128)(2,1)S(1)}, bf16[224,128]{1,0:T(8,128)(2,1)S(1)}, u32[]{:S(2)}, u32[]{:S(2)}) collective-permute-start(bf16[224,128]{1,0:T(8,128)(2,1)S(1)} %get-tuple-element.45), channel_id=1, source_target_pairs={{0,64},{32,96},{64,0},{96,32},{1,65},{33,97},{65,1},{97,33},{2,66}... | collective-permute-start | bytes 172040 | tf_op jit(solution)/shard_map/ppermute | solution.py:414
  53.3 3.6 %collective-permute-start.17 = (bf16[224,128]{1,0:T(8,128)(2,1)S(1)}, bf16[224,128]{1,0:T(8,128)(2,1)S(1)}, u32[]{:S(2)}, u32[]{:S(2)}) collective-permute-start(bf16[224,128]{1,0:T(8,128)(2,1)S(1)} %add_convert_fusion.2), channel_id=1, source_target_pairs={{0,6},{1,7},{2,0},{3,1},{4,2},{5,3},{6,4},{7,5},{8,14},{9,15},{10,... | collective-permute-start | bytes 172040 | tf_op jit(solution)/shard_map/ppermute | solution.py:414
  53.4 4.6 %collective-permute-start.16 = (bf16[224,128]{1,0:T(8,128)(2,1)S(1)}, bf16[224,128]{1,0:T(8,128)(2,1)S(1)}, u32[]{:S(2)}, u32[]{:S(2)}) collective-permute-start(bf16[224,128]{1,0:T(8,128)(2,1)S(1)} %add_convert_fusion.2), channel_id=1, source_target_pairs={{0,4},{1,5},{2,6},{3,7},{4,0},{5,1},{6,2},{7,3},{8,12},{9,13},{10,... | collective-permute-start | bytes 172040 | tf_op jit(solution)/shard_map/ppermute | solution.py:414
  54.1 4.7 %collective-permute-start.15 = (bf16[224,128]{1,0:T(8,128)(2,1)S(1)}, bf16[224,128]{1,0:T(8,128)(2,1)S(1)}, u32[]{:S(2)}, u32[]{:S(2)}) collective-permute-start(bf16[224,128]{1,0:T(8,128)(2,1)S(1)} %add_convert_fusion.2), channel_id=1, source_target_pairs={{0,2},{1,3},{2,4},{3,5},{4,6},{5,7},{6,0},{7,1},{8,10},{9,11},{10,... | collective-permute-start | bytes 172040 | tf_op jit(solution)/shard_map/ppermute | solution.py:414
  54.9 6.7 %collective-permute-start.21 = (bf16[512,128]{1,0:T(8,128)(2,1)S(1)}, bf16[512,128]{1,0:T(8,128)(2,1)S(1)}, u32[]{:S(2)}, u32[]{:S(2)}) collective-permute-start(bf16[512,128]{1,0:T(8,128)(2,1)S(1)} %get-tuple-element.35), channel_id=1, source_target_pairs={{0,32},{32,64},{64,96},{96,0},{1,33},{33,65},{65,97},{97,1},{2,34}... | collective-permute-start | bytes 393224 | tf_op jit(solution)/shard_map/ppermute | solution.py:414
  54.9 7.0 %collective-permute-start.22 = (bf16[512,128]{1,0:T(8,128)(2,1)S(1)}, bf16[512,128]{1,0:T(8,128)(2,1)S(1)}, u32[]{:S(2)}, u32[]{:S(2)}) collective-permute-start(bf16[512,128]{1,0:T(8,128)(2,1)S(1)} %get-tuple-element.36), channel_id=1, source_target_pairs={{0,64},{32,96},{64,0},{96,32},{1,65},{33,97},{65,1},{97,33},{2,66}... | collective-permute-start | bytes 393224 | tf_op jit(solution)/shard_map/ppermute | solution.py:414
  56.9 5.3 %collective-permute-start.23 = (bf16[512,128]{1,0:T(8,128)(2,1)S(1)}, bf16[512,128]{1,0:T(8,128)(2,1)S(1)}, u32[]{:S(2)}, u32[]{:S(2)}) collective-permute-start(bf16[512,128]{1,0:T(8,128)(2,1)S(1)} %get-tuple-element.37), channel_id=1, source_target_pairs={{0,96},{32,0},{64,32},{96,64},{1,97},{33,1},{65,33},{97,65},{2,98}... | collective-permute-start | bytes 393224 | tf_op jit(solution)/shard_map/ppermute | solution.py:414
  58.9 5.3 %collective-permute-start.20 = (bf16[224,128]{1,0:T(8,128)(2,1)S(1)}, bf16[224,128]{1,0:T(8,128)(2,1)S(1)}, u32[]{:S(2)}, u32[]{:S(2)}) collective-permute-start(bf16[224,128]{1,0:T(8,128)(2,1)S(1)} %add_convert_fusion.1), channel_id=1, source_target_pairs={{0,24},{1,25},{2,26},{3,27},{4,28},{5,29},{6,30},{7,31},{8,0},{9,1... | collective-permute-start | bytes 172040 | tf_op jit(solution)/shard_map/ppermute | solution.py:414
  60.5 4.5 %collective-permute-start.19 = (bf16[224,128]{1,0:T(8,128)(2,1)S(1)}, bf16[224,128]{1,0:T(8,128)(2,1)S(1)}, u32[]{:S(2)}, u32[]{:S(2)}) collective-permute-start(bf16[224,128]{1,0:T(8,128)(2,1)S(1)} %add_convert_fusion.1), channel_id=1, source_target_pairs={{0,16},{1,17},{2,18},{3,19},{4,20},{5,21},{6,22},{7,23},{8,24},{9,... | collective-permute-start | bytes 172040 | tf_op jit(solution)/shard_map/ppermute | solution.py:414
  61.6 4.2 %collective-permute-start.18 = (bf16[224,128]{1,0:T(8,128)(2,1)S(1)}, bf16[224,128]{1,0:T(8,128)(2,1)S(1)}, u32[]{:S(2)}, u32[]{:S(2)}) collective-permute-start(bf16[224,128]{1,0:T(8,128)(2,1)S(1)} %add_convert_fusion.1), channel_id=1, source_target_pairs={{0,8},{1,9},{2,10},{3,11},{4,12},{5,13},{6,14},{7,15},{8,16},{9,17... | collective-permute-start | bytes 172040 | tf_op jit(solution)/shard_map/ppermute | solution.py:414
  65.9 5.8 %collective-permute-start.24 = (bf16[224,128]{1,0:T(8,128)(2,1)S(1)}, bf16[224,128]{1,0:T(8,128)(2,1)S(1)}, u32[]{:S(2)}, u32[]{:S(2)}) collective-permute-start(bf16[224,128]{1,0:T(8,128)(2,1)S(1)} %add_convert_fusion), channel_id=1, source_target_pairs={{0,1},{1,0},{2,3},{3,2},{4,5},{5,4},{6,7},{7,6},{8,9},{9,8},{10,11... | collective-permute-start | bytes 172040 | tf_op jit(solution)/shard_map/ppermute | solution.py:465

commit v8 on v7

--- a/solution.py
+++ b/solution.py
@@ -431,7 +431,8 @@
     packed = jnp.transpose(packed, (0, 1, 3, 2, 4)).reshape(2, 7 * channels, 4 * channels)
 
     share = lax.dynamic_index_in_dim(packed, lax.axis_index("gy") % 2, 0, keepdims=False)
-    others = [rotated(share, "segment", 4, k, 1) for k in (1, 2, 3)]
+    one, three, two = [rotated(share, "segment", 4, k, 1) for k in (1, 3, 2)]
+    others = [one, two, three]
     others += [lax.ppermute(other, "gy", swap) for other in others]
     oth = lax.ppermute(own, "gy", swap)
     oth, packed = lax.optimization_barrier((oth, packed))
@@ -453,7 +454,7 @@
     got = lax.ppermute(send, "gy", swap)
     part = [(keep[k].astype(F32) + got[k].astype(F32)).astype(BF16) for k in range(4)]
     total = part[0].astype(F32)
-    for k in (1, 2, 3):
+    for k in (2, 1, 3):
         total = total + rotated(part[k], "segment", 4, k, 1).astype(F32)
     for stride in (2, 8):
         mine = total.astype(BF16)

time: 73.7 us -> 74.1 us (level)
  starting transfers between devices: 28.4 us -> 30.7 us
  waiting for transfers between devices: 15.5 us -> 13.7 us
    ppermute x15, starting transfers between devices: 13.4 us -> 15.4 us  [rotated(): return lax.ppermute(value, axis, [(i, target(i)) for i in range(count)])]
    ppermute x15, waiting for transfers between devices: 13.1 us -> 11.3 us  [rotated(): return lax.ppermute(value, axis, [(i, target(i)) for i in range(count)])]
  transfers between devices with their start and end apart: 25 -> 25, of which waited for: 15 -> 11; matrix products, arithmetic and copies ran while one was open for 2% -> 2% of each run, Pallas kernels for 9% -> 9%
where the time goes in v8:
time: 74.1 us; the launch traced here: 73.9 us
  starting transfers between devices  30.7 us (41%)
  Pallas kernels  23.5 us (32%)
  waiting for transfers between devices  13.7 us (18%)
  local copies, waits for them, and re-layouts  3.54 us (5%)
  other arithmetic  1.64 us (2%)
  between operations  0.87 us (1%)
    ppermute x15, starting transfers between devices, rotated(): return lax.ppermute(value, axis, [(i, target(i)) for i in range(count)])  15.4 us
    pallas_call x1, Pallas kernels, main_call(): pl.pallas_call(main_kernel, out_shape=[jax.ShapeDtypeStruct((512, LANES),...  14.2 us
    ppermute x15, waiting for transfers between devices, rotated(): return lax.ppermute(value, axis, [(i, target(i)) for i in range(count)])  11.3 us
    ppermute x1, starting transfers between devices, local(): near = lax.ppermute(block, 'gy', outward(1))  6.36 us
    ppermute x1, starting transfers between devices, local(): other = lax.ppermute(mine, 'gy', swap)  5.11 us
    pallas_call x1, Pallas kernels, build_call(): pl.pallas_call(build_kernel, out_shape=[jax.ShapeDtypeStruct(MATRICES, BF...  4.83 us
    pallas_call x1, Pallas kernels, grads_call(): pl.pallas_call(grads_kernel, out_shape=[jax.ShapeDtypeStruct((224, LANES)...  2.64 us
    pallas_call x1, Pallas kernels, layout_call(): pl.pallas_call(layout_kernel, out_shape=[jax.ShapeDtypeStruct((2, 32, 4,...  1.85 us
  transfers between devices with their start and end apart: 25, of which 11 were waited for; matrix products, arithmetic and copies ran while one was open for 2% of the time, Pallas kernels for 9%

profile of v8, /device:TPU:1, one launch (start us, length us, event | category | flops | bytes accessed | tf_op | source)
XLA Modules:
  0.0 73.9 jit_solution(16646086867597725331)
XLA Ops:
  0.7 1.1 %constant_dynamic-slice_fusion.1 = (bf16[1,32,4,4,128]{4,3,2,1,0:T(4,128)(2,1)S(1)}, bf16[1,32,4,4,128]{4,3,2,1,0:T(4,128)(2,1)S(1)}) fusion(bf16[2,32,4,4,128]{4,3,2,1,0:T(4,128)(2,1)} %param.4, s32[]{:T(128)S(6)} %select_n.43, bf16[2,32,4,4,128]{4,3,2,1,0:T(4,128)(2,1)} %param.3), kind=kLoop, calls=%fused_computation.26 | loop fusion | bytes 524292 | tf_op jit(solution)/shard_map/jit(dynamic_index_in_dim)/dynamic_slice | solution.py:425
  1.8 0.1 constant_dynamic-slice_fusion
  1.9 0.1 copy.13
  2.0 0.1 constant_dynamic-slice_fusion.2
  2.2 0.1 copy.10
  2.3 1.5 %collective-permute-start = (bf16[2,320,128]{2,1,0:T(8,128)(2,1)S(1)}, bf16[2,320,128]{2,1,0:T(8,128)(2,1)S(1)}, u32[]{:S(2)}, u32[]{:S(2)}) collective-permute-start(bf16[2,320,128]{2,1,0:T(8,128)(2,1)S(1)} %pad_maximum_fusion.1.own), channel_id=1, source_target_pairs={{0,1},{1,0},{2,3},{3,2},{4,5},{5,4},{6,7},{7,6},{8,9},{9,8},{10,11... | collective-permute-start | bytes 491528 | tf_op jit(solution)/shard_map/ppermute | solution.py:437
  3.8 1.1 %pad.4 = bf16[2,28,32,32]{3,2,1,0:T(8,128)(2,1)S(1)} pad(bf16[2,27,32,32]{3,2,1,0:T(8,128)(2,1)} %bitcast.62, bf16[]{:T(256)} %constant.54.clone.1), padding=0_0x0_1x0_0x0_0 | pad | bytes 225282 | tf_op jit(solution)/shard_map/jit(_pad)/pad | solution.py:430
  4.9 0.2 copy.21
  5.1 0.2 reshape.43.pack0
  5.4 0.0 collective-permute-done.oth
  5.5 6.4 %collective-permute-start.1 = (bf16[2,640,128]{2,1,0:T(8,128)(2,1)S(1)}, bf16[2,640,128]{2,1,0:T(8,128)(2,1)S(1)}, u32[]{:S(2)}, u32[]{:S(2)}) collective-permute-start(bf16[2,640,128]{2,1,0:T(8,128)(2,1)S(1)} %pad_maximum_fusion), channel_id=1, source_target_pairs={{0,2},{1,31},{2,4},{3,1},{4,6},{5,3},{6,8},{7,5},{8,10},{9,7},{10,... | collective-permute-start | bytes 983048 | tf_op jit(solution)/shard_map/ppermute | solution.py:444
  11.8 0.1 collective-permute-start.2
  11.9 2.5 %collective-permute-start.7 = (bf16[224,128]{1,0:T(8,128)(2,1)S(1)}, bf16[224,128]{1,0:T(8,128)(2,1)S(1)}, u32[]{:S(2)}, u32[]{:S(2)}) collective-permute-start(bf16[224,128]{1,0:T(8,128)(2,1)S(1)} %dynamic-slice_bitcast_fusion), channel_id=1, source_target_pairs={{0,96},{32,0},{64,32},{96,64},{1,97},{33,1},{65,33},{97,65},{2,98}... | collective-permute-start | bytes 172040 | tf_op jit(solution)/shard_map/ppermute | solution.py:414
  14.5 0.5 collective-permute-start.6
  15.0 0.6 collective-permute-start.5
  15.6 0.3 collective-permute-done.7.half3
  15.9 0.1 collective-permute-start.10
  16.0 3.9 %collective-permute-done.6.half2 = bf16[224,128]{1,0:T(8,128)(2,1)S(1)} collective-permute-done((bf16[224,128]{1,0:T(8,128)(2,1)S(1)}, bf16[224,128]{1,0:T(8,128)(2,1)S(1)}, u32[]{:S(2)}, u32[]{:S(2)}) %collective-permute-start.6) | collective-permute-done | bytes 57376 | tf_op jit(solution)/shard_map/ppermute | solution.py:414
  19.9 0.5 collective-permute-start.9
  20.3 0.8 %collective-permute-done.5.half1 = bf16[224,128]{1,0:T(8,128)(2,1)S(1)} collective-permute-done((bf16[224,128]{1,0:T(8,128)(2,1)S(1)}, bf16[224,128]{1,0:T(8,128)(2,1)S(1)}, u32[]{:S(2)}, u32[]{:S(2)}) %collective-permute-start.5) | collective-permute-done | bytes 57376 | tf_op jit(solution)/shard_map/ppermute | solution.py:414
  21.1 0.4 collective-permute-start.8
  21.5 0.0 collective-permute-done.2.far
  21.5 0.1 collective-permute-start.4
  21.6 0.0 collective-permute-done.1.near
  21.6 0.4 collective-permute-start.3
  22.0 0.0 collective-permute-done.9.rest2
  22.0 0.4 collective-permute-done.8.rest1
  22.4 4.8 %banded.1 = (bf16[8,512,768]{2,1,0:T(8,128)(2,1)S(1)}, bf16[8,512,768]{2,1,0:T(8,128)(2,1)S(1)}) custom-call(bf16[2,224,128]{2,1,0:T(8,128)(2,1)S(1)} %reshape.43.pack0, bf16[224,128]{1,0:T(8,128)(2,1)S(1)} %collective-permute-done.5.half1, bf16[224,128]{1,0:T(8,128)(2,1)S(1)} %collective-permute-done.6.half2, ...), custom_call_target="tpu_custom_call" | custom-call | flops 5000000000 | bytes 10000000 | tf_op jit(solution)/shard_map/banded/pallas_call | solution.py:311
  27.2 0.0 collective-permute-done.4.far_other
  27.3 14.2 %sections.1 = (bf16[512,128]{1,0:T(8,128)(2,1)S(1)}, bf16[512,128]{1,0:T(8,128)(2,1)S(1)}, bf16[512,128]{1,0:T(8,128)(2,1)S(1)}, bf16[512,128]{1,0:T(8,128)(2,1)...) custom-call(bf16[2,320,128]{2,1,0:T(8,128)(2,1)S(1)} %pad_maximum_fusion.1.own, ...), custom_call_target="tpu_custom_call" | custom-call | flops 20000000000 | bytes 10000000 | tf_op jit(solution)/shard_map/sections/pallas_call | solution.py:329
  41.5 2.6 %kernel_grads.1 = (bf16[224,128]{1,0:T(8,128)(2,1)S(1)}, bf16[224,128]{1,0:T(8,128)(2,1)S(1)}, bf16[224,128]{1,0:T(8,128)(2,1)S(1)}, bf16[224,128]{1,0:T(8,128)(2,1)S(1)}, bf16[4,224,128]{2,1,0:T(8,128)(2,1)S(1)}) custom-call(bf16[8,480,128]{2,1,0:T(8,128)(2,1)S(1)} %get-tuple-element.27.windows, bf16[8,320,128]{2,1,0:T(8,128)(2,1)S(1)} %get-tuple-element.28.deltas), custom_call_target="tpu_custom_call" | custom-call | flops 6000000000 | bytes 4000000 | tf_op jit(solution)/shard_map/kernel_grads/pallas_call | solution.py:359
  44.1 0.7 collective-permute-start.11
  44.8 1.1 %collective-permute-done.11 = bf16[4,224,128]{2,1,0:T(8,128)(2,1)S(1)} collective-permute-done((bf16[4,224,128]{2,1,0:T(8,128)(2,1)S(1)}, bf16[4,224,128]{2,1,0:T(8,128)(2,1)S(1)}, u32[]{:S(2)}, u32[]{:S(2)}) %collective-permute-start.11) | collective-permute-done | bytes 229408 | tf_op jit(solution)/shard_map/ppermute | solution.py:454
  45.9 0.1 fusion.3
  46.0 0.7 collective-permute-start.12
  46.7 0.8 %collective-permute-start.14 = (bf16[224,128]{1,0:T(8,128)(2,1)S(1)}, bf16[224,128]{1,0:T(8,128)(2,1)S(1)}, u32[]{:S(2)}, u32[]{:S(2)}) collective-permute-start(bf16[224,128]{1,0:T(8,128)(2,1)S(1)} %get-tuple-element.44), channel_id=1, source_target_pairs={{0,96},{32,0},{64,32},{96,64},{1,97},{33,1},{65,33},{97,65},{2,98}... | collective-permute-start | bytes 172040 | tf_op jit(solution)/shard_map/ppermute | solution.py:414
  47.5 0.6 collective-permute-start.13
  48.2 2.5 %collective-permute-done.12 = bf16[224,128]{1,0:T(8,128)(2,1)S(1)} collective-permute-done((bf16[224,128]{1,0:T(8,128)(2,1)S(1)}, bf16[224,128]{1,0:T(8,128)(2,1)S(1)}, u32[]{:S(2)}, u32[]{:S(2)}) %collective-permute-start.12) | collective-permute-done | bytes 57376 | tf_op jit(solution)/shard_map/ppermute | solution.py:414
  50.6 1.4 %collective-permute-done.13 = bf16[224,128]{1,0:T(8,128)(2,1)S(1)} collective-permute-done((bf16[224,128]{1,0:T(8,128)(2,1)S(1)}, bf16[224,128]{1,0:T(8,128)(2,1)S(1)}, u32[]{:S(2)}, u32[]{:S(2)}) %collective-permute-start.13) | collective-permute-done | bytes 57376 | tf_op jit(solution)/shard_map/ppermute | solution.py:414
  52.1 0.6 collective-permute-start.17
  52.7 0.8 %collective-permute-start.16 = (bf16[224,128]{1,0:T(8,128)(2,1)S(1)}, bf16[224,128]{1,0:T(8,128)(2,1)S(1)}, u32[]{:S(2)}, u32[]{:S(2)}) collective-permute-start(bf16[224,128]{1,0:T(8,128)(2,1)S(1)} %add_convert_fusion.2), channel_id=1, source_target_pairs={{0,4},{1,5},{2,6},{3,7},{4,0},{5,1},{6,2},{7,3},{8,12},{9,13},{10,... | collective-permute-start | bytes 172040 | tf_op jit(solution)/shard_map/ppermute | solution.py:414
  53.5 0.8 %collective-permute-start.15 = (bf16[224,128]{1,0:T(8,128)(2,1)S(1)}, bf16[224,128]{1,0:T(8,128)(2,1)S(1)}, u32[]{:S(2)}, u32[]{:S(2)}) collective-permute-start(bf16[224,128]{1,0:T(8,128)(2,1)S(1)} %add_convert_fusion.2), channel_id=1, source_target_pairs={{0,2},{1,3},{2,4},{3,5},{4,6},{5,7},{6,0},{7,1},{8,10},{9,11},{10,... | collective-permute-start | bytes 172040 | tf_op jit(solution)/shard_map/ppermute | solution.py:414
  54.3 2.1 %collective-permute-start.22 = (bf16[512,128]{1,0:T(8,128)(2,1)S(1)}, bf16[512,128]{1,0:T(8,128)(2,1)S(1)}, u32[]{:S(2)}, u32[]{:S(2)}) collective-permute-start(bf16[512,128]{1,0:T(8,128)(2,1)S(1)} %get-tuple-element.36), channel_id=1, source_target_pairs={{0,64},{32,96},{64,0},{96,32},{1,65},{33,97},{65,1},{97,33},{2,66}... | collective-permute-start | bytes 393224 | tf_op jit(solution)/shard_map/ppermute | solution.py:414
  56.3 0.0 collective-permute-done.17
  56.3 1.0 %collective-permute-start.23 = (bf16[512,128]{1,0:T(8,128)(2,1)S(1)}, bf16[512,128]{1,0:T(8,128)(2,1)S(1)}, u32[]{:S(2)}, u32[]{:S(2)}) collective-permute-start(bf16[512,128]{1,0:T(8,128)(2,1)S(1)} %get-tuple-element.37), channel_id=1, source_target_pairs={{0,96},{32,0},{64,32},{96,64},{1,97},{33,1},{65,33},{97,65},{2,98}... | collective-permute-start | bytes 393224 | tf_op jit(solution)/shard_map/ppermute | solution.py:414
  57.3 0.0 collective-permute-done.16
  57.3 0.5 collective-permute-done.15
  57.9 3.3 %collective-permute-start.20 = (bf16[224,128]{1,0:T(8,128)(2,1)S(1)}, bf16[224,128]{1,0:T(8,128)(2,1)S(1)}, u32[]{:S(2)}, u32[]{:S(2)}) collective-permute-start(bf16[224,128]{1,0:T(8,128)(2,1)S(1)} %add_convert_fusion.1), channel_id=1, source_target_pairs={{0,24},{1,25},{2,26},{3,27},{4,28},{5,29},{6,30},{7,31},{8,0},{9,1... | collective-permute-start | bytes 172040 | tf_op jit(solution)/shard_map/ppermute | solution.py:414
  61.2 0.0 collective-permute-start.19
  61.2 0.0 collective-permute-done.21.in1
  61.2 1.0 %collective-permute-start.18 = (bf16[224,128]{1,0:T(8,128)(2,1)S(1)}, bf16[224,128]{1,0:T(8,128)(2,1)S(1)}, u32[]{:S(2)}, u32[]{:S(2)}) collective-permute-start(bf16[224,128]{1,0:T(8,128)(2,1)S(1)} %add_convert_fusion.1), channel_id=1, source_target_pairs={{0,8},{1,9},{2,10},{3,11},{4,12},{5,13},{6,14},{7,15},{8,16},{9,17... | collective-permute-start | bytes 172040 | tf_op jit(solution)/shard_map/ppermute | solution.py:414
  62.2 0.0 collective-permute-done.22.in2
  62.2 0.0 collective-permute-done.23.in3
  62.2 1.9 %layout.1 = (bf16[2,32,4,4,128]{4,3,2,1,0:T(4,128)(2,1)}, f32[2,32,4,4,128]{4,3,2,1,0:T(4,128)}) custom-call(bf16[512,128]{1,0:T(8,128)(2,1)S(1)} %get-tuple-element.34.in0, bf16[512,128]{1,0:T(8,128)(2,1)S(1)} %collective-permute-done.21.in1, bf16[512,128]{1,0:T(8,128)(2,1)S(1)} %collective-permute-done.22.in2, bf16[512,128]{1,0:T(8,128)(2,1)S(1)} %collective-permute-done.23.in3), custom_call_target="tpu_custom_call" | custom-call | flops 4000000000 | bytes 4000000 | tf_op jit(solution)/shard_map/layout/pallas_call | solution.py:392
  64.1 0.0 collective-permute-done.20
  64.1 1.7 %collective-permute-done.19 = bf16[224,128]{1,0:T(8,128)(2,1)S(1)} collective-permute-done((bf16[224,128]{1,0:T(8,128)(2,1)S(1)}, bf16[224,128]{1,0:T(8,128)(2,1)S(1)}, u32[]{:S(2)}, u32[]{:S(2)}) %collective-permute-start.19) | collective-permute-done | bytes 57376 | tf_op jit(solution)/shard_map/ppermute | solution.py:414
  65.8 0.2 collective-permute-done.18
  66.1 5.1 %collective-permute-start.24 = (bf16[224,128]{1,0:T(8,128)(2,1)S(1)}, bf16[224,128]{1,0:T(8,128)(2,1)S(1)}, u32[]{:S(2)}, u32[]{:S(2)}) collective-permute-start(bf16[224,128]{1,0:T(8,128)(2,1)S(1)} %add_convert_fusion), channel_id=1, source_target_pairs={{0,1},{1,0},{2,3},{3,2},{4,5},{5,4},{6,7},{7,6},{8,9},{9,8},{10,11... | collective-permute-start | bytes 172040 | tf_op jit(solution)/shard_map/ppermute | solution.py:466
  71.2 0.9 %collective-permute-done.24 = bf16[224,128]{1,0:T(8,128)(2,1)S(1)} collective-permute-done((bf16[224,128]{1,0:T(8,128)(2,1)S(1)}, bf16[224,128]{1,0:T(8,128)(2,1)S(1)}, u32[]{:S(2)}, u32[]{:S(2)}) %collective-permute-start.24) | collective-permute-done | bytes 57376 | tf_op jit(solution)/shard_map/ppermute | solution.py:466
  72.1 0.1 stack.13
  72.3 0.1 stack.14
  72.4 0.4 maximum_bitcast_fusion
  72.8 0.1 copy.15
  72.9 1.0 %fusion = f32[1,2,27,32,32]{4,3,2,1,0:T(8,128)} fusion(bf16[2,28,32,32]{3,2,1,0:T(8,128)(2,1)S(1)} %bitcast.55), kind=kLoop, calls=%fused_computation.3 | loop fusion | flops 55296 | bytes 331776 | tf_op jit(solution)/shard_map/broadcast_in_dim | solution.py:473
  (14 shorter events, 0.3 us)
Async XLA Ops:
  2.3 3.1 %collective-permute-start = (bf16[2,320,128]{2,1,0:T(8,128)(2,1)S(1)}, bf16[2,320,128]{2,1,0:T(8,128)(2,1)S(1)}, u32[]{:S(2)}, u32[]{:S(2)}) collective-permute-start(bf16[2,320,128]{2,1,0:T(8,128)(2,1)S(1)} %pad_maximum_fusion.1.own), channel_id=1, source_target_pairs={{0,1},{1,0},{2,3},{3,2},{4,5},{5,4},{6,7},{7,6},{8,9},{9,8},{10,11... | collective-permute-start | bytes 491528 | tf_op jit(solution)/shard_map/ppermute | solution.py:437
  5.5 16.2 %collective-permute-start.1 = (bf16[2,640,128]{2,1,0:T(8,128)(2,1)S(1)}, bf16[2,640,128]{2,1,0:T(8,128)(2,1)S(1)}, u32[]{:S(2)}, u32[]{:S(2)}) collective-permute-start(bf16[2,640,128]{2,1,0:T(8,128)(2,1)S(1)} %pad_maximum_fusion), channel_id=1, source_target_pairs={{0,2},{1,31},{2,4},{3,1},{4,6},{5,3},{6,8},{7,5},{8,10},{9,7},{10,... | collective-permute-start | bytes 983048 | tf_op jit(solution)/shard_map/ppermute | solution.py:444
  11.8 9.7 %collective-permute-start.2 = (bf16[640,128]{1,0:T(8,128)(2,1)S(1)}, bf16[640,128]{1,0:T(8,128)(2,1)S(1)}, u32[]{:S(2)}, u32[]{:S(2)}) collective-permute-start(bf16[640,128]{1,0:T(8,128)(2,1)S(1)} %slice_bitcast_fusion.1), channel_id=1, source_target_pairs={{0,4},{1,29},{2,6},{3,31},{4,8},{5,1},{6,10},{7,3},{8,12},{9,5},{1... | collective-permute-start | bytes 491528 | tf_op jit(solution)/shard_map/ppermute | solution.py:445
  11.9 4.0 %collective-permute-start.7 = (bf16[224,128]{1,0:T(8,128)(2,1)S(1)}, bf16[224,128]{1,0:T(8,128)(2,1)S(1)}, u32[]{:S(2)}, u32[]{:S(2)}) collective-permute-start(bf16[224,128]{1,0:T(8,128)(2,1)S(1)} %dynamic-slice_bitcast_fusion), channel_id=1, source_target_pairs={{0,96},{32,0},{64,32},{96,64},{1,97},{33,1},{65,33},{97,65},{2,98}... | collective-permute-start | bytes 172040 | tf_op jit(solution)/shard_map/ppermute | solution.py:414
  14.5 5.4 %collective-permute-start.6 = (bf16[224,128]{1,0:T(8,128)(2,1)S(1)}, bf16[224,128]{1,0:T(8,128)(2,1)S(1)}, u32[]{:S(2)}, u32[]{:S(2)}) collective-permute-start(bf16[224,128]{1,0:T(8,128)(2,1)S(1)} %dynamic-slice_bitcast_fusion), channel_id=1, source_target_pairs={{0,64},{32,96},{64,0},{96,32},{1,65},{33,97},{65,1},{97,33},{2,66}... | collective-permute-start | bytes 172040 | tf_op jit(solution)/shard_map/ppermute | solution.py:414
  15.0 6.1 %collective-permute-start.5 = (bf16[224,128]{1,0:T(8,128)(2,1)S(1)}, bf16[224,128]{1,0:T(8,128)(2,1)S(1)}, u32[]{:S(2)}, u32[]{:S(2)}) collective-permute-start(bf16[224,128]{1,0:T(8,128)(2,1)S(1)} %dynamic-slice_bitcast_fusion), channel_id=1, source_target_pairs={{0,32},{32,64},{64,96},{96,0},{1,33},{33,65},{65,97},{97,1},{2,34}... | collective-permute-start | bytes 172040 | tf_op jit(solution)/shard_map/ppermute | solution.py:414
  15.9 6.1 %collective-permute-start.10 = (bf16[224,128]{1,0:T(8,128)(2,1)S(1)}, bf16[224,128]{1,0:T(8,128)(2,1)S(1)}, u32[]{:S(2)}, u32[]{:S(2)}) collective-permute-start(bf16[224,128]{1,0:T(8,128)(2,1)S(1)} %collective-permute-done.7.half3), channel_id=1, source_target_pairs={{0,1},{1,0},{2,3},{3,2},{4,5},{5,4},{6,7},{7,6},{8,9},{9,8},{10,11... | collective-permute-start | bytes 172040 | tf_op jit(solution)/shard_map/ppermute | solution.py:436
  19.9 2.2 %collective-permute-start.9 = (bf16[224,128]{1,0:T(8,128)(2,1)S(1)}, bf16[224,128]{1,0:T(8,128)(2,1)S(1)}, u32[]{:S(2)}, u32[]{:S(2)}) collective-permute-start(bf16[224,128]{1,0:T(8,128)(2,1)S(1)} %collective-permute-done.6.half2), channel_id=1, source_target_pairs={{0,1},{1,0},{2,3},{3,2},{4,5},{5,4},{6,7},{7,6},{8,9},{9,8},{10,11... | collective-permute-start | bytes 172040 | tf_op jit(solution)/shard_map/ppermute | solution.py:436
  21.1 1.3 %collective-permute-start.8 = (bf16[224,128]{1,0:T(8,128)(2,1)S(1)}, bf16[224,128]{1,0:T(8,128)(2,1)S(1)}, u32[]{:S(2)}, u32[]{:S(2)}) collective-permute-start(bf16[224,128]{1,0:T(8,128)(2,1)S(1)} %collective-permute-done.5.half1), channel_id=1, source_target_pairs={{0,1},{1,0},{2,3},{3,2},{4,5},{5,4},{6,7},{7,6},{8,9},{9,8},{10,11... | collective-permute-start | bytes 172040 | tf_op jit(solution)/shard_map/ppermute | solution.py:436
  21.5 5.7 %collective-permute-start.4 = (bf16[640,128]{1,0:T(8,128)(2,1)S(1)}, bf16[640,128]{1,0:T(8,128)(2,1)S(1)}, u32[]{:S(2)}, u32[]{:S(2)}) collective-permute-start(bf16[640,128]{1,0:T(8,128)(2,1)S(1)} %collective-permute-done.2.far), channel_id=1, source_target_pairs={{0,1},{1,0},{2,3},{3,2},{4,5},{5,4},{6,7},{7,6},{8,9},{9,8},{10,11... | collective-permute-start | bytes 491528 | tf_op jit(solution)/shard_map/ppermute | solution.py:448
  21.6 5.6 %collective-permute-start.3 = (bf16[2,640,128]{2,1,0:T(8,128)(2,1)S(1)}, bf16[2,640,128]{2,1,0:T(8,128)(2,1)S(1)}, u32[]{:S(2)}, u32[]{:S(2)}) collective-permute-start(bf16[2,640,128]{2,1,0:T(8,128)(2,1)S(1)} %collective-permute-done.1.near), channel_id=1, source_target_pairs={{0,1},{1,0},{2,3},{3,2},{4,5},{5,4},{6,7},{7,6},{8,9},{9,8},{10,11... | collective-permute-start | bytes 983048 | tf_op jit(solution)/shard_map/ppermute | solution.py:447
  44.1 1.9 %collective-permute-start.11 = (bf16[4,224,128]{2,1,0:T(8,128)(2,1)S(1)}, bf16[4,224,128]{2,1,0:T(8,128)(2,1)S(1)}, u32[]{:S(2)}, u32[]{:S(2)}) collective-permute-start(bf16[4,224,128]{2,1,0:T(8,128)(2,1)S(1)} %get-tuple-element.30), channel_id=1, source_target_pairs={{0,1},{1,0},{2,3},{3,2},{4,5},{5,4},{6,7},{7,6},{8,9},{9,8},{10,11... | collective-permute-start | bytes 688136 | tf_op jit(solution)/shard_map/ppermute | solution.py:454
  46.0 4.6 %collective-permute-start.12 = (bf16[224,128]{1,0:T(8,128)(2,1)S(1)}, bf16[224,128]{1,0:T(8,128)(2,1)S(1)}, u32[]{:S(2)}, u32[]{:S(2)}) collective-permute-start(bf16[224,128]{1,0:T(8,128)(2,1)S(1)} %get-tuple-element.43), channel_id=1, source_target_pairs={{0,64},{32,96},{64,0},{96,32},{1,65},{33,97},{65,1},{97,33},{2,66}... | collective-permute-start | bytes 172040 | tf_op jit(solution)/shard_map/ppermute | solution.py:414
  46.7 3.9 %collective-permute-start.14 = (bf16[224,128]{1,0:T(8,128)(2,1)S(1)}, bf16[224,128]{1,0:T(8,128)(2,1)S(1)}, u32[]{:S(2)}, u32[]{:S(2)}) collective-permute-start(bf16[224,128]{1,0:T(8,128)(2,1)S(1)} %get-tuple-element.44), channel_id=1, source_target_pairs={{0,96},{32,0},{64,32},{96,64},{1,97},{33,1},{65,33},{97,65},{2,98}... | collective-permute-start | bytes 172040 | tf_op jit(solution)/shard_map/ppermute | solution.py:414
  47.5 4.5 %collective-permute-start.13 = (bf16[224,128]{1,0:T(8,128)(2,1)S(1)}, bf16[224,128]{1,0:T(8,128)(2,1)S(1)}, u32[]{:S(2)}, u32[]{:S(2)}) collective-permute-start(bf16[224,128]{1,0:T(8,128)(2,1)S(1)} %get-tuple-element.45), channel_id=1, source_target_pairs={{0,32},{32,64},{64,96},{96,0},{1,33},{33,65},{65,97},{97,1},{2,34}... | collective-permute-start | bytes 172040 | tf_op jit(solution)/shard_map/ppermute | solution.py:414
  52.1 4.2 %collective-permute-start.17 = (bf16[224,128]{1,0:T(8,128)(2,1)S(1)}, bf16[224,128]{1,0:T(8,128)(2,1)S(1)}, u32[]{:S(2)}, u32[]{:S(2)}) collective-permute-start(bf16[224,128]{1,0:T(8,128)(2,1)S(1)} %add_convert_fusion.2), channel_id=1, source_target_pairs={{0,6},{1,7},{2,0},{3,1},{4,2},{5,3},{6,4},{7,5},{8,14},{9,15},{10,... | collective-permute-start | bytes 172040 | tf_op jit(solution)/shard_map/ppermute | solution.py:414
  52.7 4.7 %collective-permute-start.16 = (bf16[224,128]{1,0:T(8,128)(2,1)S(1)}, bf16[224,128]{1,0:T(8,128)(2,1)S(1)}, u32[]{:S(2)}, u32[]{:S(2)}) collective-permute-start(bf16[224,128]{1,0:T(8,128)(2,1)S(1)} %add_convert_fusion.2), channel_id=1, source_target_pairs={{0,4},{1,5},{2,6},{3,7},{4,0},{5,1},{6,2},{7,3},{8,12},{9,13},{10,... | collective-permute-start | bytes 172040 | tf_op jit(solution)/shard_map/ppermute | solution.py:414
  53.5 4.3 %collective-permute-start.15 = (bf16[224,128]{1,0:T(8,128)(2,1)S(1)}, bf16[224,128]{1,0:T(8,128)(2,1)S(1)}, u32[]{:S(2)}, u32[]{:S(2)}) collective-permute-start(bf16[224,128]{1,0:T(8,128)(2,1)S(1)} %add_convert_fusion.2), channel_id=1, source_target_pairs={{0,2},{1,3},{2,4},{3,5},{4,6},{5,7},{6,0},{7,1},{8,10},{9,11},{10,... | collective-permute-start | bytes 172040 | tf_op jit(solution)/shard_map/ppermute | solution.py:414
  54.3 6.9 %collective-permute-start.21 = (bf16[512,128]{1,0:T(8,128)(2,1)S(1)}, bf16[512,128]{1,0:T(8,128)(2,1)S(1)}, u32[]{:S(2)}, u32[]{:S(2)}) collective-permute-start(bf16[512,128]{1,0:T(8,128)(2,1)S(1)} %get-tuple-element.35), channel_id=1, source_target_pairs={{0,32},{32,64},{64,96},{96,0},{1,33},{33,65},{65,97},{97,1},{2,34}... | collective-permute-start | bytes 393224 | tf_op jit(solution)/shard_map/ppermute | solution.py:414
  54.3 8.0 %collective-permute-start.22 = (bf16[512,128]{1,0:T(8,128)(2,1)S(1)}, bf16[512,128]{1,0:T(8,128)(2,1)S(1)}, u32[]{:S(2)}, u32[]{:S(2)}) collective-permute-start(bf16[512,128]{1,0:T(8,128)(2,1)S(1)} %get-tuple-element.36), channel_id=1, source_target_pairs={{0,64},{32,96},{64,0},{96,32},{1,65},{33,97},{65,1},{97,33},{2,66}... | collective-permute-start | bytes 393224 | tf_op jit(solution)/shard_map/ppermute | solution.py:414
  56.3 5.9 %collective-permute-start.23 = (bf16[512,128]{1,0:T(8,128)(2,1)S(1)}, bf16[512,128]{1,0:T(8,128)(2,1)S(1)}, u32[]{:S(2)}, u32[]{:S(2)}) collective-permute-start(bf16[512,128]{1,0:T(8,128)(2,1)S(1)} %get-tuple-element.37), channel_id=1, source_target_pairs={{0,96},{32,0},{64,32},{96,64},{1,97},{33,1},{65,33},{97,65},{2,98}... | collective-permute-start | bytes 393224 | tf_op jit(solution)/shard_map/ppermute | solution.py:414
  57.9 6.2 %collective-permute-start.20 = (bf16[224,128]{1,0:T(8,128)(2,1)S(1)}, bf16[224,128]{1,0:T(8,128)(2,1)S(1)}, u32[]{:S(2)}, u32[]{:S(2)}) collective-permute-start(bf16[224,128]{1,0:T(8,128)(2,1)S(1)} %add_convert_fusion.1), channel_id=1, source_target_pairs={{0,24},{1,25},{2,26},{3,27},{4,28},{5,29},{6,30},{7,31},{8,0},{9,1... | collective-permute-start | bytes 172040 | tf_op jit(solution)/shard_map/ppermute | solution.py:414
  61.2 4.6 %collective-permute-start.19 = (bf16[224,128]{1,0:T(8,128)(2,1)S(1)}, bf16[224,128]{1,0:T(8,128)(2,1)S(1)}, u32[]{:S(2)}, u32[]{:S(2)}) collective-permute-start(bf16[224,128]{1,0:T(8,128)(2,1)S(1)} %add_convert_fusion.1), channel_id=1, source_target_pairs={{0,16},{1,17},{2,18},{3,19},{4,20},{5,21},{6,22},{7,23},{8,24},{9,... | collective-permute-start | bytes 172040 | tf_op jit(solution)/shard_map/ppermute | solution.py:414
  61.2 4.9 %collective-permute-start.18 = (bf16[224,128]{1,0:T(8,128)(2,1)S(1)}, bf16[224,128]{1,0:T(8,128)(2,1)S(1)}, u32[]{:S(2)}, u32[]{:S(2)}) collective-permute-start(bf16[224,128]{1,0:T(8,128)(2,1)S(1)} %add_convert_fusion.1), channel_id=1, source_target_pairs={{0,8},{1,9},{2,10},{3,11},{4,12},{5,13},{6,14},{7,15},{8,16},{9,17... | collective-permute-start | bytes 172040 | tf_op jit(solution)/shard_map/ppermute | solution.py:414
  66.1 6.0 %collective-permute-start.24 = (bf16[224,128]{1,0:T(8,128)(2,1)S(1)}, bf16[224,128]{1,0:T(8,128)(2,1)S(1)}, u32[]{:S(2)}, u32[]{:S(2)}) collective-permute-start(bf16[224,128]{1,0:T(8,128)(2,1)S(1)} %add_convert_fusion), channel_id=1, source_target_pairs={{0,1},{1,0},{2,3},{3,2},{4,5},{5,4},{6,7},{7,6},{8,9},{9,8},{10,11... | collective-permute-start | bytes 172040 | tf_op jit(solution)/shard_map/ppermute | solution.py:466
